TPU v7x, 512 devices: a whole 4x4x16 slice. The times are simulated.
512 devices in a mesh: tile: 32 (over y, x, core), feat: 16 (over z).
Axes of the slice: x: 4, y: 4, z: 16, core: 2. Of those that a mesh axis runs over, the one named last changes fastest.
Arguments:
- gen_points: bfloat16 [6144, 1024], P('tile', 'feat')
- reference_embeddings: bfloat16 [6144, 1024], P('tile', 'feat')
- gen_count: int32 [32], replicated, may hold values from 1 to 192, 4608 in all
- ref_count: int32 [32], replicated, may hold values from 1 to 192, 4608 in all
Outputs:
- gen_pot: float32 [6144], P('tile')
- ref_pot: float32 [6144], P('tile')
- gen_self: float32 [6144], P('tile')
- ref_self: float32 [6144], P('tile')
- divergence: float32 [], replicated
Inputs may be any that keep to these rules, and one draw needn't show every extreme that they name: The valid generated points of a block are its first gen_count entries; the counts sum to 4608 and some block is full. The valid reference points of a block are its first ref_count entries; the counts sum to 4608 and some block is full.
All inputs are finite; a program needn't handle non-finite values.
Results may differ from a plain program's by a relative error of at most 0.0003.
Values may be sent and summed in bfloat16 or wider, within the bound.
No kernel may reach another device: no remote copies, remote signals or barrier semaphores. Data moves between devices by JAX's collectives and lax.ppermute only.
A program may use at most 64 MiB of HBM per device.

v0:
```python
import jax
import jax.numpy as jnp
from jax import lax
from jax.sharding import PartitionSpec as P

ITERS = 3


epsilon = 0.25
far_below = -1e30


def merged_2(value, axis, join):
    pieces = jax.tree.map(lambda part: lax.all_gather(part, axis), value)
    head = jax.tree.map(lambda part: part[0], pieces)
    tail = jax.tree.map(lambda part: part[1:], pieces)
    so_far, _ = lax.scan(lambda so_far, section: (join(so_far, section), None), head, tail)
    return so_far


def cost_over_epsilon(row_points, row_norms, col_points, col_norms):
    inner_prod = lax.dot_general(
        row_points, col_points, (((1,), (1,)), ((), ())), preferred_element_type=jnp.float32
    )
    return (0.5 * row_norms[:, None] + 0.5 * col_norms[None, :] - inner_prod) / epsilon


def row_portion(scores):
    highest = jnp.max(scores, axis=1)
    return (highest, jnp.sum(jnp.exp(scores - highest[:, None]), axis=1))


def column_part(scores):
    highest = jnp.max(scores, axis=0)
    return (highest, jnp.sum(jnp.exp(scores - highest[None, :]), axis=0))


def joined(first_high, first_mass, second_high, second_mass):
    highest = jnp.maximum(first_high, second_high)
    return (
        highest,
        first_mass * jnp.exp(first_high - highest) + second_mass * jnp.exp(second_high - highest),
    )


def combine_pairs(left_parts, right_parts):
    result = []
    for position in range(0, len(left_parts), 2):
        result.extend(
            joined(
                left_parts[position],
                left_parts[position + 1],
                right_parts[position],
                right_parts[position + 1],
            )
        )
    return tuple(result)


def settle(highest, amount):
    return -(highest + jnp.log(amount))


def local(gen_points, reference_embeddings, gen_count, ref_count):
    tile_count = lax.axis_size("tile")
    feat_count = lax.axis_size("feat")
    tile_id = lax.axis_index("tile")
    feat_id = lax.axis_index("feat")
    rows_t = gen_points.shape[0]
    local_d = gen_points.shape[1]
    piece_rows = rows_t // feat_count
    full_width = local_d * feat_count
    groups = tile_count * piece_rows
    stacked = jnp.stack([gen_points, reference_embeddings])
    row_full = lax.all_gather(stacked, "feat", axis=2, tiled=True)
    every_row = lax.all_gather(stacked, "tile", axis=1, tiled=True)
    arrived = lax.all_to_all(
        every_row.reshape(2, tile_count, feat_count, piece_rows, local_d),
        "feat",
        split_axis=2,
        concat_axis=4,
        tiled=True,
    )
    col_full = arrived.reshape(2, groups, full_width)
    row_norms = jnp.sum(jnp.square(row_full.astype(jnp.float32)), axis=2)
    col_norms = jnp.sum(jnp.square(col_full.astype(jnp.float32)), axis=2)
    counts = jnp.stack([gen_count, ref_count])
    row_ok = jnp.arange(rows_t, dtype=jnp.int32)[None, :] < lax.dynamic_slice_in_dim(
        counts, tile_id, 1, 1
    )
    col_offsets = feat_id * piece_rows + jnp.arange(piece_rows, dtype=jnp.int32)
    col_ok = (col_offsets[None, None, :] < counts[:, :, None]).reshape(2, groups)
    point_totals = jnp.sum(counts, axis=1).astype(jnp.float32)
    log_weight = -jnp.log(point_totals)
    gen_row = jnp.zeros((rows_t,), jnp.float32)
    ref_col = jnp.zeros((groups,), jnp.float32)
    self_row = jnp.zeros((2, rows_t), jnp.float32)
    self_col = jnp.zeros((2, groups), jnp.float32)
    for sweep_index in range(ITERS + 1):
        ref_lift = jnp.where(col_ok[1], ref_col + log_weight[1], far_below)
        gen_lift = jnp.where(row_ok[0], gen_row + log_weight[0], far_below)
        lifted_cols = jnp.where(col_ok, self_col + log_weight[:, None], far_below)
        cross_cost = cost_over_epsilon(row_full[0], row_norms[0], col_full[1], col_norms[1])
        gen_high, gen_mass = row_portion(ref_lift[None, :] - cross_cost)
        cross_high, cross_mass = column_part(gen_lift[:, None] - cross_cost)
        ref_high, ref_mass = merged_2((cross_high, cross_mass), "tile", combine_pairs)
        self_parts = []
        for member in range(2):
            member_cost = cost_over_epsilon(
                row_full[member], row_norms[member], col_full[member], col_norms[member]
            )
            self_parts.extend(row_portion(lifted_cols[member][None, :] - member_cost))
        merged = merged_2(
            (gen_high, gen_mass, self_parts[0], self_parts[1], self_parts[2], self_parts[3]),
            "feat",
            combine_pairs,
        )
        gen_new = settle(merged[0], merged[1])
        ref_new = settle(ref_high, ref_mass)
        self_new = jnp.stack([settle(merged[2], merged[3]), settle(merged[4], merged[5])])
        if sweep_index == 0:
            gen_row = gen_new
            ref_col = ref_new
            self_row = self_new
        else:
            gen_row = 0.5 * (gen_row + gen_new)
            ref_col = 0.5 * (ref_col + ref_new)
            self_row = 0.5 * (self_row + self_new)
        if sweep_index < ITERS:
            own_pieces = lax.dynamic_slice_in_dim(self_row, feat_id * piece_rows, piece_rows, 1)
            self_col = lax.all_gather(own_pieces, "tile", axis=1, tiled=True)
    ref_piece = lax.dynamic_slice_in_dim(ref_col, tile_id * piece_rows, piece_rows, 0)
    ref_row = lax.all_gather(ref_piece, "feat", axis=0, tiled=True)
    loss_sums = lax.psum(
        (
            jnp.sum(jnp.where(row_ok[0], gen_row - self_row[0], 0.0)),
            jnp.sum(jnp.where(row_ok[1], ref_row - self_row[1], 0.0)),
        ),
        "tile",
    )
    divergence = loss_sums[0] / point_totals[0] + loss_sums[1] / point_totals[1]
    return (gen_row, ref_row, self_row[0], self_row[1], divergence)


def solution(mesh):
    placed = (P("tile", "feat"), P("tile", "feat"), P(), P())
    return jax.shard_map(
        local,
        mesh=mesh,
        in_specs=placed,
        out_specs=(P("tile"), P("tile"), P("tile"), P("tile"), P()),
        check_vma=False,
    )
```

profile of v0, /device:TPU:1, one launch (start us, length us, event | category | flops | bytes accessed | tf_op | source)
XLA Modules:
  0.0 1142.3 jit_solution(3601883949369531447)
XLA Ops:
  8.8 68.6 %all-gather.45.cloned.1.call-done = bf16[2,6144,64]{2,0,1:T(2,128)(2,1)} async-done(((bf16[2,192,64]{2,0,1:T(2,128)(2,1)}), bf16[2,6144,64]{2,0,1:T(2,128)(2,1)}) %all-gather.45.cloned.1.call-update) | async-done | bytes 1572880 | tf_op jit(solution)/shard_map/all_gather | solution.py:76
  77.3 4.8 copy.75
  82.1 3.3 reshape.430
  85.4 12.0 %all-to-all-start = ((bf16[16,2,24576]{2,1,0:T(2,128)(2,1)}), bf16[16,2,24576]{2,1,0:T(2,128)(2,1)}, u32[]{:S(2)}, u32[]{:S(2)}) async-start(bf16[16,2,24576]{2,1,0:T(2,128)(2,1)} %reshape.430), calls=%async_computation | async-start | bytes 3145728 | tf_op jit(solution)/shard_map/all_to_all | solution.py:77
  102.7 89.4 %all_gather.210 = bf16[2,192,1024]{1,2,0:T(8,128)(2,1)S(1)} all-gather(bf16[2,192,64]{1,2,0:T(8,128)(2,1)S(1)} %pad_maximum_fusion), channel_id=1, replica_groups=mesh['tile'=32,'feat'=16] {'feat'}, dimensions={2}, use_global_device_ids=true | all-gather | bytes 835584 | tf_op jit(solution)/shard_map/all_gather | solution.py:75
  195.3 3.8 reshape.431
  199.0 5.1 multiply_reduce_fusion
  204.2 2.0 copy.66
  209.8 2.0 subtract_reduce_fusion.12
  212.6 29.9 %all-gather.33 = f32[32,1,384]{2,1,0:T(1,128)S(1)} all-gather(f32[1,1,384]{2,1,0:T(1,128)S(1)} %reshape.307), channel_id=9, replica_groups=mesh['tile'=32,'feat'=16] {'tile'}, dimensions={0}, use_global_device_ids=true | all-gather | bytes 50688 | tf_op jit(solution)/shard_map/all_gather | solution.py:14
  243.1 22.3 %all-gather.32 = f32[32,1,384]{2,1,0:T(1,128)S(1)} all-gather(f32[1,1,384]{2,1,0:T(1,128)S(1)} %reshape.305), channel_id=8, replica_groups=mesh['tile'=32,'feat'=16] {'tile'}, dimensions={0}, use_global_device_ids=true | all-gather | bytes 50688 | tf_op jit(solution)/shard_map/all_gather | solution.py:14
  275.5 1.9 while.129
  277.5 118.5 %all-reduce.41.cloned.1.call-done = (f32[3072]{0:T(1024)}, f32[3072]{0:T(1024)}, f32[3072]{0:T(1024)}, f32[3072]{0:T(1024)}, f32[3072]{0:T(1024)}, /*index=5*/f32[3072]{0:T(1024)}) async-done(((f32[3072]{0:T(1024)}, f32[3072]{0:T(1024)}, f32[3072]{0:T(1024)}, f32[3072]{0:T(1024)}, f32[3072]{0:T(1024)}, /*index=5*/f32[3072]{0:T(1024)}), (f32[3072]{0:T(1024)}, f32[3072]{0:T(1024)}, f32[3072]{0:T(1024)}, ...) | async-done | bytes 73744
  405.1 2.0 while.128
  408.0 35.2 %all-gather.36 = f32[32,1,384]{2,1,0:T(1,128)S(1)} all-gather(f32[1,1,384]{2,1,0:T(1,128)S(1)} %reshape.313), channel_id=17, replica_groups=mesh['tile'=32,'feat'=16] {'tile'}, dimensions={0}, use_global_device_ids=true | all-gather | bytes 50688 | tf_op jit(solution)/shard_map/all_gather | solution.py:14
  443.2 23.5 %all-gather.35 = f32[32,1,384]{2,1,0:T(1,128)S(1)} all-gather(f32[1,1,384]{2,1,0:T(1,128)S(1)} %reshape.311), channel_id=16, replica_groups=mesh['tile'=32,'feat'=16] {'tile'}, dimensions={0}, use_global_device_ids=true | all-gather | bytes 50688 | tf_op jit(solution)/shard_map/all_gather | solution.py:14
  466.9 21.9 %all-gather.34 = f32[32,12,2]{1,2,0:T(2,128)S(1)} all-gather(f32[1,12,2]{1,2,0:T(2,128)S(1)} %fusion.11), channel_id=1, replica_groups=mesh['tile'=32,'feat'=16] {'tile'}, dimensions={0}, use_global_device_ids=true | all-gather | bytes 3168 | tf_op jit(solution)/shard_map/all_gather | solution.py:131
  490.3 1.9 while.131
  496.4 116.2 %all-reduce.39.cloned.1.call-done = (f32[3072]{0:T(1024)}, f32[3072]{0:T(1024)}, f32[3072]{0:T(1024)}, f32[3072]{0:T(1024)}, f32[3072]{0:T(1024)}, /*index=5*/f32[3072]{0:T(1024)}) async-done(((f32[3072]{0:T(1024)}, f32[3072]{0:T(1024)}, f32[3072]{0:T(1024)}, f32[3072]{0:T(1024)}, f32[3072]{0:T(1024)}, /*index=5*/f32[3072]{0:T(1024)}), (f32[3072]{0:T(1024)}, f32[3072]{0:T(1024)}, f32[3072]{0:T(1024)}, ...) | async-done | bytes 73744
  621.7 2.0 while.130
  623.9 35.1 %all-gather.37 = f32[32,12,2]{1,2,0:T(2,128)S(1)} all-gather(f32[1,12,2]{1,2,0:T(2,128)S(1)} %fusion.8), channel_id=1, replica_groups=mesh['tile'=32,'feat'=16] {'tile'}, dimensions={0}, use_global_device_ids=true | all-gather | bytes 3168 | tf_op jit(solution)/shard_map/all_gather | solution.py:131
  662.3 116.7 %all-reduce.37.cloned.1.call-done = (f32[3072]{0:T(1024)}, f32[3072]{0:T(1024)}, f32[3072]{0:T(1024)}, f32[3072]{0:T(1024)}, f32[3072]{0:T(1024)}, /*index=5*/f32[3072]{0:T(1024)}) async-done(((f32[3072]{0:T(1024)}, f32[3072]{0:T(1024)}, f32[3072]{0:T(1024)}, f32[3072]{0:T(1024)}, f32[3072]{0:T(1024)}, /*index=5*/f32[3072]{0:T(1024)}), (f32[3072]{0:T(1024)}, f32[3072]{0:T(1024)}, f32[3072]{0:T(1024)}, ...) | async-done | bytes 73744
  788.2 2.0 while.132
  791.2 35.4 %all-gather.39 = f32[32,1,384]{2,1,0:T(1,128)S(1)} all-gather(f32[1,1,384]{2,1,0:T(1,128)S(1)} %reshape.319), channel_id=25, replica_groups=mesh['tile'=32,'feat'=16] {'tile'}, dimensions={0}, use_global_device_ids=true | all-gather | bytes 50688 | tf_op jit(solution)/shard_map/all_gather | solution.py:14
  826.7 23.5 %all-gather.42 = f32[32,1,384]{2,1,0:T(1,128)S(1)} all-gather(f32[1,1,384]{2,1,0:T(1,128)S(1)} %reshape.325), channel_id=33, replica_groups=mesh['tile'=32,'feat'=16] {'tile'}, dimensions={0}, use_global_device_ids=true | all-gather | bytes 50688 | tf_op jit(solution)/shard_map/all_gather | solution.py:14
  850.2 21.9 %all-gather.38 = f32[32,1,384]{2,1,0:T(1,128)S(1)} all-gather(f32[1,1,384]{2,1,0:T(1,128)S(1)} %reshape.317), channel_id=24, replica_groups=mesh['tile'=32,'feat'=16] {'tile'}, dimensions={0}, use_global_device_ids=true | all-gather | bytes 50688 | tf_op jit(solution)/shard_map/all_gather | solution.py:14
  872.2 23.5 %all-gather.41 = f32[32,1,384]{2,1,0:T(1,128)S(1)} all-gather(f32[1,1,384]{2,1,0:T(1,128)S(1)} %reshape.323), channel_id=32, replica_groups=mesh['tile'=32,'feat'=16] {'tile'}, dimensions={0}, use_global_device_ids=true | all-gather | bytes 50688 | tf_op jit(solution)/shard_map/all_gather | solution.py:14
  895.9 21.9 %all-gather.40 = f32[32,12,2]{1,2,0:T(2,128)S(1)} all-gather(f32[1,12,2]{1,2,0:T(2,128)S(1)} %fusion.9), channel_id=1, replica_groups=mesh['tile'=32,'feat'=16] {'tile'}, dimensions={0}, use_global_device_ids=true | all-gather | bytes 3168 | tf_op jit(solution)/shard_map/all_gather | solution.py:131
  921.2 1.9 while.135
  926.7 117.5 %all-reduce.35.cloned.1.call-done = (f32[3072]{0:T(1024)}, f32[3072]{0:T(1024)}, f32[3072]{0:T(1024)}, f32[3072]{0:T(1024)}, f32[3072]{0:T(1024)}, /*index=5*/f32[3072]{0:T(1024)}, f32[192]{0:T(256)}) async-done(((f32[3072]{0:T(1024)}, f32[3072]{0:T(1024)}, f32[3072]{0:T(1024)}, f32[3072]{0:T(1024)}, f32[3072]{0:T(1024)}, /*index=5*/f32[3072]{0:T(1024)}, f32[192]{0:T(256)}), (f32[3072]{0:T(1024)}, ...) | async-done | bytes 74512
  1053.3 2.0 while.134
  1057.3 73.5 %all-reduce.25 = (f32[]{:T(128)}, f32[]{:T(128)}) all-reduce(f32[]{:T(128)} %get-tuple-element.662, f32[]{:T(128)} %get-tuple-element.724), channel_id=1, replica_groups=mesh['tile'=32,'feat'=16] {'tile'}, use_global_device_ids=true, to_apply=%region_52.53 | all-reduce | flops 2 | bytes 16 | tf_op jit(solution)/shard_map/psum | solution.py:134
  (974 shorter events, 93.1 us)
Async XLA Ops:
  7.2 70.2 %all-gather.45.cloned.1.call-start = ((), (), s32[]{:S(2)}) async-start(), calls=%async_computation.1 | async-start | bytes 3244032 | tf_op jit(solution)/shard_map/all_gather | solution.py:76
  82.1 15.3 %copy-start.49 = (s32[32]{0:T(128)S(1)}, s32[32]{0:T(128)}, u32[]{:S(2)}) copy-start(s32[32]{0:T(128)} %param.23) | copy-start | bytes 388
  82.1 15.3 %copy-start.50 = (s32[32]{0:T(128)S(1)}, s32[32]{0:T(128)}, u32[]{:S(2)}) copy-start(s32[32]{0:T(128)} %param.22) | copy-start | bytes 388
  85.4 109.9 %all-to-all-start = ((bf16[16,2,24576]{2,1,0:T(2,128)(2,1)}), bf16[16,2,24576]{2,1,0:T(2,128)(2,1)}, u32[]{:S(2)}, u32[]{:S(2)}) async-start(bf16[16,2,24576]{2,1,0:T(2,128)(2,1)} %reshape.430), calls=%async_computation | async-start | bytes 3145728 | tf_op jit(solution)/shard_map/all_to_all | solution.py:77
  97.4 298.5 %all-reduce.41.cloned.1.call-start = ((), (), s32[]{:S(2)}) async-start(), calls=%async_computation.5 | async-start | bytes 147456
  98.0 101.1 %copy-start.37 = (pred[384]{0:T(512)(128)(4,1)}, pred[384]{0:T(512)(128)(4,1)S(1)}, u32[]{:S(2)}) copy-start(pred[384]{0:T(512)(128)(4,1)S(1)} %squeeze.268) | copy-start | bytes 1156
  101.5 91.9 %copy-start.33 = (pred[192]{0:T(512)(128)(4,1)}, pred[192]{0:T(512)(128)(4,1)S(1)}, u32[]{:S(2)}) copy-start(pred[192]{0:T(512)(128)(4,1)S(1)} %get-tuple-element.458) | copy-start | bytes 580
  195.3 14.5 %copy-start.47 = (f32[1,192]{1,0:T(1,128)}, f32[1,192]{1,0:T(1,128)S(1)}, u32[]{:S(2)}) copy-start(f32[1,192]{1,0:T(1,128)S(1)} %get-tuple-element.712) | copy-start | bytes 2308
  207.9 34.6 %copy-start.44 = (f32[384]{0:T(512)}, f32[384]{0:T(512)S(1)}, u32[]{:S(2)}) copy-start(f32[384]{0:T(512)S(1)} %mul.196) | copy-start | bytes 4612
  209.8 58.7 %copy-start.5 = (f32[1,32,12]{2,1,0:T(8,128)S(1)}, f32[1,32,12]{2,1,0:T(8,128)}, u32[]{:S(2)}) copy-start(f32[1,32,12]{2,1,0:T(8,128)} %get-tuple-element.704) | copy-start | bytes 4612
  209.8 59.3 %copy-start.1 = (bf16[2,192,1024]{1,2,0:T(8,128)(2,1)S(1)}, bf16[2,192,1024]{1,2,0:T(8,128)(2,1)}, u32[]{:S(2)}) copy-start(bf16[2,192,1024]{1,2,0:T(8,128)(2,1)} %copy-done) | copy-start | bytes 2359300
  209.8 59.3 %copy-start.36 = (f32[384]{0:T(512)S(1)}, f32[384]{0:T(512)}, u32[]{:S(2)}) copy-start(f32[384]{0:T(512)} %get-tuple-element.456) | copy-start | bytes 4612
  211.8 57.3 %copy-start.40 = (f32[192]{0:T(256)}, f32[192]{0:T(256)S(1)}, u32[]{:S(2)}) copy-start(f32[192]{0:T(256)S(1)} %get-tuple-element.448) | copy-start | bytes 2308
  211.8 57.4 %copy-start.48 = (f32[1,192]{1,0:T(1,128)S(1)}, f32[1,192]{1,0:T(1,128)}, u32[]{:S(2)}) copy-start(f32[1,192]{1,0:T(1,128)} %copy-done.47) | copy-start | bytes 2308
  268.5 6.0 copy-start.39
  268.5 7.0 copy-start.3
  268.5 7.0 copy-start.4
  268.5 138.6 %copy-start.34 = (pred[192]{0:T(512)(128)(4,1)S(1)}, pred[192]{0:T(512)(128)(4,1)}, u32[]{:S(2)}) copy-start(pred[192]{0:T(512)(128)(4,1)} %copy-done.33) | copy-start | bytes 580
  269.2 219.7 %copy-start.30 = (pred[2,384]{1,0:T(4,128)(4,1)S(1)}, pred[2,384]{1,0:T(4,128)(4,1)}, u32[]{:S(2)}) copy-start(pred[2,384]{1,0:T(4,128)(4,1)} %get-tuple-element.669) | copy-start | bytes 2308
  269.2 219.7 %copy-start.32 = (f32[2]{0:T(128)S(1)}, f32[2]{0:T(128)}, u32[]{:S(2)}) copy-start(f32[2]{0:T(128)} %copy-done.31) | copy-start | bytes 28
  271.4 220.8 %copy-start.38 = (pred[384]{0:T(512)(128)(4,1)S(1)}, pred[384]{0:T(512)(128)(4,1)}, u32[]{:S(2)}) copy-start(pred[384]{0:T(512)(128)(4,1)} %copy-done.37) | copy-start | bytes 1156
  273.2 222.0 %copy-start.52 = (s32[2]{0:T(128)S(1)}, s32[2]{0:T(128)}, u32[]{:S(2)}) copy-start(s32[2]{0:T(128)} %copy-done.51) | copy-start | bytes 28
  275.5 337.1 %all-reduce.39.cloned.1.call-start = ((), (), s32[]{:S(2)}) async-start(), calls=%async_computation.4 | async-start | bytes 147456
  495.1 283.9 %all-reduce.37.cloned.1.call-start = ((), (), s32[]{:S(2)}) async-start(), calls=%async_computation.3 | async-start | bytes 147456
  496.1 164.9 %copy-start.19 = (f32[3072]{0:T(1024)}, f32[3072]{0:T(1024)S(1)}, u32[]{:S(2)}) copy-start(f32[3072]{0:T(1024)S(1)} %dynamic-update-slice.12) | copy-start | bytes 36868
  496.4 164.6 %copy-start.20 = (f32[3072]{0:T(1024)}, f32[3072]{0:T(1024)S(1)}, u32[]{:S(2)}) copy-start(f32[3072]{0:T(1024)S(1)} %dynamic-update-slice.13) | copy-start | bytes 36868
  660.7 394.7 %copy-start.45 = (pred[192]{0:T(512)(128)(4,1)S(1)}, pred[192]{0:T(512)(128)(4,1)}, u32[]{:S(2)}) copy-start(pred[192]{0:T(512)(128)(4,1)} %get-tuple-element.457) | copy-start | bytes 580
  661.6 382.5 %all-reduce.35.cloned.1.call-start = ((), (), s32[]{:S(2)}) async-start(), calls=%async_computation.2 | async-start | bytes 149504
  918.6 6.9 copy-start.25
  919.2 6.3 copy-start.26
  1055.4 79.2 %copy-start.42 = (f32[1,192]{1,0:T(1,128)}, f32[1,192]{1,0:T(1,128)S(1)}, u32[]{:S(2)}) copy-start(f32[1,192]{1,0:T(1,128)S(1)} %get-tuple-element.709) | copy-start | bytes 2308
  1055.4 79.2 %copy-start.43 = (f32[1,192]{1,0:T(1,128)}, f32[1,192]{1,0:T(1,128)S(1)}, u32[]{:S(2)}) copy-start(f32[1,192]{1,0:T(1,128)S(1)} %get-tuple-element.710) | copy-start | bytes 2308
  (27 other events, 45.6 us)
Sparse Core Ops, SparseCore 0:
  11.1 66.1 all-gather.44
  275.6 120.3 all-reduce.40
  495.2 117.2 all-reduce.38
  661.7 117.2 all-reduce.36
  926.2 117.9 all-reduce.34
where the time goes:
time: 1150 us; the launch traced here: 1140 us
  waiting for transfers between devices  537 us (47%)
  blocking collectives  457 us (40%)
  local copies, waits for them, and re-layouts  81 us (7%)
  other arithmetic  25.3 us (2%)
  between operations  19.7 us (2%)
  starting transfers between devices  12.2 us (1%)
    unnamed x9, waiting for transfers between devices  469 us
    all_gather x8, blocking collectives, merged_2(): pieces = jax.tree.map(lambda part: lax.all_gather(part, axis), value)  215 us
    all_gather x1, blocking collectives, local(): row_full = lax.all_gather(stacked, 'feat', axis=2, tiled=True)  89.4 us
    all_gather x3, blocking collectives, local(): self_col = lax.all_gather(own_pieces, 'tile', axis=1, tiled=True)  79 us
    psum x1, blocking collectives, local(): lax.psum((jnp.sum(jnp.where(row_ok[0], gen_row - self_row[0], 0.0)), jnp....  73.5 us
    all_gather x1, waiting for transfers between devices, local(): every_row = lax.all_gather(stacked, 'tile', axis=1, tiled=True)  68.6 us
  transfers between devices with their start and end apart: 6, of which 5 were waited for; matrix products, arithmetic and copies ran while one was open for 1% of the time, Pallas kernels for 0%

commit v1 on v0

v1 whole, which is shorter than its diff:
```python
import functools

import jax
import jax.numpy as jnp
from jax import lax
from jax.experimental import pallas as pl
from jax.experimental.pallas import tpu as pltpu
from jax.sharding import Mesh, PartitionSpec as P

EPSILON = 0.25
LOG2E = 1.4426950408889634
LN2 = 0.6931471805599453
FAR = -1.0e30

BLOCK = 192
D = 1024
NI = 8 * BLOCK
NJ = 4 * BLOCK
RI = NI // 128
RJ = NJ // 128

VMEM = pl.BlockSpec(memory_space=pltpu.VMEM)
SMEM = pl.BlockSpec(memory_space=pltpu.SMEM)
PARAMS = pltpu.CompilerParams(vmem_limit_bytes=40 * 1024 * 1024)


def f32(*shape):
    return jax.ShapeDtypeStruct(shape, jnp.float32)


def call(body, outs, ins, scratch=(), cost=None):
    return pl.pallas_call(
        body,
        out_shape=outs,
        in_specs=ins,
        out_specs=jax.tree.map(lambda _: VMEM, outs),
        scratch_shapes=list(scratch),
        compiler_params=PARAMS,
        cost_estimate=cost,
    )


def merge(parts):
    high = functools.reduce(jnp.maximum, parts)
    mass = functools.reduce(jnp.add, [jnp.exp2(part - high) for part in parts])
    return high + jnp.log(mass) * LOG2E


def lifted(pot, lift):
    return jnp.where(lift > -1.0e29, pot + lift, FAR)


def reduce_lanes(k_ref, heads, high_ref, mass_ref):
    count = len(heads)

    def step(group, carry):
        rows = pl.ds(pl.multiple_of(group * 16, 16), 16)
        tiles = [k_ref[rows, r * 128 : (r + 1) * 128] for r in range(RI)]
        for v in range(count):
            xs = [heads[v][r : r + 1, :] - tiles[r] for r in range(RI)]
            high = functools.reduce(jnp.maximum, xs)
            mass = functools.reduce(jnp.add, [jnp.exp2(x - high) for x in xs])
            high_ref[v, rows, :] = high
            mass_ref[v, rows, :] = mass
        return carry

    lax.fori_loop(0, NJ // 16, step, 0)
    results = []
    for v in range(count):
        rows_out = []
        for b in range(RJ):
            part = slice(b * 128, (b + 1) * 128)
            high = jnp.transpose(high_ref[v, part, :])
            mass = jnp.transpose(mass_ref[v, part, :])
            top = jnp.max(high, axis=0, keepdims=True)
            total = jnp.sum(mass * jnp.exp2(high - top), axis=0, keepdims=True)
            rows_out.append(top + jnp.log(total) * LOG2E)
        results.append(jnp.concatenate(rows_out, axis=0))
    return results


def reduce_rows(k_ref, heads, wide_ref):
    count = len(heads)
    for v in range(count):
        for b in range(RJ):
            row = jnp.broadcast_to(heads[v][b : b + 1, :], (128, 128))
            wide_ref[v, b * 128 : (b + 1) * 128, :] = jnp.transpose(row)
    rows_out = [[] for _ in range(count)]
    span = 4
    chunk = 32
    for t in range(RI // span):
        cols = [slice((t * span + q) * 128, (t * span + q + 1) * 128) for q in range(span)]

        def highest(group, tops):
            base = pl.multiple_of(group * chunk, chunk)
            tops = list(tops)
            for s in range(chunk // 8):
                rows = pl.ds(base + s * 8, 8)
                wides = [wide_ref[v, rows, :] for v in range(count)]
                for q in range(span):
                    tile = k_ref[rows, cols[q]]
                    for v in range(count):
                        tops[v * span + q] = jnp.maximum(tops[v * span + q], wides[v] - tile)
            return tuple(tops)

        tops = lax.fori_loop(
            0, NJ // chunk, highest, tuple(jnp.full((8, 128), -3.0e38, jnp.float32) for _ in range(count * span))
        )

        def summed(group, sums):
            base = pl.multiple_of(group * chunk, chunk)
            sums = list(sums)
            for s in range(chunk // 8):
                rows = pl.ds(base + s * 8, 8)
                wides = [wide_ref[v, rows, :] for v in range(count)]
                for q in range(span):
                    tile = k_ref[rows, cols[q]]
                    for v in range(count):
                        n = v * span + q
                        sums[n] = sums[n] + jnp.exp2((wides[v] - tile) - tops[n])
            return tuple(sums)

        sums = lax.fori_loop(
            0, NJ // chunk, summed, tuple(jnp.zeros((8, 128), jnp.float32) for _ in range(count * span))
        )
        for v in range(count):
            for q in range(span):
                high, mass = tops[v * span + q], sums[v * span + q]
                top = jnp.max(high, axis=0, keepdims=True)
                total = jnp.sum(mass * jnp.exp2(high - top), axis=0, keepdims=True)
                rows_out[v].append(top + jnp.log(total) * LOG2E)
    return [jnp.concatenate(rows, axis=0) for rows in rows_out]


def unpack_body(info, raw, a_out, b_out):
    a_is_gen = info[0] == 1
    b_is_gen = info[1] == 1
    for k in range(D // 128):
        even = raw[2 * k]
        odd = raw[2 * k + 1]
        gen = jnp.concatenate([even[:, :64], odd[:, :64]], axis=1)
        ref = jnp.concatenate([even[:, 64:], odd[:, 64:]], axis=1)
        cols = slice(k * 128, (k + 1) * 128)
        a = jnp.where(a_is_gen, gen, ref)
        for n in range(4):
            a_out[n, :, cols] = a
        b_out[:, cols] = jnp.where(b_is_gen, gen, ref)


def norm_parts(values):
    values = values.astype(jnp.float32)
    values = values * values
    return functools.reduce(jnp.add, [values[:, k * 128 : (k + 1) * 128] for k in range(D // 128)])


def cost_body(info, own, other, cols, lift_i, k_ref, part_out, sq_ref, high_ref, mass_ref):
    scale = LOG2E / EPSILON
    for b in range(RJ):
        part = slice(b * 128, (b + 1) * 128)
        total = jnp.sum(norm_parts(cols[part, :]), axis=1, keepdims=True)
        sq_ref[part, :] = jnp.broadcast_to(total * (0.5 * scale), (128, 128))
    for which, source in enumerate((own, other)):
        half = jnp.where(info[2] == which, 0, 1)
        for t in range(3):
            rows = source[t * 256 : (t + 1) * 256, :]
            norms = []
            for s in range(2):
                turned = jnp.transpose(norm_parts(rows[s * 128 : (s + 1) * 128, :]))
                norms.append(jnp.sum(turned, axis=0, keepdims=True) * (0.5 * scale))
            for b in range(3):
                part = slice(b * 256, (b + 1) * 256)
                inner = lax.dot_general(
                    cols[part, :], rows, (((1,), (1,)), ((), ())), preferred_element_type=jnp.float32
                )
                for s in range(2):
                    place = pl.ds(pl.multiple_of(half * (NI // 2) + t * 256 + s * 128, 128), 128)
                    k_ref[part, place] = (norms[s] + sq_ref[part, :]) - scale * inner[:, s * 128 : (s + 1) * 128]
    (result,) = reduce_lanes(k_ref, [lift_i[...]], high_ref, mass_ref)
    for n in range(4):
        part_out[n, 0:RJ, :] = result
        part_out[n, RJ:8, :] = jnp.zeros((8 - RJ, 128), jnp.float32)


def second_body(k_ref, got, lift_j, out, g1_out, wide_ref):
    g1 = -merge([got[n, 0:RJ, :] for n in range(4)])
    g1_out[...] = g1
    lift = lift_j[...]
    results = reduce_rows(k_ref, [lift, lifted(g1, lift)], wide_ref)
    for n in range(8):
        for v in range(2):
            out[n, v * RI : (v + 1) * RI, :] = results[v]


def third_body(k_ref, got, lift_i, out, f2_out, high_ref, mass_ref):
    f1 = -merge([got[n, 0:RI, :] for n in range(8)])
    f2 = 0.5 * (f1 - merge([got[n, RI : 2 * RI, :] for n in range(8)]))
    f2_out[...] = f2
    lift = lift_i[...]
    results = reduce_lanes(k_ref, [lifted(f1, lift), lifted(f2, lift)], high_ref, mass_ref)
    for n in range(4):
        for v in range(2):
            out[n, v * 8 : v * 8 + RJ, :] = results[v]
            out[n, v * 8 + RJ : v * 8 + 8, :] = jnp.zeros((8 - RJ, 128), jnp.float32)


def fourth_body(k_ref, got, lift_j, g1, out, g3_out, wide_ref):
    g2 = 0.5 * (g1[...] - merge([got[n, 0:RJ, :] for n in range(4)]))
    g3 = 0.5 * (g2 - merge([got[n, 8 : 8 + RJ, :] for n in range(4)]))
    g3_out[...] = g3
    lift = lift_j[...]
    results = reduce_rows(k_ref, [lifted(g2, lift), lifted(g3, lift)], wide_ref)
    for n in range(8):
        for v in range(2):
            out[n, v * RI : (v + 1) * RI, :] = results[v]


def fifth_body(info, k_ref, got, lift_i, f2, g3, out, f4_ref, high_ref, mass_ref):
    f3 = 0.5 * (f2[...] - merge([got[n, 0:RI, :] for n in range(8)]))
    f4 = 0.5 * (f3 - merge([got[n, RI : 2 * RI, :] for n in range(8)]))
    f4_ref[0:RI, :] = f4
    lift = lift_i[...]
    (result,) = reduce_lanes(k_ref, [lifted(f3, lift)], high_ref, mass_ref)
    mine = f4_ref[pl.ds(info[3], 2), :]
    for n in range(16):
        out[n, 0:RJ, :] = result
        out[n, RJ : 2 * RJ, :] = g3[...]
        out[n, 2 * RJ : 2 * RJ + 2, :] = mine
        out[n, 2 * RJ + 2 : 16, :] = jnp.zeros((14 - 2 * RJ, 128), jnp.float32)


def last_body(got, gen_weight, ref_weight, ref_full_weight, pots, g4_out, share):
    cross = [got[n * 4 + 1] for n in range(4)]
    g4 = 0.5 * (cross[0][RJ : 2 * RJ, :] - merge([part[0:RJ, :] for part in cross])) * LN2
    g4_out[0:RJ, :] = g4
    g4_out[RJ:8, :] = jnp.zeros((8 - RJ, 128), jnp.float32)
    total = jnp.sum(jnp.where(ref_full_weight[...] > 0.0, g4 * ref_full_weight[...], 0.0))
    for n in range(4):
        own = slice(2 * RJ, 2 * RJ + 2)
        gen_pot = got[n * 4 + 1][own, :] * LN2
        gen_self = got[n * 4][own, :] * LN2
        ref_self = got[n * 4 + 3][own, :] * LN2
        pots[n, 0:2, :] = gen_pot
        pots[n, 2:4, :] = gen_self
        pots[n, 4:6, :] = ref_self
        pots[n, 6:8, :] = jnp.zeros((2, 128), jnp.float32)
        total += jnp.sum(jnp.where(gen_weight[n] > 0.0, (gen_pot - gen_self) * gen_weight[n], 0.0))
        total -= jnp.sum(jnp.where(ref_weight[n] > 0.0, ref_self * ref_weight[n], 0.0))
    for n in range(8):
        share[n, :, :] = jnp.full((8, 128), total, jnp.float32)


def spread(operand, axes):
    return lax.all_to_all(operand, axes, 0, 0, tiled=True)


def local(gen_points, reference_embeddings, gen_count, ref_count):
    y, x, c, zl = (lax.axis_index(name) for name in ("y", "x", "c", "zl"))
    a_is_gen = zl < 3
    b_is_gen = zl == 0
    packed = jnp.concatenate([gen_points, reference_embeddings], axis=1)
    raw = lax.all_gather(packed, ("zh", "zl"))

    info = jnp.stack(
        [a_is_gen.astype(jnp.int32), b_is_gen.astype(jnp.int32), c, c * 6 + (3 * x) // 2]
    ).astype(jnp.int32)
    counts = jnp.stack([gen_count, ref_count]).reshape(2, 4, 4, 2)
    totals = jnp.sum(counts, axis=(1, 2, 3)).astype(jnp.float32)
    weights2 = -jnp.log(totals) * LOG2E
    place = jnp.arange(BLOCK, dtype=jnp.int32)
    a_set = jnp.where(a_is_gen, 0, 1)
    b_set = jnp.where(b_is_gen, 0, 1)
    count_i = jnp.transpose(counts[a_set, y]).reshape(8)
    count_j = counts[b_set, :, x, c]
    lift_i = jnp.where(place[None, :] < count_i[:, None], weights2[a_set], FAR).reshape(RI, 128)
    lift_j = jnp.where(place[None, :] < count_j[:, None], weights2[b_set], FAR).reshape(RJ, 128)
    spots = jnp.arange(256, dtype=jnp.int32) - 64 * (x % 2)
    inside = spots >= 0
    gen_in = inside[None, :] & (spots[None, :] < counts[0, :, x, c][:, None])
    ref_in = inside[None, :] & (spots[None, :] < counts[1, :, x, c][:, None])
    gen_weight = jnp.where(gen_in, 1.0 / totals[0], 0.0).reshape(4, 2, 128)
    ref_weight = jnp.where(ref_in, 1.0 / totals[1], 0.0).reshape(4, 2, 128)
    ref_full = jnp.where(place[None, :] < counts[1, :, x, c][:, None], 1.0 / totals[1], 0.0).reshape(RJ, 128)

    bf16 = jnp.bfloat16
    a_wide, b_own = call(
        unpack_body,
        (jax.ShapeDtypeStruct((4, BLOCK, D), bf16), jax.ShapeDtypeStruct((BLOCK, D), bf16)),
        [SMEM, VMEM],
    )(info, raw)
    b_all = lax.all_gather(b_own, "y")
    a_half = spread(a_wide, "x")
    a_other = lax.ppermute(a_half, "c", [(0, 1), (1, 0)])

    passes = [pltpu.VMEM((1, NJ, 128), jnp.float32)] * 2
    passes2 = [pltpu.VMEM((2, NJ, 128), jnp.float32)] * 2
    cost, part = call(
        cost_body,
        (f32(NJ, NI), f32(4, 8, 128)),
        [SMEM, VMEM, VMEM, VMEM, VMEM],
        [pltpu.VMEM((NJ, 128), jnp.float32)] + passes,
    )(info, a_half.reshape(NJ, D), a_other.reshape(NJ, D), b_all.reshape(NJ, D), lift_i)
    got = spread(part, "y")
    part, g1 = call(
        second_body, (f32(8, 2 * RI, 128), f32(RJ, 128)), [VMEM] * 3, passes2[:1]
    )(cost, got, lift_j)
    got = spread(part, ("x", "c"))
    part, f2 = call(
        third_body, (f32(4, 16, 128), f32(RI, 128)), [VMEM] * 3, passes2
    )(cost, got, lift_i)
    got = spread(part, "y")
    part, g3 = call(
        fourth_body, (f32(8, 2 * RI, 128), f32(RJ, 128)), [VMEM] * 4, passes2[:1]
    )(cost, got, lift_j, g1)
    got = spread(part, ("x", "c"))
    part = call(
        fifth_body,
        f32(16, 16, 128),
        [SMEM] + [VMEM] * 5,
        [pltpu.VMEM((16, 128), jnp.float32)] + passes,
    )(info, cost, got, lift_i, f2, g3)
    got = spread(part, ("y", "zl"))
    pots, g4, share = call(
        last_body, (f32(4, 8, 128), f32(8, 128), f32(8, 8, 128)), [VMEM] * 4
    )(got, gen_weight, ref_weight, ref_full)
    divergence = jnp.sum(spread(share, ("x", "c"))[:, 0, 0])

    mine = lax.dynamic_index_in_dim(pots, y, 0, keepdims=False)
    mine = lax.dynamic_slice_in_dim(mine.reshape(4, 256), 64 * (x % 2), BLOCK, 1)
    ref_pot = lax.dynamic_slice_in_dim(g4.reshape(1024), y * BLOCK, BLOCK, 0)
    return mine[0], ref_pot, mine[1], mine[2], divergence


def solution(mesh):
    fine = Mesh(mesh.devices.reshape(4, 4, 2, 4, 4), ("y", "x", "c", "zh", "zl"))
    tile, feat = ("y", "x", "c"), ("zh", "zl")
    return jax.shard_map(
        local,
        mesh=fine,
        in_specs=(P(tile, feat), P(tile, feat), P(), P()),
        out_specs=(P(tile), P(tile), P(tile), P(tile), P()),
        check_vma=False,
    )
```

time: 1150 us -> 191 us (0.17)
  waiting for transfers between devices: 537 us -> 48.8 us
  blocking collectives: 457 us -> 44.6 us
  local copies, waits for them, and re-layouts: 81 us -> 15.7 us
  starting transfers between devices: 12.2 us -> 37.6 us
  Pallas kernels: 0 us -> 24.8 us
  other arithmetic: 25.3 us -> 2.53 us
    unnamed x9 -> x1, waiting for transfers between devices: 469 us -> 0.71 us
    all_gather x12 -> x1, blocking collectives: 384 us -> 33.9 us  [local(): raw = lax.all_gather(packed, ('zh', 'zl'))]
    psum x1 -> x0, blocking collectives: 73.5 us -> none  [local(): lax.psum((jnp.sum(jnp.where(row_ok[0], gen_row - self_row[0], 0.0)), jnp....]
    all_gather x1, waiting for transfers between devices: 68.6 us -> 15.1 us  [local(): b_all = lax.all_gather(b_own, 'y')]
    slice x99 -> x2, local copies, waits for them, and re-layouts: 42.5 us -> 1.23 us  [the longest x1 0.65 us: local(): return (mine[0], ref_pot, mine[1], mine[2], divergence)]
    all_to_all x1 -> x6, waiting for transfers between devices: 0.01 us -> 33 us  [spread(): return lax.all_to_all(operand, axes, 0, 0, tiled=True)]
    pallas_call x0 -> x7, Pallas kernels: none -> 24.8 us  [the longest x1 6.81 us: local(): call(cost_body, (f32(NJ, NI), f32(4, 8, 128)), [SMEM, VMEM, VMEM, VMEM, V...]
    all_to_all x1 -> x6, starting transfers between devices: 12 us -> 26.6 us  [spread(): return lax.all_to_all(operand, axes, 0, 0, tiled=True)]
  transfers between devices with their start and end apart: 6 -> 8, of which waited for: 5 -> 7; matrix products, arithmetic and copies ran while one was open for 1% -> 3% of each run, Pallas kernels for 0% -> 0%
where the time goes in v1:
time: 191 us; the launch traced here: 190 us
  waiting for transfers between devices  48.8 us (26%)
  blocking collectives  44.6 us (23%)
  starting transfers between devices  37.6 us (20%)
  Pallas kernels  24.8 us (13%)
  local copies, waits for them, and re-layouts  15.7 us (8%)
  between operations  15.6 us (8%)
  other arithmetic  2.53 us (1%)
    all_gather x1, blocking collectives, local(): raw = lax.all_gather(packed, ('zh', 'zl'))  33.9 us
    all_to_all x6, waiting for transfers between devices, spread(): return lax.all_to_all(operand, axes, 0, 0, tiled=True)  33 us
    all_to_all x6, starting transfers between devices, spread(): return lax.all_to_all(operand, axes, 0, 0, tiled=True)  26.6 us
    all_gather x1, waiting for transfers between devices, local(): b_all = lax.all_gather(b_own, 'y')  15.1 us
    unnamed x19, local copies, waits for them, and re-layouts  12.3 us
    ppermute x1, starting transfers between devices, local(): a_other = lax.ppermute(a_half, 'c', [(0, 1), (1, 0)])  11 us
    all_to_all x1, blocking collectives, spread(): return lax.all_to_all(operand, axes, 0, 0, tiled=True)  10.7 us
    pallas_call x1, Pallas kernels, local(): call(cost_body, (f32(NJ, NI), f32(4, 8, 128)), [SMEM, VMEM, VMEM, VMEM, V...  6.81 us
  transfers between devices with their start and end apart: 8, of which 7 were waited for; matrix products, arithmetic and copies ran while one was open for 3% of the time, Pallas kernels for 0%

profile of v1, /device:TPU:1, one launch (start us, length us, event | category | flops | bytes accessed | tf_op | source)
XLA Modules:
  0.0 189.7 jit_solution(4324244332385702567)
XLA Ops:
  7.2 0.9 copy.13
  8.0 0.9 copy.14
  9.0 33.9 %all-gather = bf16[3072,128]{1,0:T(8,128)(2,1)S(1)} all-gather(bf16[192,128]{1,0:T(8,128)(2,1)S(1)} %pad_maximum_fusion), channel_id=2, replica_groups=mesh['y'=4,'x'=4,'c'=2,'zh'=4,'zl'=4] {'zh','zl'}, dimensions={0}, use_global_device_ids=true | all-gather | bytes 835584 | tf_op jit(solution)/shard_map/all_gather | solution.py:261
  43.0 2.4 %shard_map.83 = (bf16[4,192,1024]{2,1,0:T(8,128)(2,1)}, bf16[192,1024]{1,0:T(8,128)(2,1)}) custom-call(s32[4]{0:T(128)S(1)} %pad_add_fusion.info, bf16[16,192,128]{2,1,0:T(8,128)(2,1)S(1)} %bitcast.19), custom_call_target="tpu_custom_call" | custom-call | tf_op jit(solution)/shard_map/pallas_call | solution.py:285
  45.4 4.1 %all-to-all-start = ((bf16[4,192,1024]{2,1,0:T(8,128)(2,1)}), bf16[4,192,1024]{2,1,0:T(8,128)(2,1)S(1)}, u32[]{:S(2)}, u32[]{:S(2)}) async-start(bf16[4,192,1024]{2,1,0:T(8,128)(2,1)} %get-tuple-element.18), calls=%async_computation | async-start | bytes 3145728 | tf_op jit(solution)/shard_map/all_to_all | solution.py:253
  50.3 11.9 %all-to-all-done = bf16[4,192,1024]{2,1,0:T(8,128)(2,1)S(1)} async-done(((bf16[4,192,1024]{2,1,0:T(8,128)(2,1)}), bf16[4,192,1024]{2,1,0:T(8,128)(2,1)S(1)}, u32[]{:S(2)}, u32[]{:S(2)}) %all-to-all-start) | async-done | bytes 1572896 | tf_op jit(solution)/shard_map/all_to_all | solution.py:253
  62.1 11.0 %collective-permute-start = (bf16[4,192,1024]{2,1,0:T(8,128)(2,1)S(1)}, bf16[4,192,1024]{2,1,0:T(8,128)(2,1)S(1)}, u32[]{:S(2)}, u32[]{:S(2)}) collective-permute-start(bf16[4,192,1024]{2,1,0:T(8,128)(2,1)S(1)} %all-to-all-done), channel_id=1, source_target_pairs={{0,16},{16,0},{1,17},{17,1},{2,18},{18,2},{3,19},{19,3},{4,20},{20... | collective-permute-start | bytes 4718600 | tf_op jit(solution)/shard_map/ppermute | solution.py:292
  74.4 0.7 fusion
  75.5 15.1 %all-gather.4.cloned.1.call-done.cols = bf16[768,1024]{1,0:T(8,128)(2,1)} async-done(((bf16[192,1024]{1,0:T(8,128)(2,1)}), bf16[768,1024]{1,0:T(8,128)(2,1)}) %all-gather.4.cloned.1.call-update) | async-done | bytes 1572880 | tf_op jit(solution)/shard_map/all_gather | solution.py:290
  90.6 1.4 copy-done.5
  92.1 6.8 %shard_map.84 = (f32[768,1536]{1,0:T(8,128)S(1)}, f32[4,8,128]{2,1,0:T(8,128)}) custom-call(s32[4]{0:T(128)S(1)} %pad_add_fusion.info, bf16[768,1024]{1,0:T(8,128)(2,1)S(1)} %bitcast.18, bf16[768,1024]{1,0:T(8,128)(2,1)S(1)} %bitcast.20, bf16[768,1024]{1,0:T(8,128)(2,1)S(1)} %copy-done.5, f32[12,128]{1,0:T(8,128)S(1)} %select_n.83.lift_i), custom_call_target="tpu_custom_call" | custom-call | tf_op jit(solution)/shard_map/pallas_call | solution.py:296
  98.9 2.1 %copy-done = f32[768,1536]{1,0:T(8,128)} copy-done((f32[768,1536]{1,0:T(8,128)}, f32[768,1536]{1,0:T(8,128)S(1)}, u32[]{:S(2)}) %copy-start) | copy-done | bytes 4718616
  101.0 3.2 %all-to-all-start.1 = ((f32[4,8,128]{2,1,0:T(8,128)}), f32[4,8,128]{2,1,0:T(8,128)S(1)}, u32[]{:S(2)}, u32[]{:S(2)}) async-start(f32[4,8,128]{2,1,0:T(8,128)} %get-tuple-element.21), calls=%async_computation.1 | async-start | bytes 32768 | tf_op jit(solution)/shard_map/all_to_all | solution.py:253
  104.2 0.7 fusion.1
  105.0 3.4 %all-to-all-done.1.got = f32[4,8,128]{2,1,0:T(8,128)S(1)} async-done(((f32[4,8,128]{2,1,0:T(8,128)}), f32[4,8,128]{2,1,0:T(8,128)S(1)}, u32[]{:S(2)}, u32[]{:S(2)}) %all-to-all-start.1) | async-done | bytes 16416 | tf_op jit(solution)/shard_map/all_to_all | solution.py:253
  108.4 2.3 %copy-done.1 = f32[768,1536]{1,0:T(8,128)S(1)} copy-done((f32[768,1536]{1,0:T(8,128)S(1)}, f32[768,1536]{1,0:T(8,128)}, u32[]{:S(2)}) %copy-start.1) | copy-done | bytes 4718616
  110.7 3.5 %shard_map.85 = (f32[8,24,128]{2,1,0:T(8,128)S(1)}, f32[6,128]{1,0:T(8,128)S(1)}) custom-call(f32[768,1536]{1,0:T(8,128)S(1)} %copy-done.1, f32[4,8,128]{2,1,0:T(8,128)S(1)} %all-to-all-done.1.got, f32[6,128]{1,0:T(8,128)S(1)} %select_n.88.lift_j), custom_call_target="tpu_custom_call" | custom-call | tf_op jit(solution)/shard_map/pallas_call | solution.py:303
  114.2 10.7 %all_to_all.35.got = f32[8,24,128]{2,1,0:T(8,128)S(1)} all-to-all(f32[8,24,128]{2,1,0:T(8,128)S(1)} %get-tuple-element.22), channel_id=1, replica_groups=mesh['y'=4,'x'=4,'c'=2,'zh'=4,'zl'=4] {'x','c'}, dimensions={0} | all-to-all | bytes 196608 | tf_op jit(solution)/shard_map/all_to_all | solution.py:253
  125.0 3.7 %shard_map.86 = (f32[4,16,128]{2,1,0:T(8,128)}, f32[12,128]{1,0:T(8,128)S(1)}) custom-call(f32[768,1536]{1,0:T(8,128)S(1)} %copy-done.2, f32[8,24,128]{2,1,0:T(8,128)S(1)} %all_to_all.35.got, f32[12,128]{1,0:T(8,128)S(1)} %select_n.83.lift_i), custom_call_target="tpu_custom_call" | custom-call | tf_op jit(solution)/shard_map/pallas_call | solution.py:307
  128.7 3.3 %all-to-all-start.3 = ((f32[4,16,128]{2,1,0:T(8,128)}), f32[4,16,128]{2,1,0:T(8,128)S(1)}, u32[]{:S(2)}, u32[]{:S(2)}) async-start(f32[4,16,128]{2,1,0:T(8,128)} %get-tuple-element.23), calls=%async_computation.3 | async-start | bytes 65536 | tf_op jit(solution)/shard_map/all_to_all | solution.py:253
  131.9 4.3 %all-to-all-done.3.got = f32[4,16,128]{2,1,0:T(8,128)S(1)} async-done(((f32[4,16,128]{2,1,0:T(8,128)}), f32[4,16,128]{2,1,0:T(8,128)S(1)}, u32[]{:S(2)}, u32[]{:S(2)}) %all-to-all-start.3) | async-done | bytes 32800 | tf_op jit(solution)/shard_map/all_to_all | solution.py:253
  136.2 2.3 %copy-done.3 = f32[768,1536]{1,0:T(8,128)S(1)} copy-done((f32[768,1536]{1,0:T(8,128)S(1)}, f32[768,1536]{1,0:T(8,128)}, u32[]{:S(2)}) %copy-start.3) | copy-done | bytes 4718616
  138.5 4.2 %shard_map.87 = (f32[8,24,128]{2,1,0:T(8,128)}, f32[6,128]{1,0:T(8,128)S(1)}) custom-call(f32[768,1536]{1,0:T(8,128)S(1)} %copy-done.3, f32[4,16,128]{2,1,0:T(8,128)S(1)} %all-to-all-done.3.got, f32[6,128]{1,0:T(8,128)S(1)} %select_n.88.lift_j, f32[6,128]{1,0:T(8,128)S(1)} %get-tuple-element.24.g1), custom_call_target="tpu_custom_call" | custom-call | tf_op jit(solution)/shard_map/pallas_call | solution.py:311
  142.7 5.2 %all-to-all-start.4 = ((f32[8,24,128]{2,1,0:T(8,128)}), f32[8,24,128]{2,1,0:T(8,128)S(1)}, u32[]{:S(2)}, u32[]{:S(2)}) async-start(f32[8,24,128]{2,1,0:T(8,128)} %get-tuple-element.25), calls=%async_computation.4 | async-start | bytes 196608 | tf_op jit(solution)/shard_map/all_to_all | solution.py:253
  149.2 3.7 %all-to-all-done.4.got = f32[8,24,128]{2,1,0:T(8,128)S(1)} async-done(((f32[8,24,128]{2,1,0:T(8,128)}), f32[8,24,128]{2,1,0:T(8,128)S(1)}, u32[]{:S(2)}, u32[]{:S(2)}) %all-to-all-start.4) | async-done | bytes 98336 | tf_op jit(solution)/shard_map/all_to_all | solution.py:253
  152.9 2.3 %copy-done.4 = f32[768,1536]{1,0:T(8,128)S(1)} copy-done((f32[768,1536]{1,0:T(8,128)S(1)}, f32[768,1536]{1,0:T(8,128)}, u32[]{:S(2)}) %copy-start.4) | copy-done | bytes 4718616
  155.2 3.5 %shard_map.88 = f32[16,16,128]{2,1,0:T(8,128)} custom-call(s32[4]{0:T(128)S(1)} %pad_add_fusion.info, f32[768,1536]{1,0:T(8,128)S(1)} %copy-done.4, f32[8,24,128]{2,1,0:T(8,128)S(1)} %all-to-all-done.4.got, f32[12,128]{1,0:T(8,128)S(1)} %select_n.83.lift_i, f32[12,128]{1,0:T(8,128)S(1)} %get-tuple-element.26.f2, f32[6,128]{1,0:T(8,128)S(1)} %get-tuple-element.27.g3), custom_call_target="tpu_custom_call" | custom-call | tf_op jit(solution)/shard_map/pallas_call | solution.py:315
  158.7 5.2 %all-to-all-start.5 = ((f32[16,16,128]{2,1,0:T(8,128)}), f32[16,16,128]{2,1,0:T(8,128)S(1)}, u32[]{:S(2)}, u32[]{:S(2)}) async-start(f32[16,16,128]{2,1,0:T(8,128)} %shard_map.88), calls=%async_computation.5 | async-start | bytes 262144 | tf_op jit(solution)/shard_map/all_to_all | solution.py:253
  164.9 6.3 %all-to-all-done.5.got = f32[16,16,128]{2,1,0:T(8,128)S(1)} async-done(((f32[16,16,128]{2,1,0:T(8,128)}), f32[16,16,128]{2,1,0:T(8,128)S(1)}, u32[]{:S(2)}, u32[]{:S(2)}) %all-to-all-start.5) | async-done | bytes 131104 | tf_op jit(solution)/shard_map/all_to_all | solution.py:253
  171.2 0.8 shard_map.89
  172.0 5.5 %all-to-all-start.6 = ((f32[8,8,128]{2,1,0:T(8,128)}), f32[8,8,128]{2,1,0:T(8,128)S(1)}, u32[]{:S(2)}, u32[]{:S(2)}) async-start(f32[8,8,128]{2,1,0:T(8,128)} %get-tuple-element.30), calls=%async_computation.6 | async-start | bytes 65536 | tf_op jit(solution)/shard_map/all_to_all | solution.py:253
  178.8 3.5 %all-to-all-done.6 = f32[8,8,128]{2,1,0:T(8,128)S(1)} async-done(((f32[8,8,128]{2,1,0:T(8,128)}), f32[8,8,128]{2,1,0:T(8,128)S(1)}, u32[]{:S(2)}, u32[]{:S(2)}) %all-to-all-start.6) | async-done | bytes 32800 | tf_op jit(solution)/shard_map/all_to_all | solution.py:253
  (41 shorter events, 5.3 us)
Async XLA Ops:
  45.4 27.8 %copy-start.6 = (s32[32]{0:T(128)S(1)}, s32[32]{0:T(128)}, u32[]{:S(2)}) copy-start(s32[32]{0:T(128)} %param.6) | copy-start | bytes 388
  45.4 27.9 %copy-start.7 = (s32[32]{0:T(128)S(1)}, s32[32]{0:T(128)}, u32[]{:S(2)}) copy-start(s32[32]{0:T(128)} %param.7) | copy-start | bytes 388
  45.4 16.7 %all-to-all-start = ((bf16[4,192,1024]{2,1,0:T(8,128)(2,1)}), bf16[4,192,1024]{2,1,0:T(8,128)(2,1)S(1)}, u32[]{:S(2)}, u32[]{:S(2)}) async-start(bf16[4,192,1024]{2,1,0:T(8,128)(2,1)} %get-tuple-element.18), calls=%async_computation | async-start | bytes 3145728 | tf_op jit(solution)/shard_map/all_to_all | solution.py:253
  49.6 41.1 %all-gather.4.cloned.1.call-start = ((), (), s32[]{:S(2)}) async-start(), calls=%async_computation.7 | async-start | bytes 1966080 | tf_op jit(solution)/shard_map/all_gather | solution.py:290
  62.1 28.5 %collective-permute-start = (bf16[4,192,1024]{2,1,0:T(8,128)(2,1)S(1)}, bf16[4,192,1024]{2,1,0:T(8,128)(2,1)S(1)}, u32[]{:S(2)}, u32[]{:S(2)}) collective-permute-start(bf16[4,192,1024]{2,1,0:T(8,128)(2,1)S(1)} %all-to-all-done), channel_id=1, source_target_pairs={{0,16},{16,0},{1,17},{17,1},{2,18},{18,2},{3,19},{19,3},{4,20},{20... | collective-permute-start | bytes 4718600 | tf_op jit(solution)/shard_map/ppermute | solution.py:292
  90.6 1.4 copy-start.5
  98.9 2.1 %copy-start = (f32[768,1536]{1,0:T(8,128)}, f32[768,1536]{1,0:T(8,128)S(1)}, u32[]{:S(2)}) copy-start(f32[768,1536]{1,0:T(8,128)S(1)} %get-tuple-element.20.k_ref) | copy-start | bytes 14155780
  101.0 7.4 %all-to-all-start.1 = ((f32[4,8,128]{2,1,0:T(8,128)}), f32[4,8,128]{2,1,0:T(8,128)S(1)}, u32[]{:S(2)}, u32[]{:S(2)}) async-start(f32[4,8,128]{2,1,0:T(8,128)} %get-tuple-element.21), calls=%async_computation.1 | async-start | bytes 32768 | tf_op jit(solution)/shard_map/all_to_all | solution.py:253
  108.4 2.3 %copy-start.1 = (f32[768,1536]{1,0:T(8,128)S(1)}, f32[768,1536]{1,0:T(8,128)}, u32[]{:S(2)}) copy-start(f32[768,1536]{1,0:T(8,128)} %copy-done) | copy-start | bytes 14155780
  110.7 14.2 %copy-start.2 = (f32[768,1536]{1,0:T(8,128)S(1)}, f32[768,1536]{1,0:T(8,128)}, u32[]{:S(2)}) copy-start(f32[768,1536]{1,0:T(8,128)} %copy-done) | copy-start | bytes 14155780
  128.7 7.5 %all-to-all-start.3 = ((f32[4,16,128]{2,1,0:T(8,128)}), f32[4,16,128]{2,1,0:T(8,128)S(1)}, u32[]{:S(2)}, u32[]{:S(2)}) async-start(f32[4,16,128]{2,1,0:T(8,128)} %get-tuple-element.23), calls=%async_computation.3 | async-start | bytes 65536 | tf_op jit(solution)/shard_map/all_to_all | solution.py:253
  136.2 2.3 %copy-start.3 = (f32[768,1536]{1,0:T(8,128)S(1)}, f32[768,1536]{1,0:T(8,128)}, u32[]{:S(2)}) copy-start(f32[768,1536]{1,0:T(8,128)} %copy-done) | copy-start | bytes 14155780
  142.7 10.2 %all-to-all-start.4 = ((f32[8,24,128]{2,1,0:T(8,128)}), f32[8,24,128]{2,1,0:T(8,128)S(1)}, u32[]{:S(2)}, u32[]{:S(2)}) async-start(f32[8,24,128]{2,1,0:T(8,128)} %get-tuple-element.25), calls=%async_computation.4 | async-start | bytes 196608 | tf_op jit(solution)/shard_map/all_to_all | solution.py:253
  152.9 2.3 %copy-start.4 = (f32[768,1536]{1,0:T(8,128)S(1)}, f32[768,1536]{1,0:T(8,128)}, u32[]{:S(2)}) copy-start(f32[768,1536]{1,0:T(8,128)} %copy-done) | copy-start | bytes 14155780
  158.7 12.5 %all-to-all-start.5 = ((f32[16,16,128]{2,1,0:T(8,128)}), f32[16,16,128]{2,1,0:T(8,128)S(1)}, u32[]{:S(2)}, u32[]{:S(2)}) async-start(f32[16,16,128]{2,1,0:T(8,128)} %shard_map.88), calls=%async_computation.5 | async-start | bytes 262144 | tf_op jit(solution)/shard_map/all_to_all | solution.py:253
  172.0 10.2 %all-to-all-start.6 = ((f32[8,8,128]{2,1,0:T(8,128)}), f32[8,8,128]{2,1,0:T(8,128)S(1)}, u32[]{:S(2)}, u32[]{:S(2)}) async-start(f32[8,8,128]{2,1,0:T(8,128)} %get-tuple-element.30), calls=%async_computation.6 | async-start | bytes 65536 | tf_op jit(solution)/shard_map/all_to_all | solution.py:253
Sparse Core Ops, SparseCore 0:
  52.5 38.1 all-gather.3

commit v2 on v1

v2 whole, which is shorter than its diff:
```python
import functools

import jax
import jax.numpy as jnp
from jax import lax
from jax.experimental import pallas as pl
from jax.experimental.pallas import tpu as pltpu
from jax.sharding import Mesh, PartitionSpec as P

EPSILON = 0.25
LOG2E = 1.4426950408889634
LN2 = 0.6931471805599453
FAR = -1.0e30

BLOCK = 192
D = 1024
NI = 8 * BLOCK
NJ = 4 * BLOCK
RI = NI // 128
RJ = NJ // 128
SPAN = 4
CHUNK = 32
ROWS = 8
UNROLL = 4

VMEM = pl.BlockSpec(memory_space=pltpu.VMEM)
HBM = pl.BlockSpec(memory_space=pltpu.HBM)
SMEM = pl.BlockSpec(memory_space=pltpu.SMEM)
PARAMS = pltpu.CompilerParams(vmem_limit_bytes=40 * 1024 * 1024)


def f32(*shape):
    return jax.ShapeDtypeStruct(shape, jnp.float32)


def call(body, outs, ins, scratch=(), out_specs=None):
    return pl.pallas_call(
        body,
        out_shape=outs,
        in_specs=ins,
        out_specs=jax.tree.map(lambda _: VMEM, outs) if out_specs is None else out_specs,
        scratch_shapes=list(scratch),
        compiler_params=PARAMS,
    )


def merge(parts):
    high = functools.reduce(jnp.maximum, parts)
    mass = functools.reduce(jnp.add, [jnp.exp2(part - high) for part in parts])
    return high + jnp.log(mass) * LOG2E


def lifted(pot, lift):
    return jnp.where(lift > -1.0e29, pot + lift, FAR)


def row_chunks(k_hbm, k_ref, sems):
    parts = [pl.ds(b * 128, 128) for b in range(RJ)]
    return [pltpu.make_async_copy(k_hbm.at[p], k_ref.at[p], sems.at[b]) for b, p in enumerate(parts)]


def column_chunks(k_hbm, k_ref, sems):
    parts = [pl.ds(t * SPAN * 128, SPAN * 128) for t in range(RI // SPAN)]
    return [
        pltpu.make_async_copy(k_hbm.at[:, p], k_ref.at[:, p], sems.at[t]) for t, p in enumerate(parts)
    ]


def reduce_lanes_rows(k_ref, heads, high_ref, mass_ref, b):
    count = len(heads)

    def step(group, carry):
        rows = pl.ds(pl.multiple_of(b * 128 + group * ROWS, ROWS), ROWS)
        spot = pl.ds(pl.multiple_of(group * ROWS, ROWS), ROWS)
        tiles = [k_ref[rows, r * 128 : (r + 1) * 128] for r in range(RI)]
        for v in range(count):
            xs = [heads[v][r : r + 1, :] - tiles[r] for r in range(RI)]
            high = functools.reduce(jnp.maximum, xs)
            mass = functools.reduce(jnp.add, [jnp.exp2(x - high) for x in xs])
            high_ref[v, spot, :] = high
            mass_ref[v, spot, :] = mass
        return carry

    lax.fori_loop(0, 128 // ROWS, step, 0, unroll=UNROLL)
    results = []
    for v in range(count):
        high = jnp.transpose(high_ref[v])
        mass = jnp.transpose(mass_ref[v])
        top = jnp.max(high, axis=0, keepdims=True)
        total = jnp.sum(mass * jnp.exp2(high - top), axis=0, keepdims=True)
        results.append(top + jnp.log(total) * LOG2E)
    return results


def reduce_lanes(k_ref, heads, high_ref, mass_ref, copies):
    results = []
    for b in range(RJ):
        copies[b].wait()
        results.append(reduce_lanes_rows(k_ref, heads, high_ref, mass_ref, b))
    return [jnp.concatenate([rows[v] for rows in results], axis=0) for v in range(len(heads))]


def reduce_rows(k_ref, heads, wide_ref, copies):
    count = len(heads)
    for v in range(count):
        for b in range(RJ):
            row = jnp.broadcast_to(heads[v][b : b + 1, :], (128, 128))
            wide_ref[v, b * 128 : (b + 1) * 128, :] = jnp.transpose(row)
    rows_out = [[] for _ in range(count)]
    for t in range(RI // SPAN):
        copies[t].wait()
        cols = [slice((t * SPAN + q) * 128, (t * SPAN + q + 1) * 128) for q in range(SPAN)]

        def highest(group, tops):
            base = pl.multiple_of(group * CHUNK, CHUNK)
            tops = list(tops)
            for s in range(CHUNK // 8):
                rows = pl.ds(base + s * 8, 8)
                wides = [wide_ref[v, rows, :] for v in range(count)]
                for q in range(SPAN):
                    tile = k_ref[rows, cols[q]]
                    for v in range(count):
                        tops[v * SPAN + q] = jnp.maximum(tops[v * SPAN + q], wides[v] - tile)
            return tuple(tops)

        tops = lax.fori_loop(
            0, NJ // CHUNK, highest, tuple(jnp.full((8, 128), -3.0e38, jnp.float32) for _ in range(count * SPAN))
        )

        def summed(group, sums):
            base = pl.multiple_of(group * CHUNK, CHUNK)
            sums = list(sums)
            for s in range(CHUNK // 8):
                rows = pl.ds(base + s * 8, 8)
                wides = [wide_ref[v, rows, :] for v in range(count)]
                for q in range(SPAN):
                    tile = k_ref[rows, cols[q]]
                    for v in range(count):
                        n = v * SPAN + q
                        sums[n] = sums[n] + jnp.exp2((wides[v] - tile) - tops[n])
            return tuple(sums)

        sums = lax.fori_loop(
            0, NJ // CHUNK, summed, tuple(jnp.zeros((8, 128), jnp.float32) for _ in range(count * SPAN))
        )
        for v in range(count):
            for q in range(SPAN):
                high, mass = tops[v * SPAN + q], sums[v * SPAN + q]
                top = jnp.max(high, axis=0, keepdims=True)
                total = jnp.sum(mass * jnp.exp2(high - top), axis=0, keepdims=True)
                rows_out[v].append(top + jnp.log(total) * LOG2E)
    return [jnp.concatenate(rows, axis=0) for rows in rows_out]


def pack_body(gen, ref, out):
    both = jnp.concatenate([gen[...].astype(jnp.float32), ref[...].astype(jnp.float32)], axis=0)
    out[...] = jnp.transpose(both).astype(jnp.bfloat16)


def unpack_body(info, raw, a_out, b_out):
    a_is_gen = info[0] == 1
    b_is_gen = info[1] == 1
    for k in range(D // 128):
        even = raw[2 * k]
        odd = raw[2 * k + 1]
        gen = jnp.concatenate([even[:, :64], odd[:, :64]], axis=1)
        ref = jnp.concatenate([even[:, 64:], odd[:, 64:]], axis=1)
        cols = slice(k * 128, (k + 1) * 128)
        a = jnp.where(a_is_gen, gen, ref)
        for n in range(4):
            a_out[n, :, cols] = a
        b_out[:, cols] = jnp.where(b_is_gen, gen, ref)


def norm_parts(values):
    values = values.astype(jnp.float32)
    values = values * values
    return functools.reduce(jnp.add, [values[:, k * 128 : (k + 1) * 128] for k in range(D // 128)])


def cost_body(
    info, own, other, cols, lift_i, k_hbm, part_out, a_ref, b_ref, k_ref, high_ref, mass_ref, sq_ref, in_sems, out_sems
):
    scale = LOG2E / EPSILON
    c = info[2]
    loads = [
        pltpu.make_async_copy(own, a_ref.at[c], in_sems.at[0]),
        pltpu.make_async_copy(other, a_ref.at[1 - c], in_sems.at[1]),
    ]
    chunks = [pl.ds(b * 256, 256) for b in range(3)]
    loads += [pltpu.make_async_copy(cols.at[p], b_ref.at[p], in_sems.at[2 + b]) for b, p in enumerate(chunks)]
    for load in loads:
        load.start()
    stores = row_chunks(k_ref, k_hbm, out_sems)
    heads = [lift_i[...]]
    loads[0].wait()
    loads[1].wait()
    for which in range(2):
        for s in range(6):
            turned = jnp.transpose(norm_parts(a_ref[which, s * 128 : (s + 1) * 128, :]))
            sq_ref[which * 6 + s : which * 6 + s + 1, :] = jnp.sum(turned, axis=0, keepdims=True) * (0.5 * scale)
    result = []
    for b in range(3):
        loads[2 + b].wait()
        rows = b_ref[b * 256 : (b + 1) * 256, :]
        row_sq = jnp.sum(norm_parts(rows), axis=1, keepdims=True) * (0.5 * scale)
        for which in range(2):
            for t in range(3):
                inner = lax.dot_general(
                    rows,
                    a_ref[which, t * 256 : (t + 1) * 256, :],
                    (((1,), (1,)), ((), ())),
                    preferred_element_type=jnp.float32,
                )
                for s in range(2):
                    r = which * 6 + t * 2 + s
                    k_ref[b * 256 : (b + 1) * 256, r * 128 : (r + 1) * 128] = (
                        row_sq + sq_ref[r : r + 1, :]
                    ) - scale * inner[:, s * 128 : (s + 1) * 128]
        for half in (2 * b, 2 * b + 1):
            stores[half].start()
            result.append(reduce_lanes_rows(k_ref, heads, high_ref, mass_ref, half)[0])
    result = jnp.concatenate(result, axis=0)
    for n in range(4):
        part_out[n, 0:RJ, :] = result
        part_out[n, RJ:8, :] = jnp.zeros((8 - RJ, 128), jnp.float32)
    for store in stores:
        store.wait()


def second_body(k_hbm, got, lift_j, out, g1_out, k_ref, sems, wide_ref):
    copies = column_chunks(k_hbm, k_ref, sems)
    for copy in copies:
        copy.start()
    g1 = -merge([got[n, 0:RJ, :] for n in range(4)])
    g1_out[...] = g1
    lift = lift_j[...]
    results = reduce_rows(k_ref, [lift, lifted(g1, lift)], wide_ref, copies)
    for n in range(8):
        for v in range(2):
            out[n, v * RI : (v + 1) * RI, :] = results[v]


def third_body(k_hbm, got, lift_i, out, f2_out, k_ref, sems, high_ref, mass_ref):
    copies = row_chunks(k_hbm, k_ref, sems)
    for copy in copies:
        copy.start()
    f1 = -merge([got[n, 0:RI, :] for n in range(8)])
    f2 = 0.5 * (f1 - merge([got[n, RI : 2 * RI, :] for n in range(8)]))
    f2_out[...] = f2
    lift = lift_i[...]
    results = reduce_lanes(k_ref, [lifted(f1, lift), lifted(f2, lift)], high_ref, mass_ref, copies)
    for n in range(4):
        for v in range(2):
            out[n, v * 8 : v * 8 + RJ, :] = results[v]
            out[n, v * 8 + RJ : v * 8 + 8, :] = jnp.zeros((8 - RJ, 128), jnp.float32)


def fourth_body(k_hbm, got, lift_j, g1, out, g3_out, k_ref, sems, wide_ref):
    copies = column_chunks(k_hbm, k_ref, sems)
    for copy in copies:
        copy.start()
    g2 = 0.5 * (g1[...] - merge([got[n, 0:RJ, :] for n in range(4)]))
    g3 = 0.5 * (g2 - merge([got[n, 8 : 8 + RJ, :] for n in range(4)]))
    g3_out[...] = g3
    lift = lift_j[...]
    results = reduce_rows(k_ref, [lifted(g2, lift), lifted(g3, lift)], wide_ref, copies)
    for n in range(8):
        for v in range(2):
            out[n, v * RI : (v + 1) * RI, :] = results[v]


def fifth_body(info, k_hbm, got, lift_i, f2, g3, out, k_ref, sems, f4_ref, high_ref, mass_ref):
    copies = row_chunks(k_hbm, k_ref, sems)
    for copy in copies:
        copy.start()
    f3 = 0.5 * (f2[...] - merge([got[n, 0:RI, :] for n in range(8)]))
    f4 = 0.5 * (f3 - merge([got[n, RI : 2 * RI, :] for n in range(8)]))
    f4_ref[0:RI, :] = f4
    lift = lift_i[...]
    (result,) = reduce_lanes(k_ref, [lifted(f3, lift)], high_ref, mass_ref, copies)
    shifted = result - g3[...]
    mine = f4_ref[pl.ds(info[3], 2), :]
    for n in range(16):
        out[n, 0:RJ, :] = shifted
        out[n, RJ : RJ + 2, :] = mine


def last_body(got, gen_weight, ref_weight, ref_full_weight, pots, g4_out, share):
    g4 = merge([got[n * 4 + 1][0:RJ, :] for n in range(4)]) * (-0.5 * LN2)
    g4_out[0:RJ, :] = g4
    g4_out[RJ:8, :] = jnp.zeros((8 - RJ, 128), jnp.float32)
    total = jnp.sum(jnp.where(ref_full_weight[...] > 0.0, g4 * ref_full_weight[...], 0.0))
    for n in range(4):
        own = slice(RJ, RJ + 2)
        gen_pot = got[n * 4 + 1][own, :] * LN2
        gen_self = got[n * 4][own, :] * LN2
        ref_self = got[n * 4 + 3][own, :] * LN2
        pots[n, 0:2, :] = gen_pot
        pots[n, 2:4, :] = gen_self
        pots[n, 4:6, :] = ref_self
        pots[n, 6:8, :] = jnp.zeros((2, 128), jnp.float32)
        total += jnp.sum(jnp.where(gen_weight[n] > 0.0, (gen_pot - gen_self) * gen_weight[n], 0.0))
        total -= jnp.sum(jnp.where(ref_weight[n] > 0.0, ref_self * ref_weight[n], 0.0))
    for n in range(8):
        share[n, :, :] = jnp.full((8, 128), total, jnp.float32)


def held(chunks):
    return [pltpu.VMEM((NJ, NI), jnp.float32), pltpu.SemaphoreType.DMA((chunks,))]


def partials(count):
    return [pltpu.VMEM((count, 128, 128), jnp.float32)] * 2


def wide(count):
    return [pltpu.VMEM((count, NJ, 128), jnp.float32)]


def stage_cost(*args):
    scratch = [
        pltpu.VMEM((2, NJ, D), jnp.bfloat16),
        pltpu.VMEM((NJ, D), jnp.bfloat16),
        pltpu.VMEM((NJ, NI), jnp.float32),
        *partials(1),
        pltpu.VMEM((16, 128), jnp.float32),
        pltpu.SemaphoreType.DMA((5,)),
        pltpu.SemaphoreType.DMA((RJ,)),
    ]
    outs = (f32(NJ, NI), f32(4, 8, 128))
    return call(cost_body, outs, [SMEM, HBM, HBM, HBM, VMEM], scratch, (HBM, VMEM))(*args)


def stage_second(*args):
    outs = (f32(8, 2 * RI, 128), f32(RJ, 128))
    return call(second_body, outs, [HBM, VMEM, VMEM], held(RI // SPAN) + wide(2))(*args)


def stage_third(*args):
    outs = (f32(4, 16, 128), f32(RI, 128))
    return call(third_body, outs, [HBM, VMEM, VMEM], held(RJ) + partials(2))(*args)


def stage_fourth(*args):
    outs = (f32(8, 2 * RI, 128), f32(RJ, 128))
    return call(fourth_body, outs, [HBM, VMEM, VMEM, VMEM], held(RI // SPAN) + wide(2))(*args)


def stage_fifth(*args):
    scratch = held(RJ) + [pltpu.VMEM((16, 128), jnp.float32)] + partials(1)
    return call(fifth_body, f32(16, 8, 128), [SMEM, HBM] + [VMEM] * 4, scratch)(*args)


def spread(operand, axes):
    return lax.all_to_all(operand, axes, 0, 0, tiled=True)


def local(gen_points, reference_embeddings, gen_count, ref_count):
    y, x, c, zl = (lax.axis_index(name) for name in ("y", "x", "c", "zl"))
    a_is_gen = zl < 3
    b_is_gen = zl == 0
    bf16 = jnp.bfloat16
    packed = call(pack_body, jax.ShapeDtypeStruct((BLOCK, 128), bf16), [VMEM, VMEM])(
        jnp.transpose(gen_points), jnp.transpose(reference_embeddings)
    )
    raw = lax.all_gather(packed, ("zh", "zl"))

    info = jnp.stack(
        [a_is_gen.astype(jnp.int32), b_is_gen.astype(jnp.int32), c, c * 6 + (3 * y) // 2]
    ).astype(jnp.int32)
    counts = jnp.stack([gen_count, ref_count]).reshape(2, 4, 4, 2)
    totals = jnp.sum(counts, axis=(1, 2, 3)).astype(jnp.float32)
    weights2 = -jnp.log(totals) * LOG2E
    place = jnp.arange(BLOCK, dtype=jnp.int32)
    a_set = jnp.where(a_is_gen, 0, 1)
    b_set = jnp.where(b_is_gen, 0, 1)
    count_i = jnp.transpose(counts[a_set, :, x]).reshape(8)
    count_j = counts[b_set, y, :, c]
    lift_i = jnp.where(place[None, :] < count_i[:, None], weights2[a_set], FAR).reshape(RI, 128)
    lift_j = jnp.where(place[None, :] < count_j[:, None], weights2[b_set], FAR).reshape(RJ, 128)
    spots = jnp.arange(256, dtype=jnp.int32) - 64 * (y % 2)
    inside = spots >= 0
    gen_in = inside[None, :] & (spots[None, :] < counts[0, y, :, c][:, None])
    ref_in = inside[None, :] & (spots[None, :] < counts[1, y, :, c][:, None])
    gen_weight = jnp.where(gen_in, 1.0 / totals[0], 0.0).reshape(4, 2, 128)
    ref_weight = jnp.where(ref_in, 1.0 / totals[1], 0.0).reshape(4, 2, 128)
    ref_full = jnp.where(place[None, :] < counts[1, y, :, c][:, None], 1.0 / totals[1], 0.0).reshape(RJ, 128)

    a_wide, b_own = call(
        unpack_body,
        (jax.ShapeDtypeStruct((4, BLOCK, D), bf16), jax.ShapeDtypeStruct((BLOCK, D), bf16)),
        [SMEM, VMEM],
    )(info, raw)
    b_all = lax.all_gather(b_own, "x")
    a_half = spread(a_wide, "y")
    a_other = lax.ppermute(a_half, "c", [(0, 1), (1, 0)])

    cost, part = stage_cost(info, a_half.reshape(NJ, D), a_other.reshape(NJ, D), b_all.reshape(NJ, D), lift_i)
    part, g1 = stage_second(cost, spread(part, "x"), lift_j)
    part, f2 = stage_third(cost, spread(part, ("y", "c")), lift_i)
    part, g3 = stage_fourth(cost, spread(part, "x"), lift_j, g1)
    part = stage_fifth(info, cost, spread(part, ("y", "c")), lift_i, f2, g3)
    got = spread(part, ("x", "zl"))
    pots, g4, share = call(
        last_body, (f32(4, 8, 128), f32(8, 128), f32(8, 8, 128)), [VMEM] * 4
    )(got, gen_weight, ref_weight, ref_full)
    divergence = jnp.sum(spread(share, ("y", "c"))[:, 0, 0])

    mine = lax.dynamic_index_in_dim(pots, x, 0, keepdims=False)
    mine = lax.dynamic_slice_in_dim(mine.reshape(4, 256), 64 * (y % 2), BLOCK, 1)
    ref_pot = lax.dynamic_slice_in_dim(g4.reshape(1024), x * BLOCK, BLOCK, 0)
    return mine[0], ref_pot, mine[1], mine[2], divergence


def solution(mesh):
    fine = Mesh(mesh.devices.reshape(4, 4, 2, 4, 4), ("y", "x", "c", "zh", "zl"))
    tile, feat = ("y", "x", "c"), ("zh", "zl")
    return jax.shard_map(
        local,
        mesh=fine,
        in_specs=(P(tile, feat), P(tile, feat), P(), P()),
        out_specs=(P(tile), P(tile), P(tile), P(tile), P()),
        check_vma=False,
    )
```

time: 191 us -> 196 us (1.026)
  blocking collectives: 44.6 us -> 33.9 us
  starting transfers between devices: 37.6 us -> 43.9 us
  waiting for transfers between devices: 48.8 us -> 53.4 us
  Pallas kernels: 24.8 us -> 28.2 us
  local copies, waits for them, and re-layouts: 15.7 us -> 17.7 us
    all_to_all x1 -> x0, blocking collectives: 10.7 us -> none  [spread(): return lax.all_to_all(operand, axes, 0, 0, tiled=True)]
    all_to_all x6 -> x7, starting transfers between devices: 26.6 us -> 32.9 us  [spread(): return lax.all_to_all(operand, axes, 0, 0, tiled=True)]
    all_to_all x6 -> x7, waiting for transfers between devices: 33 us -> 37.7 us  [spread(): return lax.all_to_all(operand, axes, 0, 0, tiled=True)]
    pallas_call x5 -> x6, Pallas kernels: 21.6 us -> 25.1 us  [the longest x1 7.79 us: stage_cost(): call(cost_body, outs, [SMEM, HBM, HBM, HBM, VMEM], scratch, (HBM, VMEM))]
    unnamed x19 -> x21, local copies, waits for them, and re-layouts: 12.3 us -> 14.4 us
  transfers between devices with their start and end apart: 8 -> 9, of which waited for: 7 -> 8; matrix products, arithmetic and copies ran while one was open for 3% -> 3% of each run, Pallas kernels for 0% -> 0%
where the time goes in v2:
time: 196 us; the launch traced here: 195 us
  waiting for transfers between devices  53.4 us (27%)
  starting transfers between devices  43.9 us (22%)
  blocking collectives  33.9 us (17%)
  Pallas kernels  28.2 us (14%)
  local copies, waits for them, and re-layouts  17.7 us (9%)
  between operations  15.6 us (8%)
  other arithmetic  2.43 us (1%)
    all_to_all x7, waiting for transfers between devices, spread(): return lax.all_to_all(operand, axes, 0, 0, tiled=True)  37.7 us
    all_gather x1, blocking collectives, local(): raw = lax.all_gather(packed, ('zh', 'zl'))  33.9 us
    all_to_all x7, starting transfers between devices, spread(): return lax.all_to_all(operand, axes, 0, 0, tiled=True)  32.9 us
    all_gather x1, waiting for transfers between devices, local(): b_all = lax.all_gather(b_own, 'x')  15 us
    unnamed x21, local copies, waits for them, and re-layouts  14.4 us
    ppermute x1, starting transfers between devices, local(): a_other = lax.ppermute(a_half, 'c', [(0, 1), (1, 0)])  11 us
    pallas_call x1, Pallas kernels, stage_cost(): call(cost_body, outs, [SMEM, HBM, HBM, HBM, VMEM], scratch, (HBM, VMEM))  7.79 us
    pallas_call x1, Pallas kernels, stage_fourth(): call(fourth_body, outs, [HBM, VMEM, VMEM, VMEM], held(RI // SPAN) + wide(2))  4.78 us
  transfers between devices with their start and end apart: 9, of which 8 were waited for; matrix products, arithmetic and copies ran while one was open for 3% of the time, Pallas kernels for 0%

profile of v2, /device:TPU:1, one launch (start us, length us, event | category | flops | bytes accessed | tf_op | source)
XLA Modules:
  0.0 195.2 jit_solution(12689958396225585816)
XLA Ops:
  7.2 0.7 copy-done.6
  7.9 0.8 copy-done.7
  8.8 33.9 %all-gather = bf16[3072,128]{1,0:T(8,128)(2,1)S(1)} all-gather(bf16[192,128]{1,0:T(8,128)(2,1)S(1)} %shard_map.83), channel_id=2, replica_groups=mesh['y'=4,'x'=4,'c'=2,'zh'=4,'zl'=4] {'zh','zl'}, dimensions={0}, use_global_device_ids=true | all-gather | bytes 835584 | tf_op jit(solution)/shard_map/all_gather | solution.py:367
  42.8 2.4 %shard_map.84 = (bf16[4,192,1024]{2,1,0:T(8,128)(2,1)}, bf16[192,1024]{1,0:T(8,128)(2,1)}) custom-call(s32[4]{0:T(128)S(1)} %pad_add_fusion.info, bf16[16,192,128]{2,1,0:T(8,128)(2,1)S(1)} %bitcast.21), custom_call_target="tpu_custom_call" | custom-call | tf_op jit(solution)/shard_map/pallas_call | solution.py:390
  45.2 4.3 %all-to-all-start = ((bf16[4,192,1024]{2,1,0:T(8,128)(2,1)}), bf16[4,192,1024]{2,1,0:T(8,128)(2,1)S(1)}, u32[]{:S(2)}, u32[]{:S(2)}) async-start(bf16[4,192,1024]{2,1,0:T(8,128)(2,1)} %get-tuple-element.18), calls=%async_computation | async-start | bytes 3145728 | tf_op jit(solution)/shard_map/all_to_all | solution.py:356
  50.2 11.9 %all-to-all-done = bf16[4,192,1024]{2,1,0:T(8,128)(2,1)S(1)} async-done(((bf16[4,192,1024]{2,1,0:T(8,128)(2,1)}), bf16[4,192,1024]{2,1,0:T(8,128)(2,1)S(1)}, u32[]{:S(2)}, u32[]{:S(2)}) %all-to-all-start) | async-done | bytes 1572896 | tf_op jit(solution)/shard_map/all_to_all | solution.py:356
  62.1 11.0 %collective-permute-start = (bf16[4,192,1024]{2,1,0:T(8,128)(2,1)S(1)}, bf16[4,192,1024]{2,1,0:T(8,128)(2,1)S(1)}, u32[]{:S(2)}, u32[]{:S(2)}) collective-permute-start(bf16[4,192,1024]{2,1,0:T(8,128)(2,1)S(1)} %all-to-all-done), channel_id=1, source_target_pairs={{0,16},{16,0},{1,17},{17,1},{2,18},{18,2},{3,19},{19,3},{4,20},{20... | collective-permute-start | bytes 4718600 | tf_op jit(solution)/shard_map/ppermute | solution.py:397
  75.3 15.0 %all-gather.4.cloned.1.call-done.cols = bf16[768,1024]{1,0:T(8,128)(2,1)} async-done(((bf16[192,1024]{1,0:T(8,128)(2,1)}), bf16[768,1024]{1,0:T(8,128)(2,1)}) %all-gather.4.cloned.1.call-update) | async-done | bytes 1572880 | tf_op jit(solution)/shard_map/all_gather | solution.py:395
  90.3 1.4 copy-done.5
  91.7 7.8 %shard_map.85 = (f32[768,1536]{1,0:T(8,128)S(1)}, f32[4,8,128]{2,1,0:T(8,128)}) custom-call(s32[4]{0:T(128)S(1)} %pad_add_fusion.info, bf16[768,1024]{1,0:T(8,128)(2,1)S(1)} %bitcast.20, bf16[768,1024]{1,0:T(8,128)(2,1)S(1)} %bitcast.22, bf16[768,1024]{1,0:T(8,128)(2,1)S(1)} %copy-done.5, f32[12,128]{1,0:T(8,128)S(1)} %select_n.83.lift_i), custom_call_target="tpu_custom_call" | custom-call | tf_op jit(solution)/shard_map/pallas_call | solution.py:332
  99.5 2.1 %copy-done = f32[768,1536]{1,0:T(8,128)} copy-done((f32[768,1536]{1,0:T(8,128)}, f32[768,1536]{1,0:T(8,128)S(1)}, u32[]{:S(2)}) %copy-start) | copy-done | bytes 4718616
  101.6 3.2 %all-to-all-start.1 = ((f32[4,8,128]{2,1,0:T(8,128)}), f32[4,8,128]{2,1,0:T(8,128)S(1)}, u32[]{:S(2)}, u32[]{:S(2)}) async-start(f32[4,8,128]{2,1,0:T(8,128)} %get-tuple-element.21), calls=%async_computation.1 | async-start | bytes 32768 | tf_op jit(solution)/shard_map/all_to_all | solution.py:356
  105.7 3.4 %all-to-all-done.1.got = f32[4,8,128]{2,1,0:T(8,128)S(1)} async-done(((f32[4,8,128]{2,1,0:T(8,128)}), f32[4,8,128]{2,1,0:T(8,128)S(1)}, u32[]{:S(2)}, u32[]{:S(2)}) %all-to-all-start.1) | async-done | bytes 16416 | tf_op jit(solution)/shard_map/all_to_all | solution.py:356
  109.1 2.3 %copy-done.1 = f32[768,1536]{1,0:T(8,128)S(1)} copy-done((f32[768,1536]{1,0:T(8,128)S(1)}, f32[768,1536]{1,0:T(8,128)}, u32[]{:S(2)}) %copy-start.1) | copy-done | bytes 4718616
  111.4 4.7 %shard_map.86 = (f32[8,24,128]{2,1,0:T(8,128)}, f32[6,128]{1,0:T(8,128)S(1)}) custom-call(f32[768,1536]{1,0:T(8,128)S(1)} %copy-done.1, f32[4,8,128]{2,1,0:T(8,128)S(1)} %all-to-all-done.1.got, f32[6,128]{1,0:T(8,128)S(1)} %select_n.88.lift_j), custom_call_target="tpu_custom_call" | custom-call | tf_op jit(solution)/shard_map/pallas_call | solution.py:337
  116.2 6.1 %all-to-all-start.2 = ((f32[8,24,128]{2,1,0:T(8,128)}), f32[8,24,128]{2,1,0:T(8,128)S(1)}, u32[]{:S(2)}, u32[]{:S(2)}) async-start(f32[8,24,128]{2,1,0:T(8,128)} %get-tuple-element.22), calls=%async_computation.2 | async-start | bytes 196608 | tf_op jit(solution)/shard_map/all_to_all | solution.py:356
  123.5 3.7 %all-to-all-done.2.got = f32[8,24,128]{2,1,0:T(8,128)S(1)} async-done(((f32[8,24,128]{2,1,0:T(8,128)}), f32[8,24,128]{2,1,0:T(8,128)S(1)}, u32[]{:S(2)}, u32[]{:S(2)}) %all-to-all-start.2) | async-done | bytes 98336 | tf_op jit(solution)/shard_map/all_to_all | solution.py:356
  127.2 2.3 %copy-done.2 = f32[768,1536]{1,0:T(8,128)S(1)} copy-done((f32[768,1536]{1,0:T(8,128)S(1)}, f32[768,1536]{1,0:T(8,128)}, u32[]{:S(2)}) %copy-start.2) | copy-done | bytes 4718616
  129.6 4.0 %shard_map.87 = (f32[4,16,128]{2,1,0:T(8,128)}, f32[12,128]{1,0:T(8,128)S(1)}) custom-call(f32[768,1536]{1,0:T(8,128)S(1)} %copy-done.2, f32[8,24,128]{2,1,0:T(8,128)S(1)} %all-to-all-done.2.got, f32[12,128]{1,0:T(8,128)S(1)} %select_n.83.lift_i), custom_call_target="tpu_custom_call" | custom-call | tf_op jit(solution)/shard_map/pallas_call | solution.py:342
  133.6 3.3 %all-to-all-start.3 = ((f32[4,16,128]{2,1,0:T(8,128)}), f32[4,16,128]{2,1,0:T(8,128)S(1)}, u32[]{:S(2)}, u32[]{:S(2)}) async-start(f32[4,16,128]{2,1,0:T(8,128)} %get-tuple-element.23), calls=%async_computation.3 | async-start | bytes 65536 | tf_op jit(solution)/shard_map/all_to_all | solution.py:356
  136.9 4.2 %all-to-all-done.3.got = f32[4,16,128]{2,1,0:T(8,128)S(1)} async-done(((f32[4,16,128]{2,1,0:T(8,128)}), f32[4,16,128]{2,1,0:T(8,128)S(1)}, u32[]{:S(2)}, u32[]{:S(2)}) %all-to-all-start.3) | async-done | bytes 32800 | tf_op jit(solution)/shard_map/all_to_all | solution.py:356
  141.1 2.3 %copy-done.3 = f32[768,1536]{1,0:T(8,128)S(1)} copy-done((f32[768,1536]{1,0:T(8,128)S(1)}, f32[768,1536]{1,0:T(8,128)}, u32[]{:S(2)}) %copy-start.3) | copy-done | bytes 4718616
  143.5 4.8 %shard_map.88 = (f32[8,24,128]{2,1,0:T(8,128)}, f32[6,128]{1,0:T(8,128)S(1)}) custom-call(f32[768,1536]{1,0:T(8,128)S(1)} %copy-done.3, f32[4,16,128]{2,1,0:T(8,128)S(1)} %all-to-all-done.3.got, f32[6,128]{1,0:T(8,128)S(1)} %select_n.88.lift_j, f32[6,128]{1,0:T(8,128)S(1)} %get-tuple-element.24.g1), custom_call_target="tpu_custom_call" | custom-call | tf_op jit(solution)/shard_map/pallas_call | solution.py:347
  148.2 5.2 %all-to-all-start.4 = ((f32[8,24,128]{2,1,0:T(8,128)}), f32[8,24,128]{2,1,0:T(8,128)S(1)}, u32[]{:S(2)}, u32[]{:S(2)}) async-start(f32[8,24,128]{2,1,0:T(8,128)} %get-tuple-element.25), calls=%async_computation.4 | async-start | bytes 196608 | tf_op jit(solution)/shard_map/all_to_all | solution.py:356
  153.5 5.0 %all-to-all-done.4.got = f32[8,24,128]{2,1,0:T(8,128)S(1)} async-done(((f32[8,24,128]{2,1,0:T(8,128)}), f32[8,24,128]{2,1,0:T(8,128)S(1)}, u32[]{:S(2)}, u32[]{:S(2)}) %all-to-all-start.4) | async-done | bytes 98336 | tf_op jit(solution)/shard_map/all_to_all | solution.py:356
  158.5 2.3 %copy-done.4 = f32[768,1536]{1,0:T(8,128)S(1)} copy-done((f32[768,1536]{1,0:T(8,128)S(1)}, f32[768,1536]{1,0:T(8,128)}, u32[]{:S(2)}) %copy-start.4) | copy-done | bytes 4718616
  160.8 3.6 %shard_map.89 = f32[16,8,128]{2,1,0:T(8,128)} custom-call(s32[4]{0:T(128)S(1)} %pad_add_fusion.info, f32[768,1536]{1,0:T(8,128)S(1)} %copy-done.4, f32[8,24,128]{2,1,0:T(8,128)S(1)} %all-to-all-done.4.got, f32[12,128]{1,0:T(8,128)S(1)} %select_n.83.lift_i, f32[12,128]{1,0:T(8,128)S(1)} %get-tuple-element.26.f2, f32[6,128]{1,0:T(8,128)S(1)} %get-tuple-element.27.g3), custom_call_target="tpu_custom_call" | custom-call | tf_op jit(solution)/shard_map/pallas_call | solution.py:352
  164.5 5.2 %all-to-all-start.5 = ((f32[16,8,128]{2,1,0:T(8,128)}), f32[16,8,128]{2,1,0:T(8,128)S(1)}, u32[]{:S(2)}, u32[]{:S(2)}) async-start(f32[16,8,128]{2,1,0:T(8,128)} %shard_map.89), calls=%async_computation.5 | async-start | bytes 131072 | tf_op jit(solution)/shard_map/all_to_all | solution.py:356
  170.6 6.1 %all-to-all-done.5.got = f32[16,8,128]{2,1,0:T(8,128)S(1)} async-done(((f32[16,8,128]{2,1,0:T(8,128)}), f32[16,8,128]{2,1,0:T(8,128)S(1)}, u32[]{:S(2)}, u32[]{:S(2)}) %all-to-all-start.5) | async-done | bytes 65568 | tf_op jit(solution)/shard_map/all_to_all | solution.py:356
  176.7 0.8 shard_map.90
  177.5 5.5 %all-to-all-start.6 = ((f32[8,8,128]{2,1,0:T(8,128)}), f32[8,8,128]{2,1,0:T(8,128)S(1)}, u32[]{:S(2)}, u32[]{:S(2)}) async-start(f32[8,8,128]{2,1,0:T(8,128)} %get-tuple-element.30), calls=%async_computation.6 | async-start | bytes 65536 | tf_op jit(solution)/shard_map/all_to_all | solution.py:356
  184.3 3.5 %all-to-all-done.6 = f32[8,8,128]{2,1,0:T(8,128)S(1)} async-done(((f32[8,8,128]{2,1,0:T(8,128)}), f32[8,8,128]{2,1,0:T(8,128)S(1)}, u32[]{:S(2)}, u32[]{:S(2)}) %all-to-all-start.6) | async-done | bytes 32800 | tf_op jit(solution)/shard_map/all_to_all | solution.py:356
  (44 shorter events, 6.5 us)
Async XLA Ops:
  7.2 0.8 copy-start.6
  7.9 0.8 copy-start.7
  45.2 28.0 %copy-start.8 = (s32[32]{0:T(128)S(1)}, s32[32]{0:T(128)}, u32[]{:S(2)}) copy-start(s32[32]{0:T(128)} %param.6) | copy-start | bytes 388
  45.2 28.1 %copy-start.9 = (s32[32]{0:T(128)S(1)}, s32[32]{0:T(128)}, u32[]{:S(2)}) copy-start(s32[32]{0:T(128)} %param.7) | copy-start | bytes 388
  45.2 16.9 %all-to-all-start = ((bf16[4,192,1024]{2,1,0:T(8,128)(2,1)}), bf16[4,192,1024]{2,1,0:T(8,128)(2,1)S(1)}, u32[]{:S(2)}, u32[]{:S(2)}) async-start(bf16[4,192,1024]{2,1,0:T(8,128)(2,1)} %get-tuple-element.18), calls=%async_computation | async-start | bytes 3145728 | tf_op jit(solution)/shard_map/all_to_all | solution.py:356
  49.5 40.8 %all-gather.4.cloned.1.call-start = ((), (), s32[]{:S(2)}) async-start(), calls=%async_computation.7 | async-start | bytes 1966080 | tf_op jit(solution)/shard_map/all_gather | solution.py:395
  62.1 28.2 %collective-permute-start = (bf16[4,192,1024]{2,1,0:T(8,128)(2,1)S(1)}, bf16[4,192,1024]{2,1,0:T(8,128)(2,1)S(1)}, u32[]{:S(2)}, u32[]{:S(2)}) collective-permute-start(bf16[4,192,1024]{2,1,0:T(8,128)(2,1)S(1)} %all-to-all-done), channel_id=1, source_target_pairs={{0,16},{16,0},{1,17},{17,1},{2,18},{18,2},{3,19},{19,3},{4,20},{20... | collective-permute-start | bytes 4718600 | tf_op jit(solution)/shard_map/ppermute | solution.py:397
  90.3 1.4 copy-start.5
  99.5 2.1 %copy-start = (f32[768,1536]{1,0:T(8,128)}, f32[768,1536]{1,0:T(8,128)S(1)}, u32[]{:S(2)}) copy-start(f32[768,1536]{1,0:T(8,128)S(1)} %get-tuple-element.20.k_hbm) | copy-start | bytes 14155780
  101.6 7.4 %all-to-all-start.1 = ((f32[4,8,128]{2,1,0:T(8,128)}), f32[4,8,128]{2,1,0:T(8,128)S(1)}, u32[]{:S(2)}, u32[]{:S(2)}) async-start(f32[4,8,128]{2,1,0:T(8,128)} %get-tuple-element.21), calls=%async_computation.1 | async-start | bytes 32768 | tf_op jit(solution)/shard_map/all_to_all | solution.py:356
  109.1 2.3 %copy-start.1 = (f32[768,1536]{1,0:T(8,128)S(1)}, f32[768,1536]{1,0:T(8,128)}, u32[]{:S(2)}) copy-start(f32[768,1536]{1,0:T(8,128)} %copy-done) | copy-start | bytes 14155780
  116.2 11.1 %all-to-all-start.2 = ((f32[8,24,128]{2,1,0:T(8,128)}), f32[8,24,128]{2,1,0:T(8,128)S(1)}, u32[]{:S(2)}, u32[]{:S(2)}) async-start(f32[8,24,128]{2,1,0:T(8,128)} %get-tuple-element.22), calls=%async_computation.2 | async-start | bytes 196608 | tf_op jit(solution)/shard_map/all_to_all | solution.py:356
  127.2 2.3 %copy-start.2 = (f32[768,1536]{1,0:T(8,128)S(1)}, f32[768,1536]{1,0:T(8,128)}, u32[]{:S(2)}) copy-start(f32[768,1536]{1,0:T(8,128)} %copy-done) | copy-start | bytes 14155780
  133.6 7.5 %all-to-all-start.3 = ((f32[4,16,128]{2,1,0:T(8,128)}), f32[4,16,128]{2,1,0:T(8,128)S(1)}, u32[]{:S(2)}, u32[]{:S(2)}) async-start(f32[4,16,128]{2,1,0:T(8,128)} %get-tuple-element.23), calls=%async_computation.3 | async-start | bytes 65536 | tf_op jit(solution)/shard_map/all_to_all | solution.py:356
  141.1 2.3 %copy-start.3 = (f32[768,1536]{1,0:T(8,128)S(1)}, f32[768,1536]{1,0:T(8,128)}, u32[]{:S(2)}) copy-start(f32[768,1536]{1,0:T(8,128)} %copy-done) | copy-start | bytes 14155780
  148.2 10.2 %all-to-all-start.4 = ((f32[8,24,128]{2,1,0:T(8,128)}), f32[8,24,128]{2,1,0:T(8,128)S(1)}, u32[]{:S(2)}, u32[]{:S(2)}) async-start(f32[8,24,128]{2,1,0:T(8,128)} %get-tuple-element.25), calls=%async_computation.4 | async-start | bytes 196608 | tf_op jit(solution)/shard_map/all_to_all | solution.py:356
  158.5 2.3 %copy-start.4 = (f32[768,1536]{1,0:T(8,128)S(1)}, f32[768,1536]{1,0:T(8,128)}, u32[]{:S(2)}) copy-start(f32[768,1536]{1,0:T(8,128)} %copy-done) | copy-start | bytes 14155780
  164.5 12.2 %all-to-all-start.5 = ((f32[16,8,128]{2,1,0:T(8,128)}), f32[16,8,128]{2,1,0:T(8,128)S(1)}, u32[]{:S(2)}, u32[]{:S(2)}) async-start(f32[16,8,128]{2,1,0:T(8,128)} %shard_map.89), calls=%async_computation.5 | async-start | bytes 131072 | tf_op jit(solution)/shard_map/all_to_all | solution.py:356
  177.5 10.2 %all-to-all-start.6 = ((f32[8,8,128]{2,1,0:T(8,128)}), f32[8,8,128]{2,1,0:T(8,128)S(1)}, u32[]{:S(2)}, u32[]{:S(2)}) async-start(f32[8,8,128]{2,1,0:T(8,128)} %get-tuple-element.30), calls=%async_computation.6 | async-start | bytes 65536 | tf_op jit(solution)/shard_map/all_to_all | solution.py:356
Sparse Core Ops, SparseCore 0:
  52.4 37.8 all-gather.3

commit v3 on v2

v3 whole, which is shorter than its diff:
```python
import functools

import jax
import jax.numpy as jnp
from jax import lax
from jax.experimental import pallas as pl
from jax.experimental.pallas import tpu as pltpu
from jax.sharding import Mesh, PartitionSpec as P

EPSILON = 0.25
LOG2E = 1.4426950408889634
LN2 = 0.6931471805599453
FAR = -1.0e30

BLOCK = 192
D = 1024
NI = 8 * BLOCK
NJ = 4 * BLOCK
RI = NI // 128
RJ = NJ // 128
NEAR = 8
N1 = NEAR * 128
N2 = NI - N1

VMEM = pl.BlockSpec(memory_space=pltpu.VMEM)
HBM = pl.BlockSpec(memory_space=pltpu.HBM)
SMEM = pl.BlockSpec(memory_space=pltpu.SMEM)
PARAMS = pltpu.CompilerParams(vmem_limit_bytes=60 * 1024 * 1024)


def f32(*shape):
    return jax.ShapeDtypeStruct(shape, jnp.float32)


def call(body, outs, ins, scratch=(), out_specs=None):
    return pl.pallas_call(
        body,
        out_shape=outs,
        in_specs=ins,
        out_specs=jax.tree.map(lambda _: VMEM, outs) if out_specs is None else out_specs,
        scratch_shapes=list(scratch),
        compiler_params=PARAMS,
    )


def merge(got, count):
    parts = [got[n] for n in range(count)]
    high = functools.reduce(jnp.maximum, parts)
    mass = functools.reduce(jnp.add, [jnp.exp2(part - high) for part in parts])
    return high + jnp.log(mass) * LOG2E


def lifted(pot, lift):
    return jnp.where(lift > -1.0e29, pot + lift, FAR)


def tree(op, values):
    values = list(values)
    while len(values) > 1:
        values = [op(*values[n : n + 2]) if n + 1 < len(values) else values[n] for n in range(0, len(values), 2)]
    return values[0]


def fetch(k2_hbm, k2_ref, sems, b):
    rows = pl.ds(b * 128, 128)
    return pltpu.make_async_copy(k2_hbm.at[rows], k2_ref.at[rows], sems.at[b])


def start_fetch(k2_hbm, k2_ref, sems):
    for b in range(RJ):
        fetch(k2_hbm, k2_ref, sems, b).start()


def k_tile(k1_ref, k2_ref, rows, r):
    if r < NEAR:
        return k1_ref[rows, r * 128 : (r + 1) * 128]
    return k2_ref[rows, (r - NEAR) * 128 : (r - NEAR + 1) * 128]


def lanes_block(k1_ref, k2_ref, heads, high_ref, mass_ref, base):
    for group in range(16):
        rows = pl.ds(base + group * 8, 8)
        tiles = [k_tile(k1_ref, k2_ref, rows, r) for r in range(RI)]
        for v in range(len(heads)):
            xs = [heads[v][r : r + 1, :] - tiles[r] for r in range(RI)]
            high = tree(jnp.maximum, xs)
            high_ref[v, rows, :] = high
            mass_ref[v, rows, :] = tree(jnp.add, [jnp.exp2(x - high) for x in xs])


def lanes_result(count, high_ref, mass_ref):
    results = []
    for v in range(count):
        rows_out = []
        for b in range(RJ):
            high = jnp.transpose(high_ref[v, b * 128 : (b + 1) * 128, :])
            mass = jnp.transpose(mass_ref[v, b * 128 : (b + 1) * 128, :])
            top = jnp.max(high, axis=0, keepdims=True)
            total = jnp.sum(mass * jnp.exp2(high - top), axis=0, keepdims=True)
            rows_out.append((top, total))
        top = jnp.concatenate([row[0] for row in rows_out], axis=0)
        total = jnp.concatenate([row[1] for row in rows_out], axis=0)
        results.append(top + jnp.log(total) * LOG2E)
    return results


def reduce_lanes(k1_ref, k2_hbm, k2_ref, sems, heads, high_ref, mass_ref):
    def step(b, carry):
        fetch(k2_hbm, k2_ref, sems, b).wait()
        lanes_block(k1_ref, k2_ref, heads, high_ref, mass_ref, pl.multiple_of(b * 128, 128))
        return carry

    lax.fori_loop(0, RJ, step, 0)
    return lanes_result(len(heads), high_ref, mass_ref)


def reduce_rows(k1_ref, k2_hbm, k2_ref, sems, heads, head_ref, high_ref, mass_ref):
    count = len(heads)
    for v in range(count):
        head_ref[v, 0:RJ, :] = heads[v]

    def step(b, carry):
        fetch(k2_hbm, k2_ref, sems, b).wait()
        wides = [
            jnp.transpose(jnp.broadcast_to(head_ref[v, pl.ds(b, 1), :], (128, 128))) for v in range(count)
        ]
        spot = pl.ds(pl.multiple_of(b * 8, 8), 8)
        for r in range(RI):
            cols = slice(r * 128, (r + 1) * 128)
            tiles = [k_tile(k1_ref, k2_ref, pl.ds(b * 128 + group * 8, 8), r) for group in range(16)]
            for v in range(count):
                xs = [wides[v][group * 8 : group * 8 + 8, :] - tiles[group] for group in range(16)]
                high = tree(jnp.maximum, xs)
                high_ref[v, spot, cols] = high
                mass_ref[v, spot, cols] = tree(jnp.add, [jnp.exp2(x - high) for x in xs])
        return carry

    lax.fori_loop(0, RJ, step, 0)
    results = []
    for v in range(count):
        tops, totals = [], []
        for r in range(RI):
            cols = slice(r * 128, (r + 1) * 128)
            high = high_ref[v, :, cols]
            top = jnp.max(high, axis=0, keepdims=True)
            tops.append(top)
            totals.append(jnp.sum(mass_ref[v, :, cols] * jnp.exp2(high - top), axis=0, keepdims=True))
        results.append(jnp.concatenate(tops, axis=0) + jnp.log(jnp.concatenate(totals, axis=0)) * LOG2E)
    return results


def pack_body(gen, ref, out):
    both = jnp.concatenate([gen[...].astype(jnp.float32), ref[...].astype(jnp.float32)], axis=0)
    out[...] = jnp.transpose(both).astype(jnp.bfloat16)


def select_set(is_gen, raw, k):
    even, odd = raw[2 * k], raw[2 * k + 1]
    gen = jnp.concatenate([even[:, :64], odd[:, :64]], axis=1)
    ref = jnp.concatenate([even[:, 64:], odd[:, 64:]], axis=1)
    return jnp.where(is_gen, gen, ref)


def unpack_b_body(info, raw, out):
    for k in range(D // 128):
        out[:, k * 128 : (k + 1) * 128] = select_set(info[1] == 1, raw, k)


def unpack_a_body(info, raw, out):
    for k in range(D // 128):
        part = select_set(info[0] == 1, raw, k)
        for n in range(4):
            out[n, :, k * 128 : (k + 1) * 128] = part


def norm_parts(values):
    values = values.astype(jnp.float32)
    values = values * values
    return functools.reduce(jnp.add, [values[:, k * 128 : (k + 1) * 128] for k in range(D // 128)])


def cost_body(
    info, own, other, cols, lift_i, k1_ref, k2_hbm, part_out,
    a_ref, b_ref, k2_ref, high_ref, mass_ref, sq_ref, in_sems, out_sems,
):
    scale = LOG2E / EPSILON
    c = info[2]
    loads = [
        pltpu.make_async_copy(own, a_ref.at[c], in_sems.at[0]),
        pltpu.make_async_copy(other, a_ref.at[1 - c], in_sems.at[1]),
    ]
    chunks = [pl.ds(b * 256, 256) for b in range(3)]
    loads += [pltpu.make_async_copy(cols.at[p], b_ref.at[p], in_sems.at[2 + b]) for b, p in enumerate(chunks)]
    for load in loads:
        load.start()
    heads = [lift_i[...]]
    loads[0].wait()
    loads[1].wait()
    for which in range(2):
        for s in range(6):
            turned = jnp.transpose(norm_parts(a_ref[which, s * 128 : (s + 1) * 128, :]))
            sq_ref[which * 6 + s : which * 6 + s + 1, :] = jnp.sum(turned, axis=0, keepdims=True) * (0.5 * scale)
    stores = [fetch(k2_ref, k2_hbm, out_sems, b) for b in range(RJ)]
    for b in range(4):
        if b < 3:
            loads[2 + b].wait()
            rows = b_ref[b * 256 : (b + 1) * 256, :]
            row_sq = jnp.sum(norm_parts(rows), axis=1, keepdims=True) * (0.5 * scale)
            for which in range(2):
                for t in range(3):
                    inner = lax.dot_general(
                        rows,
                        a_ref[which, t * 256 : (t + 1) * 256, :],
                        (((1,), (1,)), ((), ())),
                        preferred_element_type=jnp.float32,
                    )
                    for s in range(2):
                        r = which * 6 + t * 2 + s
                        tile = (row_sq + sq_ref[r : r + 1, :]) - scale * inner[:, s * 128 : (s + 1) * 128]
                        if r < NEAR:
                            k1_ref[b * 256 : (b + 1) * 256, r * 128 : (r + 1) * 128] = tile
                        else:
                            k2_ref[b * 256 : (b + 1) * 256, (r - NEAR) * 128 : (r - NEAR + 1) * 128] = tile
        if b > 0:
            for half in (2 * b - 2, 2 * b - 1):
                lanes_block(k1_ref, k2_ref, heads, high_ref, mass_ref, half * 128)
        if b < 3:
            stores[2 * b].start()
            stores[2 * b + 1].start()
    (result,) = lanes_result(1, high_ref, mass_ref)
    for n in range(4):
        part_out[n, 0:RJ, :] = result
        part_out[n, RJ:8, :] = jnp.zeros((8 - RJ, 128), jnp.float32)
    for store in stores:
        store.wait()


def second_body(k1_ref, k2_hbm, got, lift_j, out, g1_out, k2_ref, sems, head_ref, high_ref, mass_ref):
    start_fetch(k2_hbm, k2_ref, sems)
    g1 = -merge(got, 4)[0:RJ, :]
    g1_out[...] = g1
    lift = lift_j[...]
    heads = [lift, lifted(g1, lift)]
    results = reduce_rows(k1_ref, k2_hbm, k2_ref, sems, heads, head_ref, high_ref, mass_ref)
    for n in range(8):
        for v in range(2):
            out[n, v * RI : (v + 1) * RI, :] = results[v]


def third_body(k1_ref, k2_hbm, got, lift_i, out, f2_out, k2_ref, sems, high_ref, mass_ref):
    start_fetch(k2_hbm, k2_ref, sems)
    merged = -merge(got, 8)
    f1 = merged[0:RI, :]
    f2 = 0.5 * (f1 + merged[RI : 2 * RI, :])
    f2_out[...] = f2
    lift = lift_i[...]
    heads = [lifted(f1, lift), lifted(f2, lift)]
    results = reduce_lanes(k1_ref, k2_hbm, k2_ref, sems, heads, high_ref, mass_ref)
    for n in range(4):
        for v in range(2):
            out[n, v * 8 : v * 8 + RJ, :] = results[v]
            out[n, v * 8 + RJ : v * 8 + 8, :] = jnp.zeros((8 - RJ, 128), jnp.float32)


def fourth_body(k1_ref, k2_hbm, got, lift_j, g1, out, g3_out, k2_ref, sems, head_ref, high_ref, mass_ref):
    start_fetch(k2_hbm, k2_ref, sems)
    merged = -merge(got, 4)
    g2 = 0.5 * (g1[...] + merged[0:RJ, :])
    g3 = 0.5 * (g2 + merged[8 : 8 + RJ, :])
    g3_out[...] = g3
    lift = lift_j[...]
    heads = [lifted(g2, lift), lifted(g3, lift)]
    results = reduce_rows(k1_ref, k2_hbm, k2_ref, sems, heads, head_ref, high_ref, mass_ref)
    for n in range(8):
        for v in range(2):
            out[n, v * RI : (v + 1) * RI, :] = results[v]


def fifth_body(info, k1_ref, k2_hbm, got, lift_i, f2, g3, out, k2_ref, sems, high_ref, mass_ref, f4_ref):
    start_fetch(k2_hbm, k2_ref, sems)
    merged = -merge(got, 8)
    f3 = 0.5 * (f2[...] + merged[0:RI, :])
    f4 = 0.5 * (f3 + merged[RI : 2 * RI, :])
    f4_ref[0:RI, :] = f4
    heads = [lifted(f3, lift_i[...])]
    (result,) = reduce_lanes(k1_ref, k2_hbm, k2_ref, sems, heads, high_ref, mass_ref)
    shifted = result - g3[...]
    mine = f4_ref[pl.ds(info[3], 2), :]
    for n in range(16):
        out[n, 0:RJ, :] = shifted
        out[n, RJ : RJ + 2, :] = mine


def last_body(got, gen_weight, ref_weight, ref_full_weight, pots, g4_out, share):
    g4 = merge([got[n * 4 + 1, 0:RJ, :] for n in range(4)], 4) * (-0.5 * LN2)
    g4_out[0:RJ, :] = g4
    g4_out[RJ:8, :] = jnp.zeros((8 - RJ, 128), jnp.float32)
    total = jnp.sum(jnp.where(ref_full_weight[...] > 0.0, g4 * ref_full_weight[...], 0.0))
    for n in range(4):
        own = slice(RJ, RJ + 2)
        gen_pot = got[n * 4 + 1][own, :] * LN2
        gen_self = got[n * 4][own, :] * LN2
        ref_self = got[n * 4 + 3][own, :] * LN2
        pots[n, 0:2, :] = gen_pot
        pots[n, 2:4, :] = gen_self
        pots[n, 4:6, :] = ref_self
        pots[n, 6:8, :] = jnp.zeros((2, 128), jnp.float32)
        total += jnp.sum(jnp.where(gen_weight[n] > 0.0, (gen_pot - gen_self) * gen_weight[n], 0.0))
        total -= jnp.sum(jnp.where(ref_weight[n] > 0.0, ref_self * ref_weight[n], 0.0))
    for n in range(8):
        share[n, :, :] = jnp.full((8, 128), total, jnp.float32)


F32 = jnp.float32
BF16 = jnp.bfloat16
STREAM = [pltpu.VMEM((NJ, N2), F32), pltpu.SemaphoreType.DMA((RJ,))]


def lane_scratch(count):
    return [pltpu.VMEM((count, NJ, 128), F32)] * 2


def row_scratch(count):
    return [pltpu.VMEM((count, 8, 128), F32)] + [pltpu.VMEM((count, 8 * RJ, NI), F32)] * 2


def stage_pack(*args):
    return call(pack_body, jax.ShapeDtypeStruct((BLOCK, 128), BF16), [VMEM, VMEM])(*args)


def stage_unpack_b(*args):
    return call(unpack_b_body, jax.ShapeDtypeStruct((BLOCK, D), BF16), [SMEM, VMEM])(*args)


def stage_unpack_a(*args):
    return call(unpack_a_body, jax.ShapeDtypeStruct((4, BLOCK, D), BF16), [SMEM, VMEM])(*args)


def stage_cost(*args):
    scratch = [
        pltpu.VMEM((2, NJ, D), BF16),
        pltpu.VMEM((NJ, D), BF16),
        pltpu.VMEM((NJ, N2), F32),
        *lane_scratch(1),
        pltpu.VMEM((16, 128), F32),
        pltpu.SemaphoreType.DMA((5,)),
        pltpu.SemaphoreType.DMA((RJ,)),
    ]
    outs = (f32(NJ, N1), f32(NJ, N2), f32(4, 8, 128))
    return call(cost_body, outs, [SMEM, HBM, HBM, HBM, VMEM], scratch, (VMEM, HBM, VMEM))(*args)


def stage_second(*args):
    outs = (f32(8, 2 * RI, 128), f32(RJ, 128))
    return call(second_body, outs, [VMEM, HBM, VMEM, VMEM], STREAM + row_scratch(2))(*args)


def stage_third(*args):
    outs = (f32(4, 16, 128), f32(RI, 128))
    return call(third_body, outs, [VMEM, HBM, VMEM, VMEM], STREAM + lane_scratch(2))(*args)


def stage_fourth(*args):
    outs = (f32(8, 2 * RI, 128), f32(RJ, 128))
    return call(fourth_body, outs, [VMEM, HBM, VMEM, VMEM, VMEM], STREAM + row_scratch(2))(*args)


def stage_fifth(*args):
    scratch = STREAM + lane_scratch(1) + [pltpu.VMEM((16, 128), F32)]
    return call(fifth_body, f32(16, 8, 128), [SMEM, VMEM, HBM] + [VMEM] * 4, scratch)(*args)


def spread(operand, axes):
    return lax.all_to_all(operand, axes, 0, 0, tiled=True)


def local(gen_points, reference_embeddings, gen_count, ref_count):
    y, x, c, zl = (lax.axis_index(name) for name in ("y", "x", "c", "zl"))
    a_is_gen = zl < 3
    b_is_gen = zl == 0
    packed = stage_pack(jnp.transpose(gen_points), jnp.transpose(reference_embeddings))
    raw = lax.all_gather(packed, ("zh", "zl"))

    info = jnp.stack(
        [a_is_gen.astype(jnp.int32), b_is_gen.astype(jnp.int32), c, c * 6 + (3 * y) // 2]
    ).astype(jnp.int32)
    counts = jnp.stack([gen_count, ref_count]).reshape(2, 4, 4, 2)
    totals = jnp.sum(counts, axis=(1, 2, 3)).astype(jnp.float32)
    weights2 = -jnp.log(totals) * LOG2E
    place = jnp.arange(BLOCK, dtype=jnp.int32)
    a_set = jnp.where(a_is_gen, 0, 1)
    b_set = jnp.where(b_is_gen, 0, 1)
    count_i = jnp.transpose(counts[a_set, :, x]).reshape(8)
    count_j = counts[b_set, y, :, c]
    lift_i = jnp.where(place[None, :] < count_i[:, None], weights2[a_set], FAR).reshape(RI, 128)
    lift_j = jnp.where(place[None, :] < count_j[:, None], weights2[b_set], FAR).reshape(RJ, 128)
    spots = jnp.arange(256, dtype=jnp.int32) - 64 * (y % 2)
    inside = spots >= 0
    gen_in = inside[None, :] & (spots[None, :] < counts[0, y, :, c][:, None])
    ref_in = inside[None, :] & (spots[None, :] < counts[1, y, :, c][:, None])
    gen_weight = jnp.where(gen_in, 1.0 / totals[0], 0.0).reshape(4, 2, 128)
    ref_weight = jnp.where(ref_in, 1.0 / totals[1], 0.0).reshape(4, 2, 128)
    ref_full = jnp.where(place[None, :] < counts[1, y, :, c][:, None], 1.0 / totals[1], 0.0).reshape(RJ, 128)

    b_all = lax.all_gather(stage_unpack_b(info, raw), "x")
    a_half = spread(stage_unpack_a(info, raw), "y")
    a_other = lax.ppermute(a_half, "c", [(0, 1), (1, 0)])

    k1, k2, part = stage_cost(
        info, a_half.reshape(NJ, D), a_other.reshape(NJ, D), b_all.reshape(NJ, D), lift_i
    )
    part, g1 = stage_second(k1, k2, spread(part, "x"), lift_j)
    part, f2 = stage_third(k1, k2, spread(part, ("y", "c")), lift_i)
    part, g3 = stage_fourth(k1, k2, spread(part, "x"), lift_j, g1)
    part = stage_fifth(info, k1, k2, spread(part, ("y", "c")), lift_i, f2, g3)
    got = spread(part, ("x", "zl"))
    pots, g4, share = call(
        last_body, (f32(4, 8, 128), f32(8, 128), f32(8, 8, 128)), [VMEM] * 4
    )(got, gen_weight, ref_weight, ref_full)
    divergence = jnp.sum(spread(share, ("y", "c"))[:, 0, 0])

    mine = lax.dynamic_index_in_dim(pots, x, 0, keepdims=False)
    mine = lax.dynamic_slice_in_dim(mine.reshape(4, 256), 64 * (y % 2), BLOCK, 1)
    ref_pot = lax.dynamic_slice_in_dim(g4.reshape(1024), x * BLOCK, BLOCK, 0)
    return mine[0], ref_pot, mine[1], mine[2], divergence


def solution(mesh):
    fine = Mesh(mesh.devices.reshape(4, 4, 2, 4, 4), ("y", "x", "c", "zh", "zl"))
    tile, feat = ("y", "x", "c"), ("zh", "zl")
    return jax.shard_map(
        local,
        mesh=fine,
        in_specs=(P(tile, feat), P(tile, feat), P(), P()),
        out_specs=(P(tile), P(tile), P(tile), P(tile), P()),
        check_vma=False,
    )
```

time: 196 us -> 200 us (1.020)
  Pallas kernels: 28.2 us -> 40.2 us
  local copies, waits for them, and re-layouts: 17.7 us -> 10.8 us
  waiting for transfers between devices: 53.4 us -> 48.4 us
  blocking collectives: 33.9 us -> 36.5 us
    pallas_call x7 -> x8, Pallas kernels: 27.5 us -> 38.6 us  [the longest x1 9.56 us: stage_cost(): call(cost_body, outs, [SMEM, HBM, HBM, HBM, VMEM], scratch, (VMEM, HBM, V...]
    unnamed x21 -> x19, local copies, waits for them, and re-layouts: 14.4 us -> 4.38 us
    all_to_all x7, waiting for transfers between devices: 37.7 us -> 34 us  [spread(): return lax.all_to_all(operand, axes, 0, 0, tiled=True)]
    all_gather x1, blocking collectives: 33.9 us -> 36.5 us  [local(): raw = lax.all_gather(packed, ('zh', 'zl'))]
  transfers between devices with their start and end apart: 9 -> 9, of which waited for: 8 -> 8; matrix products, arithmetic and copies ran while one was open for 3% -> 4% of each run, Pallas kernels for 0% -> 1%
where the time goes in v3:
time: 200 us; the launch traced here: 199 us
  waiting for transfers between devices  48.4 us (24%)
  starting transfers between devices  43.6 us (22%)
  Pallas kernels  40.2 us (20%)
  blocking collectives  36.5 us (18%)
  between operations  15.6 us (8%)
  local copies, waits for them, and re-layouts  10.8 us (5%)
  other arithmetic  3.54 us (2%)
    all_gather x1, blocking collectives, local(): raw = lax.all_gather(packed, ('zh', 'zl'))  36.5 us
    all_to_all x7, waiting for transfers between devices, spread(): return lax.all_to_all(operand, axes, 0, 0, tiled=True)  34 us
    all_to_all x7, starting transfers between devices, spread(): return lax.all_to_all(operand, axes, 0, 0, tiled=True)  32.8 us
    all_gather x1, waiting for transfers between devices, local(): b_all = lax.all_gather(stage_unpack_b(info, raw), 'x')  14.4 us
    ppermute x1, starting transfers between devices, local(): a_other = lax.ppermute(a_half, 'c', [(0, 1), (1, 0)])  10.7 us
    pallas_call x1, Pallas kernels, stage_cost(): call(cost_body, outs, [SMEM, HBM, HBM, HBM, VMEM], scratch, (VMEM, HBM, V...  9.56 us
    pallas_call x1, Pallas kernels, stage_second(): call(second_body, outs, [VMEM, HBM, VMEM, VMEM], STREAM + row_scratch(2))  6.1 us
    pallas_call x1, Pallas kernels, stage_fourth(): call(fourth_body, outs, [VMEM, HBM, VMEM, VMEM, VMEM], STREAM + row_scrat...  6.1 us
  transfers between devices with their start and end apart: 9, of which 8 were waited for; matrix products, arithmetic and copies ran while one was open for 4% of the time, Pallas kernels for 1%

profile of v3, /device:TPU:1, one launch (start us, length us, event | category | flops | bytes accessed | tf_op | source)
XLA Modules:
  0.0 198.6 jit_solution(6624571013617370458)
XLA Ops:
  7.2 1.5 shard_map.83
  8.7 36.5 %all-gather = bf16[3072,128]{1,0:T(8,128)(2,1)} all-gather(bf16[192,128]{1,0:T(8,128)(2,1)} %shard_map.83), channel_id=2, replica_groups=mesh['y'=4,'x'=4,'c'=2,'zh'=4,'zl'=4] {'zh','zl'}, dimensions={0}, use_global_device_ids=true | all-gather | bytes 835584 | tf_op jit(solution)/shard_map/all_gather | solution.py:382
  45.8 2.8 %shard_map.84 = bf16[4,192,1024]{2,1,0:T(8,128)(2,1)} custom-call(s32[4]{0:T(128)} %pad_add_fusion.info, bf16[16,192,128]{2,1,0:T(8,128)(2,1)} %bitcast.20), custom_call_target="tpu_custom_call" | custom-call | tf_op jit(solution)/shard_map/pallas_call | solution.py:336
  48.5 4.2 %all-to-all-start = ((bf16[4,192,1024]{2,1,0:T(8,128)(2,1)}), bf16[4,192,1024]{2,1,0:T(8,128)(2,1)S(1)}, u32[]{:S(2)}, u32[]{:S(2)}) async-start(bf16[4,192,1024]{2,1,0:T(8,128)(2,1)} %shard_map.84), calls=%async_computation | async-start | bytes 3145728 | tf_op jit(solution)/shard_map/all_to_all | solution.py:374
  52.8 2.2 %shard_map.85 = bf16[192,1024]{1,0:T(8,128)(2,1)} custom-call(s32[4]{0:T(128)} %pad_add_fusion.info, bf16[16,192,128]{2,1,0:T(8,128)(2,1)} %bitcast.21), custom_call_target="tpu_custom_call" | custom-call | tf_op jit(solution)/shard_map/pallas_call | solution.py:332
  55.0 10.6 %all-to-all-done = bf16[4,192,1024]{2,1,0:T(8,128)(2,1)S(1)} async-done(((bf16[4,192,1024]{2,1,0:T(8,128)(2,1)}), bf16[4,192,1024]{2,1,0:T(8,128)(2,1)S(1)}, u32[]{:S(2)}, u32[]{:S(2)}) %all-to-all-start) | async-done | bytes 1572896 | tf_op jit(solution)/shard_map/all_to_all | solution.py:374
  65.6 10.7 %collective-permute-start = (bf16[4,192,1024]{2,1,0:T(8,128)(2,1)S(1)}, bf16[4,192,1024]{2,1,0:T(8,128)(2,1)S(1)}, u32[]{:S(2)}, u32[]{:S(2)}) collective-permute-start(bf16[4,192,1024]{2,1,0:T(8,128)(2,1)S(1)} %all-to-all-done), channel_id=1, source_target_pairs={{0,16},{16,0},{1,17},{17,1},{2,18},{18,2},{3,19},{19,3},{4,20},{20... | collective-permute-start | bytes 4718600 | tf_op jit(solution)/shard_map/ppermute | solution.py:407
  77.5 0.7 fusion
  79.1 14.4 %all-gather.4.cloned.1.call-done.cols = bf16[768,1024]{1,0:T(8,128)(2,1)} async-done(((bf16[192,1024]{1,0:T(8,128)(2,1)}), bf16[768,1024]{1,0:T(8,128)(2,1)}) %all-gather.4.cloned.1.call-update) | async-done | bytes 1572880 | tf_op jit(solution)/shard_map/all_gather | solution.py:405
  93.4 1.2 copy-done.1
  94.7 9.6 %shard_map.86 = (f32[768,1024]{1,0:T(8,128)}, f32[768,512]{1,0:T(8,128)}, f32[4,8,128]{2,1,0:T(8,128)}) custom-call(s32[4]{0:T(128)} %pad_add_fusion.info, bf16[768,1024]{1,0:T(8,128)(2,1)} %bitcast.22, bf16[768,1024]{1,0:T(8,128)(2,1)} %bitcast.23, bf16[768,1024]{1,0:T(8,128)(2,1)} %all-gather.4.cloned.1.call-done.cols, f32[12,128]{1,0:T(8,128)} %select_n.83.lift_i), custom_call_target="tpu_custom_call" | custom-call | tf_op jit(solution)/shard_map/pallas_call | solution.py:350
  104.3 3.2 %all-to-all-start.1 = ((f32[4,8,128]{2,1,0:T(8,128)}), f32[4,8,128]{2,1,0:T(8,128)S(1)}, u32[]{:S(2)}, u32[]{:S(2)}) async-start(f32[4,8,128]{2,1,0:T(8,128)} %get-tuple-element.19), calls=%async_computation.1 | async-start | bytes 32768 | tf_op jit(solution)/shard_map/all_to_all | solution.py:374
  107.5 0.7 fusion.1
  108.9 2.8 %all-to-all-done.1.got = f32[4,8,128]{2,1,0:T(8,128)S(1)} async-done(((f32[4,8,128]{2,1,0:T(8,128)}), f32[4,8,128]{2,1,0:T(8,128)S(1)}, u32[]{:S(2)}, u32[]{:S(2)}) %all-to-all-start.1) | async-done | bytes 16416 | tf_op jit(solution)/shard_map/all_to_all | solution.py:374
  112.3 6.1 %shard_map.87 = (f32[8,24,128]{2,1,0:T(8,128)}, f32[6,128]{1,0:T(8,128)}) custom-call(f32[768,1024]{1,0:T(8,128)} %get-tuple-element.17.k1_ref, f32[768,512]{1,0:T(8,128)} %get-tuple-element.18.k2_hbm, f32[4,8,128]{2,1,0:T(8,128)} %copy-done.6, f32[6,128]{1,0:T(8,128)} %select_n.88.lift_j), custom_call_target="tpu_custom_call" | custom-call | tf_op jit(solution)/shard_map/pallas_call | solution.py:355
  118.4 6.1 %all-to-all-start.2 = ((f32[8,24,128]{2,1,0:T(8,128)}), f32[8,24,128]{2,1,0:T(8,128)S(1)}, u32[]{:S(2)}, u32[]{:S(2)}) async-start(f32[8,24,128]{2,1,0:T(8,128)} %get-tuple-element.20), calls=%async_computation.2 | async-start | bytes 196608 | tf_op jit(solution)/shard_map/all_to_all | solution.py:374
  125.8 3.7 %all-to-all-done.2.got = f32[8,24,128]{2,1,0:T(8,128)S(1)} async-done(((f32[8,24,128]{2,1,0:T(8,128)}), f32[8,24,128]{2,1,0:T(8,128)S(1)}, u32[]{:S(2)}, u32[]{:S(2)}) %all-to-all-start.2) | async-done | bytes 98336 | tf_op jit(solution)/shard_map/all_to_all | solution.py:374
  130.1 5.6 %shard_map.88 = (f32[4,16,128]{2,1,0:T(8,128)}, f32[12,128]{1,0:T(8,128)}) custom-call(f32[768,1024]{1,0:T(8,128)} %get-tuple-element.17.k1_ref, f32[768,512]{1,0:T(8,128)} %get-tuple-element.18.k2_hbm, f32[8,24,128]{2,1,0:T(8,128)} %copy-done.3, f32[12,128]{1,0:T(8,128)} %select_n.83.lift_i), custom_call_target="tpu_custom_call" | custom-call | tf_op jit(solution)/shard_map/pallas_call | solution.py:360
  135.8 3.3 %all-to-all-start.3 = ((f32[4,16,128]{2,1,0:T(8,128)}), f32[4,16,128]{2,1,0:T(8,128)S(1)}, u32[]{:S(2)}, u32[]{:S(2)}) async-start(f32[4,16,128]{2,1,0:T(8,128)} %get-tuple-element.21), calls=%async_computation.3 | async-start | bytes 65536 | tf_op jit(solution)/shard_map/all_to_all | solution.py:374
  139.1 4.2 %all-to-all-done.3.got = f32[4,16,128]{2,1,0:T(8,128)S(1)} async-done(((f32[4,16,128]{2,1,0:T(8,128)}), f32[4,16,128]{2,1,0:T(8,128)S(1)}, u32[]{:S(2)}, u32[]{:S(2)}) %all-to-all-start.3) | async-done | bytes 32800 | tf_op jit(solution)/shard_map/all_to_all | solution.py:374
  143.9 6.1 %shard_map.89 = (f32[8,24,128]{2,1,0:T(8,128)}, f32[6,128]{1,0:T(8,128)}) custom-call(f32[768,1024]{1,0:T(8,128)} %get-tuple-element.17.k1_ref, f32[768,512]{1,0:T(8,128)} %get-tuple-element.18.k2_hbm, f32[4,16,128]{2,1,0:T(8,128)} %copy-done.5, f32[6,128]{1,0:T(8,128)} %select_n.88.lift_j, f32[6,128]{1,0:T(8,128)} %get-tuple-element.22.g1), custom_call_target="tpu_custom_call" | custom-call | tf_op jit(solution)/shard_map/pallas_call | solution.py:365
  150.0 5.2 %all-to-all-start.4 = ((f32[8,24,128]{2,1,0:T(8,128)}), f32[8,24,128]{2,1,0:T(8,128)S(1)}, u32[]{:S(2)}, u32[]{:S(2)}) async-start(f32[8,24,128]{2,1,0:T(8,128)} %get-tuple-element.23), calls=%async_computation.4 | async-start | bytes 196608 | tf_op jit(solution)/shard_map/all_to_all | solution.py:374
  155.3 5.0 %all-to-all-done.4.got = f32[8,24,128]{2,1,0:T(8,128)S(1)} async-done(((f32[8,24,128]{2,1,0:T(8,128)}), f32[8,24,128]{2,1,0:T(8,128)S(1)}, u32[]{:S(2)}, u32[]{:S(2)}) %all-to-all-start.4) | async-done | bytes 98336 | tf_op jit(solution)/shard_map/all_to_all | solution.py:374
  160.9 4.7 %shard_map.90 = f32[16,8,128]{2,1,0:T(8,128)} custom-call(s32[4]{0:T(128)} %pad_add_fusion.info, f32[768,1024]{1,0:T(8,128)} %get-tuple-element.17.k1_ref, f32[768,512]{1,0:T(8,128)} %get-tuple-element.18.k2_hbm, f32[8,24,128]{2,1,0:T(8,128)} %copy-done.2, f32[12,128]{1,0:T(8,128)} %select_n.83.lift_i, f32[12,128]{1,0:T(8,128)} %get-tuple-element.24.f2, ...), custom_call_target="tpu_custom_call" | custom-call | tf_op jit(solution)/shard_map/pallas_call | solution.py:370
  165.7 5.3 %all-to-all-start.5 = ((f32[16,8,128]{2,1,0:T(8,128)}), f32[16,8,128]{2,1,0:T(8,128)S(1)}, u32[]{:S(2)}, u32[]{:S(2)}) async-start(f32[16,8,128]{2,1,0:T(8,128)} %shard_map.90), calls=%async_computation.5 | async-start | bytes 131072 | tf_op jit(solution)/shard_map/all_to_all | solution.py:374
  172.3 0.7 and_select_fusion
  173.0 4.9 %all-to-all-done.5.got = f32[16,8,128]{2,1,0:T(8,128)S(1)} async-done(((f32[16,8,128]{2,1,0:T(8,128)}), f32[16,8,128]{2,1,0:T(8,128)S(1)}, u32[]{:S(2)}, u32[]{:S(2)}) %all-to-all-start.5) | async-done | bytes 65568 | tf_op jit(solution)/shard_map/all_to_all | solution.py:374
  178.6 1.6 shard_map.91
  180.2 0.7 constant_dynamic-slice_fusion
  180.9 5.5 %all-to-all-start.6 = ((f32[8,8,128]{2,1,0:T(8,128)}), f32[8,8,128]{2,1,0:T(8,128)S(1)}, u32[]{:S(2)}, u32[]{:S(2)}) async-start(f32[8,8,128]{2,1,0:T(8,128)} %get-tuple-element.28), calls=%async_computation.6 | async-start | bytes 65536 | tf_op jit(solution)/shard_map/all_to_all | solution.py:374
  187.0 1.3 dynamic_slice.37
  188.3 2.8 %all-to-all-done.6 = f32[8,8,128]{2,1,0:T(8,128)S(1)} async-done(((f32[8,8,128]{2,1,0:T(8,128)}), f32[8,8,128]{2,1,0:T(8,128)S(1)}, u32[]{:S(2)}, u32[]{:S(2)}) %all-to-all-start.6) | async-done | bytes 32800 | tf_op jit(solution)/shard_map/all_to_all | solution.py:374
  (43 shorter events, 9.0 us)
Async XLA Ops:
  48.5 17.0 %all-to-all-start = ((bf16[4,192,1024]{2,1,0:T(8,128)(2,1)}), bf16[4,192,1024]{2,1,0:T(8,128)(2,1)S(1)}, u32[]{:S(2)}, u32[]{:S(2)}) async-start(bf16[4,192,1024]{2,1,0:T(8,128)(2,1)} %shard_map.84), calls=%async_computation | async-start | bytes 3145728 | tf_op jit(solution)/shard_map/all_to_all | solution.py:374
  52.7 23.6 %copy-start.7 = (s32[32]{0:T(128)S(1)}, s32[32]{0:T(128)}, u32[]{:S(2)}) copy-start(s32[32]{0:T(128)} %param.6) | copy-start | bytes 388
  52.7 23.7 %copy-start.8 = (s32[32]{0:T(128)S(1)}, s32[32]{0:T(128)}, u32[]{:S(2)}) copy-start(s32[32]{0:T(128)} %param.7) | copy-start | bytes 388
  52.7 40.7 %all-gather.4.cloned.1.call-start = ((), (), s32[]{:S(2)}) async-start(), calls=%async_computation.7 | async-start | bytes 1966080 | tf_op jit(solution)/shard_map/all_gather | solution.py:405
  65.6 27.9 %copy-start = (bf16[4,192,1024]{2,1,0:T(8,128)(2,1)}, bf16[4,192,1024]{2,1,0:T(8,128)(2,1)S(1)}, u32[]{:S(2)}) copy-start(bf16[4,192,1024]{2,1,0:T(8,128)(2,1)S(1)} %all-to-all-done) | copy-start | bytes 4718596
  65.6 27.9 %collective-permute-start = (bf16[4,192,1024]{2,1,0:T(8,128)(2,1)S(1)}, bf16[4,192,1024]{2,1,0:T(8,128)(2,1)S(1)}, u32[]{:S(2)}, u32[]{:S(2)}) collective-permute-start(bf16[4,192,1024]{2,1,0:T(8,128)(2,1)S(1)} %all-to-all-done), channel_id=1, source_target_pairs={{0,16},{16,0},{1,17},{17,1},{2,18},{18,2},{3,19},{19,3},{4,20},{20... | collective-permute-start | bytes 4718600 | tf_op jit(solution)/shard_map/ppermute | solution.py:407
  93.4 1.2 copy-start.1
  104.3 7.4 %all-to-all-start.1 = ((f32[4,8,128]{2,1,0:T(8,128)}), f32[4,8,128]{2,1,0:T(8,128)S(1)}, u32[]{:S(2)}, u32[]{:S(2)}) async-start(f32[4,8,128]{2,1,0:T(8,128)} %get-tuple-element.19), calls=%async_computation.1 | async-start | bytes 32768 | tf_op jit(solution)/shard_map/all_to_all | solution.py:374
  111.7 0.6 copy-start.6
  118.4 11.1 %all-to-all-start.2 = ((f32[8,24,128]{2,1,0:T(8,128)}), f32[8,24,128]{2,1,0:T(8,128)S(1)}, u32[]{:S(2)}, u32[]{:S(2)}) async-start(f32[8,24,128]{2,1,0:T(8,128)} %get-tuple-element.20), calls=%async_computation.2 | async-start | bytes 196608 | tf_op jit(solution)/shard_map/all_to_all | solution.py:374
  129.5 0.6 copy-start.3
  135.8 7.5 %all-to-all-start.3 = ((f32[4,16,128]{2,1,0:T(8,128)}), f32[4,16,128]{2,1,0:T(8,128)S(1)}, u32[]{:S(2)}, u32[]{:S(2)}) async-start(f32[4,16,128]{2,1,0:T(8,128)} %get-tuple-element.21), calls=%async_computation.3 | async-start | bytes 65536 | tf_op jit(solution)/shard_map/all_to_all | solution.py:374
  143.3 0.6 copy-start.5
  150.0 10.2 %all-to-all-start.4 = ((f32[8,24,128]{2,1,0:T(8,128)}), f32[8,24,128]{2,1,0:T(8,128)S(1)}, u32[]{:S(2)}, u32[]{:S(2)}) async-start(f32[8,24,128]{2,1,0:T(8,128)} %get-tuple-element.23), calls=%async_computation.4 | async-start | bytes 196608 | tf_op jit(solution)/shard_map/all_to_all | solution.py:374
  160.3 0.6 copy-start.2
  165.7 12.3 %all-to-all-start.5 = ((f32[16,8,128]{2,1,0:T(8,128)}), f32[16,8,128]{2,1,0:T(8,128)S(1)}, u32[]{:S(2)}, u32[]{:S(2)}) async-start(f32[16,8,128]{2,1,0:T(8,128)} %shard_map.90), calls=%async_computation.5 | async-start | bytes 131072 | tf_op jit(solution)/shard_map/all_to_all | solution.py:374
  177.9 0.6 copy-start.4
  180.9 10.2 %all-to-all-start.6 = ((f32[8,8,128]{2,1,0:T(8,128)}), f32[8,8,128]{2,1,0:T(8,128)S(1)}, u32[]{:S(2)}, u32[]{:S(2)}) async-start(f32[8,8,128]{2,1,0:T(8,128)} %get-tuple-element.28), calls=%async_computation.6 | async-start | bytes 65536 | tf_op jit(solution)/shard_map/all_to_all | solution.py:374
Sparse Core Ops, SparseCore 0:
  55.7 37.7 all-gather.3

commit v4 on v3

--- a/solution.py
+++ b/solution.py
@@ -21,25 +21,25 @@
 NEAR = 8
 N1 = NEAR * 128
 N2 = NI - N1
+ROOM = 18 * NJ
 
 VMEM = pl.BlockSpec(memory_space=pltpu.VMEM)
 HBM = pl.BlockSpec(memory_space=pltpu.HBM)
 SMEM = pl.BlockSpec(memory_space=pltpu.SMEM)
-PARAMS = pltpu.CompilerParams(vmem_limit_bytes=60 * 1024 * 1024)
 
 
 def f32(*shape):
     return jax.ShapeDtypeStruct(shape, jnp.float32)
 
 
-def call(body, outs, ins, scratch=(), out_specs=None):
+def call(body, outs, ins, scratch=(), out_specs=None, mib=40):
     return pl.pallas_call(
         body,
         out_shape=outs,
         in_specs=ins,
         out_specs=jax.tree.map(lambda _: VMEM, outs) if out_specs is None else out_specs,
         scratch_shapes=list(scratch),
-        compiler_params=PARAMS,
+        compiler_params=pltpu.CompilerParams(vmem_limit_bytes=mib * 1024 * 1024),
     )
 
 
@@ -71,21 +71,30 @@
         fetch(k2_hbm, k2_ref, sems, b).start()
 
 
-def k_tile(k1_ref, k2_ref, rows, r):
-    if r < NEAR:
-        return k1_ref[rows, r * 128 : (r + 1) * 128]
-    return k2_ref[rows, (r - NEAR) * 128 : (r - NEAR + 1) * 128]
-
-
-def lanes_block(k1_ref, k2_ref, heads, high_ref, mass_ref, base):
+def lanes_block(tiles_of, count, heads, high_ref, mass_ref, base, joined=False):
     for group in range(16):
         rows = pl.ds(base + group * 8, 8)
-        tiles = [k_tile(k1_ref, k2_ref, rows, r) for r in range(RI)]
-        for v in range(len(heads)):
-            xs = [heads[v][r : r + 1, :] - tiles[r] for r in range(RI)]
+        tiles = tiles_of(rows)
+        for v in range(count):
+            xs = [heads[v][r : r + 1, :] - tile for r, tile in tiles]
             high = tree(jnp.maximum, xs)
+            if joined:
+                before = high_ref[v, rows, :]
+                high = jnp.maximum(high, before)
+                xs.append(before)
+            masses = [jnp.exp2(x - high) for x in xs]
+            if joined:
+                masses[-1] = masses[-1] * mass_ref[v, rows, :]
             high_ref[v, rows, :] = high
-            mass_ref[v, rows, :] = tree(jnp.add, [jnp.exp2(x - high) for x in xs])
+            mass_ref[v, rows, :] = tree(jnp.add, masses)
+
+
+def near_tiles(k1_ref):
+    return lambda rows: [(r, k1_ref[rows, r * 128 : (r + 1) * 128]) for r in range(NEAR)]
+
+
+def far_tiles(k2_ref):
+    return lambda rows: [(r, k2_ref[rows, (r - NEAR) * 128 : (r - NEAR + 1) * 128]) for r in range(NEAR, RI)]
 
 
 def lanes_result(count, high_ref, mass_ref):
@@ -105,37 +114,55 @@
 
 
 def reduce_lanes(k1_ref, k2_hbm, k2_ref, sems, heads, high_ref, mass_ref):
-    def step(b, carry):
+    count = len(heads)
+
+    def near(b, carry):
+        lanes_block(near_tiles(k1_ref), count, heads, high_ref, mass_ref, pl.multiple_of(b * 128, 128))
+        return carry
+
+    def far(b, carry):
         fetch(k2_hbm, k2_ref, sems, b).wait()
-        lanes_block(k1_ref, k2_ref, heads, high_ref, mass_ref, pl.multiple_of(b * 128, 128))
+        lanes_block(far_tiles(k2_ref), count, heads, high_ref, mass_ref, pl.multiple_of(b * 128, 128), True)
         return carry
 
-    lax.fori_loop(0, RJ, step, 0)
-    return lanes_result(len(heads), high_ref, mass_ref)
-
-
-def reduce_rows(k1_ref, k2_hbm, k2_ref, sems, heads, head_ref, high_ref, mass_ref):
+    lax.fori_loop(0, RJ, near, 0)
+    lax.fori_loop(0, RJ, far, 0)
+    return lanes_result(count, high_ref, mass_ref)
+
+
+def reduce_rows(k1_ref, k2_hbm, k2_ref, sems, heads, head_ref, wide_ref, high_ref, mass_ref):
     count = len(heads)
     for v in range(count):
         head_ref[v, 0:RJ, :] = heads[v]
 
-    def step(b, carry):
+    def block(b, wides, tile, r):
+        spot = pl.ds(pl.multiple_of(b * 8, 8), 8)
+        cols = slice(r * 128, (r + 1) * 128)
+        tiles = [tile(pl.ds(b * 128 + group * 8, 8)) for group in range(16)]
+        for v in range(count):
+            xs = [wides[v][group * 8 : group * 8 + 8, :] - tiles[group] for group in range(16)]
+            high = tree(jnp.maximum, xs)
+            high_ref[v, spot, cols] = high
+            mass_ref[v, spot, cols] = tree(jnp.add, [jnp.exp2(x - high) for x in xs])
+
+    def near(b, carry):
+        wides = []
+        for v in range(count):
+            wides.append(jnp.transpose(jnp.broadcast_to(head_ref[v, pl.ds(b, 1), :], (128, 128))))
+            wide_ref[v, pl.ds(pl.multiple_of(b * 128, 128), 128), :] = wides[v]
+        for r in range(NEAR):
+            block(b, wides, lambda rows: k1_ref[rows, r * 128 : (r + 1) * 128], r)
+        return carry
+
+    def far(b, carry):
         fetch(k2_hbm, k2_ref, sems, b).wait()
-        wides = [
-            jnp.transpose(jnp.broadcast_to(head_ref[v, pl.ds(b, 1), :], (128, 128))) for v in range(count)
-        ]
-        spot = pl.ds(pl.multiple_of(b * 8, 8), 8)
-        for r in range(RI):
-            cols = slice(r * 128, (r + 1) * 128)
-            tiles = [k_tile(k1_ref, k2_ref, pl.ds(b * 128 + group * 8, 8), r) for group in range(16)]
-            for v in range(count):
-                xs = [wides[v][group * 8 : group * 8 + 8, :] - tiles[group] for group in range(16)]
-                high = tree(jnp.maximum, xs)
-                high_ref[v, spot, cols] = high
-                mass_ref[v, spot, cols] = tree(jnp.add, [jnp.exp2(x - high) for x in xs])
+        wides = [wide_ref[v, pl.ds(pl.multiple_of(b * 128, 128), 128), :] for v in range(count)]
+        for r in range(NEAR, RI):
+            block(b, wides, lambda rows: k2_ref[rows, (r - NEAR) * 128 : (r - NEAR + 1) * 128], r)
         return carry
 
-    lax.fori_loop(0, RJ, step, 0)
+    lax.fori_loop(0, RJ, near, 0)
+    lax.fori_loop(0, RJ, far, 0)
     results = []
     for v in range(count):
         tops, totals = [], []
@@ -179,54 +206,58 @@
     return functools.reduce(jnp.add, [values[:, k * 128 : (k + 1) * 128] for k in range(D // 128)])
 
 
+def join_body(info, own, other, a_out, norm_out):
+    first = info[2] == 0
+    for half in range(2):
+        for s in range(6):
+            part = slice(s * 128, (s + 1) * 128)
+            near, far = (own, other) if half == 0 else (other, own)
+            rows = jnp.where(first, near[part, :], far[part, :])
+            r = half * 6 + s
+            a_out[r * 128 : (r + 1) * 128, :] = rows
+            turned = jnp.transpose(norm_parts(rows))
+            norm_out[r : r + 1, :] = jnp.sum(turned, axis=0, keepdims=True) * (0.5 * LOG2E / EPSILON)
+    norm_out[RI:16, :] = jnp.zeros((16 - RI, 128), jnp.float32)
+
+
 def cost_body(
-    info, own, other, cols, lift_i, k1_ref, k2_hbm, part_out,
-    a_ref, b_ref, k2_ref, high_ref, mass_ref, sq_ref, in_sems, out_sems,
+    a_ref, norm_ref, b_ref, lift_i, k1_ref, k2_hbm, part_out, k2_ref, high_ref, mass_ref, sq_ref, out_sems
 ):
     scale = LOG2E / EPSILON
-    c = info[2]
-    loads = [
-        pltpu.make_async_copy(own, a_ref.at[c], in_sems.at[0]),
-        pltpu.make_async_copy(other, a_ref.at[1 - c], in_sems.at[1]),
-    ]
-    chunks = [pl.ds(b * 256, 256) for b in range(3)]
-    loads += [pltpu.make_async_copy(cols.at[p], b_ref.at[p], in_sems.at[2 + b]) for b, p in enumerate(chunks)]
-    for load in loads:
-        load.start()
     heads = [lift_i[...]]
-    loads[0].wait()
-    loads[1].wait()
-    for which in range(2):
-        for s in range(6):
-            turned = jnp.transpose(norm_parts(a_ref[which, s * 128 : (s + 1) * 128, :]))
-            sq_ref[which * 6 + s : which * 6 + s + 1, :] = jnp.sum(turned, axis=0, keepdims=True) * (0.5 * scale)
+    for b in range(RJ):
+        part = slice(b * 128, (b + 1) * 128)
+        total = jnp.sum(norm_parts(b_ref[part, :]), axis=1, keepdims=True) * (0.5 * scale)
+        sq_ref[part, :] = jnp.broadcast_to(total, (128, 128))
     stores = [fetch(k2_ref, k2_hbm, out_sems, b) for b in range(RJ)]
-    for b in range(4):
-        if b < 3:
-            loads[2 + b].wait()
-            rows = b_ref[b * 256 : (b + 1) * 256, :]
-            row_sq = jnp.sum(norm_parts(rows), axis=1, keepdims=True) * (0.5 * scale)
-            for which in range(2):
-                for t in range(3):
-                    inner = lax.dot_general(
-                        rows,
-                        a_ref[which, t * 256 : (t + 1) * 256, :],
-                        (((1,), (1,)), ((), ())),
-                        preferred_element_type=jnp.float32,
-                    )
-                    for s in range(2):
-                        r = which * 6 + t * 2 + s
-                        tile = (row_sq + sq_ref[r : r + 1, :]) - scale * inner[:, s * 128 : (s + 1) * 128]
-                        if r < NEAR:
-                            k1_ref[b * 256 : (b + 1) * 256, r * 128 : (r + 1) * 128] = tile
-                        else:
-                            k2_ref[b * 256 : (b + 1) * 256, (r - NEAR) * 128 : (r - NEAR + 1) * 128] = tile
-        if b > 0:
-            for half in (2 * b - 2, 2 * b - 1):
-                lanes_block(k1_ref, k2_ref, heads, high_ref, mass_ref, half * 128)
-        if b < 3:
-            stores[2 * b].start()
-            stores[2 * b + 1].start()
+    order = [4, 5, 0, 1, 2, 3]
+    for step in range(RI // 2 + 1):
+        if step < RI // 2:
+            n = order[step]
+            inner = lax.dot_general(
+                b_ref[...],
+                a_ref[n * 256 : (n + 1) * 256, :],
+                (((1,), (1,)), ((), ())),
+                preferred_element_type=jnp.float32,
+            )
+            for s in range(2):
+                r = 2 * n + s
+                tile = (sq_ref[...] + norm_ref[r : r + 1, :]) - scale * inner[:, s * 128 : (s + 1) * 128]
+                if r < NEAR:
+                    k1_ref[:, r * 128 : (r + 1) * 128] = tile
+                else:
+                    k2_ref[:, (r - NEAR) * 128 : (r - NEAR + 1) * 128] = tile
+        if step > 0:
+            done = 2 * order[step - 1]
+            source, at = (k1_ref, done) if done < NEAR else (k2_ref, done - NEAR)
+            pair = lambda rows: [
+                (done + s, source[rows, (at + s) * 128 : (at + s + 1) * 128]) for s in range(2)
+            ]
+            for b in range(RJ):
+                lanes_block(pair, 1, heads, high_ref, mass_ref, b * 128, step > 1)
+        if step == 1:
+            for store in stores:
+                store.start()
     (result,) = lanes_result(1, high_ref, mass_ref)
     for n in range(4):
         part_out[n, 0:RJ, :] = result
@@ -235,13 +266,13 @@
         store.wait()
 
 
-def second_body(k1_ref, k2_hbm, got, lift_j, out, g1_out, k2_ref, sems, head_ref, high_ref, mass_ref):
+def second_body(k1_ref, k2_hbm, got, lift_j, out, g1_out, k2_ref, sems, head_ref, wide_ref, high_ref, mass_ref):
     start_fetch(k2_hbm, k2_ref, sems)
     g1 = -merge(got, 4)[0:RJ, :]
     g1_out[...] = g1
     lift = lift_j[...]
     heads = [lift, lifted(g1, lift)]
-    results = reduce_rows(k1_ref, k2_hbm, k2_ref, sems, heads, head_ref, high_ref, mass_ref)
+    results = reduce_rows(k1_ref, k2_hbm, k2_ref, sems, heads, head_ref, wide_ref, high_ref, mass_ref)
     for n in range(8):
         for v in range(2):
             out[n, v * RI : (v + 1) * RI, :] = results[v]
@@ -262,7 +293,7 @@
             out[n, v * 8 + RJ : v * 8 + 8, :] = jnp.zeros((8 - RJ, 128), jnp.float32)
 
 
-def fourth_body(k1_ref, k2_hbm, got, lift_j, g1, out, g3_out, k2_ref, sems, head_ref, high_ref, mass_ref):
+def fourth_body(k1_ref, k2_hbm, got, lift_j, g1, out, g3_out, k2_ref, sems, head_ref, wide_ref, high_ref, mass_ref):
     start_fetch(k2_hbm, k2_ref, sems)
     merged = -merge(got, 4)
     g2 = 0.5 * (g1[...] + merged[0:RJ, :])
@@ -270,7 +301,7 @@
     g3_out[...] = g3
     lift = lift_j[...]
     heads = [lifted(g2, lift), lifted(g3, lift)]
-    results = reduce_rows(k1_ref, k2_hbm, k2_ref, sems, heads, head_ref, high_ref, mass_ref)
+    results = reduce_rows(k1_ref, k2_hbm, k2_ref, sems, heads, head_ref, wide_ref, high_ref, mass_ref)
     for n in range(8):
         for v in range(2):
             out[n, v * RI : (v + 1) * RI, :] = results[v]
@@ -321,7 +352,7 @@
 
 
 def row_scratch(count):
-    return [pltpu.VMEM((count, 8, 128), F32)] + [pltpu.VMEM((count, 8 * RJ, NI), F32)] * 2
+    return [pltpu.VMEM((count, 8, 128), F32), pltpu.VMEM((count, NJ, 128), F32)] + [pltpu.VMEM((count, 8 * RJ, NI), F32)] * 2
 
 
 def stage_pack(*args):
@@ -336,18 +367,20 @@
     return call(unpack_a_body, jax.ShapeDtypeStruct((4, BLOCK, D), BF16), [SMEM, VMEM])(*args)
 
 
+def stage_join(*args):
+    outs = (jax.ShapeDtypeStruct((NI, D), BF16), f32(16, 128))
+    return call(join_body, outs, [SMEM, VMEM, VMEM])(*args)
+
+
 def stage_cost(*args):
     scratch = [
-        pltpu.VMEM((2, NJ, D), BF16),
-        pltpu.VMEM((NJ, D), BF16),
         pltpu.VMEM((NJ, N2), F32),
         *lane_scratch(1),
-        pltpu.VMEM((16, 128), F32),
-        pltpu.SemaphoreType.DMA((5,)),
+        pltpu.VMEM((NJ, 128), F32),
         pltpu.SemaphoreType.DMA((RJ,)),
     ]
-    outs = (f32(NJ, N1), f32(NJ, N2), f32(4, 8, 128))
-    return call(cost_body, outs, [SMEM, HBM, HBM, HBM, VMEM], scratch, (VMEM, HBM, VMEM))(*args)
+    outs = (f32(NJ, N1), f32(ROOM, N2), f32(4, 8, 128))
+    return call(cost_body, outs, [VMEM] * 4, scratch, (VMEM, HBM, VMEM))(*args)
 
 
 def stage_second(*args):
@@ -406,9 +439,8 @@
     a_half = spread(stage_unpack_a(info, raw), "y")
     a_other = lax.ppermute(a_half, "c", [(0, 1), (1, 0)])
 
-    k1, k2, part = stage_cost(
-        info, a_half.reshape(NJ, D), a_other.reshape(NJ, D), b_all.reshape(NJ, D), lift_i
-    )
+    a_all, norms = stage_join(info, a_half.reshape(NJ, D), a_other.reshape(NJ, D))
+    k1, k2, part = stage_cost(a_all, norms, b_all.reshape(NJ, D), lift_i)
     part, g1 = stage_second(k1, k2, spread(part, "x"), lift_j)
     part, f2 = stage_third(k1, k2, spread(part, ("y", "c")), lift_i)
     part, g3 = stage_fourth(k1, k2, spread(part, "x"), lift_j, g1)

time: 200 us -> 179 us (0.90)
  Pallas kernels: 40.2 us -> 24.4 us
  blocking collectives: 36.5 us -> 33.9 us
    all_gather x1, waiting for transfers between devices: 14.4 us -> 10.1 us  [local(): b_all = lax.all_gather(stage_unpack_b(info, raw), 'x')]
    all_to_all x7, waiting for transfers between devices: 34 us -> 36.8 us  [spread(): return lax.all_to_all(operand, axes, 0, 0, tiled=True)]
    pallas_call x1, Pallas kernels: 6.1 us -> 3.37 us  [stage_second(): call(second_body, outs, [VMEM, HBM, VMEM, VMEM], STREAM + row_scratch(2))]
    pallas_call x1, Pallas kernels: 5.64 us -> 2.91 us  [stage_third(): call(third_body, outs, [VMEM, HBM, VMEM, VMEM], STREAM + lane_scratch(2))]
    pallas_call x1, Pallas kernels: 6.1 us -> 3.38 us  [stage_fourth(): call(fourth_body, outs, [VMEM, HBM, VMEM, VMEM, VMEM], STREAM + row_scrat...]
    all_gather x1, blocking collectives: 36.5 us -> 33.9 us  [local(): raw = lax.all_gather(packed, ('zh', 'zl'))]
    pallas_call x1 -> x2, Pallas kernels: 9.56 us -> 7.16 us  [the longest x1 4.95 us: stage_cost(): return call(cost_body, outs, [VMEM] * 4, scratch, (VMEM, HBM, VMEM))(*args)]
    unnamed x19 -> x15, local copies, waits for them, and re-layouts: 4.38 us -> 6.46 us
  transfers between devices with their start and end apart: 9 -> 9, of which waited for: 8 -> 9; matrix products, arithmetic and copies ran while one was open for 4% -> 3% of each run, Pallas kernels for 1% -> 2%
where the time goes in v4:
time: 179 us; the launch traced here: 178 us
  waiting for transfers between devices  47.9 us (27%)
  starting transfers between devices  43.8 us (24%)
  blocking collectives  33.9 us (19%)
  Pallas kernels  24.4 us (14%)
  between operations  15.6 us (9%)
  local copies, waits for them, and re-layouts  9.75 us (5%)
  other arithmetic  2.43 us (1%)
    all_to_all x7, waiting for transfers between devices, spread(): return lax.all_to_all(operand, axes, 0, 0, tiled=True)  36.8 us
    all_gather x1, blocking collectives, local(): raw = lax.all_gather(packed, ('zh', 'zl'))  33.9 us
    all_to_all x7, starting transfers between devices, spread(): return lax.all_to_all(operand, axes, 0, 0, tiled=True)  32.8 us
    ppermute x1, starting transfers between devices, local(): a_other = lax.ppermute(a_half, 'c', [(0, 1), (1, 0)])  11 us
    all_gather x1, waiting for transfers between devices, local(): b_all = lax.all_gather(stage_unpack_b(info, raw), 'x')  10.1 us
    unnamed x15, local copies, waits for them, and re-layouts  6.46 us
    pallas_call x1, Pallas kernels, stage_cost(): return call(cost_body, outs, [VMEM] * 4, scratch, (VMEM, HBM, VMEM))(*args)  4.95 us
  transfers between devices with their start and end apart: 9, of which 9 were waited for; matrix products, arithmetic and copies ran while one was open for 3% of the time, Pallas kernels for 2%

profile of v4, /device:TPU:1, one launch (start us, length us, event | category | flops | bytes accessed | tf_op | source)
XLA Modules:
  0.0 177.8 jit_solution(7107775449887852675)
XLA Ops:
  7.2 0.7 copy-done.3
  7.9 0.8 copy-done.4
  8.8 33.9 %all-gather = bf16[3072,128]{1,0:T(8,128)(2,1)S(1)} all-gather(bf16[192,128]{1,0:T(8,128)(2,1)S(1)} %shard_map.83), channel_id=2, replica_groups=mesh['y'=4,'x'=4,'c'=2,'zh'=4,'zl'=4] {'zh','zl'}, dimensions={0}, use_global_device_ids=true | all-gather | bytes 835584 | tf_op jit(solution)/shard_map/all_gather | solution.py:415
  42.8 2.2 %shard_map.84 = bf16[4,192,1024]{2,1,0:T(8,128)(2,1)} custom-call(s32[4]{0:T(128)S(1)} %pad_add_fusion.info, bf16[16,192,128]{2,1,0:T(8,128)(2,1)S(1)} %bitcast.20), custom_call_target="tpu_custom_call" | custom-call | tf_op jit(solution)/shard_map/pallas_call | solution.py:367
  45.0 4.2 %all-to-all-start = ((bf16[4,192,1024]{2,1,0:T(8,128)(2,1)}), bf16[4,192,1024]{2,1,0:T(8,128)(2,1)S(1)}, u32[]{:S(2)}, u32[]{:S(2)}) async-start(bf16[4,192,1024]{2,1,0:T(8,128)(2,1)} %shard_map.84), calls=%async_computation | async-start | bytes 3145728 | tf_op jit(solution)/shard_map/all_to_all | solution.py:407
  49.2 1.6 shard_map.86
  50.8 10.9 %all-to-all-done = bf16[4,192,1024]{2,1,0:T(8,128)(2,1)S(1)} async-done(((bf16[4,192,1024]{2,1,0:T(8,128)(2,1)}), bf16[4,192,1024]{2,1,0:T(8,128)(2,1)S(1)}, u32[]{:S(2)}, u32[]{:S(2)}) %all-to-all-start) | async-done | bytes 1572896 | tf_op jit(solution)/shard_map/all_to_all | solution.py:407
  61.7 11.0 %collective-permute-start = (bf16[4,192,1024]{2,1,0:T(8,128)(2,1)S(1)}, bf16[4,192,1024]{2,1,0:T(8,128)(2,1)}, u32[]{:S(2)}, u32[]{:S(2)}) collective-permute-start(bf16[4,192,1024]{2,1,0:T(8,128)(2,1)S(1)} %all-to-all-done), channel_id=1, source_target_pairs={{0,16},{16,0},{1,17},{17,1},{2,18},{18,2},{3,19},{19,3},{4,20},{20... | collective-permute-start | bytes 4718600 | tf_op jit(solution)/shard_map/ppermute | solution.py:440
  75.0 1.0 collective-permute-done
  75.9 2.2 %shard_map.85 = (bf16[1536,1024]{1,0:T(8,128)(2,1)S(1)}, f32[16,128]{1,0:T(8,128)S(1)}) custom-call(s32[4]{0:T(128)S(1)} %pad_add_fusion.info, bf16[768,1024]{1,0:T(8,128)(2,1)S(1)} %bitcast.22, bf16[768,1024]{1,0:T(8,128)(2,1)} %bitcast.8.other), custom_call_target="tpu_custom_call" | custom-call | tf_op jit(solution)/shard_map/pallas_call | solution.py:372
  78.1 1.6 copy-done
  79.8 10.1 %all-gather.4.cloned.1.call-done.b_ref = bf16[768,1024]{1,0:T(8,128)(2,1)} async-done(((bf16[192,1024]{1,0:T(8,128)(2,1)}), bf16[768,1024]{1,0:T(8,128)(2,1)}) %all-gather.4.cloned.1.call-update) | async-done | bytes 1572880 | tf_op jit(solution)/shard_map/all_gather | solution.py:438
  89.9 1.9 %copy-done.1 = bf16[1536,1024]{1,0:T(8,128)(2,1)S(1)} copy-done((bf16[1536,1024]{1,0:T(8,128)(2,1)S(1)}, bf16[1536,1024]{1,0:T(8,128)(2,1)}, u32[]{:S(2)}) %copy-start.1) | copy-done | bytes 3145752
  91.8 1.4 copy-done.2
  93.2 5.0 %shard_map.87 = (f32[768,1024]{1,0:T(8,128)S(1)}, f32[13824,512]{1,0:T(8,128)}, f32[4,8,128]{2,1,0:T(8,128)}) custom-call(bf16[1536,1024]{1,0:T(8,128)(2,1)S(1)} %copy-done.1, f32[16,128]{1,0:T(8,128)S(1)} %get-tuple-element.20.norm_ref, bf16[768,1024]{1,0:T(8,128)(2,1)S(1)} %copy-done.2, f32[12,128]{1,0:T(8,128)S(1)} %select_n.83.lift_i), custom_call_target="tpu_custom_call" | custom-call | tf_op jit(solution)/shard_map/pallas_call | solution.py:383
  98.2 3.3 %all-to-all-start.1 = ((f32[4,8,128]{2,1,0:T(8,128)}), f32[4,8,128]{2,1,0:T(8,128)S(1)}, u32[]{:S(2)}, u32[]{:S(2)}) async-start(f32[4,8,128]{2,1,0:T(8,128)} %get-tuple-element.23), calls=%async_computation.1 | async-start | bytes 32768 | tf_op jit(solution)/shard_map/all_to_all | solution.py:407
  102.2 3.4 %all-to-all-done.1.got = f32[4,8,128]{2,1,0:T(8,128)S(1)} async-done(((f32[4,8,128]{2,1,0:T(8,128)}), f32[4,8,128]{2,1,0:T(8,128)S(1)}, u32[]{:S(2)}, u32[]{:S(2)}) %all-to-all-start.1) | async-done | bytes 16416 | tf_op jit(solution)/shard_map/all_to_all | solution.py:407
  105.6 3.4 %shard_map.88 = (f32[8,24,128]{2,1,0:T(8,128)}, f32[6,128]{1,0:T(8,128)S(1)}) custom-call(f32[768,1024]{1,0:T(8,128)S(1)} %get-tuple-element.21.k1_ref, f32[13824,512]{1,0:T(8,128)} %get-tuple-element.22.k2_hbm, f32[4,8,128]{2,1,0:T(8,128)S(1)} %all-to-all-done.1.got, f32[6,128]{1,0:T(8,128)S(1)} %select_n.88.lift_j), custom_call_target="tpu_custom_call" | custom-call | tf_op jit(solution)/shard_map/pallas_call | solution.py:388
  109.0 6.1 %all-to-all-start.2 = ((f32[8,24,128]{2,1,0:T(8,128)}), f32[8,24,128]{2,1,0:T(8,128)S(1)}, u32[]{:S(2)}, u32[]{:S(2)}) async-start(f32[8,24,128]{2,1,0:T(8,128)} %get-tuple-element.24), calls=%async_computation.2 | async-start | bytes 196608 | tf_op jit(solution)/shard_map/all_to_all | solution.py:407
  116.4 3.7 %all-to-all-done.2.got = f32[8,24,128]{2,1,0:T(8,128)S(1)} async-done(((f32[8,24,128]{2,1,0:T(8,128)}), f32[8,24,128]{2,1,0:T(8,128)S(1)}, u32[]{:S(2)}, u32[]{:S(2)}) %all-to-all-start.2) | async-done | bytes 98336 | tf_op jit(solution)/shard_map/all_to_all | solution.py:407
  120.1 2.9 %shard_map.89 = (f32[4,16,128]{2,1,0:T(8,128)}, f32[12,128]{1,0:T(8,128)S(1)}) custom-call(f32[768,1024]{1,0:T(8,128)S(1)} %get-tuple-element.21.k1_ref, f32[13824,512]{1,0:T(8,128)} %get-tuple-element.22.k2_hbm, f32[8,24,128]{2,1,0:T(8,128)S(1)} %all-to-all-done.2.got, f32[12,128]{1,0:T(8,128)S(1)} %select_n.83.lift_i), custom_call_target="tpu_custom_call" | custom-call | tf_op jit(solution)/shard_map/pallas_call | solution.py:393
  123.0 3.3 %all-to-all-start.3 = ((f32[4,16,128]{2,1,0:T(8,128)}), f32[4,16,128]{2,1,0:T(8,128)S(1)}, u32[]{:S(2)}, u32[]{:S(2)}) async-start(f32[4,16,128]{2,1,0:T(8,128)} %get-tuple-element.25), calls=%async_computation.3 | async-start | bytes 65536 | tf_op jit(solution)/shard_map/all_to_all | solution.py:407
  126.3 4.2 %all-to-all-done.3.got = f32[4,16,128]{2,1,0:T(8,128)S(1)} async-done(((f32[4,16,128]{2,1,0:T(8,128)}), f32[4,16,128]{2,1,0:T(8,128)S(1)}, u32[]{:S(2)}, u32[]{:S(2)}) %all-to-all-start.3) | async-done | bytes 32800 | tf_op jit(solution)/shard_map/all_to_all | solution.py:407
  130.5 3.4 %shard_map.90 = (f32[8,24,128]{2,1,0:T(8,128)}, f32[6,128]{1,0:T(8,128)S(1)}) custom-call(f32[768,1024]{1,0:T(8,128)S(1)} %get-tuple-element.21.k1_ref, f32[13824,512]{1,0:T(8,128)} %get-tuple-element.22.k2_hbm, f32[4,16,128]{2,1,0:T(8,128)S(1)} %all-to-all-done.3.got, f32[6,128]{1,0:T(8,128)S(1)} %select_n.88.lift_j, f32[6,128]{1,0:T(8,128)S(1)} %get-tuple-element.26.g1), custom_call_target="tpu_custom_call" | custom-call | tf_op jit(solution)/shard_map/pallas_call | solution.py:398
  133.9 5.2 %all-to-all-start.4 = ((f32[8,24,128]{2,1,0:T(8,128)}), f32[8,24,128]{2,1,0:T(8,128)S(1)}, u32[]{:S(2)}, u32[]{:S(2)}) async-start(f32[8,24,128]{2,1,0:T(8,128)} %get-tuple-element.27), calls=%async_computation.4 | async-start | bytes 196608 | tf_op jit(solution)/shard_map/all_to_all | solution.py:407
  139.2 5.0 %all-to-all-done.4.got = f32[8,24,128]{2,1,0:T(8,128)S(1)} async-done(((f32[8,24,128]{2,1,0:T(8,128)}), f32[8,24,128]{2,1,0:T(8,128)S(1)}, u32[]{:S(2)}, u32[]{:S(2)}) %all-to-all-start.4) | async-done | bytes 98336 | tf_op jit(solution)/shard_map/all_to_all | solution.py:407
  144.2 2.9 %shard_map.91 = f32[16,8,128]{2,1,0:T(8,128)} custom-call(s32[4]{0:T(128)S(1)} %pad_add_fusion.info, f32[768,1024]{1,0:T(8,128)S(1)} %get-tuple-element.21.k1_ref, f32[13824,512]{1,0:T(8,128)} %get-tuple-element.22.k2_hbm, f32[8,24,128]{2,1,0:T(8,128)S(1)} %all-to-all-done.4.got, f32[12,128]{1,0:T(8,128)S(1)} %select_n.83.lift_i, ...), custom_call_target="tpu_custom_call" | custom-call | tf_op jit(solution)/shard_map/pallas_call | solution.py:403
  147.1 5.3 %all-to-all-start.5 = ((f32[16,8,128]{2,1,0:T(8,128)}), f32[16,8,128]{2,1,0:T(8,128)S(1)}, u32[]{:S(2)}, u32[]{:S(2)}) async-start(f32[16,8,128]{2,1,0:T(8,128)} %shard_map.91), calls=%async_computation.5 | async-start | bytes 131072 | tf_op jit(solution)/shard_map/all_to_all | solution.py:407
  153.2 6.1 %all-to-all-done.5.got = f32[16,8,128]{2,1,0:T(8,128)S(1)} async-done(((f32[16,8,128]{2,1,0:T(8,128)}), f32[16,8,128]{2,1,0:T(8,128)S(1)}, u32[]{:S(2)}, u32[]{:S(2)}) %all-to-all-start.5) | async-done | bytes 65568 | tf_op jit(solution)/shard_map/all_to_all | solution.py:407
  159.3 0.8 shard_map.92
  160.1 5.5 %all-to-all-start.6 = ((f32[8,8,128]{2,1,0:T(8,128)}), f32[8,8,128]{2,1,0:T(8,128)S(1)}, u32[]{:S(2)}, u32[]{:S(2)}) async-start(f32[8,8,128]{2,1,0:T(8,128)} %get-tuple-element.32), calls=%async_computation.6 | async-start | bytes 65536 | tf_op jit(solution)/shard_map/all_to_all | solution.py:407
  166.9 3.5 %all-to-all-done.6 = f32[8,8,128]{2,1,0:T(8,128)S(1)} async-done(((f32[8,8,128]{2,1,0:T(8,128)}), f32[8,8,128]{2,1,0:T(8,128)S(1)}, u32[]{:S(2)}, u32[]{:S(2)}) %all-to-all-start.6) | async-done | bytes 32800 | tf_op jit(solution)/shard_map/all_to_all | solution.py:407
  (40 shorter events, 5.9 us)
Async XLA Ops:
  7.2 0.8 copy-start.3
  7.9 0.8 copy-start.4
  45.0 16.8 %all-to-all-start = ((bf16[4,192,1024]{2,1,0:T(8,128)(2,1)}), bf16[4,192,1024]{2,1,0:T(8,128)(2,1)S(1)}, u32[]{:S(2)}, u32[]{:S(2)}) async-start(bf16[4,192,1024]{2,1,0:T(8,128)(2,1)} %shard_map.84), calls=%async_computation | async-start | bytes 3145728 | tf_op jit(solution)/shard_map/all_to_all | solution.py:407
  49.2 23.6 %copy-start.5 = (s32[32]{0:T(128)S(1)}, s32[32]{0:T(128)}, u32[]{:S(2)}) copy-start(s32[32]{0:T(128)} %param.6) | copy-start | bytes 388
  49.2 23.7 %copy-start.6 = (s32[32]{0:T(128)S(1)}, s32[32]{0:T(128)}, u32[]{:S(2)}) copy-start(s32[32]{0:T(128)} %param.7) | copy-start | bytes 388
  49.2 40.8 %all-gather.4.cloned.1.call-start = ((), (), s32[]{:S(2)}) async-start(), calls=%async_computation.7 | async-start | bytes 1966080 | tf_op jit(solution)/shard_map/all_gather | solution.py:438
  61.7 14.2 %collective-permute-start = (bf16[4,192,1024]{2,1,0:T(8,128)(2,1)S(1)}, bf16[4,192,1024]{2,1,0:T(8,128)(2,1)}, u32[]{:S(2)}, u32[]{:S(2)}) collective-permute-start(bf16[4,192,1024]{2,1,0:T(8,128)(2,1)S(1)} %all-to-all-done), channel_id=1, source_target_pairs={{0,16},{16,0},{1,17},{17,1},{2,18},{18,2},{3,19},{19,3},{4,20},{20... | collective-permute-start | bytes 4718600 | tf_op jit(solution)/shard_map/ppermute | solution.py:440
  78.1 1.7 copy-start
  89.9 1.9 %copy-start.1 = (bf16[1536,1024]{1,0:T(8,128)(2,1)S(1)}, bf16[1536,1024]{1,0:T(8,128)(2,1)}, u32[]{:S(2)}) copy-start(bf16[1536,1024]{1,0:T(8,128)(2,1)} %copy-done) | copy-start | bytes 9437188
  91.8 1.4 copy-start.2
  98.2 7.4 %all-to-all-start.1 = ((f32[4,8,128]{2,1,0:T(8,128)}), f32[4,8,128]{2,1,0:T(8,128)S(1)}, u32[]{:S(2)}, u32[]{:S(2)}) async-start(f32[4,8,128]{2,1,0:T(8,128)} %get-tuple-element.23), calls=%async_computation.1 | async-start | bytes 32768 | tf_op jit(solution)/shard_map/all_to_all | solution.py:407
  109.0 11.1 %all-to-all-start.2 = ((f32[8,24,128]{2,1,0:T(8,128)}), f32[8,24,128]{2,1,0:T(8,128)S(1)}, u32[]{:S(2)}, u32[]{:S(2)}) async-start(f32[8,24,128]{2,1,0:T(8,128)} %get-tuple-element.24), calls=%async_computation.2 | async-start | bytes 196608 | tf_op jit(solution)/shard_map/all_to_all | solution.py:407
  123.0 7.5 %all-to-all-start.3 = ((f32[4,16,128]{2,1,0:T(8,128)}), f32[4,16,128]{2,1,0:T(8,128)S(1)}, u32[]{:S(2)}, u32[]{:S(2)}) async-start(f32[4,16,128]{2,1,0:T(8,128)} %get-tuple-element.25), calls=%async_computation.3 | async-start | bytes 65536 | tf_op jit(solution)/shard_map/all_to_all | solution.py:407
  133.9 10.2 %all-to-all-start.4 = ((f32[8,24,128]{2,1,0:T(8,128)}), f32[8,24,128]{2,1,0:T(8,128)S(1)}, u32[]{:S(2)}, u32[]{:S(2)}) async-start(f32[8,24,128]{2,1,0:T(8,128)} %get-tuple-element.27), calls=%async_computation.4 | async-start | bytes 196608 | tf_op jit(solution)/shard_map/all_to_all | solution.py:407
  147.1 12.3 %all-to-all-start.5 = ((f32[16,8,128]{2,1,0:T(8,128)}), f32[16,8,128]{2,1,0:T(8,128)S(1)}, u32[]{:S(2)}, u32[]{:S(2)}) async-start(f32[16,8,128]{2,1,0:T(8,128)} %shard_map.91), calls=%async_computation.5 | async-start | bytes 131072 | tf_op jit(solution)/shard_map/all_to_all | solution.py:407
  160.1 10.2 %all-to-all-start.6 = ((f32[8,8,128]{2,1,0:T(8,128)}), f32[8,8,128]{2,1,0:T(8,128)S(1)}, u32[]{:S(2)}, u32[]{:S(2)}) async-start(f32[8,8,128]{2,1,0:T(8,128)} %get-tuple-element.32), calls=%async_computation.6 | async-start | bytes 65536 | tf_op jit(solution)/shard_map/all_to_all | solution.py:407
Sparse Core Ops, SparseCore 0:
  52.1 37.7 all-gather.3

commit v5 on v4

--- a/solution.py
+++ b/solution.py
@@ -176,9 +176,14 @@
     return results
 
 
-def pack_body(gen, ref, out):
-    both = jnp.concatenate([gen[...].astype(jnp.float32), ref[...].astype(jnp.float32)], axis=0)
-    out[...] = jnp.transpose(both).astype(jnp.bfloat16)
+def pack_body(gen, ref, out, both, sems):
+    copies = [pltpu.make_async_copy(part, both.at[n], sems.at[n]) for n, part in enumerate((gen, ref))]
+    for copy in copies:
+        copy.start()
+    for copy in copies:
+        copy.wait()
+    wide = jnp.concatenate([both[0].astype(jnp.float32), both[1].astype(jnp.float32)], axis=0)
+    out[...] = jnp.transpose(wide).astype(jnp.bfloat16)
 
 
 def select_set(is_gen, raw, k):
@@ -193,7 +198,8 @@
         out[:, k * 128 : (k + 1) * 128] = select_set(info[1] == 1, raw, k)
 
 
-def unpack_a_body(info, raw, out):
+def unpack_a_body(info, raw, b_own, out):
+    del b_own
     for k in range(D // 128):
         part = select_set(info[0] == 1, raw, k)
         for n in range(4):
@@ -356,7 +362,9 @@
 
 
 def stage_pack(*args):
-    return call(pack_body, jax.ShapeDtypeStruct((BLOCK, 128), BF16), [VMEM, VMEM])(*args)
+    scratch = [pltpu.VMEM((2, 64, BLOCK), BF16), pltpu.SemaphoreType.DMA((2,))]
+    out = jax.ShapeDtypeStruct((BLOCK, 128), BF16)
+    return call(pack_body, out, [HBM, HBM], scratch, mib=60)(*args)
 
 
 def stage_unpack_b(*args):
@@ -364,7 +372,7 @@
 
 
 def stage_unpack_a(*args):
-    return call(unpack_a_body, jax.ShapeDtypeStruct((4, BLOCK, D), BF16), [SMEM, VMEM])(*args)
+    return call(unpack_a_body, jax.ShapeDtypeStruct((4, BLOCK, D), BF16), [SMEM, VMEM, HBM])(*args)
 
 
 def stage_join(*args):
@@ -435,8 +443,9 @@
     ref_weight = jnp.where(ref_in, 1.0 / totals[1], 0.0).reshape(4, 2, 128)
     ref_full = jnp.where(place[None, :] < counts[1, y, :, c][:, None], 1.0 / totals[1], 0.0).reshape(RJ, 128)
 
-    b_all = lax.all_gather(stage_unpack_b(info, raw), "x")
-    a_half = spread(stage_unpack_a(info, raw), "y")
+    b_own = stage_unpack_b(info, raw)
+    b_all = lax.all_gather(b_own, "x")
+    a_half = spread(stage_unpack_a(info, raw, b_own), "y")
     a_other = lax.ppermute(a_half, "c", [(0, 1), (1, 0)])
 
     a_all, norms = stage_join(info, a_half.reshape(NJ, D), a_other.reshape(NJ, D))

time: 179 us -> 181 us (1.011)
  waiting for transfers between devices: 47.9 us -> 50.3 us
    unnamed x15 -> x11, local copies, waits for them, and re-layouts: 6.46 us -> 4.94 us
  transfers between devices with their start and end apart: 9 -> 9, of which waited for: 9 -> 9; matrix products, arithmetic and copies ran while one was open for 3% -> 3% of each run, Pallas kernels for 2% -> 1%
where the time goes in v5:
time: 181 us; the launch traced here: 180 us
  waiting for transfers between devices  50.3 us (28%)
  starting transfers between devices  44 us (24%)
  blocking collectives  34.2 us (19%)
  Pallas kernels  25 us (14%)
  between operations  15.6 us (9%)
  local copies, waits for them, and re-layouts  8.23 us (5%)
  other arithmetic  2.43 us (1%)
    all_to_all x7, waiting for transfers between devices, spread(): return lax.all_to_all(operand, axes, 0, 0, tiled=True)  37.7 us
    all_gather x1, blocking collectives, local(): raw = lax.all_gather(packed, ('zh', 'zl'))  34.2 us
    all_to_all x7, starting transfers between devices, spread(): return lax.all_to_all(operand, axes, 0, 0, tiled=True)  32.9 us
    all_gather x1, waiting for transfers between devices, local(): b_all = lax.all_gather(b_own, 'x')  11.1 us
    ppermute x1, starting transfers between devices, local(): a_other = lax.ppermute(a_half, 'c', [(0, 1), (1, 0)])  11 us
    pallas_call x1, Pallas kernels, stage_cost(): return call(cost_body, outs, [VMEM] * 4, scratch, (VMEM, HBM, VMEM))(*args)  4.99 us
    unnamed x11, local copies, waits for them, and re-layouts  4.94 us
  transfers between devices with their start and end apart: 9, of which 9 were waited for; matrix products, arithmetic and copies ran while one was open for 3% of the time, Pallas kernels for 1%

profile of v5, /device:TPU:1, one launch (start us, length us, event | category | flops | bytes accessed | tf_op | source)
XLA Modules:
  0.0 179.7 jit_solution(17065099201077905890)
XLA Ops:
  7.2 1.5 shard_map.83
  8.7 34.2 %all-gather = bf16[3072,128]{1,0:T(8,128)(2,1)S(1)} all-gather(bf16[192,128]{1,0:T(8,128)(2,1)} %shard_map.83), channel_id=2, replica_groups=mesh['y'=4,'x'=4,'c'=2,'zh'=4,'zl'=4] {'zh','zl'}, dimensions={0}, use_global_device_ids=true | all-gather | bytes 835584 | tf_op jit(solution)/shard_map/all_gather | solution.py:423
  43.0 1.6 shard_map.84.b_own
  44.5 2.2 %shard_map.85 = bf16[4,192,1024]{2,1,0:T(8,128)(2,1)} custom-call(s32[4]{0:T(128)S(1)} %pad_add_fusion.info, bf16[16,192,128]{2,1,0:T(8,128)(2,1)S(1)} %bitcast.21, bf16[192,1024]{1,0:T(8,128)(2,1)} %shard_map.84.b_own), custom_call_target="tpu_custom_call" | custom-call | tf_op jit(solution)/shard_map/pallas_call | solution.py:375
  46.7 4.3 %all-to-all-start = ((bf16[4,192,1024]{2,1,0:T(8,128)(2,1)}), bf16[4,192,1024]{2,1,0:T(8,128)(2,1)S(1)}, u32[]{:S(2)}, u32[]{:S(2)}) async-start(bf16[4,192,1024]{2,1,0:T(8,128)(2,1)} %shard_map.85), calls=%async_computation | async-start | bytes 3145728 | tf_op jit(solution)/shard_map/all_to_all | solution.py:415
  51.8 11.9 %all-to-all-done = bf16[4,192,1024]{2,1,0:T(8,128)(2,1)S(1)} async-done(((bf16[4,192,1024]{2,1,0:T(8,128)(2,1)}), bf16[4,192,1024]{2,1,0:T(8,128)(2,1)S(1)}, u32[]{:S(2)}, u32[]{:S(2)}) %all-to-all-start) | async-done | bytes 1572896 | tf_op jit(solution)/shard_map/all_to_all | solution.py:415
  63.6 11.0 %collective-permute-start = (bf16[4,192,1024]{2,1,0:T(8,128)(2,1)S(1)}, bf16[4,192,1024]{2,1,0:T(8,128)(2,1)S(1)}, u32[]{:S(2)}, u32[]{:S(2)}) collective-permute-start(bf16[4,192,1024]{2,1,0:T(8,128)(2,1)S(1)} %all-to-all-done), channel_id=1, source_target_pairs={{0,16},{16,0},{1,17},{17,1},{2,18},{18,2},{3,19},{19,3},{4,20},{20... | collective-permute-start | bytes 4718600 | tf_op jit(solution)/shard_map/ppermute | solution.py:449
  76.9 0.8 collective-permute-done
  77.7 1.3 shard_map.86
  79.0 1.6 copy-done
  80.7 11.1 %all-gather.4.cloned.1.call-done.b_ref = bf16[768,1024]{1,0:T(8,128)(2,1)} async-done(((bf16[192,1024]{1,0:T(8,128)(2,1)}), bf16[768,1024]{1,0:T(8,128)(2,1)}) %all-gather.4.cloned.1.call-update) | async-done | bytes 1572880 | tf_op jit(solution)/shard_map/all_gather | solution.py:447
  91.7 1.9 %copy-done.1 = bf16[1536,1024]{1,0:T(8,128)(2,1)S(1)} copy-done((bf16[1536,1024]{1,0:T(8,128)(2,1)S(1)}, bf16[1536,1024]{1,0:T(8,128)(2,1)}, u32[]{:S(2)}) %copy-start.1) | copy-done | bytes 3145752
  93.6 1.4 copy-done.2
  95.0 5.0 %shard_map.87 = (f32[768,1024]{1,0:T(8,128)S(1)}, f32[13824,512]{1,0:T(8,128)}, f32[4,8,128]{2,1,0:T(8,128)}) custom-call(bf16[1536,1024]{1,0:T(8,128)(2,1)S(1)} %copy-done.1, f32[16,128]{1,0:T(8,128)S(1)} %get-tuple-element.20.norm_ref, bf16[768,1024]{1,0:T(8,128)(2,1)S(1)} %copy-done.2, f32[12,128]{1,0:T(8,128)S(1)} %select_n.83.lift_i), custom_call_target="tpu_custom_call" | custom-call | tf_op jit(solution)/shard_map/pallas_call | solution.py:391
  100.0 3.2 %all-to-all-start.1 = ((f32[4,8,128]{2,1,0:T(8,128)}), f32[4,8,128]{2,1,0:T(8,128)S(1)}, u32[]{:S(2)}, u32[]{:S(2)}) async-start(f32[4,8,128]{2,1,0:T(8,128)} %get-tuple-element.23), calls=%async_computation.1 | async-start | bytes 32768 | tf_op jit(solution)/shard_map/all_to_all | solution.py:415
  103.3 0.7 fusion.1
  104.1 3.4 %all-to-all-done.1.got = f32[4,8,128]{2,1,0:T(8,128)S(1)} async-done(((f32[4,8,128]{2,1,0:T(8,128)}), f32[4,8,128]{2,1,0:T(8,128)S(1)}, u32[]{:S(2)}, u32[]{:S(2)}) %all-to-all-start.1) | async-done | bytes 16416 | tf_op jit(solution)/shard_map/all_to_all | solution.py:415
  107.5 3.4 %shard_map.88 = (f32[8,24,128]{2,1,0:T(8,128)}, f32[6,128]{1,0:T(8,128)S(1)}) custom-call(f32[768,1024]{1,0:T(8,128)S(1)} %get-tuple-element.21.k1_ref, f32[13824,512]{1,0:T(8,128)} %get-tuple-element.22.k2_hbm, f32[4,8,128]{2,1,0:T(8,128)S(1)} %all-to-all-done.1.got, f32[6,128]{1,0:T(8,128)S(1)} %select_n.88.lift_j), custom_call_target="tpu_custom_call" | custom-call | tf_op jit(solution)/shard_map/pallas_call | solution.py:396
  110.9 6.1 %all-to-all-start.2 = ((f32[8,24,128]{2,1,0:T(8,128)}), f32[8,24,128]{2,1,0:T(8,128)S(1)}, u32[]{:S(2)}, u32[]{:S(2)}) async-start(f32[8,24,128]{2,1,0:T(8,128)} %get-tuple-element.24), calls=%async_computation.2 | async-start | bytes 196608 | tf_op jit(solution)/shard_map/all_to_all | solution.py:415
  118.3 3.7 %all-to-all-done.2.got = f32[8,24,128]{2,1,0:T(8,128)S(1)} async-done(((f32[8,24,128]{2,1,0:T(8,128)}), f32[8,24,128]{2,1,0:T(8,128)S(1)}, u32[]{:S(2)}, u32[]{:S(2)}) %all-to-all-start.2) | async-done | bytes 98336 | tf_op jit(solution)/shard_map/all_to_all | solution.py:415
  122.0 2.9 %shard_map.89 = (f32[4,16,128]{2,1,0:T(8,128)}, f32[12,128]{1,0:T(8,128)S(1)}) custom-call(f32[768,1024]{1,0:T(8,128)S(1)} %get-tuple-element.21.k1_ref, f32[13824,512]{1,0:T(8,128)} %get-tuple-element.22.k2_hbm, f32[8,24,128]{2,1,0:T(8,128)S(1)} %all-to-all-done.2.got, f32[12,128]{1,0:T(8,128)S(1)} %select_n.83.lift_i), custom_call_target="tpu_custom_call" | custom-call | tf_op jit(solution)/shard_map/pallas_call | solution.py:401
  124.9 3.3 %all-to-all-start.3 = ((f32[4,16,128]{2,1,0:T(8,128)}), f32[4,16,128]{2,1,0:T(8,128)S(1)}, u32[]{:S(2)}, u32[]{:S(2)}) async-start(f32[4,16,128]{2,1,0:T(8,128)} %get-tuple-element.25), calls=%async_computation.3 | async-start | bytes 65536 | tf_op jit(solution)/shard_map/all_to_all | solution.py:415
  128.3 4.2 %all-to-all-done.3.got = f32[4,16,128]{2,1,0:T(8,128)S(1)} async-done(((f32[4,16,128]{2,1,0:T(8,128)}), f32[4,16,128]{2,1,0:T(8,128)S(1)}, u32[]{:S(2)}, u32[]{:S(2)}) %all-to-all-start.3) | async-done | bytes 32800 | tf_op jit(solution)/shard_map/all_to_all | solution.py:415
  132.4 3.4 %shard_map.90 = (f32[8,24,128]{2,1,0:T(8,128)}, f32[6,128]{1,0:T(8,128)S(1)}) custom-call(f32[768,1024]{1,0:T(8,128)S(1)} %get-tuple-element.21.k1_ref, f32[13824,512]{1,0:T(8,128)} %get-tuple-element.22.k2_hbm, f32[4,16,128]{2,1,0:T(8,128)S(1)} %all-to-all-done.3.got, f32[6,128]{1,0:T(8,128)S(1)} %select_n.88.lift_j, f32[6,128]{1,0:T(8,128)S(1)} %get-tuple-element.26.g1), custom_call_target="tpu_custom_call" | custom-call | tf_op jit(solution)/shard_map/pallas_call | solution.py:406
  135.9 5.2 %all-to-all-start.4 = ((f32[8,24,128]{2,1,0:T(8,128)}), f32[8,24,128]{2,1,0:T(8,128)S(1)}, u32[]{:S(2)}, u32[]{:S(2)}) async-start(f32[8,24,128]{2,1,0:T(8,128)} %get-tuple-element.27), calls=%async_computation.4 | async-start | bytes 196608 | tf_op jit(solution)/shard_map/all_to_all | solution.py:415
  141.1 5.0 %all-to-all-done.4.got = f32[8,24,128]{2,1,0:T(8,128)S(1)} async-done(((f32[8,24,128]{2,1,0:T(8,128)}), f32[8,24,128]{2,1,0:T(8,128)S(1)}, u32[]{:S(2)}, u32[]{:S(2)}) %all-to-all-start.4) | async-done | bytes 98336 | tf_op jit(solution)/shard_map/all_to_all | solution.py:415
  146.1 2.9 %shard_map.91 = f32[16,8,128]{2,1,0:T(8,128)} custom-call(s32[4]{0:T(128)S(1)} %pad_add_fusion.info, f32[768,1024]{1,0:T(8,128)S(1)} %get-tuple-element.21.k1_ref, f32[13824,512]{1,0:T(8,128)} %get-tuple-element.22.k2_hbm, f32[8,24,128]{2,1,0:T(8,128)S(1)} %all-to-all-done.4.got, f32[12,128]{1,0:T(8,128)S(1)} %select_n.83.lift_i, ...), custom_call_target="tpu_custom_call" | custom-call | tf_op jit(solution)/shard_map/pallas_call | solution.py:411
  149.0 5.3 %all-to-all-start.5 = ((f32[16,8,128]{2,1,0:T(8,128)}), f32[16,8,128]{2,1,0:T(8,128)S(1)}, u32[]{:S(2)}, u32[]{:S(2)}) async-start(f32[16,8,128]{2,1,0:T(8,128)} %shard_map.91), calls=%async_computation.5 | async-start | bytes 131072 | tf_op jit(solution)/shard_map/all_to_all | solution.py:415
  155.2 6.1 %all-to-all-done.5.got = f32[16,8,128]{2,1,0:T(8,128)S(1)} async-done(((f32[16,8,128]{2,1,0:T(8,128)}), f32[16,8,128]{2,1,0:T(8,128)S(1)}, u32[]{:S(2)}, u32[]{:S(2)}) %all-to-all-start.5) | async-done | bytes 65568 | tf_op jit(solution)/shard_map/all_to_all | solution.py:415
  161.3 0.8 shard_map.92
  162.1 5.5 %all-to-all-start.6 = ((f32[8,8,128]{2,1,0:T(8,128)}), f32[8,8,128]{2,1,0:T(8,128)S(1)}, u32[]{:S(2)}, u32[]{:S(2)}) async-start(f32[8,8,128]{2,1,0:T(8,128)} %get-tuple-element.32), calls=%async_computation.6 | async-start | bytes 65536 | tf_op jit(solution)/shard_map/all_to_all | solution.py:415
  168.8 3.5 %all-to-all-done.6 = f32[8,8,128]{2,1,0:T(8,128)S(1)} async-done(((f32[8,8,128]{2,1,0:T(8,128)}), f32[8,8,128]{2,1,0:T(8,128)S(1)}, u32[]{:S(2)}, u32[]{:S(2)}) %all-to-all-start.6) | async-done | bytes 32800 | tf_op jit(solution)/shard_map/all_to_all | solution.py:415
  (36 shorter events, 5.7 us)
Async XLA Ops:
  46.7 28.0 %copy-start.3 = (s32[32]{0:T(128)S(1)}, s32[32]{0:T(128)}, u32[]{:S(2)}) copy-start(s32[32]{0:T(128)} %param.6) | copy-start | bytes 388
  46.7 28.1 %copy-start.4 = (s32[32]{0:T(128)S(1)}, s32[32]{0:T(128)}, u32[]{:S(2)}) copy-start(s32[32]{0:T(128)} %param.7) | copy-start | bytes 388
  46.7 16.9 %all-to-all-start = ((bf16[4,192,1024]{2,1,0:T(8,128)(2,1)}), bf16[4,192,1024]{2,1,0:T(8,128)(2,1)S(1)}, u32[]{:S(2)}, u32[]{:S(2)}) async-start(bf16[4,192,1024]{2,1,0:T(8,128)(2,1)} %shard_map.85), calls=%async_computation | async-start | bytes 3145728 | tf_op jit(solution)/shard_map/all_to_all | solution.py:415
  51.1 40.7 %all-gather.4.cloned.1.call-start = ((), (), s32[]{:S(2)}) async-start(), calls=%async_computation.7 | async-start | bytes 1966080 | tf_op jit(solution)/shard_map/all_gather | solution.py:447
  63.6 14.1 %collective-permute-start = (bf16[4,192,1024]{2,1,0:T(8,128)(2,1)S(1)}, bf16[4,192,1024]{2,1,0:T(8,128)(2,1)S(1)}, u32[]{:S(2)}, u32[]{:S(2)}) collective-permute-start(bf16[4,192,1024]{2,1,0:T(8,128)(2,1)S(1)} %all-to-all-done), channel_id=1, source_target_pairs={{0,16},{16,0},{1,17},{17,1},{2,18},{18,2},{3,19},{19,3},{4,20},{20... | collective-permute-start | bytes 4718600 | tf_op jit(solution)/shard_map/ppermute | solution.py:449
  79.0 1.6 copy-start
  91.7 1.9 %copy-start.1 = (bf16[1536,1024]{1,0:T(8,128)(2,1)S(1)}, bf16[1536,1024]{1,0:T(8,128)(2,1)}, u32[]{:S(2)}) copy-start(bf16[1536,1024]{1,0:T(8,128)(2,1)} %copy-done) | copy-start | bytes 9437188
  93.6 1.4 copy-start.2
  100.0 7.4 %all-to-all-start.1 = ((f32[4,8,128]{2,1,0:T(8,128)}), f32[4,8,128]{2,1,0:T(8,128)S(1)}, u32[]{:S(2)}, u32[]{:S(2)}) async-start(f32[4,8,128]{2,1,0:T(8,128)} %get-tuple-element.23), calls=%async_computation.1 | async-start | bytes 32768 | tf_op jit(solution)/shard_map/all_to_all | solution.py:415
  110.9 11.1 %all-to-all-start.2 = ((f32[8,24,128]{2,1,0:T(8,128)}), f32[8,24,128]{2,1,0:T(8,128)S(1)}, u32[]{:S(2)}, u32[]{:S(2)}) async-start(f32[8,24,128]{2,1,0:T(8,128)} %get-tuple-element.24), calls=%async_computation.2 | async-start | bytes 196608 | tf_op jit(solution)/shard_map/all_to_all | solution.py:415
  124.9 7.5 %all-to-all-start.3 = ((f32[4,16,128]{2,1,0:T(8,128)}), f32[4,16,128]{2,1,0:T(8,128)S(1)}, u32[]{:S(2)}, u32[]{:S(2)}) async-start(f32[4,16,128]{2,1,0:T(8,128)} %get-tuple-element.25), calls=%async_computation.3 | async-start | bytes 65536 | tf_op jit(solution)/shard_map/all_to_all | solution.py:415
  135.9 10.2 %all-to-all-start.4 = ((f32[8,24,128]{2,1,0:T(8,128)}), f32[8,24,128]{2,1,0:T(8,128)S(1)}, u32[]{:S(2)}, u32[]{:S(2)}) async-start(f32[8,24,128]{2,1,0:T(8,128)} %get-tuple-element.27), calls=%async_computation.4 | async-start | bytes 196608 | tf_op jit(solution)/shard_map/all_to_all | solution.py:415
  149.0 12.2 %all-to-all-start.5 = ((f32[16,8,128]{2,1,0:T(8,128)}), f32[16,8,128]{2,1,0:T(8,128)S(1)}, u32[]{:S(2)}, u32[]{:S(2)}) async-start(f32[16,8,128]{2,1,0:T(8,128)} %shard_map.91), calls=%async_computation.5 | async-start | bytes 131072 | tf_op jit(solution)/shard_map/all_to_all | solution.py:415
  162.1 10.2 %all-to-all-start.6 = ((f32[8,8,128]{2,1,0:T(8,128)}), f32[8,8,128]{2,1,0:T(8,128)S(1)}, u32[]{:S(2)}, u32[]{:S(2)}) async-start(f32[8,8,128]{2,1,0:T(8,128)} %get-tuple-element.32), calls=%async_computation.6 | async-start | bytes 65536 | tf_op jit(solution)/shard_map/all_to_all | solution.py:415
Sparse Core Ops, SparseCore 0:
  54.0 37.7 all-gather.3

commit v6 on v5

--- a/solution.py
+++ b/solution.py
@@ -186,24 +186,17 @@
     out[...] = jnp.transpose(wide).astype(jnp.bfloat16)
 
 
-def select_set(is_gen, raw, k):
-    even, odd = raw[2 * k], raw[2 * k + 1]
-    gen = jnp.concatenate([even[:, :64], odd[:, :64]], axis=1)
-    ref = jnp.concatenate([even[:, 64:], odd[:, 64:]], axis=1)
-    return jnp.where(is_gen, gen, ref)
-
-
-def unpack_b_body(info, raw, out):
+def unpack_body(info, raw, a_out, b_out):
     for k in range(D // 128):
-        out[:, k * 128 : (k + 1) * 128] = select_set(info[1] == 1, raw, k)
-
-
-def unpack_a_body(info, raw, b_own, out):
-    del b_own
-    for k in range(D // 128):
-        part = select_set(info[0] == 1, raw, k)
+        cols = slice(k * 128, (k + 1) * 128)
+        even, odd = raw[2 * k], raw[2 * k + 1]
+        gen = jnp.concatenate([even[:, :64], odd[:, :64]], axis=1)
+        ref = jnp.concatenate([even[:, 64:], odd[:, 64:]], axis=1)
+        a = jnp.where(info[0] == 1, gen, ref)
+        b = jnp.where(info[1] == 1, gen, ref)
         for n in range(4):
-            out[n, :, k * 128 : (k + 1) * 128] = part
+            a_out[n, :, cols] = a
+            b_out[n, :, cols] = b
 
 
 def norm_parts(values):
@@ -212,7 +205,8 @@
     return functools.reduce(jnp.add, [values[:, k * 128 : (k + 1) * 128] for k in range(D // 128)])
 
 
-def join_body(info, own, other, a_out, norm_out):
+def join_body(info, own, other, cols, a_out, norm_out):
+    del cols
     first = info[2] == 0
     for half in range(2):
         for s in range(6):
@@ -367,17 +361,14 @@
     return call(pack_body, out, [HBM, HBM], scratch, mib=60)(*args)
 
 
-def stage_unpack_b(*args):
-    return call(unpack_b_body, jax.ShapeDtypeStruct((BLOCK, D), BF16), [SMEM, VMEM])(*args)
-
-
-def stage_unpack_a(*args):
-    return call(unpack_a_body, jax.ShapeDtypeStruct((4, BLOCK, D), BF16), [SMEM, VMEM, HBM])(*args)
+def stage_unpack(*args):
+    outs = (jax.ShapeDtypeStruct((4, BLOCK, D), BF16),) * 2
+    return call(unpack_body, outs, [SMEM, VMEM])(*args)
 
 
 def stage_join(*args):
     outs = (jax.ShapeDtypeStruct((NI, D), BF16), f32(16, 128))
-    return call(join_body, outs, [SMEM, VMEM, VMEM])(*args)
+    return call(join_body, outs, [SMEM, VMEM, VMEM, HBM])(*args)
 
 
 def stage_cost(*args):
@@ -443,13 +434,14 @@
     ref_weight = jnp.where(ref_in, 1.0 / totals[1], 0.0).reshape(4, 2, 128)
     ref_full = jnp.where(place[None, :] < counts[1, y, :, c][:, None], 1.0 / totals[1], 0.0).reshape(RJ, 128)
 
-    b_own = stage_unpack_b(info, raw)
-    b_all = lax.all_gather(b_own, "x")
-    a_half = spread(stage_unpack_a(info, raw, b_own), "y")
+    a_wide, b_wide = stage_unpack(info, raw)
+    a_half = spread(a_wide, "y")
     a_other = lax.ppermute(a_half, "c", [(0, 1), (1, 0)])
-
-    a_all, norms = stage_join(info, a_half.reshape(NJ, D), a_other.reshape(NJ, D))
-    k1, k2, part = stage_cost(a_all, norms, b_all.reshape(NJ, D), lift_i)
+    b_all = spread(b_wide, "x")
+
+    b_all = b_all.reshape(NJ, D)
+    a_all, norms = stage_join(info, a_half.reshape(NJ, D), a_other.reshape(NJ, D), b_all)
+    k1, k2, part = stage_cost(a_all, norms, b_all, lift_i)
     part, g1 = stage_second(k1, k2, spread(part, "x"), lift_j)
     part, f2 = stage_third(k1, k2, spread(part, ("y", "c")), lift_i)
     part, g3 = stage_fourth(k1, k2, spread(part, "x"), lift_j, g1)

time: 181 us -> 171 us (0.945)
  blocking collectives: 34.2 us -> 50.7 us
  between operations: 15.6 us -> 2.22 us
  waiting for transfers between devices: 50.3 us -> 44.2 us
  local copies, waits for them, and re-layouts: 8.23 us -> 4.71 us
  starting transfers between devices: 44 us -> 41.1 us
    all_to_all x0 -> x1, blocking collectives: none -> 16.6 us  [spread(): return lax.all_to_all(operand, axes, 0, 0, tiled=True)]
    all_gather x1 -> x0, waiting for transfers between devices: 11.1 us -> none  [local(): b_all = lax.all_gather(b_own, 'x')]
    all_to_all x7, waiting for transfers between devices: 37.7 us -> 44.2 us  [spread(): return lax.all_to_all(operand, axes, 0, 0, tiled=True)]
    unnamed x11, local copies, waits for them, and re-layouts: 4.94 us -> 1.42 us
    all_to_all x7, starting transfers between devices: 32.9 us -> 30.1 us  [spread(): return lax.all_to_all(operand, axes, 0, 0, tiled=True)]
    pallas_call x3 -> x2, Pallas kernels: 5.11 us -> 4.29 us  [the longest x1 2.86 us: stage_join(): return call(join_body, outs, [SMEM, VMEM, VMEM, HBM])(*args)]
  transfers between devices with their start and end apart: 9 -> 8, of which waited for: 9 -> 7; matrix products, arithmetic and copies ran while one was open for 3% -> 3% of each run, Pallas kernels for 1% -> 0%
where the time goes in v6:
time: 171 us; the launch traced here: 170 us
  blocking collectives  50.7 us (30%)
  waiting for transfers between devices  44.2 us (26%)
  starting transfers between devices  41.1 us (24%)
  Pallas kernels  24.2 us (14%)
  local copies, waits for them, and re-layouts  4.71 us (3%)
  other arithmetic  2.42 us (1%)
  between operations  2.22 us (1%)
    all_to_all x7, waiting for transfers between devices, spread(): return lax.all_to_all(operand, axes, 0, 0, tiled=True)  44.2 us
    all_gather x1, blocking collectives, local(): raw = lax.all_gather(packed, ('zh', 'zl'))  34.2 us
    all_to_all x7, starting transfers between devices, spread(): return lax.all_to_all(operand, axes, 0, 0, tiled=True)  30.1 us
    all_to_all x1, blocking collectives, spread(): return lax.all_to_all(operand, axes, 0, 0, tiled=True)  16.6 us
    ppermute x1, starting transfers between devices, local(): a_other = lax.ppermute(a_half, 'c', [(0, 1), (1, 0)])  11 us
    pallas_call x1, Pallas kernels, stage_cost(): return call(cost_body, outs, [VMEM] * 4, scratch, (VMEM, HBM, VMEM))(*args)  5 us
    pallas_call x1, Pallas kernels, stage_fourth(): call(fourth_body, outs, [VMEM, HBM, VMEM, VMEM, VMEM], STREAM + row_scrat...  3.42 us
  transfers between devices with their start and end apart: 8, of which 7 were waited for; matrix products, arithmetic and copies ran while one was open for 3% of the time, Pallas kernels for 0%

profile of v6, /device:TPU:1, one launch (start us, length us, event | category | flops | bytes accessed | tf_op | source)
XLA Modules:
  0.0 169.6 jit_solution(11912886241831652386)
XLA Ops:
  0.6 1.5 shard_map.83
  2.2 34.2 %all-gather = bf16[3072,128]{1,0:T(8,128)(2,1)S(1)} all-gather(bf16[192,128]{1,0:T(8,128)(2,1)} %shard_map.83), channel_id=2, replica_groups=mesh['y'=4,'x'=4,'c'=2,'zh'=4,'zl'=4] {'zh','zl'}, dimensions={0}, use_global_device_ids=true | all-gather | bytes 835584 | tf_op jit(solution)/shard_map/all_gather | solution.py:414
  36.4 1.4 shard_map.84
  37.9 16.6 %all_to_all.40 = bf16[4,192,1024]{2,1,0:T(8,128)(2,1)S(1)} all-to-all(bf16[4,192,1024]{2,1,0:T(8,128)(2,1)S(1)} %get-tuple-element.21), channel_id=1, replica_groups=mesh['y'=4,'x'=4,'c'=2,'zh'=4,'zl'=4] {'y'}, dimensions={0} | all-to-all | bytes 3145728 | tf_op jit(solution)/shard_map/all_to_all | solution.py:406
  54.4 11.0 %collective-permute-start = (bf16[4,192,1024]{2,1,0:T(8,128)(2,1)S(1)}, bf16[4,192,1024]{2,1,0:T(8,128)(2,1)}, u32[]{:S(2)}, u32[]{:S(2)}) collective-permute-start(bf16[4,192,1024]{2,1,0:T(8,128)(2,1)S(1)} %all_to_all.40), channel_id=1, source_target_pairs={{0,16},{16,0},{1,17},{17,1},{2,18},{18,2},{3,19},{19,3},{4,20},{20... | collective-permute-start | bytes 4718600 | tf_op jit(solution)/shard_map/ppermute | solution.py:439
  65.5 4.0 %all-to-all-start.1 = ((bf16[4,192,1024]{2,1,0:T(8,128)(2,1)}), bf16[4,192,1024]{2,1,0:T(8,128)(2,1)S(1)}, u32[]{:S(2)}, u32[]{:S(2)}) async-start(bf16[4,192,1024]{2,1,0:T(8,128)(2,1)} %copy-done.2), calls=%async_computation.1 | async-start | bytes 3145728 | tf_op jit(solution)/shard_map/all_to_all | solution.py:406
  70.7 0.7 fusion
  71.7 18.4 %all-to-all-done.1 = bf16[4,192,1024]{2,1,0:T(8,128)(2,1)S(1)} async-done(((bf16[4,192,1024]{2,1,0:T(8,128)(2,1)}), bf16[4,192,1024]{2,1,0:T(8,128)(2,1)S(1)}, u32[]{:S(2)}, u32[]{:S(2)}) %all-to-all-start.1) | async-done | bytes 1572896 | tf_op jit(solution)/shard_map/all_to_all | solution.py:406
  90.1 2.9 %shard_map.85 = (bf16[1536,1024]{1,0:T(8,128)(2,1)S(1)}, f32[16,128]{1,0:T(8,128)S(1)}) custom-call(s32[4]{0:T(128)S(1)} %pad_add_fusion.info, bf16[768,1024]{1,0:T(8,128)(2,1)S(1)} %bitcast.23, bf16[768,1024]{1,0:T(8,128)(2,1)} %bitcast.8.other, bf16[768,1024]{1,0:T(8,128)(2,1)S(1)} %bitcast.21), custom_call_target="tpu_custom_call" | custom-call | tf_op jit(solution)/shard_map/pallas_call | solution.py:371
  93.0 1.4 copy-done.1
  94.4 5.0 %shard_map.86 = (f32[768,1024]{1,0:T(8,128)S(1)}, f32[13824,512]{1,0:T(8,128)}, f32[4,8,128]{2,1,0:T(8,128)}) custom-call(bf16[1536,1024]{1,0:T(8,128)(2,1)S(1)} %get-tuple-element.23.a_ref, f32[16,128]{1,0:T(8,128)S(1)} %get-tuple-element.24.norm_ref, bf16[768,1024]{1,0:T(8,128)(2,1)S(1)} %bitcast.22, f32[12,128]{1,0:T(8,128)S(1)} %select_n.83.lift_i), custom_call_target="tpu_custom_call" | custom-call | tf_op jit(solution)/shard_map/pallas_call | solution.py:382
  99.4 3.3 %all-to-all-start.2 = ((f32[4,8,128]{2,1,0:T(8,128)}), f32[4,8,128]{2,1,0:T(8,128)S(1)}, u32[]{:S(2)}, u32[]{:S(2)}) async-start(f32[4,8,128]{2,1,0:T(8,128)} %get-tuple-element.27), calls=%async_computation.2 | async-start | bytes 32768 | tf_op jit(solution)/shard_map/all_to_all | solution.py:406
  102.6 0.7 fusion.1
  103.4 3.4 %all-to-all-done.2.got = f32[4,8,128]{2,1,0:T(8,128)S(1)} async-done(((f32[4,8,128]{2,1,0:T(8,128)}), f32[4,8,128]{2,1,0:T(8,128)S(1)}, u32[]{:S(2)}, u32[]{:S(2)}) %all-to-all-start.2) | async-done | bytes 16416 | tf_op jit(solution)/shard_map/all_to_all | solution.py:406
  106.8 3.4 %shard_map.87 = (f32[8,24,128]{2,1,0:T(8,128)}, f32[6,128]{1,0:T(8,128)S(1)}) custom-call(f32[768,1024]{1,0:T(8,128)S(1)} %get-tuple-element.25.k1_ref, f32[13824,512]{1,0:T(8,128)} %get-tuple-element.26.k2_hbm, f32[4,8,128]{2,1,0:T(8,128)S(1)} %all-to-all-done.2.got, f32[6,128]{1,0:T(8,128)S(1)} %select_n.88.lift_j), custom_call_target="tpu_custom_call" | custom-call | tf_op jit(solution)/shard_map/pallas_call | solution.py:387
  110.3 5.5 %all-to-all-start.3 = ((f32[8,24,128]{2,1,0:T(8,128)}), f32[8,24,128]{2,1,0:T(8,128)S(1)}, u32[]{:S(2)}, u32[]{:S(2)}) async-start(f32[8,24,128]{2,1,0:T(8,128)} %get-tuple-element.28), calls=%async_computation.3 | async-start | bytes 196608 | tf_op jit(solution)/shard_map/all_to_all | solution.py:406
  117.1 3.7 %all-to-all-done.3.got = f32[8,24,128]{2,1,0:T(8,128)S(1)} async-done(((f32[8,24,128]{2,1,0:T(8,128)}), f32[8,24,128]{2,1,0:T(8,128)S(1)}, u32[]{:S(2)}, u32[]{:S(2)}) %all-to-all-start.3) | async-done | bytes 98336 | tf_op jit(solution)/shard_map/all_to_all | solution.py:406
  120.8 2.9 %shard_map.88 = (f32[4,16,128]{2,1,0:T(8,128)}, f32[12,128]{1,0:T(8,128)S(1)}) custom-call(f32[768,1024]{1,0:T(8,128)S(1)} %get-tuple-element.25.k1_ref, f32[13824,512]{1,0:T(8,128)} %get-tuple-element.26.k2_hbm, f32[8,24,128]{2,1,0:T(8,128)S(1)} %all-to-all-done.3.got, f32[12,128]{1,0:T(8,128)S(1)} %select_n.83.lift_i), custom_call_target="tpu_custom_call" | custom-call | tf_op jit(solution)/shard_map/pallas_call | solution.py:392
  123.7 3.3 %all-to-all-start.4 = ((f32[4,16,128]{2,1,0:T(8,128)}), f32[4,16,128]{2,1,0:T(8,128)S(1)}, u32[]{:S(2)}, u32[]{:S(2)}) async-start(f32[4,16,128]{2,1,0:T(8,128)} %get-tuple-element.29), calls=%async_computation.4 | async-start | bytes 65536 | tf_op jit(solution)/shard_map/all_to_all | solution.py:406
  127.1 4.2 %all-to-all-done.4.got = f32[4,16,128]{2,1,0:T(8,128)S(1)} async-done(((f32[4,16,128]{2,1,0:T(8,128)}), f32[4,16,128]{2,1,0:T(8,128)S(1)}, u32[]{:S(2)}, u32[]{:S(2)}) %all-to-all-start.4) | async-done | bytes 32800 | tf_op jit(solution)/shard_map/all_to_all | solution.py:406
  131.3 3.4 %shard_map.89 = (f32[8,24,128]{2,1,0:T(8,128)}, f32[6,128]{1,0:T(8,128)S(1)}) custom-call(f32[768,1024]{1,0:T(8,128)S(1)} %get-tuple-element.25.k1_ref, f32[13824,512]{1,0:T(8,128)} %get-tuple-element.26.k2_hbm, f32[4,16,128]{2,1,0:T(8,128)S(1)} %all-to-all-done.4.got, f32[6,128]{1,0:T(8,128)S(1)} %select_n.88.lift_j, f32[6,128]{1,0:T(8,128)S(1)} %get-tuple-element.30.g1), custom_call_target="tpu_custom_call" | custom-call | tf_op jit(solution)/shard_map/pallas_call | solution.py:397
  134.7 5.2 %all-to-all-start.5 = ((f32[8,24,128]{2,1,0:T(8,128)}), f32[8,24,128]{2,1,0:T(8,128)S(1)}, u32[]{:S(2)}, u32[]{:S(2)}) async-start(f32[8,24,128]{2,1,0:T(8,128)} %get-tuple-element.31), calls=%async_computation.5 | async-start | bytes 196608 | tf_op jit(solution)/shard_map/all_to_all | solution.py:406
  139.9 5.0 %all-to-all-done.5.got = f32[8,24,128]{2,1,0:T(8,128)S(1)} async-done(((f32[8,24,128]{2,1,0:T(8,128)}), f32[8,24,128]{2,1,0:T(8,128)S(1)}, u32[]{:S(2)}, u32[]{:S(2)}) %all-to-all-start.5) | async-done | bytes 98336 | tf_op jit(solution)/shard_map/all_to_all | solution.py:406
  144.9 2.9 %shard_map.90 = f32[16,8,128]{2,1,0:T(8,128)} custom-call(s32[4]{0:T(128)S(1)} %pad_add_fusion.info, f32[768,1024]{1,0:T(8,128)S(1)} %get-tuple-element.25.k1_ref, f32[13824,512]{1,0:T(8,128)} %get-tuple-element.26.k2_hbm, f32[8,24,128]{2,1,0:T(8,128)S(1)} %all-to-all-done.5.got, f32[12,128]{1,0:T(8,128)S(1)} %select_n.83.lift_i, ...), custom_call_target="tpu_custom_call" | custom-call | tf_op jit(solution)/shard_map/pallas_call | solution.py:402
  147.9 3.5 %all-to-all-start.6 = ((f32[16,8,128]{2,1,0:T(8,128)}), f32[16,8,128]{2,1,0:T(8,128)S(1)}, u32[]{:S(2)}, u32[]{:S(2)}) async-start(f32[16,8,128]{2,1,0:T(8,128)} %shard_map.90), calls=%async_computation.6 | async-start | bytes 131072 | tf_op jit(solution)/shard_map/all_to_all | solution.py:406
  152.2 6.1 %all-to-all-done.6.got = f32[16,8,128]{2,1,0:T(8,128)S(1)} async-done(((f32[16,8,128]{2,1,0:T(8,128)}), f32[16,8,128]{2,1,0:T(8,128)S(1)}, u32[]{:S(2)}, u32[]{:S(2)}) %all-to-all-start.6) | async-done | bytes 65568 | tf_op jit(solution)/shard_map/all_to_all | solution.py:406
  158.3 0.8 shard_map.91
  159.1 5.2 %all-to-all-start.7 = ((f32[8,8,128]{2,1,0:T(8,128)}), f32[8,8,128]{2,1,0:T(8,128)S(1)}, u32[]{:S(2)}, u32[]{:S(2)}) async-start(f32[8,8,128]{2,1,0:T(8,128)} %get-tuple-element.36), calls=%async_computation.7 | async-start | bytes 65536 | tf_op jit(solution)/shard_map/all_to_all | solution.py:406
  164.3 0.6 fusion.3
  164.9 0.6 dynamic_slice.37
  165.6 3.5 %all-to-all-done.7 = f32[8,8,128]{2,1,0:T(8,128)S(1)} async-done(((f32[8,8,128]{2,1,0:T(8,128)}), f32[8,8,128]{2,1,0:T(8,128)S(1)}, u32[]{:S(2)}, u32[]{:S(2)}) %all-to-all-start.7) | async-done | bytes 32800 | tf_op jit(solution)/shard_map/all_to_all | solution.py:406
  169.0 0.6 slice_reduce_fusion
  (33 shorter events, 2.4 us)
Async XLA Ops:
  37.9 16.6 %copy-start.2 = (bf16[4,192,1024]{2,1,0:T(8,128)(2,1)}, bf16[4,192,1024]{2,1,0:T(8,128)(2,1)S(1)}, u32[]{:S(2)}) copy-start(bf16[4,192,1024]{2,1,0:T(8,128)(2,1)S(1)} %get-tuple-element.22) | copy-start | bytes 4718596
  54.4 35.7 %collective-permute-start = (bf16[4,192,1024]{2,1,0:T(8,128)(2,1)S(1)}, bf16[4,192,1024]{2,1,0:T(8,128)(2,1)}, u32[]{:S(2)}, u32[]{:S(2)}) collective-permute-start(bf16[4,192,1024]{2,1,0:T(8,128)(2,1)S(1)} %all_to_all.40), channel_id=1, source_target_pairs={{0,16},{16,0},{1,17},{17,1},{2,18},{18,2},{3,19},{19,3},{4,20},{20... | collective-permute-start | bytes 4718600 | tf_op jit(solution)/shard_map/ppermute | solution.py:439
  65.5 4.1 %copy-start.3 = (s32[32]{0:T(128)S(1)}, s32[32]{0:T(128)}, u32[]{:S(2)}) copy-start(s32[32]{0:T(128)} %param.6) | copy-start | bytes 388
  65.5 4.1 %copy-start.4 = (s32[32]{0:T(128)S(1)}, s32[32]{0:T(128)}, u32[]{:S(2)}) copy-start(s32[32]{0:T(128)} %param.7) | copy-start | bytes 388
  65.5 24.6 %all-to-all-start.1 = ((bf16[4,192,1024]{2,1,0:T(8,128)(2,1)}), bf16[4,192,1024]{2,1,0:T(8,128)(2,1)S(1)}, u32[]{:S(2)}, u32[]{:S(2)}) async-start(bf16[4,192,1024]{2,1,0:T(8,128)(2,1)} %copy-done.2), calls=%async_computation.1 | async-start | bytes 3145728 | tf_op jit(solution)/shard_map/all_to_all | solution.py:406
  90.1 2.9 %copy-start = (bf16[4,192,1024]{2,1,0:T(8,128)(2,1)}, bf16[4,192,1024]{2,1,0:T(8,128)(2,1)S(1)}, u32[]{:S(2)}) copy-start(bf16[4,192,1024]{2,1,0:T(8,128)(2,1)S(1)} %all-to-all-done.1) | copy-start | bytes 4718596
  93.0 1.4 copy-start.1
  99.4 7.4 %all-to-all-start.2 = ((f32[4,8,128]{2,1,0:T(8,128)}), f32[4,8,128]{2,1,0:T(8,128)S(1)}, u32[]{:S(2)}, u32[]{:S(2)}) async-start(f32[4,8,128]{2,1,0:T(8,128)} %get-tuple-element.27), calls=%async_computation.2 | async-start | bytes 32768 | tf_op jit(solution)/shard_map/all_to_all | solution.py:406
  110.3 10.5 %all-to-all-start.3 = ((f32[8,24,128]{2,1,0:T(8,128)}), f32[8,24,128]{2,1,0:T(8,128)S(1)}, u32[]{:S(2)}, u32[]{:S(2)}) async-start(f32[8,24,128]{2,1,0:T(8,128)} %get-tuple-element.28), calls=%async_computation.3 | async-start | bytes 196608 | tf_op jit(solution)/shard_map/all_to_all | solution.py:406
  123.7 7.5 %all-to-all-start.4 = ((f32[4,16,128]{2,1,0:T(8,128)}), f32[4,16,128]{2,1,0:T(8,128)S(1)}, u32[]{:S(2)}, u32[]{:S(2)}) async-start(f32[4,16,128]{2,1,0:T(8,128)} %get-tuple-element.29), calls=%async_computation.4 | async-start | bytes 65536 | tf_op jit(solution)/shard_map/all_to_all | solution.py:406
  134.7 10.2 %all-to-all-start.5 = ((f32[8,24,128]{2,1,0:T(8,128)}), f32[8,24,128]{2,1,0:T(8,128)S(1)}, u32[]{:S(2)}, u32[]{:S(2)}) async-start(f32[8,24,128]{2,1,0:T(8,128)} %get-tuple-element.31), calls=%async_computation.5 | async-start | bytes 196608 | tf_op jit(solution)/shard_map/all_to_all | solution.py:406
  147.9 10.4 %all-to-all-start.6 = ((f32[16,8,128]{2,1,0:T(8,128)}), f32[16,8,128]{2,1,0:T(8,128)S(1)}, u32[]{:S(2)}, u32[]{:S(2)}) async-start(f32[16,8,128]{2,1,0:T(8,128)} %shard_map.90), calls=%async_computation.6 | async-start | bytes 131072 | tf_op jit(solution)/shard_map/all_to_all | solution.py:406
  159.1 9.9 %all-to-all-start.7 = ((f32[8,8,128]{2,1,0:T(8,128)}), f32[8,8,128]{2,1,0:T(8,128)S(1)}, u32[]{:S(2)}, u32[]{:S(2)}) async-start(f32[8,8,128]{2,1,0:T(8,128)} %get-tuple-element.36), calls=%async_computation.7 | async-start | bytes 65536 | tf_op jit(solution)/shard_map/all_to_all | solution.py:406

commit v7 on v6

--- a/solution.py
+++ b/solution.py
@@ -186,17 +186,16 @@
     out[...] = jnp.transpose(wide).astype(jnp.bfloat16)
 
 
-def unpack_body(info, raw, a_out, b_out):
+def unpack_body(which, info, raw, *refs):
+    out = refs[-1]
     for k in range(D // 128):
         cols = slice(k * 128, (k + 1) * 128)
         even, odd = raw[2 * k], raw[2 * k + 1]
         gen = jnp.concatenate([even[:, :64], odd[:, :64]], axis=1)
         ref = jnp.concatenate([even[:, 64:], odd[:, 64:]], axis=1)
-        a = jnp.where(info[0] == 1, gen, ref)
-        b = jnp.where(info[1] == 1, gen, ref)
+        part = jnp.where(info[which] == 1, gen, ref)
         for n in range(4):
-            a_out[n, :, cols] = a
-            b_out[n, :, cols] = b
+            out[n, :, cols] = part
 
 
 def norm_parts(values):
@@ -205,9 +204,10 @@
     return functools.reduce(jnp.add, [values[:, k * 128 : (k + 1) * 128] for k in range(D // 128)])
 
 
-def join_body(info, own, other, cols, a_out, norm_out):
+def join_body(info, gen_count, ref_count, own, other, cols, a_out, norm_out, lift_i, lift_j, weights):
     del cols
-    first = info[2] == 0
+    c, x, y = info[2], info[4], info[5]
+    first = c == 0
     for half in range(2):
         for s in range(6):
             part = slice(s * 128, (s + 1) * 128)
@@ -219,12 +219,45 @@
             norm_out[r : r + 1, :] = jnp.sum(turned, axis=0, keepdims=True) * (0.5 * LOG2E / EPSILON)
     norm_out[RI:16, :] = jnp.zeros((16 - RI, 128), jnp.float32)
 
+    def total(counts):
+        return jnp.full((8, 128), functools.reduce(jnp.add, [counts[n] for n in range(32)]).astype(jnp.float32))
+
+    def number(is_gen, t):
+        return jnp.where(is_gen, gen_count[t], ref_count[t])
+
+    def flat(rows):
+        shape = (rows, 128)
+        return lax.broadcasted_iota(jnp.int32, shape, 0) * 128 + lax.broadcasted_iota(jnp.int32, shape, 1)
+
+    def valid(spots, starts, counts):
+        inside = [(spots >= start) & (spots < start + count) for start, count in zip(starts, counts)]
+        return functools.reduce(jnp.logical_or, inside)
+
+    a_is_gen, b_is_gen = info[0] == 1, info[1] == 1
+    totals = total(gen_count), total(ref_count)
+    gen_log, ref_log = (-jnp.log(value) * LOG2E for value in totals)
+    counts = [number(a_is_gen, ((n % 4) * 4 + x) * 2 + n // 4) for n in range(8)]
+    ok = valid(flat(16), [n * BLOCK for n in range(8)], counts)
+    log_a = jnp.where(a_is_gen, gen_log, ref_log)
+    lift_i[...] = jnp.where(ok, jnp.concatenate([log_a, log_a], axis=0), FAR)
+    here = [(y * 4 + n) * 2 + c for n in range(4)]
+    starts = [n * BLOCK for n in range(4)]
+    ok = valid(flat(8), starts, [number(b_is_gen, t) for t in here])
+    lift_j[...] = jnp.where(ok, jnp.where(b_is_gen, gen_log, ref_log), FAR)
+    shift = 64 * lax.rem(y, 2)
+    windows = [n * 256 + shift for n in range(4)]
+    for n, counts in enumerate((gen_count, ref_count)):
+        ok = valid(flat(8), windows, [counts[t] for t in here])
+        weights[n * 8 : n * 8 + 8, :] = jnp.where(ok, 1.0 / totals[n], 0.0)
+    ok = valid(flat(8), starts, [ref_count[t] for t in here])
+    weights[16:24, :] = jnp.where(ok, 1.0 / totals[1], 0.0)
+
 
 def cost_body(
     a_ref, norm_ref, b_ref, lift_i, k1_ref, k2_hbm, part_out, k2_ref, high_ref, mass_ref, sq_ref, out_sems
 ):
     scale = LOG2E / EPSILON
-    heads = [lift_i[...]]
+    heads = [lift_i[0:RI, :]]
     for b in range(RJ):
         part = slice(b * 128, (b + 1) * 128)
         total = jnp.sum(norm_parts(b_ref[part, :]), axis=1, keepdims=True) * (0.5 * scale)
@@ -270,7 +303,7 @@
     start_fetch(k2_hbm, k2_ref, sems)
     g1 = -merge(got, 4)[0:RJ, :]
     g1_out[...] = g1
-    lift = lift_j[...]
+    lift = lift_j[0:RJ, :]
     heads = [lift, lifted(g1, lift)]
     results = reduce_rows(k1_ref, k2_hbm, k2_ref, sems, heads, head_ref, wide_ref, high_ref, mass_ref)
     for n in range(8):
@@ -284,7 +317,7 @@
     f1 = merged[0:RI, :]
     f2 = 0.5 * (f1 + merged[RI : 2 * RI, :])
     f2_out[...] = f2
-    lift = lift_i[...]
+    lift = lift_i[0:RI, :]
     heads = [lifted(f1, lift), lifted(f2, lift)]
     results = reduce_lanes(k1_ref, k2_hbm, k2_ref, sems, heads, high_ref, mass_ref)
     for n in range(4):
@@ -299,7 +332,7 @@
     g2 = 0.5 * (g1[...] + merged[0:RJ, :])
     g3 = 0.5 * (g2 + merged[8 : 8 + RJ, :])
     g3_out[...] = g3
-    lift = lift_j[...]
+    lift = lift_j[0:RJ, :]
     heads = [lifted(g2, lift), lifted(g3, lift)]
     results = reduce_rows(k1_ref, k2_hbm, k2_ref, sems, heads, head_ref, wide_ref, high_ref, mass_ref)
     for n in range(8):
@@ -313,7 +346,7 @@
     f3 = 0.5 * (f2[...] + merged[0:RI, :])
     f4 = 0.5 * (f3 + merged[RI : 2 * RI, :])
     f4_ref[0:RI, :] = f4
-    heads = [lifted(f3, lift_i[...])]
+    heads = [lifted(f3, lift_i[0:RI, :])]
     (result,) = reduce_lanes(k1_ref, k2_hbm, k2_ref, sems, heads, high_ref, mass_ref)
     shifted = result - g3[...]
     mine = f4_ref[pl.ds(info[3], 2), :]
@@ -322,11 +355,12 @@
         out[n, RJ : RJ + 2, :] = mine
 
 
-def last_body(got, gen_weight, ref_weight, ref_full_weight, pots, g4_out, share):
+def last_body(got, weights, pots, g4_out, share):
     g4 = merge([got[n * 4 + 1, 0:RJ, :] for n in range(4)], 4) * (-0.5 * LN2)
     g4_out[0:RJ, :] = g4
     g4_out[RJ:8, :] = jnp.zeros((8 - RJ, 128), jnp.float32)
-    total = jnp.sum(jnp.where(ref_full_weight[...] > 0.0, g4 * ref_full_weight[...], 0.0))
+    weight = weights[16 : 16 + RJ, :]
+    total = jnp.sum(jnp.where(weight > 0.0, g4 * weight, 0.0))
     for n in range(4):
         own = slice(RJ, RJ + 2)
         gen_pot = got[n * 4 + 1][own, :] * LN2
@@ -336,8 +370,10 @@
         pots[n, 2:4, :] = gen_self
         pots[n, 4:6, :] = ref_self
         pots[n, 6:8, :] = jnp.zeros((2, 128), jnp.float32)
-        total += jnp.sum(jnp.where(gen_weight[n] > 0.0, (gen_pot - gen_self) * gen_weight[n], 0.0))
-        total -= jnp.sum(jnp.where(ref_weight[n] > 0.0, ref_self * ref_weight[n], 0.0))
+        weight = weights[2 * n : 2 * n + 2, :]
+        total += jnp.sum(jnp.where(weight > 0.0, (gen_pot - gen_self) * weight, 0.0))
+        weight = weights[8 + 2 * n : 8 + 2 * n + 2, :]
+        total -= jnp.sum(jnp.where(weight > 0.0, ref_self * weight, 0.0))
     for n in range(8):
         share[n, :, :] = jnp.full((8, 128), total, jnp.float32)
 
@@ -361,14 +397,14 @@
     return call(pack_body, out, [HBM, HBM], scratch, mib=60)(*args)
 
 
-def stage_unpack(*args):
-    outs = (jax.ShapeDtypeStruct((4, BLOCK, D), BF16),) * 2
-    return call(unpack_body, outs, [SMEM, VMEM])(*args)
+def stage_unpack(which, *args):
+    out = jax.ShapeDtypeStruct((4, BLOCK, D), BF16)
+    return call(functools.partial(unpack_body, which), out, [SMEM, VMEM, HBM][: len(args)])(*args)
 
 
 def stage_join(*args):
-    outs = (jax.ShapeDtypeStruct((NI, D), BF16), f32(16, 128))
-    return call(join_body, outs, [SMEM, VMEM, VMEM, HBM])(*args)
+    outs = (jax.ShapeDtypeStruct((NI, D), BF16), f32(16, 128), f32(16, 128), f32(8, 128), f32(24, 128))
+    return call(join_body, outs, [SMEM, SMEM, SMEM, VMEM, VMEM, HBM])(*args)
 
 
 def stage_cost(*args):
@@ -414,42 +450,22 @@
     raw = lax.all_gather(packed, ("zh", "zl"))
 
     info = jnp.stack(
-        [a_is_gen.astype(jnp.int32), b_is_gen.astype(jnp.int32), c, c * 6 + (3 * y) // 2]
+        [a_is_gen.astype(jnp.int32), b_is_gen.astype(jnp.int32), c, c * 6 + (3 * y) // 2, x, y]
     ).astype(jnp.int32)
-    counts = jnp.stack([gen_count, ref_count]).reshape(2, 4, 4, 2)
-    totals = jnp.sum(counts, axis=(1, 2, 3)).astype(jnp.float32)
-    weights2 = -jnp.log(totals) * LOG2E
-    place = jnp.arange(BLOCK, dtype=jnp.int32)
-    a_set = jnp.where(a_is_gen, 0, 1)
-    b_set = jnp.where(b_is_gen, 0, 1)
-    count_i = jnp.transpose(counts[a_set, :, x]).reshape(8)
-    count_j = counts[b_set, y, :, c]
-    lift_i = jnp.where(place[None, :] < count_i[:, None], weights2[a_set], FAR).reshape(RI, 128)
-    lift_j = jnp.where(place[None, :] < count_j[:, None], weights2[b_set], FAR).reshape(RJ, 128)
-    spots = jnp.arange(256, dtype=jnp.int32) - 64 * (y % 2)
-    inside = spots >= 0
-    gen_in = inside[None, :] & (spots[None, :] < counts[0, y, :, c][:, None])
-    ref_in = inside[None, :] & (spots[None, :] < counts[1, y, :, c][:, None])
-    gen_weight = jnp.where(gen_in, 1.0 / totals[0], 0.0).reshape(4, 2, 128)
-    ref_weight = jnp.where(ref_in, 1.0 / totals[1], 0.0).reshape(4, 2, 128)
-    ref_full = jnp.where(place[None, :] < counts[1, y, :, c][:, None], 1.0 / totals[1], 0.0).reshape(RJ, 128)
-
-    a_wide, b_wide = stage_unpack(info, raw)
-    a_half = spread(a_wide, "y")
+    a_half = spread(stage_unpack(0, info, raw), "y")
     a_other = lax.ppermute(a_half, "c", [(0, 1), (1, 0)])
-    b_all = spread(b_wide, "x")
-
+    b_all = spread(stage_unpack(1, info, raw, a_half), "x")
     b_all = b_all.reshape(NJ, D)
-    a_all, norms = stage_join(info, a_half.reshape(NJ, D), a_other.reshape(NJ, D), b_all)
+    a_all, norms, lift_i, lift_j, weights = stage_join(
+        info, gen_count, ref_count, a_half.reshape(NJ, D), a_other.reshape(NJ, D), b_all
+    )
     k1, k2, part = stage_cost(a_all, norms, b_all, lift_i)
     part, g1 = stage_second(k1, k2, spread(part, "x"), lift_j)
     part, f2 = stage_third(k1, k2, spread(part, ("y", "c")), lift_i)
     part, g3 = stage_fourth(k1, k2, spread(part, "x"), lift_j, g1)
     part = stage_fifth(info, k1, k2, spread(part, ("y", "c")), lift_i, f2, g3)
     got = spread(part, ("x", "zl"))
-    pots, g4, share = call(
-        last_body, (f32(4, 8, 128), f32(8, 128), f32(8, 8, 128)), [VMEM] * 4
-    )(got, gen_weight, ref_weight, ref_full)
+    pots, g4, share = call(last_body, (f32(4, 8, 128), f32(8, 128), f32(8, 8, 128)), [VMEM, VMEM])(got, weights)
     divergence = jnp.sum(spread(share, ("y", "c"))[:, 0, 0])
 
     mine = lax.dynamic_index_in_dim(pots, x, 0, keepdims=False)

time: 171 us -> 162 us (0.947)
  blocking collectives: 50.7 us -> 107 us
  waiting for transfers between devices: 44.2 us -> 10.4 us
  starting transfers between devices: 41.1 us -> 19.7 us
  local copies, waits for them, and re-layouts: 4.71 us -> 1.39 us
  Pallas kernels: 24.2 us -> 21.1 us
  other arithmetic: 2.42 us -> 0.61 us
    all_to_all x1 -> x6, blocking collectives: 16.6 us -> 73.2 us  [spread(): return lax.all_to_all(operand, axes, 0, 0, tiled=True)]
    all_to_all x7 -> x2, waiting for transfers between devices: 44.2 us -> 10.4 us  [spread(): return lax.all_to_all(operand, axes, 0, 0, tiled=True)]
    all_to_all x7 -> x2, starting transfers between devices: 30.1 us -> 8.69 us  [spread(): return lax.all_to_all(operand, axes, 0, 0, tiled=True)]
    pallas_call x3 -> x4, Pallas kernels: 5.04 us -> 4.16 us  [the longest x2 2.03 us: stage_unpack(): call(functools.partial(unpack_body, which), out, [SMEM, VMEM, HBM][:len(a...]
  transfers between devices with their start and end apart: 8 -> 3, of which waited for: 7 -> 2; matrix products, arithmetic and copies ran while one was open for 3% -> 1% of each run, Pallas kernels for 0% -> 1%
where the time goes in v7:
time: 162 us; the launch traced here: 161 us
  blocking collectives  107 us (66%)
  Pallas kernels  21.1 us (13%)
  starting transfers between devices  19.7 us (12%)
  waiting for transfers between devices  10.4 us (6%)
    all_to_all x6, blocking collectives, spread(): return lax.all_to_all(operand, axes, 0, 0, tiled=True)  73.2 us
    all_gather x1, blocking collectives, local(): raw = lax.all_gather(packed, ('zh', 'zl'))  34.2 us
    ppermute x1, starting transfers between devices, local(): a_other = lax.ppermute(a_half, 'c', [(0, 1), (1, 0)])  11 us
    all_to_all x2, waiting for transfers between devices, spread(): return lax.all_to_all(operand, axes, 0, 0, tiled=True)  10.4 us
    all_to_all x2, starting transfers between devices, spread(): return lax.all_to_all(operand, axes, 0, 0, tiled=True)  8.69 us
    pallas_call x1, Pallas kernels, stage_cost(): return call(cost_body, outs, [VMEM] * 4, scratch, (VMEM, HBM, VMEM))(*args)  4.67 us
  transfers between devices with their start and end apart: 3, of which 2 were waited for; matrix products, arithmetic and copies ran while one was open for 1% of the time, Pallas kernels for 1%

profile of v7, /device:TPU:1, one launch (start us, length us, event | category | flops | bytes accessed | tf_op | source)
XLA Modules:
  0.0 161.4 jit_solution(4614659378121887916)
XLA Ops:
  0.6 1.5 shard_map.83
  2.2 34.2 %all-gather = bf16[3072,128]{1,0:T(8,128)(2,1)S(1)} all-gather(bf16[192,128]{1,0:T(8,128)(2,1)} %shard_map.83), channel_id=2, replica_groups=mesh['y'=4,'x'=4,'c'=2,'zh'=4,'zl'=4] {'zh','zl'}, dimensions={0}, use_global_device_ids=true | all-gather | bytes 835584 | tf_op jit(solution)/shard_map/all_gather | solution.py:450
  36.3 0.1 stack.35.info
  36.4 1.0 shard_map.84
  37.5 16.6 %all_to_all.40.refs_0_ = bf16[4,192,1024]{2,1,0:T(8,128)(2,1)S(1)} all-to-all(bf16[4,192,1024]{2,1,0:T(8,128)(2,1)S(1)} %shard_map.84), channel_id=1, replica_groups=mesh['y'=4,'x'=4,'c'=2,'zh'=4,'zl'=4] {'y'}, dimensions={0} | all-to-all | bytes 3145728 | tf_op jit(solution)/shard_map/all_to_all | solution.py:442
  54.0 11.0 %collective-permute-start = (bf16[4,192,1024]{2,1,0:T(8,128)(2,1)S(1)}, bf16[4,192,1024]{2,1,0:T(8,128)(2,1)S(1)}, u32[]{:S(2)}, u32[]{:S(2)}) collective-permute-start(bf16[4,192,1024]{2,1,0:T(8,128)(2,1)S(1)} %all_to_all.40.refs_0_), channel_id=1, source_target_pairs={{0,16},{16,0},{1,17},{17,1},{2,18},{18,2},{3,19},{19,3},{4,20},{20... | collective-permute-start | bytes 4718600 | tf_op jit(solution)/shard_map/ppermute | solution.py:456
  65.1 1.0 shard_map.85
  66.1 0.0 copy-start
  66.1 0.0 copy-start.1
  66.1 24.5 %all_to_all.41 = bf16[4,192,1024]{2,1,0:T(8,128)(2,1)S(1)} all-to-all(bf16[4,192,1024]{2,1,0:T(8,128)(2,1)S(1)} %shard_map.85), channel_id=1, replica_groups=mesh['y'=4,'x'=4,'c'=2,'zh'=4,'zl'=4] {'x'}, dimensions={0} | all-to-all | bytes 3145728 | tf_op jit(solution)/shard_map/all_to_all | solution.py:442
  90.6 0.0 collective-permute-done
  90.6 0.0 copy-done
  90.6 0.0 copy-done.1
  90.6 1.4 shard_map.86
  92.0 4.7 %shard_map.87 = (f32[768,1024]{1,0:T(8,128)S(1)}, f32[13824,512]{1,0:T(8,128)}, f32[4,8,128]{2,1,0:T(8,128)S(1)}) custom-call(bf16[1536,1024]{1,0:T(8,128)(2,1)S(1)} %get-tuple-element.22.a_ref, f32[16,128]{1,0:T(8,128)S(1)} %get-tuple-element.23.norm_ref, bf16[768,1024]{1,0:T(8,128)(2,1)S(1)} %bitcast.18, f32[16,128]{1,0:T(8,128)S(1)} %get-tuple-element.24.lift_i), custom_call_target="tpu_custom_call" | custom-call | tf_op jit(solution)/shard_map/pallas_call | solution.py:418
  96.7 6.6 %all_to_all.42.got = f32[4,8,128]{2,1,0:T(8,128)S(1)} all-to-all(f32[4,8,128]{2,1,0:T(8,128)S(1)} %get-tuple-element.27), channel_id=1, replica_groups=mesh['y'=4,'x'=4,'c'=2,'zh'=4,'zl'=4] {'x'}, dimensions={0} | all-to-all | bytes 32768 | tf_op jit(solution)/shard_map/all_to_all | solution.py:442
  103.2 2.8 %shard_map.88 = (f32[8,24,128]{2,1,0:T(8,128)S(1)}, f32[6,128]{1,0:T(8,128)S(1)}) custom-call(f32[768,1024]{1,0:T(8,128)S(1)} %get-tuple-element.25.k1_ref, f32[13824,512]{1,0:T(8,128)} %get-tuple-element.26.k2_hbm, f32[4,8,128]{2,1,0:T(8,128)S(1)} %all_to_all.42.got, f32[8,128]{1,0:T(8,128)S(1)} %get-tuple-element.28.lift_j), custom_call_target="tpu_custom_call" | custom-call | tf_op jit(solution)/shard_map/pallas_call | solution.py:423
  106.0 9.6 %all_to_all.43.got = f32[8,24,128]{2,1,0:T(8,128)S(1)} all-to-all(f32[8,24,128]{2,1,0:T(8,128)S(1)} %get-tuple-element.29), channel_id=1, replica_groups=mesh['y'=4,'x'=4,'c'=2,'zh'=4,'zl'=4] {'y','c'}, dimensions={0} | all-to-all | bytes 196608 | tf_op jit(solution)/shard_map/all_to_all | solution.py:442
  115.6 2.3 %shard_map.89 = (f32[4,16,128]{2,1,0:T(8,128)S(1)}, f32[12,128]{1,0:T(8,128)S(1)}) custom-call(f32[768,1024]{1,0:T(8,128)S(1)} %get-tuple-element.25.k1_ref, f32[13824,512]{1,0:T(8,128)} %get-tuple-element.26.k2_hbm, f32[8,24,128]{2,1,0:T(8,128)S(1)} %all_to_all.43.got, f32[16,128]{1,0:T(8,128)S(1)} %get-tuple-element.24.lift_i), custom_call_target="tpu_custom_call" | custom-call | tf_op jit(solution)/shard_map/pallas_call | solution.py:428
  117.9 6.7 %all_to_all.44.got = f32[4,16,128]{2,1,0:T(8,128)S(1)} all-to-all(f32[4,16,128]{2,1,0:T(8,128)S(1)} %get-tuple-element.30), channel_id=1, replica_groups=mesh['y'=4,'x'=4,'c'=2,'zh'=4,'zl'=4] {'x'}, dimensions={0} | all-to-all | bytes 65536 | tf_op jit(solution)/shard_map/all_to_all | solution.py:442
  124.6 2.8 %shard_map.90 = (f32[8,24,128]{2,1,0:T(8,128)S(1)}, f32[6,128]{1,0:T(8,128)S(1)}) custom-call(f32[768,1024]{1,0:T(8,128)S(1)} %get-tuple-element.25.k1_ref, f32[13824,512]{1,0:T(8,128)} %get-tuple-element.26.k2_hbm, f32[4,16,128]{2,1,0:T(8,128)S(1)} %all_to_all.44.got, f32[8,128]{1,0:T(8,128)S(1)} %get-tuple-element.28.lift_j, f32[6,128]{1,0:T(8,128)S(1)} %get-tuple-element.31.g1), custom_call_target="tpu_custom_call" | custom-call | tf_op jit(solution)/shard_map/pallas_call | solution.py:433
  127.4 9.3 %all_to_all.45.got = f32[8,24,128]{2,1,0:T(8,128)S(1)} all-to-all(f32[8,24,128]{2,1,0:T(8,128)S(1)} %get-tuple-element.32), channel_id=1, replica_groups=mesh['y'=4,'x'=4,'c'=2,'zh'=4,'zl'=4] {'y','c'}, dimensions={0} | all-to-all | bytes 196608 | tf_op jit(solution)/shard_map/all_to_all | solution.py:442
  136.7 2.9 %shard_map.91 = f32[16,8,128]{2,1,0:T(8,128)} custom-call(s32[6]{0:T(128)S(1)} %stack.35.info, f32[768,1024]{1,0:T(8,128)S(1)} %get-tuple-element.25.k1_ref, f32[13824,512]{1,0:T(8,128)} %get-tuple-element.26.k2_hbm, f32[8,24,128]{2,1,0:T(8,128)S(1)} %all_to_all.45.got, f32[16,128]{1,0:T(8,128)S(1)} %get-tuple-element.24.lift_i, ...), custom_call_target="tpu_custom_call" | custom-call | tf_op jit(solution)/shard_map/pallas_call | solution.py:438
  139.6 3.5 %all-to-all-start.6 = ((f32[16,8,128]{2,1,0:T(8,128)}), f32[16,8,128]{2,1,0:T(8,128)S(1)}, u32[]{:S(2)}, u32[]{:S(2)}) async-start(f32[16,8,128]{2,1,0:T(8,128)} %shard_map.91), calls=%async_computation.6 | async-start | bytes 131072 | tf_op jit(solution)/shard_map/all_to_all | solution.py:442
  143.1 6.9 %all-to-all-done.6.got = f32[16,8,128]{2,1,0:T(8,128)S(1)} async-done(((f32[16,8,128]{2,1,0:T(8,128)}), f32[16,8,128]{2,1,0:T(8,128)S(1)}, u32[]{:S(2)}, u32[]{:S(2)}) %all-to-all-start.6) | async-done | bytes 65568 | tf_op jit(solution)/shard_map/all_to_all | solution.py:442
  150.1 0.8 shard_map.92
  150.8 5.2 %all-to-all-start.7 = ((f32[8,8,128]{2,1,0:T(8,128)}), f32[8,8,128]{2,1,0:T(8,128)S(1)}, u32[]{:S(2)}, u32[]{:S(2)}) async-start(f32[8,8,128]{2,1,0:T(8,128)} %get-tuple-element.38), calls=%async_computation.7 | async-start | bytes 65536 | tf_op jit(solution)/shard_map/all_to_all | solution.py:442
  156.0 0.6 fusion
  156.7 0.6 dynamic_slice.12
  157.3 3.5 %all-to-all-done.7 = f32[8,8,128]{2,1,0:T(8,128)S(1)} async-done(((f32[8,8,128]{2,1,0:T(8,128)}), f32[8,8,128]{2,1,0:T(8,128)S(1)}, u32[]{:S(2)}, u32[]{:S(2)}) %all-to-all-start.7) | async-done | bytes 32800 | tf_op jit(solution)/shard_map/all_to_all | solution.py:442
  160.8 0.6 slice_reduce_fusion
  (2 shorter events, 0.0 us)
Async XLA Ops:
  54.0 36.6 %collective-permute-start = (bf16[4,192,1024]{2,1,0:T(8,128)(2,1)S(1)}, bf16[4,192,1024]{2,1,0:T(8,128)(2,1)S(1)}, u32[]{:S(2)}, u32[]{:S(2)}) collective-permute-start(bf16[4,192,1024]{2,1,0:T(8,128)(2,1)S(1)} %all_to_all.40.refs_0_), channel_id=1, source_target_pairs={{0,16},{16,0},{1,17},{17,1},{2,18},{18,2},{3,19},{19,3},{4,20},{20... | collective-permute-start | bytes 4718600 | tf_op jit(solution)/shard_map/ppermute | solution.py:456
  66.1 24.5 %copy-start = (s32[32]{0:T(128)S(1)}, s32[32]{0:T(128)}, u32[]{:S(2)}) copy-start(s32[32]{0:T(128)} %gen_count.1) | copy-start | bytes 388
  66.1 24.5 %copy-start.1 = (s32[32]{0:T(128)S(1)}, s32[32]{0:T(128)}, u32[]{:S(2)}) copy-start(s32[32]{0:T(128)} %ref_count.1) | copy-start | bytes 388
  139.6 10.4 %all-to-all-start.6 = ((f32[16,8,128]{2,1,0:T(8,128)}), f32[16,8,128]{2,1,0:T(8,128)S(1)}, u32[]{:S(2)}, u32[]{:S(2)}) async-start(f32[16,8,128]{2,1,0:T(8,128)} %shard_map.91), calls=%async_computation.6 | async-start | bytes 131072 | tf_op jit(solution)/shard_map/all_to_all | solution.py:442
  150.8 9.9 %all-to-all-start.7 = ((f32[8,8,128]{2,1,0:T(8,128)}), f32[8,8,128]{2,1,0:T(8,128)S(1)}, u32[]{:S(2)}, u32[]{:S(2)}) async-start(f32[8,8,128]{2,1,0:T(8,128)} %get-tuple-element.38), calls=%async_computation.7 | async-start | bytes 65536 | tf_op jit(solution)/shard_map/all_to_all | solution.py:442

commit v8 on v7

--- a/solution.py
+++ b/solution.py
@@ -193,7 +193,7 @@
         even, odd = raw[2 * k], raw[2 * k + 1]
         gen = jnp.concatenate([even[:, :64], odd[:, :64]], axis=1)
         ref = jnp.concatenate([even[:, 64:], odd[:, 64:]], axis=1)
-        part = jnp.where(info[which] == 1, gen, ref)
+        part = jnp.where(info[6 + which] == 1, gen, ref)
         for n in range(4):
             out[n, :, cols] = part
 
@@ -204,15 +204,19 @@
     return functools.reduce(jnp.add, [values[:, k * 128 : (k + 1) * 128] for k in range(D // 128)])
 
 
-def join_body(info, gen_count, ref_count, own, other, cols, a_out, norm_out, lift_i, lift_j, weights):
-    del cols
+def join_body(
+    info, gen_count, ref_count, one, two, from_0, from_1, a_out, b_out, norm_out, lift_i, lift_j, weights
+):
     c, x, y = info[2], info[4], info[5]
     first = c == 0
+    for s in range(6):
+        part = slice(s * 128, (s + 1) * 128)
+        b_out[part, :] = jnp.where(first, two[part, :], one[part, :])
     for half in range(2):
         for s in range(6):
             part = slice(s * 128, (s + 1) * 128)
-            near, far = (own, other) if half == 0 else (other, own)
-            rows = jnp.where(first, near[part, :], far[part, :])
+            on_0, on_1 = (one, from_0) if half == 0 else (from_1, two)
+            rows = jnp.where(first, on_0[part, :], on_1[part, :])
             r = half * 6 + s
             a_out[r * 128 : (r + 1) * 128, :] = rows
             turned = jnp.transpose(norm_parts(rows))
@@ -403,8 +407,9 @@
 
 
 def stage_join(*args):
-    outs = (jax.ShapeDtypeStruct((NI, D), BF16), f32(16, 128), f32(16, 128), f32(8, 128), f32(24, 128))
-    return call(join_body, outs, [SMEM, SMEM, SMEM, VMEM, VMEM, HBM])(*args)
+    points = tuple(jax.ShapeDtypeStruct((rows, D), BF16) for rows in (NI, NJ))
+    outs = points + (f32(16, 128), f32(16, 128), f32(8, 128), f32(24, 128))
+    return call(join_body, outs, [SMEM] * 3 + [VMEM] * 4)(*args)
 
 
 def stage_cost(*args):
@@ -438,8 +443,8 @@
     return call(fifth_body, f32(16, 8, 128), [SMEM, VMEM, HBM] + [VMEM] * 4, scratch)(*args)
 
 
-def spread(operand, axes):
-    return lax.all_to_all(operand, axes, 0, 0, tiled=True)
+def spread(operand, axes, groups=None):
+    return lax.all_to_all(operand, axes, 0, 0, tiled=True, axis_index_groups=groups)
 
 
 def local(gen_points, reference_embeddings, gen_count, ref_count):
@@ -450,15 +455,25 @@
     raw = lax.all_gather(packed, ("zh", "zl"))
 
     info = jnp.stack(
-        [a_is_gen.astype(jnp.int32), b_is_gen.astype(jnp.int32), c, c * 6 + (3 * y) // 2, x, y]
+        [
+            a_is_gen.astype(jnp.int32),
+            b_is_gen.astype(jnp.int32),
+            c,
+            c * 6 + (3 * y) // 2,
+            x,
+            y,
+            jnp.where(c == 0, a_is_gen, b_is_gen).astype(jnp.int32),
+            jnp.where(c == 0, b_is_gen, a_is_gen).astype(jnp.int32),
+        ]
     ).astype(jnp.int32)
-    a_half = spread(stage_unpack(0, info, raw), "y")
-    a_other = lax.ppermute(a_half, "c", [(0, 1), (1, 0)])
-    b_all = spread(stage_unpack(1, info, raw, a_half), "x")
-    b_all = b_all.reshape(NJ, D)
-    a_all, norms, lift_i, lift_j, weights = stage_join(
-        info, gen_count, ref_count, a_half.reshape(NJ, D), a_other.reshape(NJ, D), b_all
-    )
+    along_y = [[[(i * 4 + n) * 2 + core for i in range(4)] for n in range(4)] for core in range(2)]
+    along_x = [[[(n * 4 + i) * 2 + core for i in range(4)] for n in range(4)] for core in range(2)]
+    one = spread(stage_unpack(0, info, raw), ("y", "x", "c"), along_y[0] + along_x[1])
+    from_0 = lax.ppermute(one, "c", [(0, 1)])
+    two = spread(stage_unpack(1, info, raw, one), ("y", "x", "c"), along_x[0] + along_y[1])
+    from_1 = lax.ppermute(two, "c", [(1, 0)])
+    blocks = [part.reshape(NJ, D) for part in (one, two, from_0, from_1)]
+    a_all, b_all, norms, lift_i, lift_j, weights = stage_join(info, gen_count, ref_count, *blocks)
     k1, k2, part = stage_cost(a_all, norms, b_all, lift_i)
     part, g1 = stage_second(k1, k2, spread(part, "x"), lift_j)
     part, f2 = stage_third(k1, k2, spread(part, ("y", "c")), lift_i)

time: 162 us -> 160 us (0.988)
  blocking collectives: 107 us -> 82 us
  waiting for transfers between devices: 10.4 us -> 24.5 us
  starting transfers between devices: 19.7 us -> 26.9 us
    all_to_all x6 -> x5, blocking collectives: 73.2 us -> 47.8 us  [spread(): lax.all_to_all(operand, axes, 0, 0, tiled=True, axis_index_groups=groups)]
    all_to_all x2 -> x3, waiting for transfers between devices: 10.4 us -> 21.6 us  [spread(): lax.all_to_all(operand, axes, 0, 0, tiled=True, axis_index_groups=groups)]
    all_to_all x2 -> x3, starting transfers between devices: 8.69 us -> 13 us  [spread(): lax.all_to_all(operand, axes, 0, 0, tiled=True, axis_index_groups=groups)]
    ppermute x1 -> x2, waiting for transfers between devices: 0.01 us -> 2.91 us  [the longest x1 2.91 us: local(): from_1 = lax.ppermute(two, 'c', [(1, 0)])]
    ppermute x1 -> x2, starting transfers between devices: 11 us -> 13.9 us  [the longest x1 12.6 us: local(): from_1 = lax.ppermute(two, 'c', [(1, 0)])]
  transfers between devices with their start and end apart: 3 -> 5, of which waited for: 2 -> 4; matrix products, arithmetic and copies ran while one was open for 1% -> 1% of each run, Pallas kernels for 1% -> 0%
where the time goes in v8:
time: 160 us; the launch traced here: 159 us
  blocking collectives  82 us (51%)
  starting transfers between devices  26.9 us (17%)
  waiting for transfers between devices  24.5 us (15%)
  Pallas kernels  21.9 us (14%)
  local copies, waits for them, and re-layouts  2.55 us (2%)
    all_to_all x5, blocking collectives, spread(): lax.all_to_all(operand, axes, 0, 0, tiled=True, axis_index_groups=groups)  47.8 us
    all_gather x1, blocking collectives, local(): raw = lax.all_gather(packed, ('zh', 'zl'))  34.2 us
    all_to_all x3, waiting for transfers between devices, spread(): lax.all_to_all(operand, axes, 0, 0, tiled=True, axis_index_groups=groups)  21.6 us
    all_to_all x3, starting transfers between devices, spread(): lax.all_to_all(operand, axes, 0, 0, tiled=True, axis_index_groups=groups)  13 us
    ppermute x1, starting transfers between devices, local(): from_1 = lax.ppermute(two, 'c', [(1, 0)])  12.6 us
    pallas_call x1, Pallas kernels, stage_cost(): return call(cost_body, outs, [VMEM] * 4, scratch, (VMEM, HBM, VMEM))(*args)  4.62 us
  transfers between devices with their start and end apart: 5, of which 4 were waited for; matrix products, arithmetic and copies ran while one was open for 1% of the time, Pallas kernels for 0%

profile of v8, /device:TPU:1, one launch (start us, length us, event | category | flops | bytes accessed | tf_op | source)
XLA Modules:
  0.0 159.3 jit_solution(4325642289066794440)
XLA Ops:
  0.7 1.5 shard_map.83
  2.2 34.2 %all-gather = bf16[3072,128]{1,0:T(8,128)(2,1)S(1)} all-gather(bf16[192,128]{1,0:T(8,128)(2,1)} %shard_map.83), channel_id=2, replica_groups=mesh['y'=4,'x'=4,'c'=2,'zh'=4,'zl'=4] {'zh','zl'}, dimensions={0}, use_global_device_ids=true | all-gather | bytes 835584 | tf_op jit(solution)/shard_map/all_gather | solution.py:455
  36.4 0.1 stack.51.info
  36.4 1.0 shard_map.84
  37.5 16.4 %all_to_all.40.refs_0_ = bf16[4,192,1024]{2,1,0:T(8,128)(2,1)S(1)} all-to-all(bf16[4,192,1024]{2,1,0:T(8,128)(2,1)S(1)} %shard_map.84), channel_id=1, replica_groups={{0,128,256,384},{32,160,288,416},{64,192,320,448},{96,224,352,480},{16,..., dimensions={0} | all-to-all | bytes 3145728 | tf_op jit(solution)/shard_map/all_to_all | solution.py:447
  53.8 1.0 shard_map.85
  54.9 1.2 copy-done
  56.0 4.3 %all-to-all-start.1 = ((bf16[4,192,1024]{2,1,0:T(8,128)(2,1)}), bf16[4,192,1024]{2,1,0:T(8,128)(2,1)S(1)}, u32[]{:S(2)}, u32[]{:S(2)}) async-start(bf16[4,192,1024]{2,1,0:T(8,128)(2,1)} %copy-done), calls=%async_computation.1 | async-start | bytes 3145728 | tf_op jit(solution)/shard_map/all_to_all | solution.py:447
  60.3 1.3 collective-permute-start
  61.6 11.3 %all-to-all-done.1 = bf16[4,192,1024]{2,1,0:T(8,128)(2,1)S(1)} async-done(((bf16[4,192,1024]{2,1,0:T(8,128)(2,1)}), bf16[4,192,1024]{2,1,0:T(8,128)(2,1)S(1)}, u32[]{:S(2)}, u32[]{:S(2)}) %all-to-all-start.1) | async-done | bytes 1572896 | tf_op jit(solution)/shard_map/all_to_all | solution.py:447
  72.9 12.6 %collective-permute-start.1 = (bf16[4,192,1024]{2,1,0:T(8,128)(2,1)S(1)}, bf16[4,192,1024]{2,1,0:T(8,128)(2,1)S(1)}, u32[]{:S(2)}, u32[]{:S(2)}) collective-permute-start(bf16[4,192,1024]{2,1,0:T(8,128)(2,1)S(1)} %all-to-all-done.1), channel_id=1, source_target_pairs={{16,0},{17,1},{18,2},{19,3},{20,4},{21,5},{22,6},{23,7},{24,8},{25... | collective-permute-start | bytes 4718600 | tf_op jit(solution)/shard_map/ppermute | solution.py:474
  85.5 0.0 collective-permute-done
  85.5 2.9 %collective-permute-done.1 = bf16[4,192,1024]{2,1,0:T(8,128)(2,1)S(1)} collective-permute-done((bf16[4,192,1024]{2,1,0:T(8,128)(2,1)S(1)}, bf16[4,192,1024]{2,1,0:T(8,128)(2,1)S(1)}, u32[]{:S(2)}, u32[]{:S(2)}) %collective-permute-start.1) | collective-permute-done | bytes 1572896 | tf_op jit(solution)/shard_map/ppermute | solution.py:474
  88.4 0.0 copy-done.1
  88.4 2.3 %shard_map.86 = (bf16[1536,1024]{1,0:T(8,128)(2,1)S(1)}, bf16[768,1024]{1,0:T(8,128)(2,1)S(1)}, f32[16,128]{1,0:T(8,128)S(1)}, f32[16,128]{1,0:T(8,128)S(1)}, f3...) custom-call(s32[8]{0:T(128)S(1)} %stack.51.info, s32[32]{0:T(128)S(1)} %copy-done.1, s32[32]{0:T(128)S(1)} %copy-done.2, ...), custom_call_target="tpu_custom_call" | custom-call | tf_op jit(solution)/shard_map/pallas_call | solution.py:412
  90.8 4.6 %shard_map.87 = (f32[768,1024]{1,0:T(8,128)S(1)}, f32[13824,512]{1,0:T(8,128)}, f32[4,8,128]{2,1,0:T(8,128)S(1)}) custom-call(bf16[1536,1024]{1,0:T(8,128)(2,1)S(1)} %get-tuple-element.23.a_ref, f32[16,128]{1,0:T(8,128)S(1)} %get-tuple-element.24.norm_ref, bf16[768,1024]{1,0:T(8,128)(2,1)S(1)} %get-tuple-element.25.b_ref, f32[16,128]{1,0:T(8,128)S(1)} %get-tuple-element.26.lift_i), custom_call_target="tpu_custom_call" | custom-call | tf_op jit(solution)/shard_map/pallas_call | solution.py:423
  95.4 6.6 %all_to_all.41.got = f32[4,8,128]{2,1,0:T(8,128)S(1)} all-to-all(f32[4,8,128]{2,1,0:T(8,128)S(1)} %get-tuple-element.29), channel_id=1, replica_groups=mesh['y'=4,'x'=4,'c'=2,'zh'=4,'zl'=4] {'x'}, dimensions={0} | all-to-all | bytes 32768 | tf_op jit(solution)/shard_map/all_to_all | solution.py:447
  102.0 2.7 %shard_map.88 = (f32[8,24,128]{2,1,0:T(8,128)S(1)}, f32[6,128]{1,0:T(8,128)S(1)}) custom-call(f32[768,1024]{1,0:T(8,128)S(1)} %get-tuple-element.27.k1_ref, f32[13824,512]{1,0:T(8,128)} %get-tuple-element.28.k2_hbm, f32[4,8,128]{2,1,0:T(8,128)S(1)} %all_to_all.41.got, f32[8,128]{1,0:T(8,128)S(1)} %get-tuple-element.30.lift_j), custom_call_target="tpu_custom_call" | custom-call | tf_op jit(solution)/shard_map/pallas_call | solution.py:428
  104.7 8.9 %all_to_all.42.got = f32[8,24,128]{2,1,0:T(8,128)S(1)} all-to-all(f32[8,24,128]{2,1,0:T(8,128)S(1)} %get-tuple-element.31), channel_id=1, replica_groups=mesh['y'=4,'x'=4,'c'=2,'zh'=4,'zl'=4] {'y','c'}, dimensions={0} | all-to-all | bytes 196608 | tf_op jit(solution)/shard_map/all_to_all | solution.py:447
  113.6 2.3 %shard_map.89 = (f32[4,16,128]{2,1,0:T(8,128)S(1)}, f32[12,128]{1,0:T(8,128)S(1)}) custom-call(f32[768,1024]{1,0:T(8,128)S(1)} %get-tuple-element.27.k1_ref, f32[13824,512]{1,0:T(8,128)} %get-tuple-element.28.k2_hbm, f32[8,24,128]{2,1,0:T(8,128)S(1)} %all_to_all.42.got, f32[16,128]{1,0:T(8,128)S(1)} %get-tuple-element.26.lift_i), custom_call_target="tpu_custom_call" | custom-call | tf_op jit(solution)/shard_map/pallas_call | solution.py:433
  115.9 6.7 %all_to_all.43.got = f32[4,16,128]{2,1,0:T(8,128)S(1)} all-to-all(f32[4,16,128]{2,1,0:T(8,128)S(1)} %get-tuple-element.32), channel_id=1, replica_groups=mesh['y'=4,'x'=4,'c'=2,'zh'=4,'zl'=4] {'x'}, dimensions={0} | all-to-all | bytes 65536 | tf_op jit(solution)/shard_map/all_to_all | solution.py:447
  122.6 2.7 %shard_map.90 = (f32[8,24,128]{2,1,0:T(8,128)S(1)}, f32[6,128]{1,0:T(8,128)S(1)}) custom-call(f32[768,1024]{1,0:T(8,128)S(1)} %get-tuple-element.27.k1_ref, f32[13824,512]{1,0:T(8,128)} %get-tuple-element.28.k2_hbm, f32[4,16,128]{2,1,0:T(8,128)S(1)} %all_to_all.43.got, f32[8,128]{1,0:T(8,128)S(1)} %get-tuple-element.30.lift_j, f32[6,128]{1,0:T(8,128)S(1)} %get-tuple-element.33.g1), custom_call_target="tpu_custom_call" | custom-call | tf_op jit(solution)/shard_map/pallas_call | solution.py:438
  125.3 9.3 %all_to_all.44.got = f32[8,24,128]{2,1,0:T(8,128)S(1)} all-to-all(f32[8,24,128]{2,1,0:T(8,128)S(1)} %get-tuple-element.34), channel_id=1, replica_groups=mesh['y'=4,'x'=4,'c'=2,'zh'=4,'zl'=4] {'y','c'}, dimensions={0} | all-to-all | bytes 196608 | tf_op jit(solution)/shard_map/all_to_all | solution.py:447
  134.6 2.9 %shard_map.91 = f32[16,8,128]{2,1,0:T(8,128)} custom-call(s32[8]{0:T(128)S(1)} %stack.51.info, f32[768,1024]{1,0:T(8,128)S(1)} %get-tuple-element.27.k1_ref, f32[13824,512]{1,0:T(8,128)} %get-tuple-element.28.k2_hbm, f32[8,24,128]{2,1,0:T(8,128)S(1)} %all_to_all.44.got, f32[16,128]{1,0:T(8,128)S(1)} %get-tuple-element.26.lift_i, ...), custom_call_target="tpu_custom_call" | custom-call | tf_op jit(solution)/shard_map/pallas_call | solution.py:443
  137.6 3.5 %all-to-all-start.6 = ((f32[16,8,128]{2,1,0:T(8,128)}), f32[16,8,128]{2,1,0:T(8,128)S(1)}, u32[]{:S(2)}, u32[]{:S(2)}) async-start(f32[16,8,128]{2,1,0:T(8,128)} %shard_map.91), calls=%async_computation.6 | async-start | bytes 131072 | tf_op jit(solution)/shard_map/all_to_all | solution.py:447
  141.1 6.9 %all-to-all-done.6.got = f32[16,8,128]{2,1,0:T(8,128)S(1)} async-done(((f32[16,8,128]{2,1,0:T(8,128)}), f32[16,8,128]{2,1,0:T(8,128)S(1)}, u32[]{:S(2)}, u32[]{:S(2)}) %all-to-all-start.6) | async-done | bytes 65568 | tf_op jit(solution)/shard_map/all_to_all | solution.py:447
  148.0 0.8 shard_map.92
  148.8 5.2 %all-to-all-start.7 = ((f32[8,8,128]{2,1,0:T(8,128)}), f32[8,8,128]{2,1,0:T(8,128)S(1)}, u32[]{:S(2)}, u32[]{:S(2)}) async-start(f32[8,8,128]{2,1,0:T(8,128)} %get-tuple-element.40), calls=%async_computation.7 | async-start | bytes 65536 | tf_op jit(solution)/shard_map/all_to_all | solution.py:447
  154.0 0.6 fusion
  154.6 0.6 dynamic_slice.12
  155.3 3.5 %all-to-all-done.7 = f32[8,8,128]{2,1,0:T(8,128)S(1)} async-done(((f32[8,8,128]{2,1,0:T(8,128)}), f32[8,8,128]{2,1,0:T(8,128)S(1)}, u32[]{:S(2)}, u32[]{:S(2)}) %all-to-all-start.7) | async-done | bytes 32800 | tf_op jit(solution)/shard_map/all_to_all | solution.py:447
  158.7 0.6 slice_reduce_fusion
  (6 shorter events, 0.0 us)
Async XLA Ops:
  54.9 1.2 copy-start
  56.0 32.4 %copy-start.1 = (s32[32]{0:T(128)S(1)}, s32[32]{0:T(128)}, u32[]{:S(2)}) copy-start(s32[32]{0:T(128)} %gen_count.1) | copy-start | bytes 388
  56.0 32.4 %copy-start.2 = (s32[32]{0:T(128)S(1)}, s32[32]{0:T(128)}, u32[]{:S(2)}) copy-start(s32[32]{0:T(128)} %ref_count.1) | copy-start | bytes 388
  56.0 16.9 %all-to-all-start.1 = ((bf16[4,192,1024]{2,1,0:T(8,128)(2,1)}), bf16[4,192,1024]{2,1,0:T(8,128)(2,1)S(1)}, u32[]{:S(2)}, u32[]{:S(2)}) async-start(bf16[4,192,1024]{2,1,0:T(8,128)(2,1)} %copy-done), calls=%async_computation.1 | async-start | bytes 3145728 | tf_op jit(solution)/shard_map/all_to_all | solution.py:447
  60.3 25.2 %collective-permute-start = (bf16[4,192,1024]{2,1,0:T(8,128)(2,1)S(1)}, bf16[4,192,1024]{2,1,0:T(8,128)(2,1)}, u32[]{:S(2)}, u32[]{:S(2)}) collective-permute-start(bf16[4,192,1024]{2,1,0:T(8,128)(2,1)S(1)} %all_to_all.40.refs_0_), channel_id=1, source_target_pairs={{0,16},{1,17},{2,18},{3,19},{4,20},{5,21},{6,22},{7,23},{8,24},{9,... | collective-permute-start | bytes 4718600 | tf_op jit(solution)/shard_map/ppermute | solution.py:472
  72.9 15.5 %collective-permute-start.1 = (bf16[4,192,1024]{2,1,0:T(8,128)(2,1)S(1)}, bf16[4,192,1024]{2,1,0:T(8,128)(2,1)S(1)}, u32[]{:S(2)}, u32[]{:S(2)}) collective-permute-start(bf16[4,192,1024]{2,1,0:T(8,128)(2,1)S(1)} %all-to-all-done.1), channel_id=1, source_target_pairs={{16,0},{17,1},{18,2},{19,3},{20,4},{21,5},{22,6},{23,7},{24,8},{25... | collective-permute-start | bytes 4718600 | tf_op jit(solution)/shard_map/ppermute | solution.py:474
  137.6 10.4 %all-to-all-start.6 = ((f32[16,8,128]{2,1,0:T(8,128)}), f32[16,8,128]{2,1,0:T(8,128)S(1)}, u32[]{:S(2)}, u32[]{:S(2)}) async-start(f32[16,8,128]{2,1,0:T(8,128)} %shard_map.91), calls=%async_computation.6 | async-start | bytes 131072 | tf_op jit(solution)/shard_map/all_to_all | solution.py:447
  148.8 9.9 %all-to-all-start.7 = ((f32[8,8,128]{2,1,0:T(8,128)}), f32[8,8,128]{2,1,0:T(8,128)S(1)}, u32[]{:S(2)}, u32[]{:S(2)}) async-start(f32[8,8,128]{2,1,0:T(8,128)} %get-tuple-element.40), calls=%async_computation.7 | async-start | bytes 65536 | tf_op jit(solution)/shard_map/all_to_all | solution.py:447

commit v9 on v8

--- a/solution.py
+++ b/solution.py
@@ -17,10 +17,10 @@
 NI = 8 * BLOCK
 NJ = 4 * BLOCK
 RI = NI // 128
+RH = RI // 2
 RJ = NJ // 128
 NEAR = 8
-N1 = NEAR * 128
-N2 = NI - N1
+N2 = NI - NEAR * 128
 ROOM = 18 * NJ
 
 VMEM = pl.BlockSpec(memory_space=pltpu.VMEM)
@@ -89,12 +89,22 @@
             mass_ref[v, rows, :] = tree(jnp.add, masses)
 
 
-def near_tiles(k1_ref):
-    return lambda rows: [(r, k1_ref[rows, r * 128 : (r + 1) * 128]) for r in range(NEAR)]
+def near_tile(k1a_ref, k1b_ref, rows, r):
+    if r < RH:
+        return k1a_ref[rows, r * 128 : (r + 1) * 128]
+    return k1b_ref[rows, (r - RH) * 128 : (r - RH + 1) * 128]
+
+
+def near_tiles(k1a_ref, k1b_ref):
+    return lambda rows: [(r, near_tile(k1a_ref, k1b_ref, rows, r)) for r in range(NEAR)]
 
 
 def far_tiles(k2_ref):
     return lambda rows: [(r, k2_ref[rows, (r - NEAR) * 128 : (r - NEAR + 1) * 128]) for r in range(NEAR, RI)]
+
+
+def turned(swap, value):
+    return jnp.where(swap, jnp.concatenate([value[RH:RI, :], value[0:RH, :]], axis=0), value)
 
 
 def lanes_result(count, high_ref, mass_ref):
@@ -113,11 +123,11 @@
     return results
 
 
-def reduce_lanes(k1_ref, k2_hbm, k2_ref, sems, heads, high_ref, mass_ref):
+def reduce_lanes(k1a_ref, k1b_ref, k2_hbm, k2_ref, sems, heads, high_ref, mass_ref):
     count = len(heads)
 
     def near(b, carry):
-        lanes_block(near_tiles(k1_ref), count, heads, high_ref, mass_ref, pl.multiple_of(b * 128, 128))
+        lanes_block(near_tiles(k1a_ref, k1b_ref), count, heads, high_ref, mass_ref, pl.multiple_of(b * 128, 128))
         return carry
 
     def far(b, carry):
@@ -130,7 +140,7 @@
     return lanes_result(count, high_ref, mass_ref)
 
 
-def reduce_rows(k1_ref, k2_hbm, k2_ref, sems, heads, head_ref, wide_ref, high_ref, mass_ref):
+def reduce_rows(k1a_ref, k1b_ref, k2_hbm, k2_ref, sems, heads, head_ref, wide_ref, high_ref, mass_ref):
     count = len(heads)
     for v in range(count):
         head_ref[v, 0:RJ, :] = heads[v]
@@ -151,7 +161,7 @@
             wides.append(jnp.transpose(jnp.broadcast_to(head_ref[v, pl.ds(b, 1), :], (128, 128))))
             wide_ref[v, pl.ds(pl.multiple_of(b * 128, 128), 128), :] = wides[v]
         for r in range(NEAR):
-            block(b, wides, lambda rows: k1_ref[rows, r * 128 : (r + 1) * 128], r)
+            block(b, wides, lambda rows: near_tile(k1a_ref, k1b_ref, rows, r), r)
         return carry
 
     def far(b, carry):
@@ -204,24 +214,12 @@
     return functools.reduce(jnp.add, [values[:, k * 128 : (k + 1) * 128] for k in range(D // 128)])
 
 
-def join_body(
-    info, gen_count, ref_count, one, two, from_0, from_1, a_out, b_out, norm_out, lift_i, lift_j, weights
-):
+def join_body(info, gen_count, ref_count, one, two, a_out, b_out, lift_i, lift_j, weights):
     c, x, y = info[2], info[4], info[5]
-    first = c == 0
     for s in range(6):
         part = slice(s * 128, (s + 1) * 128)
-        b_out[part, :] = jnp.where(first, two[part, :], one[part, :])
-    for half in range(2):
-        for s in range(6):
-            part = slice(s * 128, (s + 1) * 128)
-            on_0, on_1 = (one, from_0) if half == 0 else (from_1, two)
-            rows = jnp.where(first, on_0[part, :], on_1[part, :])
-            r = half * 6 + s
-            a_out[r * 128 : (r + 1) * 128, :] = rows
-            turned = jnp.transpose(norm_parts(rows))
-            norm_out[r : r + 1, :] = jnp.sum(turned, axis=0, keepdims=True) * (0.5 * LOG2E / EPSILON)
-    norm_out[RI:16, :] = jnp.zeros((16 - RI, 128), jnp.float32)
+        a_out[part, :] = jnp.where(c == 0, one[part, :], two[part, :])
+        b_out[part, :] = jnp.where(c == 0, two[part, :], one[part, :])
 
     def total(counts):
         return jnp.full((8, 128), functools.reduce(jnp.add, [counts[n] for n in range(32)]).astype(jnp.float32))
@@ -240,7 +238,7 @@
     a_is_gen, b_is_gen = info[0] == 1, info[1] == 1
     totals = total(gen_count), total(ref_count)
     gen_log, ref_log = (-jnp.log(value) * LOG2E for value in totals)
-    counts = [number(a_is_gen, ((n % 4) * 4 + x) * 2 + n // 4) for n in range(8)]
+    counts = [number(a_is_gen, ((n % 4) * 4 + x) * 2 + (c if n < 4 else 1 - c)) for n in range(8)]
     ok = valid(flat(16), [n * BLOCK for n in range(8)], counts)
     log_a = jnp.where(a_is_gen, gen_log, ref_log)
     lift_i[...] = jnp.where(ok, jnp.concatenate([log_a, log_a], axis=0), FAR)
@@ -257,41 +255,66 @@
     weights[16:24, :] = jnp.where(ok, 1.0 / totals[1], 0.0)
 
 
-def cost_body(
-    a_ref, norm_ref, b_ref, lift_i, k1_ref, k2_hbm, part_out, k2_ref, high_ref, mass_ref, sq_ref, out_sems
-):
+def a_norms(a_ref):
+    rows = []
+    for s in range(RH):
+        flipped = jnp.transpose(norm_parts(a_ref[s * 128 : (s + 1) * 128, :]))
+        rows.append(jnp.sum(flipped, axis=0, keepdims=True) * (0.5 * LOG2E / EPSILON))
+    return rows
+
+
+def cost_tiles(a_ref, b_ref, sq_ref, norms, n):
+    inner = lax.dot_general(
+        b_ref[...],
+        a_ref[n * 256 : (n + 1) * 256, :],
+        (((1,), (1,)), ((), ())),
+        preferred_element_type=jnp.float32,
+    )
     scale = LOG2E / EPSILON
-    heads = [lift_i[0:RI, :]]
+    return [(sq_ref[...] + norms[2 * n + s]) - scale * inner[:, s * 128 : (s + 1) * 128] for s in range(2)]
+
+
+def reduce_pair(head, source, at, high_ref, mass_ref, base, joined):
+    heads = [head[base : base + 2, :]]
+    pair = lambda rows: [(s, source[rows, at + s * 128 : at + (s + 1) * 128]) for s in range(2)]
+    for b in range(RJ):
+        lanes_block(pair, 1, heads, high_ref, mass_ref, b * 128, joined)
+
+
+def cost_own_body(a_ref, b_ref, lift_i, k1a_ref, high_ref, mass_ref, sq_ref):
+    head = lift_i[...]
+    norms = a_norms(a_ref)
     for b in range(RJ):
         part = slice(b * 128, (b + 1) * 128)
-        total = jnp.sum(norm_parts(b_ref[part, :]), axis=1, keepdims=True) * (0.5 * scale)
+        total = jnp.sum(norm_parts(b_ref[part, :]), axis=1, keepdims=True) * (0.5 * LOG2E / EPSILON)
         sq_ref[part, :] = jnp.broadcast_to(total, (128, 128))
+    for n in range(4):
+        if n < 3:
+            for s, tile in enumerate(cost_tiles(a_ref, b_ref, sq_ref, norms, n)):
+                k1a_ref[:, (2 * n + s) * 128 : (2 * n + s + 1) * 128] = tile
+        if n > 0:
+            reduce_pair(head, k1a_ref, (n - 1) * 256, high_ref, mass_ref, 2 * n - 2, n > 1)
+
+
+def cost_other_body(
+    a_ref, b_ref, lift_i, high_in, mass_in, sq_ref, k1b_ref, k2_hbm, part_out, k2_ref, high_ref, mass_ref, out_sems
+):
+    head = lift_i[...]
+    norms = a_norms(a_ref)
+    high_ref[...] = high_in[...]
+    mass_ref[...] = mass_in[...]
     stores = [fetch(k2_ref, k2_hbm, out_sems, b) for b in range(RJ)]
-    order = [4, 5, 0, 1, 2, 3]
-    for step in range(RI // 2 + 1):
-        if step < RI // 2:
+    order = [1, 2, 0]
+    for step in range(4):
+        if step < 3:
             n = order[step]
-            inner = lax.dot_general(
-                b_ref[...],
-                a_ref[n * 256 : (n + 1) * 256, :],
-                (((1,), (1,)), ((), ())),
-                preferred_element_type=jnp.float32,
-            )
-            for s in range(2):
-                r = 2 * n + s
-                tile = (sq_ref[...] + norm_ref[r : r + 1, :]) - scale * inner[:, s * 128 : (s + 1) * 128]
-                if r < NEAR:
-                    k1_ref[:, r * 128 : (r + 1) * 128] = tile
-                else:
-                    k2_ref[:, (r - NEAR) * 128 : (r - NEAR + 1) * 128] = tile
+            target, at = (k1b_ref, 0) if n == 0 else (k2_ref, (n - 1) * 256)
+            for s, tile in enumerate(cost_tiles(a_ref, b_ref, sq_ref, norms, n)):
+                target[:, at + s * 128 : at + (s + 1) * 128] = tile
         if step > 0:
-            done = 2 * order[step - 1]
-            source, at = (k1_ref, done) if done < NEAR else (k2_ref, done - NEAR)
-            pair = lambda rows: [
-                (done + s, source[rows, (at + s) * 128 : (at + s + 1) * 128]) for s in range(2)
-            ]
-            for b in range(RJ):
-                lanes_block(pair, 1, heads, high_ref, mass_ref, b * 128, step > 1)
+            n = order[step - 1]
+            source, at = (k1b_ref, 0) if n == 0 else (k2_ref, (n - 1) * 256)
+            reduce_pair(head, source, at, high_ref, mass_ref, RH + 2 * n, True)
         if step == 1:
             for store in stores:
                 store.start()
@@ -303,34 +326,35 @@
         store.wait()
 
 
-def second_body(k1_ref, k2_hbm, got, lift_j, out, g1_out, k2_ref, sems, head_ref, wide_ref, high_ref, mass_ref):
+def second_body(info, k1a_ref, k1b_ref, k2_hbm, got, lift_j, out, g1_out, k2_ref, sems, head_ref, wide_ref, high_ref, mass_ref):
     start_fetch(k2_hbm, k2_ref, sems)
     g1 = -merge(got, 4)[0:RJ, :]
     g1_out[...] = g1
     lift = lift_j[0:RJ, :]
     heads = [lift, lifted(g1, lift)]
-    results = reduce_rows(k1_ref, k2_hbm, k2_ref, sems, heads, head_ref, wide_ref, high_ref, mass_ref)
+    results = reduce_rows(k1a_ref, k1b_ref, k2_hbm, k2_ref, sems, heads, head_ref, wide_ref, high_ref, mass_ref)
+    sent = [turned(info[2] == 1, value) for value in results]
     for n in range(8):
         for v in range(2):
-            out[n, v * RI : (v + 1) * RI, :] = results[v]
-
-
-def third_body(k1_ref, k2_hbm, got, lift_i, out, f2_out, k2_ref, sems, high_ref, mass_ref):
+            out[n, v * RI : (v + 1) * RI, :] = sent[v]
+
+
+def third_body(info, k1a_ref, k1b_ref, k2_hbm, got, lift_i, out, f2_out, k2_ref, sems, high_ref, mass_ref):
     start_fetch(k2_hbm, k2_ref, sems)
     merged = -merge(got, 8)
-    f1 = merged[0:RI, :]
-    f2 = 0.5 * (f1 + merged[RI : 2 * RI, :])
+    f1 = turned(info[2] == 1, merged[0:RI, :])
+    f2 = 0.5 * (f1 + turned(info[2] == 1, merged[RI : 2 * RI, :]))
     f2_out[...] = f2
     lift = lift_i[0:RI, :]
     heads = [lifted(f1, lift), lifted(f2, lift)]
-    results = reduce_lanes(k1_ref, k2_hbm, k2_ref, sems, heads, high_ref, mass_ref)
+    results = reduce_lanes(k1a_ref, k1b_ref, k2_hbm, k2_ref, sems, heads, high_ref, mass_ref)
     for n in range(4):
         for v in range(2):
             out[n, v * 8 : v * 8 + RJ, :] = results[v]
             out[n, v * 8 + RJ : v * 8 + 8, :] = jnp.zeros((8 - RJ, 128), jnp.float32)
 
 
-def fourth_body(k1_ref, k2_hbm, got, lift_j, g1, out, g3_out, k2_ref, sems, head_ref, wide_ref, high_ref, mass_ref):
+def fourth_body(info, k1a_ref, k1b_ref, k2_hbm, got, lift_j, g1, out, g3_out, k2_ref, sems, head_ref, wide_ref, high_ref, mass_ref):
     start_fetch(k2_hbm, k2_ref, sems)
     merged = -merge(got, 4)
     g2 = 0.5 * (g1[...] + merged[0:RJ, :])
@@ -338,20 +362,21 @@
     g3_out[...] = g3
     lift = lift_j[0:RJ, :]
     heads = [lifted(g2, lift), lifted(g3, lift)]
-    results = reduce_rows(k1_ref, k2_hbm, k2_ref, sems, heads, head_ref, wide_ref, high_ref, mass_ref)
+    results = reduce_rows(k1a_ref, k1b_ref, k2_hbm, k2_ref, sems, heads, head_ref, wide_ref, high_ref, mass_ref)
+    sent = [turned(info[2] == 1, value) for value in results]
     for n in range(8):
         for v in range(2):
-            out[n, v * RI : (v + 1) * RI, :] = results[v]
-
-
-def fifth_body(info, k1_ref, k2_hbm, got, lift_i, f2, g3, out, k2_ref, sems, high_ref, mass_ref, f4_ref):
+            out[n, v * RI : (v + 1) * RI, :] = sent[v]
+
+
+def fifth_body(info, k1a_ref, k1b_ref, k2_hbm, got, lift_i, f2, g3, out, k2_ref, sems, high_ref, mass_ref, f4_ref):
     start_fetch(k2_hbm, k2_ref, sems)
     merged = -merge(got, 8)
-    f3 = 0.5 * (f2[...] + merged[0:RI, :])
-    f4 = 0.5 * (f3 + merged[RI : 2 * RI, :])
+    f3 = 0.5 * (f2[...] + turned(info[2] == 1, merged[0:RI, :]))
+    f4 = 0.5 * (f3 + turned(info[2] == 1, merged[RI : 2 * RI, :]))
     f4_ref[0:RI, :] = f4
     heads = [lifted(f3, lift_i[0:RI, :])]
-    (result,) = reduce_lanes(k1_ref, k2_hbm, k2_ref, sems, heads, high_ref, mass_ref)
+    (result,) = reduce_lanes(k1a_ref, k1b_ref, k2_hbm, k2_ref, sems, heads, high_ref, mass_ref)
     shifted = result - g3[...]
     mine = f4_ref[pl.ds(info[3], 2), :]
     for n in range(16):
@@ -407,40 +432,43 @@
 
 
 def stage_join(*args):
-    points = tuple(jax.ShapeDtypeStruct((rows, D), BF16) for rows in (NI, NJ))
-    outs = points + (f32(16, 128), f32(16, 128), f32(8, 128), f32(24, 128))
-    return call(join_body, outs, [SMEM] * 3 + [VMEM] * 4)(*args)
-
-
-def stage_cost(*args):
-    scratch = [
-        pltpu.VMEM((NJ, N2), F32),
-        *lane_scratch(1),
-        pltpu.VMEM((NJ, 128), F32),
-        pltpu.SemaphoreType.DMA((RJ,)),
-    ]
-    outs = (f32(NJ, N1), f32(ROOM, N2), f32(4, 8, 128))
-    return call(cost_body, outs, [VMEM] * 4, scratch, (VMEM, HBM, VMEM))(*args)
+    points = (jax.ShapeDtypeStruct((NJ, D), BF16),) * 2
+    outs = points + (f32(16, 128), f32(8, 128), f32(24, 128))
+    return call(join_body, outs, [SMEM] * 3 + [VMEM] * 2)(*args)
+
+
+def stage_cost_own(*args):
+    outs = (f32(NJ, NI // 2), f32(1, NJ, 128), f32(1, NJ, 128), f32(NJ, 128))
+    return call(cost_own_body, outs, [VMEM] * 3)(*args)
+
+
+def stage_cost_other(*args):
+    scratch = [pltpu.VMEM((NJ, N2), F32), *lane_scratch(1), pltpu.SemaphoreType.DMA((RJ,))]
+    outs = (f32(NJ, NI // 2 - N2), f32(ROOM, N2), f32(4, 8, 128))
+    return call(cost_other_body, outs, [VMEM] * 6, scratch, (VMEM, HBM, VMEM))(*args)
+
+
+K_SPECS = [SMEM, VMEM, VMEM, HBM]
 
 
 def stage_second(*args):
     outs = (f32(8, 2 * RI, 128), f32(RJ, 128))
-    return call(second_body, outs, [VMEM, HBM, VMEM, VMEM], STREAM + row_scratch(2))(*args)
+    return call(second_body, outs, K_SPECS + [VMEM] * 2, STREAM + row_scratch(2))(*args)
 
 
 def stage_third(*args):
     outs = (f32(4, 16, 128), f32(RI, 128))
-    return call(third_body, outs, [VMEM, HBM, VMEM, VMEM], STREAM + lane_scratch(2))(*args)
+    return call(third_body, outs, K_SPECS + [VMEM] * 2, STREAM + lane_scratch(2))(*args)
 
 
 def stage_fourth(*args):
     outs = (f32(8, 2 * RI, 128), f32(RJ, 128))
-    return call(fourth_body, outs, [VMEM, HBM, VMEM, VMEM, VMEM], STREAM + row_scratch(2))(*args)
+    return call(fourth_body, outs, K_SPECS + [VMEM] * 3, STREAM + row_scratch(2))(*args)
 
 
 def stage_fifth(*args):
     scratch = STREAM + lane_scratch(1) + [pltpu.VMEM((16, 128), F32)]
-    return call(fifth_body, f32(16, 8, 128), [SMEM, VMEM, HBM] + [VMEM] * 4, scratch)(*args)
+    return call(fifth_body, f32(16, 8, 128), K_SPECS + [VMEM] * 4, scratch)(*args)
 
 
 def spread(operand, axes, groups=None):
@@ -459,7 +487,7 @@
             a_is_gen.astype(jnp.int32),
             b_is_gen.astype(jnp.int32),
             c,
-            c * 6 + (3 * y) // 2,
+            (3 * y) // 2,
             x,
             y,
             jnp.where(c == 0, a_is_gen, b_is_gen).astype(jnp.int32),
@@ -469,16 +497,18 @@
     along_y = [[[(i * 4 + n) * 2 + core for i in range(4)] for n in range(4)] for core in range(2)]
     along_x = [[[(n * 4 + i) * 2 + core for i in range(4)] for n in range(4)] for core in range(2)]
     one = spread(stage_unpack(0, info, raw), ("y", "x", "c"), along_y[0] + along_x[1])
-    from_0 = lax.ppermute(one, "c", [(0, 1)])
     two = spread(stage_unpack(1, info, raw, one), ("y", "x", "c"), along_x[0] + along_y[1])
-    from_1 = lax.ppermute(two, "c", [(1, 0)])
-    blocks = [part.reshape(NJ, D) for part in (one, two, from_0, from_1)]
-    a_all, b_all, norms, lift_i, lift_j, weights = stage_join(info, gen_count, ref_count, *blocks)
-    k1, k2, part = stage_cost(a_all, norms, b_all, lift_i)
-    part, g1 = stage_second(k1, k2, spread(part, "x"), lift_j)
-    part, f2 = stage_third(k1, k2, spread(part, ("y", "c")), lift_i)
-    part, g3 = stage_fourth(k1, k2, spread(part, "x"), lift_j, g1)
-    part = stage_fifth(info, k1, k2, spread(part, ("y", "c")), lift_i, f2, g3)
+    a_own, b_all, lift_i, lift_j, weights = stage_join(
+        info, gen_count, ref_count, one.reshape(NJ, D), two.reshape(NJ, D)
+    )
+    a_other = lax.ppermute(a_own, "c", [(0, 1), (1, 0)])
+    k1a, high, mass, b_norms = stage_cost_own(a_own, b_all, lift_i)
+    k1b, k2, part = stage_cost_other(a_other, b_all, lift_i, high, mass, b_norms)
+    k = (info, k1a, k1b, k2)
+    part, g1 = stage_second(*k, spread(part, "x"), lift_j)
+    part, f2 = stage_third(*k, spread(part, ("y", "c")), lift_i)
+    part, g3 = stage_fourth(*k, spread(part, "x"), lift_j, g1)
+    part = stage_fifth(*k, spread(part, ("y", "c")), lift_i, f2, g3)
     got = spread(part, ("x", "zl"))
     pots, g4, share = call(last_body, (f32(4, 8, 128), f32(8, 128), f32(8, 8, 128)), [VMEM, VMEM])(got, weights)
     divergence = jnp.sum(spread(share, ("y", "c"))[:, 0, 0])

time: 160 us -> 159 us (level)
  blocking collectives: 82 us -> 98.6 us
  waiting for transfers between devices: 24.5 us -> 11.1 us
  starting transfers between devices: 26.9 us -> 22.4 us
    all_to_all x5 -> x6, blocking collectives: 47.8 us -> 64.5 us  [spread(): lax.all_to_all(operand, axes, 0, 0, tiled=True, axis_index_groups=groups)]
    all_to_all x3 -> x2, waiting for transfers between devices: 21.6 us -> 10.4 us  [spread(): lax.all_to_all(operand, axes, 0, 0, tiled=True, axis_index_groups=groups)]
    all_to_all x3 -> x2, starting transfers between devices: 13 us -> 8.7 us  [spread(): lax.all_to_all(operand, axes, 0, 0, tiled=True, axis_index_groups=groups)]
    ppermute x2 -> x1, waiting for transfers between devices: 2.91 us -> 0.77 us  [local(): a_other = lax.ppermute(a_own, 'c', [(0, 1), (1, 0)])]
    pallas_call x6 -> x7, Pallas kernels: 17.7 us -> 18.6 us  [the longest x1 3.34 us: stage_fourth(): call(fourth_body, outs, K_SPECS + [VMEM] * 3, STREAM + row_scratch(2))]
    ppermute x2 -> x1, starting transfers between devices: 13.9 us -> 13.7 us  [local(): a_other = lax.ppermute(a_own, 'c', [(0, 1), (1, 0)])]
  transfers between devices with their start and end apart: 5 -> 3, of which waited for: 4 -> 3; matrix products, arithmetic and copies ran while one was open for 1% -> 1% of each run, Pallas kernels for 0% -> 1%
where the time goes in v9:
time: 159 us; the launch traced here: 158 us
  blocking collectives  98.6 us (62%)
  Pallas kernels  22.9 us (14%)
  starting transfers between devices  22.4 us (14%)
  waiting for transfers between devices  11.1 us (7%)
    all_to_all x6, blocking collectives, spread(): lax.all_to_all(operand, axes, 0, 0, tiled=True, axis_index_groups=groups)  64.5 us
    all_gather x1, blocking collectives, local(): raw = lax.all_gather(packed, ('zh', 'zl'))  34.2 us
    ppermute x1, starting transfers between devices, local(): a_other = lax.ppermute(a_own, 'c', [(0, 1), (1, 0)])  13.7 us
    all_to_all x2, waiting for transfers between devices, spread(): lax.all_to_all(operand, axes, 0, 0, tiled=True, axis_index_groups=groups)  10.4 us
    all_to_all x2, starting transfers between devices, spread(): lax.all_to_all(operand, axes, 0, 0, tiled=True, axis_index_groups=groups)  8.7 us
    pallas_call x1, Pallas kernels, stage_fourth(): call(fourth_body, outs, K_SPECS + [VMEM] * 3, STREAM + row_scratch(2))  3.34 us
    pallas_call x1, Pallas kernels, stage_second(): call(second_body, outs, K_SPECS + [VMEM] * 2, STREAM + row_scratch(2))  3.34 us
  transfers between devices with their start and end apart: 3, of which 3 were waited for; matrix products, arithmetic and copies ran while one was open for 1% of the time, Pallas kernels for 1%

profile of v9, /device:TPU:1, one launch (start us, length us, event | category | flops | bytes accessed | tf_op | source)
XLA Modules:
  0.0 158.0 jit_solution(18201292686907073833)
XLA Ops:
  0.7 1.5 shard_map.83
  2.2 34.2 %all-gather = bf16[3072,128]{1,0:T(8,128)(2,1)S(1)} all-gather(bf16[192,128]{1,0:T(8,128)(2,1)} %shard_map.83), channel_id=2, replica_groups=mesh['y'=4,'x'=4,'c'=2,'zh'=4,'zl'=4] {'zh','zl'}, dimensions={0}, use_global_device_ids=true | all-gather | bytes 835584 | tf_op jit(solution)/shard_map/all_gather | solution.py:483
  36.4 0.1 stack.51.info
  36.4 1.0 shard_map.84
  37.5 16.4 %all_to_all.40.refs_0_ = bf16[4,192,1024]{2,1,0:T(8,128)(2,1)S(1)} all-to-all(bf16[4,192,1024]{2,1,0:T(8,128)(2,1)S(1)} %shard_map.84), channel_id=1, replica_groups={{0,128,256,384},{32,160,288,416},{64,192,320,448},{96,224,352,480},{16,..., dimensions={0} | all-to-all | bytes 3145728 | tf_op jit(solution)/shard_map/all_to_all | solution.py:475
  53.8 1.0 shard_map.85
  54.9 0.0 copy-start
  54.9 0.0 copy-start.1
  54.9 16.7 %all_to_all.41 = bf16[4,192,1024]{2,1,0:T(8,128)(2,1)S(1)} all-to-all(bf16[4,192,1024]{2,1,0:T(8,128)(2,1)S(1)} %shard_map.85), channel_id=1, replica_groups={{0,32,64,96},{128,160,192,224},{256,288,320,352},{384,416,448,480},{16,..., dimensions={0} | all-to-all | bytes 3145728 | tf_op jit(solution)/shard_map/all_to_all | solution.py:475
  71.5 0.0 copy-done
  71.5 0.0 copy-done.1
  71.6 0.8 shard_map.86
  72.4 13.7 %collective-permute-start = (bf16[768,1024]{1,0:T(8,128)(2,1)S(1)}, bf16[768,1024]{1,0:T(8,128)(2,1)S(1)}, u32[]{:S(2)}, u32[]{:S(2)}) collective-permute-start(bf16[768,1024]{1,0:T(8,128)(2,1)S(1)} %get-tuple-element.26.a_ref), channel_id=1, source_target_pairs={{0,16},{16,0},{1,17},{17,1},{2,18},{18,2},{3,19},{19,3},{4,20},{20... | collective-permute-start | bytes 4718600 | tf_op jit(solution)/shard_map/ppermute | solution.py:504
  86.1 2.2 %shard_map.87 = (f32[768,768]{1,0:T(8,128)S(1)}, f32[1,768,128]{2,1,0:T(8,128)S(1)}, f32[1,768,128]{2,1,0:T(8,128)S(1)}, f32[768,128]{1,0:T(8,128)S(1)}) custom-call(bf16[768,1024]{1,0:T(8,128)(2,1)S(1)} %get-tuple-element.26.a_ref, bf16[768,1024]{1,0:T(8,128)(2,1)S(1)} %get-tuple-element.27.b_ref, f32[16,128]{1,0:T(8,128)S(1)} %get-tuple-element.28.lift_i), custom_call_target="tpu_custom_call" | custom-call | tf_op jit(solution)/shard_map/pallas_call | solution.py:442
  88.3 0.8 collective-permute-done.a_ref
  89.1 3.1 %shard_map.88 = (f32[768,256]{1,0:T(8,128)S(1)}, f32[13824,512]{1,0:T(8,128)}, f32[4,8,128]{2,1,0:T(8,128)S(1)}) custom-call(bf16[768,1024]{1,0:T(8,128)(2,1)S(1)} %collective-permute-done.a_ref, bf16[768,1024]{1,0:T(8,128)(2,1)S(1)} %get-tuple-element.27.b_ref, f32[16,128]{1,0:T(8,128)S(1)} %get-tuple-element.28.lift_i, ...), custom_call_target="tpu_custom_call" | custom-call | tf_op jit(solution)/shard_map/pallas_call | solution.py:448
  92.3 6.6 %all_to_all.42.got = f32[4,8,128]{2,1,0:T(8,128)S(1)} all-to-all(f32[4,8,128]{2,1,0:T(8,128)S(1)} %get-tuple-element.35), channel_id=1, replica_groups=mesh['y'=4,'x'=4,'c'=2,'zh'=4,'zl'=4] {'x'}, dimensions={0} | all-to-all | bytes 32768 | tf_op jit(solution)/shard_map/all_to_all | solution.py:475
  98.8 3.3 %shard_map.89 = (f32[8,24,128]{2,1,0:T(8,128)S(1)}, f32[6,128]{1,0:T(8,128)S(1)}) custom-call(s32[8]{0:T(128)S(1)} %stack.51.info, f32[768,768]{1,0:T(8,128)S(1)} %get-tuple-element.29.k1a_ref, f32[768,256]{1,0:T(8,128)S(1)} %get-tuple-element.33.k1b_ref, f32[13824,512]{1,0:T(8,128)} %get-tuple-element.34.k2_hbm, f32[4,8,128]{2,1,0:T(8,128)S(1)} %all_to_all.42.got, ...), custom_call_target="tpu_custom_call" | custom-call | tf_op jit(solution)/shard_map/pallas_call | solution.py:456
  102.2 8.9 %all_to_all.43.got = f32[8,24,128]{2,1,0:T(8,128)S(1)} all-to-all(f32[8,24,128]{2,1,0:T(8,128)S(1)} %get-tuple-element.37), channel_id=1, replica_groups=mesh['y'=4,'x'=4,'c'=2,'zh'=4,'zl'=4] {'y','c'}, dimensions={0} | all-to-all | bytes 196608 | tf_op jit(solution)/shard_map/all_to_all | solution.py:475
  111.0 2.9 %shard_map.90 = (f32[4,16,128]{2,1,0:T(8,128)S(1)}, f32[12,128]{1,0:T(8,128)S(1)}) custom-call(s32[8]{0:T(128)S(1)} %stack.51.info, f32[768,768]{1,0:T(8,128)S(1)} %get-tuple-element.29.k1a_ref, f32[768,256]{1,0:T(8,128)S(1)} %get-tuple-element.33.k1b_ref, f32[13824,512]{1,0:T(8,128)} %get-tuple-element.34.k2_hbm, f32[8,24,128]{2,1,0:T(8,128)S(1)} %all_to_all.43.got, ...), custom_call_target="tpu_custom_call" | custom-call | tf_op jit(solution)/shard_map/pallas_call | solution.py:461
  113.9 6.7 %all_to_all.44.got = f32[4,16,128]{2,1,0:T(8,128)S(1)} all-to-all(f32[4,16,128]{2,1,0:T(8,128)S(1)} %get-tuple-element.38), channel_id=1, replica_groups=mesh['y'=4,'x'=4,'c'=2,'zh'=4,'zl'=4] {'x'}, dimensions={0} | all-to-all | bytes 65536 | tf_op jit(solution)/shard_map/all_to_all | solution.py:475
  120.6 3.3 %shard_map.91 = (f32[8,24,128]{2,1,0:T(8,128)S(1)}, f32[6,128]{1,0:T(8,128)S(1)}) custom-call(s32[8]{0:T(128)S(1)} %stack.51.info, f32[768,768]{1,0:T(8,128)S(1)} %get-tuple-element.29.k1a_ref, f32[768,256]{1,0:T(8,128)S(1)} %get-tuple-element.33.k1b_ref, f32[13824,512]{1,0:T(8,128)} %get-tuple-element.34.k2_hbm, f32[4,16,128]{2,1,0:T(8,128)S(1)} %all_to_all.44.got, ...), custom_call_target="tpu_custom_call" | custom-call | tf_op jit(solution)/shard_map/pallas_call | solution.py:466
  123.9 9.3 %all_to_all.45.got = f32[8,24,128]{2,1,0:T(8,128)S(1)} all-to-all(f32[8,24,128]{2,1,0:T(8,128)S(1)} %get-tuple-element.40), channel_id=1, replica_groups=mesh['y'=4,'x'=4,'c'=2,'zh'=4,'zl'=4] {'y','c'}, dimensions={0} | all-to-all | bytes 196608 | tf_op jit(solution)/shard_map/all_to_all | solution.py:475
  133.3 2.9 %shard_map.92 = f32[16,8,128]{2,1,0:T(8,128)} custom-call(s32[8]{0:T(128)S(1)} %stack.51.info, f32[768,768]{1,0:T(8,128)S(1)} %get-tuple-element.29.k1a_ref, f32[768,256]{1,0:T(8,128)S(1)} %get-tuple-element.33.k1b_ref, f32[13824,512]{1,0:T(8,128)} %get-tuple-element.34.k2_hbm, f32[8,24,128]{2,1,0:T(8,128)S(1)} %all_to_all.45.got, ...), custom_call_target="tpu_custom_call" | custom-call | tf_op jit(solution)/shard_map/pallas_call | solution.py:471
  136.2 3.5 %all-to-all-start.6 = ((f32[16,8,128]{2,1,0:T(8,128)}), f32[16,8,128]{2,1,0:T(8,128)S(1)}, u32[]{:S(2)}, u32[]{:S(2)}) async-start(f32[16,8,128]{2,1,0:T(8,128)} %shard_map.92), calls=%async_computation.6 | async-start | bytes 131072 | tf_op jit(solution)/shard_map/all_to_all | solution.py:475
  139.7 6.9 %all-to-all-done.6.got = f32[16,8,128]{2,1,0:T(8,128)S(1)} async-done(((f32[16,8,128]{2,1,0:T(8,128)}), f32[16,8,128]{2,1,0:T(8,128)S(1)}, u32[]{:S(2)}, u32[]{:S(2)}) %all-to-all-start.6) | async-done | bytes 65568 | tf_op jit(solution)/shard_map/all_to_all | solution.py:475
  146.6 0.8 shard_map.93
  147.4 5.2 %all-to-all-start.7 = ((f32[8,8,128]{2,1,0:T(8,128)}), f32[8,8,128]{2,1,0:T(8,128)S(1)}, u32[]{:S(2)}, u32[]{:S(2)}) async-start(f32[8,8,128]{2,1,0:T(8,128)} %get-tuple-element.46), calls=%async_computation.7 | async-start | bytes 65536 | tf_op jit(solution)/shard_map/all_to_all | solution.py:475
  152.6 0.6 fusion
  153.3 0.6 dynamic_slice.12
  153.9 3.5 %all-to-all-done.7 = f32[8,8,128]{2,1,0:T(8,128)S(1)} async-done(((f32[8,8,128]{2,1,0:T(8,128)}), f32[8,8,128]{2,1,0:T(8,128)S(1)}, u32[]{:S(2)}, u32[]{:S(2)}) %all-to-all-start.7) | async-done | bytes 32800 | tf_op jit(solution)/shard_map/all_to_all | solution.py:475
  157.4 0.6 slice_reduce_fusion
  (2 shorter events, 0.0 us)
Async XLA Ops:
  54.9 16.7 %copy-start = (s32[32]{0:T(128)S(1)}, s32[32]{0:T(128)}, u32[]{:S(2)}) copy-start(s32[32]{0:T(128)} %gen_count.1) | copy-start | bytes 388
  54.9 16.7 %copy-start.1 = (s32[32]{0:T(128)S(1)}, s32[32]{0:T(128)}, u32[]{:S(2)}) copy-start(s32[32]{0:T(128)} %ref_count.1) | copy-start | bytes 388
  72.4 16.8 %collective-permute-start = (bf16[768,1024]{1,0:T(8,128)(2,1)S(1)}, bf16[768,1024]{1,0:T(8,128)(2,1)S(1)}, u32[]{:S(2)}, u32[]{:S(2)}) collective-permute-start(bf16[768,1024]{1,0:T(8,128)(2,1)S(1)} %get-tuple-element.26.a_ref), channel_id=1, source_target_pairs={{0,16},{16,0},{1,17},{17,1},{2,18},{18,2},{3,19},{19,3},{4,20},{20... | collective-permute-start | bytes 4718600 | tf_op jit(solution)/shard_map/ppermute | solution.py:504
  136.2 10.4 %all-to-all-start.6 = ((f32[16,8,128]{2,1,0:T(8,128)}), f32[16,8,128]{2,1,0:T(8,128)S(1)}, u32[]{:S(2)}, u32[]{:S(2)}) async-start(f32[16,8,128]{2,1,0:T(8,128)} %shard_map.92), calls=%async_computation.6 | async-start | bytes 131072 | tf_op jit(solution)/shard_map/all_to_all | solution.py:475
  147.4 9.9 %all-to-all-start.7 = ((f32[8,8,128]{2,1,0:T(8,128)}), f32[8,8,128]{2,1,0:T(8,128)S(1)}, u32[]{:S(2)}, u32[]{:S(2)}) async-start(f32[8,8,128]{2,1,0:T(8,128)} %get-tuple-element.46), calls=%async_computation.7 | async-start | bytes 65536 | tf_op jit(solution)/shard_map/all_to_all | solution.py:475

commit v10 on v9

--- a/solution.py
+++ b/solution.py
@@ -103,8 +103,8 @@
     return lambda rows: [(r, k2_ref[rows, (r - NEAR) * 128 : (r - NEAR + 1) * 128]) for r in range(NEAR, RI)]
 
 
-def turned(swap, value):
-    return jnp.where(swap, jnp.concatenate([value[RH:RI, :], value[0:RH, :]], axis=0), value)
+def turned(core, value):
+    return jnp.where(core > 0.5, jnp.concatenate([value[RH:RI, :], value[0:RH, :]], axis=0), value)
 
 
 def lanes_result(count, high_ref, mass_ref):
@@ -203,7 +203,7 @@
         even, odd = raw[2 * k], raw[2 * k + 1]
         gen = jnp.concatenate([even[:, :64], odd[:, :64]], axis=1)
         ref = jnp.concatenate([even[:, 64:], odd[:, 64:]], axis=1)
-        part = jnp.where(info[6 + which] == 1, gen, ref)
+        part = jnp.where(info[5 + which] == 1, gen, ref)
         for n in range(4):
             out[n, :, cols] = part
 
@@ -215,7 +215,7 @@
 
 
 def join_body(info, gen_count, ref_count, one, two, a_out, b_out, lift_i, lift_j, weights):
-    c, x, y = info[2], info[4], info[5]
+    c, x, y = info[2], info[3], info[4]
     for s in range(6):
         part = slice(s * 128, (s + 1) * 128)
         a_out[part, :] = jnp.where(c == 0, one[part, :], two[part, :])
@@ -242,10 +242,14 @@
     ok = valid(flat(16), [n * BLOCK for n in range(8)], counts)
     log_a = jnp.where(a_is_gen, gen_log, ref_log)
     lift_i[...] = jnp.where(ok, jnp.concatenate([log_a, log_a], axis=0), FAR)
+    core = jnp.full((1, 128), c.astype(jnp.float32))
+    lift_i[14:15, :] = core
+    lift_i[15:16, :] = jnp.full((1, 128), y.astype(jnp.float32))
     here = [(y * 4 + n) * 2 + c for n in range(4)]
     starts = [n * BLOCK for n in range(4)]
     ok = valid(flat(8), starts, [number(b_is_gen, t) for t in here])
     lift_j[...] = jnp.where(ok, jnp.where(b_is_gen, gen_log, ref_log), FAR)
+    lift_j[6:7, :] = core
     shift = 64 * lax.rem(y, 2)
     windows = [n * 256 + shift for n in range(4)]
     for n, counts in enumerate((gen_count, ref_count)):
@@ -326,24 +330,26 @@
         store.wait()
 
 
-def second_body(info, k1a_ref, k1b_ref, k2_hbm, got, lift_j, out, g1_out, k2_ref, sems, head_ref, wide_ref, high_ref, mass_ref):
+def second_body(k1a_ref, k1b_ref, k2_hbm, got, lift_j, out, g1_out, k2_ref, sems, head_ref, wide_ref, high_ref, mass_ref):
+    core = lift_j[6:7, :]
     start_fetch(k2_hbm, k2_ref, sems)
     g1 = -merge(got, 4)[0:RJ, :]
     g1_out[...] = g1
     lift = lift_j[0:RJ, :]
     heads = [lift, lifted(g1, lift)]
     results = reduce_rows(k1a_ref, k1b_ref, k2_hbm, k2_ref, sems, heads, head_ref, wide_ref, high_ref, mass_ref)
-    sent = [turned(info[2] == 1, value) for value in results]
+    sent = [turned(core, value) for value in results]
     for n in range(8):
         for v in range(2):
             out[n, v * RI : (v + 1) * RI, :] = sent[v]
 
 
-def third_body(info, k1a_ref, k1b_ref, k2_hbm, got, lift_i, out, f2_out, k2_ref, sems, high_ref, mass_ref):
+def third_body(k1a_ref, k1b_ref, k2_hbm, got, lift_i, out, f2_out, k2_ref, sems, high_ref, mass_ref):
+    core = lift_i[14:15, :]
     start_fetch(k2_hbm, k2_ref, sems)
     merged = -merge(got, 8)
-    f1 = turned(info[2] == 1, merged[0:RI, :])
-    f2 = 0.5 * (f1 + turned(info[2] == 1, merged[RI : 2 * RI, :]))
+    f1 = turned(core, merged[0:RI, :])
+    f2 = 0.5 * (f1 + turned(core, merged[RI : 2 * RI, :]))
     f2_out[...] = f2
     lift = lift_i[0:RI, :]
     heads = [lifted(f1, lift), lifted(f2, lift)]
@@ -354,7 +360,8 @@
             out[n, v * 8 + RJ : v * 8 + 8, :] = jnp.zeros((8 - RJ, 128), jnp.float32)
 
 
-def fourth_body(info, k1a_ref, k1b_ref, k2_hbm, got, lift_j, g1, out, g3_out, k2_ref, sems, head_ref, wide_ref, high_ref, mass_ref):
+def fourth_body(k1a_ref, k1b_ref, k2_hbm, got, lift_j, g1, out, g3_out, k2_ref, sems, head_ref, wide_ref, high_ref, mass_ref):
+    core = lift_j[6:7, :]
     start_fetch(k2_hbm, k2_ref, sems)
     merged = -merge(got, 4)
     g2 = 0.5 * (g1[...] + merged[0:RJ, :])
@@ -363,22 +370,25 @@
     lift = lift_j[0:RJ, :]
     heads = [lifted(g2, lift), lifted(g3, lift)]
     results = reduce_rows(k1a_ref, k1b_ref, k2_hbm, k2_ref, sems, heads, head_ref, wide_ref, high_ref, mass_ref)
-    sent = [turned(info[2] == 1, value) for value in results]
+    sent = [turned(core, value) for value in results]
     for n in range(8):
         for v in range(2):
             out[n, v * RI : (v + 1) * RI, :] = sent[v]
 
 
-def fifth_body(info, k1a_ref, k1b_ref, k2_hbm, got, lift_i, f2, g3, out, k2_ref, sems, high_ref, mass_ref, f4_ref):
+def fifth_body(k1a_ref, k1b_ref, k2_hbm, got, lift_i, f2, g3, out, k2_ref, sems, high_ref, mass_ref):
+    core = lift_i[14:15, :]
     start_fetch(k2_hbm, k2_ref, sems)
     merged = -merge(got, 8)
-    f3 = 0.5 * (f2[...] + turned(info[2] == 1, merged[0:RI, :]))
-    f4 = 0.5 * (f3 + turned(info[2] == 1, merged[RI : 2 * RI, :]))
-    f4_ref[0:RI, :] = f4
+    f3 = 0.5 * (f2[...] + turned(core, merged[0:RI, :]))
+    f4 = 0.5 * (f3 + turned(core, merged[RI : 2 * RI, :]))
     heads = [lifted(f3, lift_i[0:RI, :])]
     (result,) = reduce_lanes(k1a_ref, k1b_ref, k2_hbm, k2_ref, sems, heads, high_ref, mass_ref)
     shifted = result - g3[...]
-    mine = f4_ref[pl.ds(info[3], 2), :]
+    along_y = lift_i[15:16, :]
+    mine = f4[4:6, :]
+    for n, row in ((2, 3), (1, 1), (0, 0)):
+        mine = jnp.where(along_y < n + 0.5, f4[row : row + 2, :], mine)
     for n in range(16):
         out[n, 0:RJ, :] = shifted
         out[n, RJ : RJ + 2, :] = mine
@@ -448,7 +458,7 @@
     return call(cost_other_body, outs, [VMEM] * 6, scratch, (VMEM, HBM, VMEM))(*args)
 
 
-K_SPECS = [SMEM, VMEM, VMEM, HBM]
+K_SPECS = [VMEM, VMEM, HBM]
 
 
 def stage_second(*args):
@@ -467,8 +477,7 @@
 
 
 def stage_fifth(*args):
-    scratch = STREAM + lane_scratch(1) + [pltpu.VMEM((16, 128), F32)]
-    return call(fifth_body, f32(16, 8, 128), K_SPECS + [VMEM] * 4, scratch)(*args)
+    return call(fifth_body, f32(16, 8, 128), K_SPECS + [VMEM] * 4, STREAM + lane_scratch(1))(*args)
 
 
 def spread(operand, axes, groups=None):
@@ -487,7 +496,6 @@
             a_is_gen.astype(jnp.int32),
             b_is_gen.astype(jnp.int32),
             c,
-            (3 * y) // 2,
             x,
             y,
             jnp.where(c == 0, a_is_gen, b_is_gen).astype(jnp.int32),
@@ -504,7 +512,7 @@
     a_other = lax.ppermute(a_own, "c", [(0, 1), (1, 0)])
     k1a, high, mass, b_norms = stage_cost_own(a_own, b_all, lift_i)
     k1b, k2, part = stage_cost_other(a_other, b_all, lift_i, high, mass, b_norms)
-    k = (info, k1a, k1b, k2)
+    k = (k1a, k1b, k2)
     part, g1 = stage_second(*k, spread(part, "x"), lift_j)
     part, f2 = stage_third(*k, spread(part, ("y", "c")), lift_i)
     part, g3 = stage_fourth(*k, spread(part, "x"), lift_j, g1)

time: 159 us -> 156 us (0.981)
  Pallas kernels: 22.9 us -> 20.8 us
where the time goes in v10:
time: 156 us
  blocking collectives  98.6 us (63%)
  starting transfers between devices  22.4 us (14%)
  Pallas kernels  20.8 us (13%)
  waiting for transfers between devices  11.1 us (7%)
    all_to_all x6, blocking collectives, spread(): lax.all_to_all(operand, axes, 0, 0, tiled=True, axis_index_groups=groups)  64.4 us
    all_gather x1, blocking collectives, local(): raw = lax.all_gather(packed, ('zh', 'zl'))  34.2 us
    ppermute x1, starting transfers between devices, local(): a_other = lax.ppermute(a_own, 'c', [(0, 1), (1, 0)])  13.7 us
    all_to_all x2, waiting for transfers between devices, spread(): lax.all_to_all(operand, axes, 0, 0, tiled=True, axis_index_groups=groups)  10.4 us
    all_to_all x2, starting transfers between devices, spread(): lax.all_to_all(operand, axes, 0, 0, tiled=True, axis_index_groups=groups)  8.7 us
    pallas_call x1, Pallas kernels, stage_cost_other(): call(cost_other_body, outs, [VMEM] * 6, scratch, (VMEM, HBM, VMEM))(*args)  3.14 us
  transfers between devices with their start and end apart: 3, of which 3 were waited for; matrix products, arithmetic and copies ran while one was open for 1% of the time, Pallas kernels for 1%

profile of v10, /device:TPU:1, one launch (start us, length us, event | category | flops | bytes accessed | tf_op | source)
XLA Modules:
  0.0 155.8 jit_solution(15123539641692111450)
XLA Ops:
  0.7 1.5 shard_map.83
  2.2 34.2 %all-gather = bf16[3072,128]{1,0:T(8,128)(2,1)S(1)} all-gather(bf16[192,128]{1,0:T(8,128)(2,1)} %shard_map.83), channel_id=2, replica_groups=mesh['y'=4,'x'=4,'c'=2,'zh'=4,'zl'=4] {'zh','zl'}, dimensions={0}, use_global_device_ids=true | all-gather | bytes 835584 | tf_op jit(solution)/shard_map/all_gather | solution.py:492
  36.4 0.1 stack.47.info
  36.4 1.0 shard_map.84
  37.5 16.4 %all_to_all.40.refs_0_ = bf16[4,192,1024]{2,1,0:T(8,128)(2,1)S(1)} all-to-all(bf16[4,192,1024]{2,1,0:T(8,128)(2,1)S(1)} %shard_map.84), channel_id=1, replica_groups={{0,128,256,384},{32,160,288,416},{64,192,320,448},{96,224,352,480},{16,..., dimensions={0} | all-to-all | bytes 3145728 | tf_op jit(solution)/shard_map/all_to_all | solution.py:484
  53.8 1.0 shard_map.85
  54.8 0.0 copy-start
  54.9 0.0 copy-start.1
  54.9 16.7 %all_to_all.41 = bf16[4,192,1024]{2,1,0:T(8,128)(2,1)S(1)} all-to-all(bf16[4,192,1024]{2,1,0:T(8,128)(2,1)S(1)} %shard_map.85), channel_id=1, replica_groups={{0,32,64,96},{128,160,192,224},{256,288,320,352},{384,416,448,480},{16,..., dimensions={0} | all-to-all | bytes 3145728 | tf_op jit(solution)/shard_map/all_to_all | solution.py:484
  71.5 0.0 copy-done
  71.5 0.0 copy-done.1
  71.5 0.8 shard_map.86
  72.3 13.7 %collective-permute-start = (bf16[768,1024]{1,0:T(8,128)(2,1)S(1)}, bf16[768,1024]{1,0:T(8,128)(2,1)S(1)}, u32[]{:S(2)}, u32[]{:S(2)}) collective-permute-start(bf16[768,1024]{1,0:T(8,128)(2,1)S(1)} %get-tuple-element.26.a_ref), channel_id=1, source_target_pairs={{0,16},{16,0},{1,17},{17,1},{2,18},{18,2},{3,19},{19,3},{4,20},{20... | collective-permute-start | bytes 4718600 | tf_op jit(solution)/shard_map/ppermute | solution.py:512
  86.1 2.2 %shard_map.87 = (f32[768,768]{1,0:T(8,128)S(1)}, f32[1,768,128]{2,1,0:T(8,128)S(1)}, f32[1,768,128]{2,1,0:T(8,128)S(1)}, f32[768,128]{1,0:T(8,128)S(1)}) custom-call(bf16[768,1024]{1,0:T(8,128)(2,1)S(1)} %get-tuple-element.26.a_ref, bf16[768,1024]{1,0:T(8,128)(2,1)S(1)} %get-tuple-element.27.b_ref, f32[16,128]{1,0:T(8,128)S(1)} %get-tuple-element.28.lift_i), custom_call_target="tpu_custom_call" | custom-call | tf_op jit(solution)/shard_map/pallas_call | solution.py:452
  88.3 0.8 collective-permute-done.a_ref
  89.1 3.1 %shard_map.88 = (f32[768,256]{1,0:T(8,128)S(1)}, f32[13824,512]{1,0:T(8,128)}, f32[4,8,128]{2,1,0:T(8,128)S(1)}) custom-call(bf16[768,1024]{1,0:T(8,128)(2,1)S(1)} %collective-permute-done.a_ref, bf16[768,1024]{1,0:T(8,128)(2,1)S(1)} %get-tuple-element.27.b_ref, f32[16,128]{1,0:T(8,128)S(1)} %get-tuple-element.28.lift_i, ...), custom_call_target="tpu_custom_call" | custom-call | tf_op jit(solution)/shard_map/pallas_call | solution.py:458
  92.3 6.6 %all_to_all.42.got = f32[4,8,128]{2,1,0:T(8,128)S(1)} all-to-all(f32[4,8,128]{2,1,0:T(8,128)S(1)} %get-tuple-element.35), channel_id=1, replica_groups=mesh['y'=4,'x'=4,'c'=2,'zh'=4,'zl'=4] {'x'}, dimensions={0} | all-to-all | bytes 32768 | tf_op jit(solution)/shard_map/all_to_all | solution.py:484
  98.8 2.8 %shard_map.89 = (f32[8,24,128]{2,1,0:T(8,128)S(1)}, f32[6,128]{1,0:T(8,128)S(1)}) custom-call(f32[768,768]{1,0:T(8,128)S(1)} %get-tuple-element.29.k1a_ref, f32[768,256]{1,0:T(8,128)S(1)} %get-tuple-element.33.k1b_ref, f32[13824,512]{1,0:T(8,128)} %get-tuple-element.34.k2_hbm, f32[4,8,128]{2,1,0:T(8,128)S(1)} %all_to_all.42.got, ...), custom_call_target="tpu_custom_call" | custom-call | tf_op jit(solution)/shard_map/pallas_call | solution.py:466
  101.6 8.9 %all_to_all.43.got = f32[8,24,128]{2,1,0:T(8,128)S(1)} all-to-all(f32[8,24,128]{2,1,0:T(8,128)S(1)} %get-tuple-element.37), channel_id=1, replica_groups=mesh['y'=4,'x'=4,'c'=2,'zh'=4,'zl'=4] {'y','c'}, dimensions={0} | all-to-all | bytes 196608 | tf_op jit(solution)/shard_map/all_to_all | solution.py:484
  110.5 2.3 %shard_map.90 = (f32[4,16,128]{2,1,0:T(8,128)S(1)}, f32[12,128]{1,0:T(8,128)S(1)}) custom-call(f32[768,768]{1,0:T(8,128)S(1)} %get-tuple-element.29.k1a_ref, f32[768,256]{1,0:T(8,128)S(1)} %get-tuple-element.33.k1b_ref, f32[13824,512]{1,0:T(8,128)} %get-tuple-element.34.k2_hbm, f32[8,24,128]{2,1,0:T(8,128)S(1)} %all_to_all.43.got, ...), custom_call_target="tpu_custom_call" | custom-call | tf_op jit(solution)/shard_map/pallas_call | solution.py:471
  112.8 6.7 %all_to_all.44.got = f32[4,16,128]{2,1,0:T(8,128)S(1)} all-to-all(f32[4,16,128]{2,1,0:T(8,128)S(1)} %get-tuple-element.38), channel_id=1, replica_groups=mesh['y'=4,'x'=4,'c'=2,'zh'=4,'zl'=4] {'x'}, dimensions={0} | all-to-all | bytes 65536 | tf_op jit(solution)/shard_map/all_to_all | solution.py:484
  119.5 2.8 %shard_map.91 = (f32[8,24,128]{2,1,0:T(8,128)S(1)}, f32[6,128]{1,0:T(8,128)S(1)}) custom-call(f32[768,768]{1,0:T(8,128)S(1)} %get-tuple-element.29.k1a_ref, f32[768,256]{1,0:T(8,128)S(1)} %get-tuple-element.33.k1b_ref, f32[13824,512]{1,0:T(8,128)} %get-tuple-element.34.k2_hbm, f32[4,16,128]{2,1,0:T(8,128)S(1)} %all_to_all.44.got, ...), custom_call_target="tpu_custom_call" | custom-call | tf_op jit(solution)/shard_map/pallas_call | solution.py:476
  122.3 9.3 %all_to_all.45.got = f32[8,24,128]{2,1,0:T(8,128)S(1)} all-to-all(f32[8,24,128]{2,1,0:T(8,128)S(1)} %get-tuple-element.40), channel_id=1, replica_groups=mesh['y'=4,'x'=4,'c'=2,'zh'=4,'zl'=4] {'y','c'}, dimensions={0} | all-to-all | bytes 196608 | tf_op jit(solution)/shard_map/all_to_all | solution.py:484
  131.6 2.4 %shard_map.92 = f32[16,8,128]{2,1,0:T(8,128)} custom-call(f32[768,768]{1,0:T(8,128)S(1)} %get-tuple-element.29.k1a_ref, f32[768,256]{1,0:T(8,128)S(1)} %get-tuple-element.33.k1b_ref, f32[13824,512]{1,0:T(8,128)} %get-tuple-element.34.k2_hbm, f32[8,24,128]{2,1,0:T(8,128)S(1)} %all_to_all.45.got, f32[16,128]{1,0:T(8,128)S(1)} %get-tuple-element.28.lift_i, ...), custom_call_target="tpu_custom_call" | custom-call | tf_op jit(solution)/shard_map/pallas_call | solution.py:480
  134.0 3.5 %all-to-all-start.6 = ((f32[16,8,128]{2,1,0:T(8,128)}), f32[16,8,128]{2,1,0:T(8,128)S(1)}, u32[]{:S(2)}, u32[]{:S(2)}) async-start(f32[16,8,128]{2,1,0:T(8,128)} %shard_map.92), calls=%async_computation.6 | async-start | bytes 131072 | tf_op jit(solution)/shard_map/all_to_all | solution.py:484
  137.5 6.9 %all-to-all-done.6.got = f32[16,8,128]{2,1,0:T(8,128)S(1)} async-done(((f32[16,8,128]{2,1,0:T(8,128)}), f32[16,8,128]{2,1,0:T(8,128)S(1)}, u32[]{:S(2)}, u32[]{:S(2)}) %all-to-all-start.6) | async-done | bytes 65568 | tf_op jit(solution)/shard_map/all_to_all | solution.py:484
  144.4 0.8 shard_map.93
  145.2 5.2 %all-to-all-start.7 = ((f32[8,8,128]{2,1,0:T(8,128)}), f32[8,8,128]{2,1,0:T(8,128)S(1)}, u32[]{:S(2)}, u32[]{:S(2)}) async-start(f32[8,8,128]{2,1,0:T(8,128)} %get-tuple-element.46), calls=%async_computation.7 | async-start | bytes 65536 | tf_op jit(solution)/shard_map/all_to_all | solution.py:484
  150.4 0.6 fusion
  151.1 0.6 dynamic_slice.12
  151.7 3.5 %all-to-all-done.7 = f32[8,8,128]{2,1,0:T(8,128)S(1)} async-done(((f32[8,8,128]{2,1,0:T(8,128)}), f32[8,8,128]{2,1,0:T(8,128)S(1)}, u32[]{:S(2)}, u32[]{:S(2)}) %all-to-all-start.7) | async-done | bytes 32800 | tf_op jit(solution)/shard_map/all_to_all | solution.py:484
  155.1 0.6 slice_reduce_fusion
  (2 shorter events, 0.0 us)
Async XLA Ops:
  54.8 16.7 %copy-start = (s32[32]{0:T(128)S(1)}, s32[32]{0:T(128)}, u32[]{:S(2)}) copy-start(s32[32]{0:T(128)} %gen_count.1) | copy-start | bytes 388
  54.9 16.7 %copy-start.1 = (s32[32]{0:T(128)S(1)}, s32[32]{0:T(128)}, u32[]{:S(2)}) copy-start(s32[32]{0:T(128)} %ref_count.1) | copy-start | bytes 388
  72.3 16.8 %collective-permute-start = (bf16[768,1024]{1,0:T(8,128)(2,1)S(1)}, bf16[768,1024]{1,0:T(8,128)(2,1)S(1)}, u32[]{:S(2)}, u32[]{:S(2)}) collective-permute-start(bf16[768,1024]{1,0:T(8,128)(2,1)S(1)} %get-tuple-element.26.a_ref), channel_id=1, source_target_pairs={{0,16},{16,0},{1,17},{17,1},{2,18},{18,2},{3,19},{19,3},{4,20},{20... | collective-permute-start | bytes 4718600 | tf_op jit(solution)/shard_map/ppermute | solution.py:512
  134.0 10.4 %all-to-all-start.6 = ((f32[16,8,128]{2,1,0:T(8,128)}), f32[16,8,128]{2,1,0:T(8,128)S(1)}, u32[]{:S(2)}, u32[]{:S(2)}) async-start(f32[16,8,128]{2,1,0:T(8,128)} %shard_map.92), calls=%async_computation.6 | async-start | bytes 131072 | tf_op jit(solution)/shard_map/all_to_all | solution.py:484
  145.2 9.9 %all-to-all-start.7 = ((f32[8,8,128]{2,1,0:T(8,128)}), f32[8,8,128]{2,1,0:T(8,128)S(1)}, u32[]{:S(2)}, u32[]{:S(2)}) async-start(f32[8,8,128]{2,1,0:T(8,128)} %get-tuple-element.46), calls=%async_computation.7 | async-start | bytes 65536 | tf_op jit(solution)/shard_map/all_to_all | solution.py:484

commit v11 on v10

--- a/solution.py
+++ b/solution.py
@@ -21,6 +21,7 @@
 RJ = NJ // 128
 NEAR = 8
 N2 = NI - NEAR * 128
+PACK_MIB = 40
 ROOM = 18 * NJ
 
 VMEM = pl.BlockSpec(memory_space=pltpu.VMEM)
@@ -192,20 +193,30 @@
         copy.start()
     for copy in copies:
         copy.wait()
-    wide = jnp.concatenate([both[0].astype(jnp.float32), both[1].astype(jnp.float32)], axis=0)
-    out[...] = jnp.transpose(wide).astype(jnp.bfloat16)
-
-
-def unpack_body(which, info, raw, *refs):
-    out = refs[-1]
+    for n in range(2):
+        points = jnp.transpose(both[n].astype(jnp.float32))
+        rows = jnp.concatenate([points[:96, :], points[96:, :]], axis=1).astype(jnp.bfloat16)
+        for z in range(16):
+            if (z % 4) // 2 == n:
+                out[z] = rows
+
+
+def unpack_body(raw, own_out, wide_out):
     for k in range(D // 128):
         cols = slice(k * 128, (k + 1) * 128)
         even, odd = raw[2 * k], raw[2 * k + 1]
-        gen = jnp.concatenate([even[:, :64], odd[:, :64]], axis=1)
-        ref = jnp.concatenate([even[:, 64:], odd[:, 64:]], axis=1)
-        part = jnp.where(info[5 + which] == 1, gen, ref)
-        for n in range(4):
-            out[n, :, cols] = part
+        for half, lanes in enumerate((slice(0, 64), slice(64, 128))):
+            part = jnp.concatenate([even[:, lanes], odd[:, lanes]], axis=1)
+            rows = slice(half * 96, half * 96 + 96)
+            own_out[rows, cols] = part
+            for n in range(4):
+                wide_out[n, rows, cols] = part
+
+
+def widen_body(info, own, swapped, out):
+    part = jnp.where(info[0] != info[1], swapped[...], own[...])
+    for n in range(4):
+        out[n] = part
 
 
 def norm_parts(values):
@@ -214,12 +225,8 @@
     return functools.reduce(jnp.add, [values[:, k * 128 : (k + 1) * 128] for k in range(D // 128)])
 
 
-def join_body(info, gen_count, ref_count, one, two, a_out, b_out, lift_i, lift_j, weights):
+def masks(info, gen_count, ref_count, lift_i, lift_j, weights):
     c, x, y = info[2], info[3], info[4]
-    for s in range(6):
-        part = slice(s * 128, (s + 1) * 128)
-        a_out[part, :] = jnp.where(c == 0, one[part, :], two[part, :])
-        b_out[part, :] = jnp.where(c == 0, two[part, :], one[part, :])
 
     def total(counts):
         return jnp.full((8, 128), functools.reduce(jnp.add, [counts[n] for n in range(32)]).astype(jnp.float32))
@@ -285,7 +292,10 @@
         lanes_block(pair, 1, heads, high_ref, mass_ref, b * 128, joined)
 
 
-def cost_own_body(a_ref, b_ref, lift_i, k1a_ref, high_ref, mass_ref, sq_ref):
+def cost_own_body(
+    info, gen_count, ref_count, a_ref, b_ref, k1a_ref, high_ref, mass_ref, sq_ref, lift_i, lift_j, weights
+):
+    masks(info, gen_count, ref_count, lift_i, lift_j, weights)
     head = lift_i[...]
     norms = a_norms(a_ref)
     for b in range(RJ):
@@ -430,26 +440,27 @@
     return [pltpu.VMEM((count, 8, 128), F32), pltpu.VMEM((count, NJ, 128), F32)] + [pltpu.VMEM((count, 8 * RJ, NI), F32)] * 2
 
 
+def bf16(*shape):
+    return jax.ShapeDtypeStruct(shape, BF16)
+
+
 def stage_pack(*args):
     scratch = [pltpu.VMEM((2, 64, BLOCK), BF16), pltpu.SemaphoreType.DMA((2,))]
-    out = jax.ShapeDtypeStruct((BLOCK, 128), BF16)
-    return call(pack_body, out, [HBM, HBM], scratch, mib=60)(*args)
-
-
-def stage_unpack(which, *args):
-    out = jax.ShapeDtypeStruct((4, BLOCK, D), BF16)
-    return call(functools.partial(unpack_body, which), out, [SMEM, VMEM, HBM][: len(args)])(*args)
-
-
-def stage_join(*args):
-    points = (jax.ShapeDtypeStruct((NJ, D), BF16),) * 2
-    outs = points + (f32(16, 128), f32(8, 128), f32(24, 128))
-    return call(join_body, outs, [SMEM] * 3 + [VMEM] * 2)(*args)
+    return call(pack_body, bf16(16, 96, 128), [HBM, HBM], scratch, mib=PACK_MIB)(*args)
+
+
+def stage_unpack(*args):
+    return call(unpack_body, (bf16(BLOCK, D), bf16(4, BLOCK, D)), [VMEM])(*args)
+
+
+def stage_widen(*args):
+    return call(widen_body, bf16(4, BLOCK, D), [SMEM, VMEM, VMEM])(*args)
 
 
 def stage_cost_own(*args):
     outs = (f32(NJ, NI // 2), f32(1, NJ, 128), f32(1, NJ, 128), f32(NJ, 128))
-    return call(cost_own_body, outs, [VMEM] * 3)(*args)
+    outs += (f32(16, 128), f32(8, 128), f32(24, 128))
+    return call(cost_own_body, outs, [SMEM] * 3 + [VMEM] * 2)(*args)
 
 
 def stage_cost_other(*args):
@@ -480,17 +491,16 @@
     return call(fifth_body, f32(16, 8, 128), K_SPECS + [VMEM] * 4, STREAM + lane_scratch(1))(*args)
 
 
-def spread(operand, axes, groups=None):
-    return lax.all_to_all(operand, axes, 0, 0, tiled=True, axis_index_groups=groups)
+def spread(operand, axes):
+    return lax.all_to_all(operand, axes, 0, 0, tiled=True)
 
 
 def local(gen_points, reference_embeddings, gen_count, ref_count):
     y, x, c, zl = (lax.axis_index(name) for name in ("y", "x", "c", "zl"))
-    a_is_gen = zl < 3
-    b_is_gen = zl == 0
+    a_is_gen = zl < 2
+    b_is_gen = (zl == 0) | (zl == 2)
     packed = stage_pack(jnp.transpose(gen_points), jnp.transpose(reference_embeddings))
-    raw = lax.all_gather(packed, ("zh", "zl"))
-
+    raw = spread(packed, ("zh", "zl"))
     info = jnp.stack(
         [
             a_is_gen.astype(jnp.int32),
@@ -498,19 +508,17 @@
             c,
             x,
             y,
-            jnp.where(c == 0, a_is_gen, b_is_gen).astype(jnp.int32),
-            jnp.where(c == 0, b_is_gen, a_is_gen).astype(jnp.int32),
         ]
     ).astype(jnp.int32)
-    along_y = [[[(i * 4 + n) * 2 + core for i in range(4)] for n in range(4)] for core in range(2)]
-    along_x = [[[(n * 4 + i) * 2 + core for i in range(4)] for n in range(4)] for core in range(2)]
-    one = spread(stage_unpack(0, info, raw), ("y", "x", "c"), along_y[0] + along_x[1])
-    two = spread(stage_unpack(1, info, raw, one), ("y", "x", "c"), along_x[0] + along_y[1])
-    a_own, b_all, lift_i, lift_j, weights = stage_join(
-        info, gen_count, ref_count, one.reshape(NJ, D), two.reshape(NJ, D)
+    own, wide_a = stage_unpack(raw)
+    swapped = lax.ppermute(own, "zl", [(1, 2), (2, 1)])
+    one = spread(wide_a, "y")
+    two = spread(stage_widen(info, own, swapped), "x")
+    a_own, b_all = lax.optimization_barrier((one.reshape(NJ, D), two.reshape(NJ, D)))
+    a_other = lax.ppermute(a_own, "c", [(0, 1), (1, 0)])
+    k1a, high, mass, b_norms, lift_i, lift_j, weights = stage_cost_own(
+        info, gen_count, ref_count, a_own, b_all
     )
-    a_other = lax.ppermute(a_own, "c", [(0, 1), (1, 0)])
-    k1a, high, mass, b_norms = stage_cost_own(a_own, b_all, lift_i)
     k1b, k2, part = stage_cost_other(a_other, b_all, lift_i, high, mass, b_norms)
     k = (k1a, k1b, k2)
     part, g1 = stage_second(*k, spread(part, "x"), lift_j)

time: 156 us -> 164 us (1.051)
  blocking collectives: 98.6 us -> 81.3 us
  starting transfers between devices: 22.4 us -> 35 us
  waiting for transfers between devices: 11.1 us -> 20.8 us
  local copies, waits for them, and re-layouts: 1.39 us -> 4.65 us
    all_gather x1 -> x0, blocking collectives: 34.2 us -> none  [local(): raw = lax.all_gather(packed, ('zh', 'zl'))]
    all_to_all x6, blocking collectives: 64.4 us -> 81.3 us  [spread(): return lax.all_to_all(operand, axes, 0, 0, tiled=True)]
    all_to_all x2 -> x3, starting transfers between devices: 8.7 us -> 22.8 us  [spread(): return lax.all_to_all(operand, axes, 0, 0, tiled=True)]
    all_to_all x2 -> x3, waiting for transfers between devices: 10.4 us -> 20.7 us  [spread(): return lax.all_to_all(operand, axes, 0, 0, tiled=True)]
    unnamed x4 -> x12, local copies, waits for them, and re-layouts: 0.01 us -> 3.27 us
    ppermute x1, starting transfers between devices: 13.7 us -> 11.5 us  [local(): a_other = lax.ppermute(a_own, 'c', [(0, 1), (1, 0)])]
    pallas_call x5 -> x4, Pallas kernels: 6.57 us -> 5.49 us  [the longest x1 2.85 us: stage_cost_own(): return call(cost_own_body, outs, [SMEM] * 3 + [VMEM] * 2)(*args)]
  transfers between devices with their start and end apart: 3 -> 5, of which waited for: 3 -> 4; matrix products, arithmetic and copies ran while one was open for 1% -> 1% of each run, Pallas kernels for 1% -> 2%
where the time goes in v11:
time: 164 us; the launch traced here: 163 us
  blocking collectives  81.3 us (50%)
  starting transfers between devices  35 us (21%)
  waiting for transfers between devices  20.8 us (13%)
  Pallas kernels  19.7 us (12%)
  local copies, waits for them, and re-layouts  4.65 us (3%)
    all_to_all x6, blocking collectives, spread(): return lax.all_to_all(operand, axes, 0, 0, tiled=True)  81.3 us
    all_to_all x3, starting transfers between devices, spread(): return lax.all_to_all(operand, axes, 0, 0, tiled=True)  22.8 us
    all_to_all x3, waiting for transfers between devices, spread(): return lax.all_to_all(operand, axes, 0, 0, tiled=True)  20.7 us
    ppermute x1, starting transfers between devices, local(): a_other = lax.ppermute(a_own, 'c', [(0, 1), (1, 0)])  11.5 us
  transfers between devices with their start and end apart: 5, of which 4 were waited for; matrix products, arithmetic and copies ran while one was open for 1% of the time, Pallas kernels for 2%

profile of v11, /device:TPU:1, one launch (start us, length us, event | category | flops | bytes accessed | tf_op | source)
XLA Modules:
  0.0 162.9 jit_solution(1477276958044766521)
XLA Ops:
  0.6 0.7 copy-done.2
  1.4 0.8 copy-done.3
  2.1 0.3 shard_map.83
  2.4 33.5 %all_to_all.45.raw = bf16[16,96,128]{2,1,0:T(8,128)(2,1)S(1)} all-to-all(bf16[16,96,128]{2,1,0:T(8,128)(2,1)S(1)} %shard_map.83), channel_id=1, replica_groups=mesh['y'=4,'x'=4,'c'=2,'zh'=4,'zl'=4] {'zh','zl'}, dimensions={0} | all-to-all | bytes 786432 | tf_op jit(solution)/shard_map/all_to_all | solution.py:495
  36.0 1.7 %shard_map.84 = (bf16[192,1024]{1,0:T(8,128)(2,1)S(1)}, bf16[4,192,1024]{2,1,0:T(8,128)(2,1)}) custom-call(bf16[16,96,128]{2,1,0:T(8,128)(2,1)S(1)} %all_to_all.45.raw), custom_call_target="tpu_custom_call" | custom-call | tf_op jit(solution)/shard_map/pallas_call | solution.py:453
  37.7 4.2 %all-to-all-start.1 = ((bf16[4,192,1024]{2,1,0:T(8,128)(2,1)}), bf16[4,192,1024]{2,1,0:T(8,128)(2,1)S(1)}, u32[]{:S(2)}, u32[]{:S(2)}) async-start(bf16[4,192,1024]{2,1,0:T(8,128)(2,1)} %get-tuple-element.28), calls=%async_computation.1 | async-start | bytes 3145728 | tf_op jit(solution)/shard_map/all_to_all | solution.py:495
  41.9 0.7 collective-permute-start
  42.7 0.8 copy-done
  43.4 1.0 copy-done.1
  44.4 0.6 shard_map.85
  45.1 10.2 %all-to-all-done.1 = bf16[4,192,1024]{2,1,0:T(8,128)(2,1)S(1)} async-done(((bf16[4,192,1024]{2,1,0:T(8,128)(2,1)}), bf16[4,192,1024]{2,1,0:T(8,128)(2,1)S(1)}, u32[]{:S(2)}, u32[]{:S(2)}) %all-to-all-start.1) | async-done | bytes 1572896 | tf_op jit(solution)/shard_map/all_to_all | solution.py:495
  55.3 16.4 %all_to_all.46 = bf16[4,192,1024]{2,1,0:T(8,128)(2,1)S(1)} all-to-all(bf16[4,192,1024]{2,1,0:T(8,128)(2,1)S(1)} %shard_map.85), channel_id=1, replica_groups=mesh['y'=4,'x'=4,'c'=2,'zh'=4,'zl'=4] {'x'}, dimensions={0} | all-to-all | bytes 3145728 | tf_op jit(solution)/shard_map/all_to_all | solution.py:495
  71.7 11.5 %collective-permute-start.1 = (bf16[768,1024]{1,0:T(8,128)(2,1)S(1)}, bf16[768,1024]{1,0:T(8,128)(2,1)S(1)}, u32[]{:S(2)}, u32[]{:S(2)}) collective-permute-start(bf16[768,1024]{1,0:T(8,128)(2,1)S(1)} %bitcast.15), channel_id=1, source_target_pairs={{0,16},{16,0},{1,17},{17,1},{2,18},{18,2},{3,19},{19,3},{4,20},{20... | collective-permute-start | bytes 4718600 | tf_op jit(solution)/shard_map/ppermute | solution.py:518
  83.3 2.8 %shard_map.86 = (f32[768,768]{1,0:T(8,128)S(1)}, f32[1,768,128]{2,1,0:T(8,128)S(1)}, f32[1,768,128]{2,1,0:T(8,128)S(1)}, f32[768,128]{1,0:T(8,128)S(1)}, f32[16,...) custom-call(s32[5]{0:T(128)S(1)} %stack.31.info, s32[32]{0:T(128)S(1)} %copy-done.4, s32[32]{0:T(128)S(1)} %copy-done.5, ...), custom_call_target="tpu_custom_call" | custom-call | tf_op jit(solution)/shard_map/pallas_call | solution.py:463
  86.1 0.1 collective-permute-done.1.a_ref
  86.3 3.2 %shard_map.87 = (f32[768,256]{1,0:T(8,128)S(1)}, f32[13824,512]{1,0:T(8,128)}, f32[4,8,128]{2,1,0:T(8,128)S(1)}) custom-call(bf16[768,1024]{1,0:T(8,128)(2,1)S(1)} %collective-permute-done.1.a_ref, bf16[768,1024]{1,0:T(8,128)(2,1)S(1)} %bitcast.14, f32[16,128]{1,0:T(8,128)S(1)} %get-tuple-element.33.lift_i, f32[1,768,128]{2,1,0:T(8,128)S(1)} %get-tuple-element.34.high_in, ...), custom_call_target="tpu_custom_call" | custom-call | tf_op jit(solution)/shard_map/pallas_call | solution.py:469
  89.4 6.6 %all_to_all.47.got = f32[4,8,128]{2,1,0:T(8,128)S(1)} all-to-all(f32[4,8,128]{2,1,0:T(8,128)S(1)} %get-tuple-element.39), channel_id=1, replica_groups=mesh['y'=4,'x'=4,'c'=2,'zh'=4,'zl'=4] {'x'}, dimensions={0} | all-to-all | bytes 32768 | tf_op jit(solution)/shard_map/all_to_all | solution.py:495
  96.0 2.8 %shard_map.88 = (f32[8,24,128]{2,1,0:T(8,128)S(1)}, f32[6,128]{1,0:T(8,128)S(1)}) custom-call(f32[768,768]{1,0:T(8,128)S(1)} %get-tuple-element.32.k1a_ref, f32[768,256]{1,0:T(8,128)S(1)} %get-tuple-element.37.k1b_ref, f32[13824,512]{1,0:T(8,128)} %get-tuple-element.38.k2_hbm, f32[4,8,128]{2,1,0:T(8,128)S(1)} %all_to_all.47.got, ...), custom_call_target="tpu_custom_call" | custom-call | tf_op jit(solution)/shard_map/pallas_call | solution.py:477
  98.8 8.9 %all_to_all.48.got = f32[8,24,128]{2,1,0:T(8,128)S(1)} all-to-all(f32[8,24,128]{2,1,0:T(8,128)S(1)} %get-tuple-element.41), channel_id=1, replica_groups=mesh['y'=4,'x'=4,'c'=2,'zh'=4,'zl'=4] {'y','c'}, dimensions={0} | all-to-all | bytes 196608 | tf_op jit(solution)/shard_map/all_to_all | solution.py:495
  107.7 2.3 %shard_map.89 = (f32[4,16,128]{2,1,0:T(8,128)S(1)}, f32[12,128]{1,0:T(8,128)S(1)}) custom-call(f32[768,768]{1,0:T(8,128)S(1)} %get-tuple-element.32.k1a_ref, f32[768,256]{1,0:T(8,128)S(1)} %get-tuple-element.37.k1b_ref, f32[13824,512]{1,0:T(8,128)} %get-tuple-element.38.k2_hbm, f32[8,24,128]{2,1,0:T(8,128)S(1)} %all_to_all.48.got, ...), custom_call_target="tpu_custom_call" | custom-call | tf_op jit(solution)/shard_map/pallas_call | solution.py:482
  110.0 6.7 %all_to_all.49.got = f32[4,16,128]{2,1,0:T(8,128)S(1)} all-to-all(f32[4,16,128]{2,1,0:T(8,128)S(1)} %get-tuple-element.42), channel_id=1, replica_groups=mesh['y'=4,'x'=4,'c'=2,'zh'=4,'zl'=4] {'x'}, dimensions={0} | all-to-all | bytes 65536 | tf_op jit(solution)/shard_map/all_to_all | solution.py:495
  116.7 2.8 %shard_map.90 = (f32[8,24,128]{2,1,0:T(8,128)S(1)}, f32[6,128]{1,0:T(8,128)S(1)}) custom-call(f32[768,768]{1,0:T(8,128)S(1)} %get-tuple-element.32.k1a_ref, f32[768,256]{1,0:T(8,128)S(1)} %get-tuple-element.37.k1b_ref, f32[13824,512]{1,0:T(8,128)} %get-tuple-element.38.k2_hbm, f32[4,16,128]{2,1,0:T(8,128)S(1)} %all_to_all.49.got, ...), custom_call_target="tpu_custom_call" | custom-call | tf_op jit(solution)/shard_map/pallas_call | solution.py:487
  119.5 9.3 %all_to_all.50.got = f32[8,24,128]{2,1,0:T(8,128)S(1)} all-to-all(f32[8,24,128]{2,1,0:T(8,128)S(1)} %get-tuple-element.44), channel_id=1, replica_groups=mesh['y'=4,'x'=4,'c'=2,'zh'=4,'zl'=4] {'y','c'}, dimensions={0} | all-to-all | bytes 196608 | tf_op jit(solution)/shard_map/all_to_all | solution.py:495
  128.8 2.4 %shard_map.91 = f32[16,8,128]{2,1,0:T(8,128)} custom-call(f32[768,768]{1,0:T(8,128)S(1)} %get-tuple-element.32.k1a_ref, f32[768,256]{1,0:T(8,128)S(1)} %get-tuple-element.37.k1b_ref, f32[13824,512]{1,0:T(8,128)} %get-tuple-element.38.k2_hbm, f32[8,24,128]{2,1,0:T(8,128)S(1)} %all_to_all.50.got, f32[16,128]{1,0:T(8,128)S(1)} %get-tuple-element.33.lift_i, ...), custom_call_target="tpu_custom_call" | custom-call | tf_op jit(solution)/shard_map/pallas_call | solution.py:491
  131.2 13.2 %all-to-all-start.7 = ((f32[16,8,128]{2,1,0:T(8,128)}), f32[16,8,128]{2,1,0:T(8,128)S(1)}, u32[]{:S(2)}, u32[]{:S(2)}) async-start(f32[16,8,128]{2,1,0:T(8,128)} %shard_map.91), calls=%async_computation.7 | async-start | bytes 131072 | tf_op jit(solution)/shard_map/all_to_all | solution.py:495
  144.4 7.0 %all-to-all-done.7.got = f32[16,8,128]{2,1,0:T(8,128)S(1)} async-done(((f32[16,8,128]{2,1,0:T(8,128)}), f32[16,8,128]{2,1,0:T(8,128)S(1)}, u32[]{:S(2)}, u32[]{:S(2)}) %all-to-all-start.7) | async-done | bytes 65568 | tf_op jit(solution)/shard_map/all_to_all | solution.py:495
  151.3 0.8 shard_map.92
  152.1 5.5 %all-to-all-start.8 = ((f32[8,8,128]{2,1,0:T(8,128)}), f32[8,8,128]{2,1,0:T(8,128)S(1)}, u32[]{:S(2)}, u32[]{:S(2)}) async-start(f32[8,8,128]{2,1,0:T(8,128)} %get-tuple-element.50), calls=%async_computation.8 | async-start | bytes 65536 | tf_op jit(solution)/shard_map/all_to_all | solution.py:495
  157.6 0.6 fusion
  158.2 0.6 dynamic_slice.12
  158.9 3.5 %all-to-all-done.8 = f32[8,8,128]{2,1,0:T(8,128)S(1)} async-done(((f32[8,8,128]{2,1,0:T(8,128)}), f32[8,8,128]{2,1,0:T(8,128)S(1)}, u32[]{:S(2)}, u32[]{:S(2)}) %all-to-all-start.8) | async-done | bytes 32800 | tf_op jit(solution)/shard_map/all_to_all | solution.py:495
  162.3 0.6 slice_reduce_fusion
  (12 shorter events, 0.1 us)
Async XLA Ops:
  0.6 0.8 copy-start.2
  1.4 0.8 copy-start.3
  37.7 17.6 %all-to-all-start.1 = ((bf16[4,192,1024]{2,1,0:T(8,128)(2,1)}), bf16[4,192,1024]{2,1,0:T(8,128)(2,1)S(1)}, u32[]{:S(2)}, u32[]{:S(2)}) async-start(bf16[4,192,1024]{2,1,0:T(8,128)(2,1)} %get-tuple-element.28), calls=%async_computation.1 | async-start | bytes 3145728 | tf_op jit(solution)/shard_map/all_to_all | solution.py:495
  41.9 0.8 collective-permute-start
  42.7 0.8 copy-start
  43.4 1.0 copy-start.1
  45.1 38.2 %copy-start.4 = (s32[32]{0:T(128)S(1)}, s32[32]{0:T(128)}, u32[]{:S(2)}) copy-start(s32[32]{0:T(128)} %gen_count.1) | copy-start | bytes 388
  45.1 38.2 %copy-start.5 = (s32[32]{0:T(128)S(1)}, s32[32]{0:T(128)}, u32[]{:S(2)}) copy-start(s32[32]{0:T(128)} %ref_count.1) | copy-start | bytes 388
  71.7 14.6 %collective-permute-start.1 = (bf16[768,1024]{1,0:T(8,128)(2,1)S(1)}, bf16[768,1024]{1,0:T(8,128)(2,1)S(1)}, u32[]{:S(2)}, u32[]{:S(2)}) collective-permute-start(bf16[768,1024]{1,0:T(8,128)(2,1)S(1)} %bitcast.15), channel_id=1, source_target_pairs={{0,16},{16,0},{1,17},{17,1},{2,18},{18,2},{3,19},{19,3},{4,20},{20... | collective-permute-start | bytes 4718600 | tf_op jit(solution)/shard_map/ppermute | solution.py:518
  131.2 20.2 %all-to-all-start.7 = ((f32[16,8,128]{2,1,0:T(8,128)}), f32[16,8,128]{2,1,0:T(8,128)S(1)}, u32[]{:S(2)}, u32[]{:S(2)}) async-start(f32[16,8,128]{2,1,0:T(8,128)} %shard_map.91), calls=%async_computation.7 | async-start | bytes 131072 | tf_op jit(solution)/shard_map/all_to_all | solution.py:495
  152.1 10.2 %all-to-all-start.8 = ((f32[8,8,128]{2,1,0:T(8,128)}), f32[8,8,128]{2,1,0:T(8,128)S(1)}, u32[]{:S(2)}, u32[]{:S(2)}) async-start(f32[8,8,128]{2,1,0:T(8,128)} %get-tuple-element.50), calls=%async_computation.8 | async-start | bytes 65536 | tf_op jit(solution)/shard_map/all_to_all | solution.py:495

commit v12 on v10

--- a/solution.py
+++ b/solution.py
@@ -203,7 +203,7 @@
         even, odd = raw[2 * k], raw[2 * k + 1]
         gen = jnp.concatenate([even[:, :64], odd[:, :64]], axis=1)
         ref = jnp.concatenate([even[:, 64:], odd[:, 64:]], axis=1)
-        part = jnp.where(info[5 + which] == 1, gen, ref)
+        part = jnp.where(info[which] == 1, gen, ref)
         for n in range(4):
             out[n, :, cols] = part
 
@@ -214,12 +214,8 @@
     return functools.reduce(jnp.add, [values[:, k * 128 : (k + 1) * 128] for k in range(D // 128)])
 
 
-def join_body(info, gen_count, ref_count, one, two, a_out, b_out, lift_i, lift_j, weights):
+def masks(info, gen_count, ref_count, lift_i, lift_j, weights):
     c, x, y = info[2], info[3], info[4]
-    for s in range(6):
-        part = slice(s * 128, (s + 1) * 128)
-        a_out[part, :] = jnp.where(c == 0, one[part, :], two[part, :])
-        b_out[part, :] = jnp.where(c == 0, two[part, :], one[part, :])
 
     def total(counts):
         return jnp.full((8, 128), functools.reduce(jnp.add, [counts[n] for n in range(32)]).astype(jnp.float32))
@@ -257,6 +253,8 @@
         weights[n * 8 : n * 8 + 8, :] = jnp.where(ok, 1.0 / totals[n], 0.0)
     ok = valid(flat(8), starts, [ref_count[t] for t in here])
     weights[16:24, :] = jnp.where(ok, 1.0 / totals[1], 0.0)
+    weights[22:23, :] = jnp.full((1, 128), x.astype(jnp.float32))
+    weights[23:24, :] = jnp.full((1, 128), lax.rem(y, 2).astype(jnp.float32))
 
 
 def a_norms(a_ref):
@@ -285,7 +283,10 @@
         lanes_block(pair, 1, heads, high_ref, mass_ref, b * 128, joined)
 
 
-def cost_own_body(a_ref, b_ref, lift_i, k1a_ref, high_ref, mass_ref, sq_ref):
+def cost_own_body(
+    info, gen_count, ref_count, a_ref, b_ref, k1a_ref, high_ref, mass_ref, sq_ref, lift_i, lift_j, weights
+):
+    masks(info, gen_count, ref_count, lift_i, lift_j, weights)
     head = lift_i[...]
     norms = a_norms(a_ref)
     for b in range(RJ):
@@ -394,27 +395,39 @@
         out[n, RJ : RJ + 2, :] = mine
 
 
-def last_body(got, weights, pots, g4_out, share):
+def last_body(got, weights, gen_pot, ref_pot, gen_self, ref_self, share):
     g4 = merge([got[n * 4 + 1, 0:RJ, :] for n in range(4)], 4) * (-0.5 * LN2)
-    g4_out[0:RJ, :] = g4
-    g4_out[RJ:8, :] = jnp.zeros((8 - RJ, 128), jnp.float32)
     weight = weights[16 : 16 + RJ, :]
     total = jnp.sum(jnp.where(weight > 0.0, g4 * weight, 0.0))
+    own = [[got[n * 4 + plane, RJ : RJ + 2, :] * LN2 for n in range(4)] for plane in (1, 0, 3)]
     for n in range(4):
-        own = slice(RJ, RJ + 2)
-        gen_pot = got[n * 4 + 1][own, :] * LN2
-        gen_self = got[n * 4][own, :] * LN2
-        ref_self = got[n * 4 + 3][own, :] * LN2
-        pots[n, 0:2, :] = gen_pot
-        pots[n, 2:4, :] = gen_self
-        pots[n, 4:6, :] = ref_self
-        pots[n, 6:8, :] = jnp.zeros((2, 128), jnp.float32)
         weight = weights[2 * n : 2 * n + 2, :]
-        total += jnp.sum(jnp.where(weight > 0.0, (gen_pot - gen_self) * weight, 0.0))
+        total += jnp.sum(jnp.where(weight > 0.0, (own[0][n] - own[1][n]) * weight, 0.0))
         weight = weights[8 + 2 * n : 8 + 2 * n + 2, :]
-        total -= jnp.sum(jnp.where(weight > 0.0, ref_self * weight, 0.0))
+        total -= jnp.sum(jnp.where(weight > 0.0, own[2][n] * weight, 0.0))
     for n in range(8):
         share[n, :, :] = jnp.full((8, 128), total, jnp.float32)
+
+    along_x, odd_y = weights[22:23, :], weights[23:24, :]
+    low = lax.broadcasted_iota(jnp.int32, (1, 128), 1) < 64
+
+    def chosen(rows):
+        result = rows[0]
+        for n in range(1, 4):
+            result = jnp.where(along_x > n - 0.5, rows[n], result)
+        return result
+
+    def write(out, window, late):
+        rolled = jnp.concatenate([window[:, 64:], window[:, :64]], axis=1)
+        first = jnp.where(late, jnp.where(low, rolled[0:1, :], rolled[1:2, :]), window[0:1, :])
+        second = jnp.where(late, rolled[1:2, :], window[1:2, :])
+        out[0:1, 0:128] = first
+        out[0:1, 128:192] = second[:, 0:64]
+
+    for out, rows in zip((gen_pot, gen_self, ref_self), own):
+        write(out, chosen(rows), odd_y > 0.5)
+    odd_x = ((along_x > 0.5) & (along_x < 1.5)) | (along_x > 2.5)
+    write(ref_pot, chosen([g4[row : row + 2, :] for row in (0, 1, 3, 4)]), odd_x)
 
 
 F32 = jnp.float32
@@ -441,15 +454,10 @@
     return call(functools.partial(unpack_body, which), out, [SMEM, VMEM, HBM][: len(args)])(*args)
 
 
-def stage_join(*args):
-    points = (jax.ShapeDtypeStruct((NJ, D), BF16),) * 2
-    outs = points + (f32(16, 128), f32(8, 128), f32(24, 128))
-    return call(join_body, outs, [SMEM] * 3 + [VMEM] * 2)(*args)
-
-
 def stage_cost_own(*args):
     outs = (f32(NJ, NI // 2), f32(1, NJ, 128), f32(1, NJ, 128), f32(NJ, 128))
-    return call(cost_own_body, outs, [VMEM] * 3)(*args)
+    outs += (f32(16, 128), f32(8, 128), f32(24, 128))
+    return call(cost_own_body, outs, [SMEM] * 3 + [VMEM] * 2)(*args)
 
 
 def stage_cost_other(*args):
@@ -480,8 +488,8 @@
     return call(fifth_body, f32(16, 8, 128), K_SPECS + [VMEM] * 4, STREAM + lane_scratch(1))(*args)
 
 
-def spread(operand, axes, groups=None):
-    return lax.all_to_all(operand, axes, 0, 0, tiled=True, axis_index_groups=groups)
+def spread(operand, axes):
+    return lax.all_to_all(operand, axes, 0, 0, tiled=True)
 
 
 def local(gen_points, reference_embeddings, gen_count, ref_count):
@@ -498,19 +506,15 @@
             c,
             x,
             y,
-            jnp.where(c == 0, a_is_gen, b_is_gen).astype(jnp.int32),
-            jnp.where(c == 0, b_is_gen, a_is_gen).astype(jnp.int32),
         ]
     ).astype(jnp.int32)
-    along_y = [[[(i * 4 + n) * 2 + core for i in range(4)] for n in range(4)] for core in range(2)]
-    along_x = [[[(n * 4 + i) * 2 + core for i in range(4)] for n in range(4)] for core in range(2)]
-    one = spread(stage_unpack(0, info, raw), ("y", "x", "c"), along_y[0] + along_x[1])
-    two = spread(stage_unpack(1, info, raw, one), ("y", "x", "c"), along_x[0] + along_y[1])
-    a_own, b_all, lift_i, lift_j, weights = stage_join(
-        info, gen_count, ref_count, one.reshape(NJ, D), two.reshape(NJ, D)
+    one = spread(stage_unpack(0, info, raw), "y")
+    two = spread(stage_unpack(1, info, raw, one), "x")
+    a_own, b_all = lax.optimization_barrier((one.reshape(NJ, D), two.reshape(NJ, D)))
+    a_other = lax.ppermute(a_own, "c", [(0, 1), (1, 0)])
+    k1a, high, mass, b_norms, lift_i, lift_j, weights = stage_cost_own(
+        info, gen_count, ref_count, a_own, b_all
     )
-    a_other = lax.ppermute(a_own, "c", [(0, 1), (1, 0)])
-    k1a, high, mass, b_norms = stage_cost_own(a_own, b_all, lift_i)
     k1b, k2, part = stage_cost_other(a_other, b_all, lift_i, high, mass, b_norms)
     k = (k1a, k1b, k2)
     part, g1 = stage_second(*k, spread(part, "x"), lift_j)
@@ -518,13 +522,10 @@
     part, g3 = stage_fourth(*k, spread(part, "x"), lift_j, g1)
     part = stage_fifth(*k, spread(part, ("y", "c")), lift_i, f2, g3)
     got = spread(part, ("x", "zl"))
-    pots, g4, share = call(last_body, (f32(4, 8, 128), f32(8, 128), f32(8, 8, 128)), [VMEM, VMEM])(got, weights)
+    outs = (f32(1, BLOCK),) * 4 + (f32(8, 8, 128),)
+    *pots, share = call(last_body, outs, [VMEM, VMEM])(got, weights)
     divergence = jnp.sum(spread(share, ("y", "c"))[:, 0, 0])
-
-    mine = lax.dynamic_index_in_dim(pots, x, 0, keepdims=False)
-    mine = lax.dynamic_slice_in_dim(mine.reshape(4, 256), 64 * (y % 2), BLOCK, 1)
-    ref_pot = lax.dynamic_slice_in_dim(g4.reshape(1024), x * BLOCK, BLOCK, 0)
-    return mine[0], ref_pot, mine[1], mine[2], divergence
+    return *(pot.reshape(BLOCK) for pot in pots), divergence
 
 
 def solution(mesh):

time: 156 us -> 152 us (0.974)
  blocking collectives: 98.6 us -> 117 us
  waiting for transfers between devices: 11.1 us -> 0.17 us
  starting transfers between devices: 22.4 us -> 12.5 us
    all_to_all x6 -> x8, blocking collectives: 64.4 us -> 83.1 us  [spread(): return lax.all_to_all(operand, axes, 0, 0, tiled=True)]
    all_to_all x2 -> x0, waiting for transfers between devices: 10.4 us -> none  [spread(): lax.all_to_all(operand, axes, 0, 0, tiled=True, axis_index_groups=groups)]
    all_to_all x2 -> x0, starting transfers between devices: 8.7 us -> none  [spread(): lax.all_to_all(operand, axes, 0, 0, tiled=True, axis_index_groups=groups)]
    pallas_call x3 -> x2, Pallas kernels: 3.8 us -> 3.5 us  [the longest x1 2.81 us: stage_cost_own(): return call(cost_own_body, outs, [SMEM] * 3 + [VMEM] * 2)(*args)]
  transfers between devices with their start and end apart: 3 -> 1, of which waited for: 3 -> 1; matrix products, arithmetic and copies ran while one was open for 1% -> 0% of each run, Pallas kernels for 1% -> 2%
where the time goes in v12:
time: 152 us; the launch traced here: 151 us
  blocking collectives  117 us (77%)
  Pallas kernels  19.9 us (13%)
  starting transfers between devices  12.5 us (8%)
    all_to_all x8, blocking collectives, spread(): return lax.all_to_all(operand, axes, 0, 0, tiled=True)  83.1 us
    all_gather x1, blocking collectives, local(): raw = lax.all_gather(packed, ('zh', 'zl'))  34.2 us
    ppermute x1, starting transfers between devices, local(): a_other = lax.ppermute(a_own, 'c', [(0, 1), (1, 0)])  12.5 us
    pallas_call x1, Pallas kernels, stage_cost_other(): call(cost_other_body, outs, [VMEM] * 6, scratch, (VMEM, HBM, VMEM))(*args)  3.15 us
  transfers between devices with their start and end apart: 1, of which 1 were waited for; matrix products, arithmetic and copies ran while one was open for 0% of the time, Pallas kernels for 2%

profile of v12, /device:TPU:1, one launch (start us, length us, event | category | flops | bytes accessed | tf_op | source)
XLA Modules:
  0.0 151.2 jit_solution(4582642347450966066)
XLA Ops:
  0.6 1.5 shard_map.83
  2.2 34.2 %all-gather = bf16[3072,128]{1,0:T(8,128)(2,1)S(1)} all-gather(bf16[192,128]{1,0:T(8,128)(2,1)} %shard_map.83), channel_id=2, replica_groups=mesh['y'=4,'x'=4,'c'=2,'zh'=4,'zl'=4] {'zh','zl'}, dimensions={0}, use_global_device_ids=true | all-gather | bytes 835584 | tf_op jit(solution)/shard_map/all_gather | solution.py:500
  36.3 0.1 stack.31.info
  36.4 1.0 shard_map.84
  37.4 16.6 %all_to_all.40.refs_0_ = bf16[4,192,1024]{2,1,0:T(8,128)(2,1)S(1)} all-to-all(bf16[4,192,1024]{2,1,0:T(8,128)(2,1)S(1)} %shard_map.84), channel_id=1, replica_groups=mesh['y'=4,'x'=4,'c'=2,'zh'=4,'zl'=4] {'y'}, dimensions={0} | all-to-all | bytes 3145728 | tf_op jit(solution)/shard_map/all_to_all | solution.py:492
  54.0 1.0 shard_map.85
  55.0 0.0 copy-start
  55.0 0.0 copy-start.1
  55.0 16.5 %all_to_all.41 = bf16[4,192,1024]{2,1,0:T(8,128)(2,1)S(1)} all-to-all(bf16[4,192,1024]{2,1,0:T(8,128)(2,1)S(1)} %shard_map.85), channel_id=1, replica_groups=mesh['y'=4,'x'=4,'c'=2,'zh'=4,'zl'=4] {'x'}, dimensions={0} | all-to-all | bytes 3145728 | tf_op jit(solution)/shard_map/all_to_all | solution.py:492
  71.5 12.5 %collective-permute-start = (bf16[768,1024]{1,0:T(8,128)(2,1)S(1)}, bf16[768,1024]{1,0:T(8,128)(2,1)S(1)}, u32[]{:S(2)}, u32[]{:S(2)}) collective-permute-start(bf16[768,1024]{1,0:T(8,128)(2,1)S(1)} %bitcast.16), channel_id=1, source_target_pairs={{0,16},{16,0},{1,17},{17,1},{2,18},{18,2},{3,19},{19,3},{4,20},{20... | collective-permute-start | bytes 4718600 | tf_op jit(solution)/shard_map/ppermute | solution.py:514
  84.0 0.0 copy-done
  84.0 0.0 copy-done.1
  84.0 2.8 %shard_map.86 = (f32[768,768]{1,0:T(8,128)S(1)}, f32[1,768,128]{2,1,0:T(8,128)S(1)}, f32[1,768,128]{2,1,0:T(8,128)S(1)}, f32[768,128]{1,0:T(8,128)S(1)}, f32[16,...) custom-call(s32[5]{0:T(128)S(1)} %stack.31.info, s32[32]{0:T(128)S(1)} %copy-done, s32[32]{0:T(128)S(1)} %copy-done.1, ...), custom_call_target="tpu_custom_call" | custom-call | tf_op jit(solution)/shard_map/pallas_call | solution.py:460
  86.9 0.2 collective-permute-done.a_ref
  87.0 3.1 %shard_map.87 = (f32[768,256]{1,0:T(8,128)S(1)}, f32[13824,512]{1,0:T(8,128)}, f32[4,8,128]{2,1,0:T(8,128)S(1)}) custom-call(bf16[768,1024]{1,0:T(8,128)(2,1)S(1)} %collective-permute-done.a_ref, bf16[768,1024]{1,0:T(8,128)(2,1)S(1)} %bitcast.15, f32[16,128]{1,0:T(8,128)S(1)} %get-tuple-element.31.lift_i, f32[1,768,128]{2,1,0:T(8,128)S(1)} %get-tuple-element.32.high_in, ...), custom_call_target="tpu_custom_call" | custom-call | tf_op jit(solution)/shard_map/pallas_call | solution.py:466
  90.2 6.6 %all_to_all.42.got = f32[4,8,128]{2,1,0:T(8,128)S(1)} all-to-all(f32[4,8,128]{2,1,0:T(8,128)S(1)} %get-tuple-element.37), channel_id=1, replica_groups=mesh['y'=4,'x'=4,'c'=2,'zh'=4,'zl'=4] {'x'}, dimensions={0} | all-to-all | bytes 32768 | tf_op jit(solution)/shard_map/all_to_all | solution.py:492
  96.8 2.8 %shard_map.88 = (f32[8,24,128]{2,1,0:T(8,128)S(1)}, f32[6,128]{1,0:T(8,128)S(1)}) custom-call(f32[768,768]{1,0:T(8,128)S(1)} %get-tuple-element.30.k1a_ref, f32[768,256]{1,0:T(8,128)S(1)} %get-tuple-element.35.k1b_ref, f32[13824,512]{1,0:T(8,128)} %get-tuple-element.36.k2_hbm, f32[4,8,128]{2,1,0:T(8,128)S(1)} %all_to_all.42.got, ...), custom_call_target="tpu_custom_call" | custom-call | tf_op jit(solution)/shard_map/pallas_call | solution.py:474
  99.6 8.9 %all_to_all.43.got = f32[8,24,128]{2,1,0:T(8,128)S(1)} all-to-all(f32[8,24,128]{2,1,0:T(8,128)S(1)} %get-tuple-element.39), channel_id=1, replica_groups=mesh['y'=4,'x'=4,'c'=2,'zh'=4,'zl'=4] {'y','c'}, dimensions={0} | all-to-all | bytes 196608 | tf_op jit(solution)/shard_map/all_to_all | solution.py:492
  108.4 2.3 %shard_map.89 = (f32[4,16,128]{2,1,0:T(8,128)S(1)}, f32[12,128]{1,0:T(8,128)S(1)}) custom-call(f32[768,768]{1,0:T(8,128)S(1)} %get-tuple-element.30.k1a_ref, f32[768,256]{1,0:T(8,128)S(1)} %get-tuple-element.35.k1b_ref, f32[13824,512]{1,0:T(8,128)} %get-tuple-element.36.k2_hbm, f32[8,24,128]{2,1,0:T(8,128)S(1)} %all_to_all.43.got, ...), custom_call_target="tpu_custom_call" | custom-call | tf_op jit(solution)/shard_map/pallas_call | solution.py:479
  110.8 6.7 %all_to_all.44.got = f32[4,16,128]{2,1,0:T(8,128)S(1)} all-to-all(f32[4,16,128]{2,1,0:T(8,128)S(1)} %get-tuple-element.40), channel_id=1, replica_groups=mesh['y'=4,'x'=4,'c'=2,'zh'=4,'zl'=4] {'x'}, dimensions={0} | all-to-all | bytes 65536 | tf_op jit(solution)/shard_map/all_to_all | solution.py:492
  117.4 2.8 %shard_map.90 = (f32[8,24,128]{2,1,0:T(8,128)S(1)}, f32[6,128]{1,0:T(8,128)S(1)}) custom-call(f32[768,768]{1,0:T(8,128)S(1)} %get-tuple-element.30.k1a_ref, f32[768,256]{1,0:T(8,128)S(1)} %get-tuple-element.35.k1b_ref, f32[13824,512]{1,0:T(8,128)} %get-tuple-element.36.k2_hbm, f32[4,16,128]{2,1,0:T(8,128)S(1)} %all_to_all.44.got, ...), custom_call_target="tpu_custom_call" | custom-call | tf_op jit(solution)/shard_map/pallas_call | solution.py:484
  120.2 9.3 %all_to_all.45.got = f32[8,24,128]{2,1,0:T(8,128)S(1)} all-to-all(f32[8,24,128]{2,1,0:T(8,128)S(1)} %get-tuple-element.42), channel_id=1, replica_groups=mesh['y'=4,'x'=4,'c'=2,'zh'=4,'zl'=4] {'y','c'}, dimensions={0} | all-to-all | bytes 196608 | tf_op jit(solution)/shard_map/all_to_all | solution.py:492
  129.6 1.8 %shard_map.91 = f32[16,8,128]{2,1,0:T(8,128)S(1)} custom-call(f32[768,768]{1,0:T(8,128)S(1)} %get-tuple-element.30.k1a_ref, f32[768,256]{1,0:T(8,128)S(1)} %get-tuple-element.35.k1b_ref, f32[13824,512]{1,0:T(8,128)} %get-tuple-element.36.k2_hbm, f32[8,24,128]{2,1,0:T(8,128)S(1)} %all_to_all.45.got, f32[16,128]{1,0:T(8,128)S(1)} %get-tuple-element.31.lift_i, ...), custom_call_target="tpu_custom_call" | custom-call | tf_op jit(solution)/shard_map/pallas_call | solution.py:488
  131.3 9.5 %all_to_all.46.got = f32[16,8,128]{2,1,0:T(8,128)S(1)} all-to-all(f32[16,8,128]{2,1,0:T(8,128)S(1)} %shard_map.91), channel_id=1, replica_groups=mesh['y'=4,'x'=4,'c'=2,'zh'=4,'zl'=4] {'x','zl'}, dimensions={0} | all-to-all | bytes 131072 | tf_op jit(solution)/shard_map/all_to_all | solution.py:492
  140.9 0.7 shard_map.92
  141.6 9.0 %all_to_all.47 = f32[8,8,128]{2,1,0:T(8,128)S(1)} all-to-all(f32[8,8,128]{2,1,0:T(8,128)S(1)} %get-tuple-element.50), channel_id=1, replica_groups=mesh['y'=4,'x'=4,'c'=2,'zh'=4,'zl'=4] {'y','c'}, dimensions={0} | all-to-all | bytes 65536 | tf_op jit(solution)/shard_map/all_to_all | solution.py:492
  150.6 0.6 slice_reduce_fusion
Async XLA Ops:
  55.0 29.0 %copy-start = (s32[32]{0:T(128)S(1)}, s32[32]{0:T(128)}, u32[]{:S(2)}) copy-start(s32[32]{0:T(128)} %gen_count.1) | copy-start | bytes 388
  55.0 29.0 %copy-start.1 = (s32[32]{0:T(128)S(1)}, s32[32]{0:T(128)}, u32[]{:S(2)}) copy-start(s32[32]{0:T(128)} %ref_count.1) | copy-start | bytes 388
  71.5 15.5 %collective-permute-start = (bf16[768,1024]{1,0:T(8,128)(2,1)S(1)}, bf16[768,1024]{1,0:T(8,128)(2,1)S(1)}, u32[]{:S(2)}, u32[]{:S(2)}) collective-permute-start(bf16[768,1024]{1,0:T(8,128)(2,1)S(1)} %bitcast.16), channel_id=1, source_target_pairs={{0,16},{16,0},{1,17},{17,1},{2,18},{18,2},{3,19},{19,3},{4,20},{20... | collective-permute-start | bytes 4718600 | tf_op jit(solution)/shard_map/ppermute | solution.py:514

commit v13 on v12

--- a/solution.py
+++ b/solution.py
@@ -21,6 +21,7 @@
 RJ = NJ // 128
 NEAR = 8
 N2 = NI - NEAR * 128
+UNPACK_MIB = 60
 ROOM = 18 * NJ
 
 VMEM = pl.BlockSpec(memory_space=pltpu.VMEM)
@@ -32,7 +33,7 @@
     return jax.ShapeDtypeStruct(shape, jnp.float32)
 
 
-def call(body, outs, ins, scratch=(), out_specs=None, mib=40):
+def call(body, outs, ins, scratch=(), out_specs=None, mib=40, cost=None):
     return pl.pallas_call(
         body,
         out_shape=outs,
@@ -40,6 +41,7 @@
         out_specs=jax.tree.map(lambda _: VMEM, outs) if out_specs is None else out_specs,
         scratch_shapes=list(scratch),
         compiler_params=pltpu.CompilerParams(vmem_limit_bytes=mib * 1024 * 1024),
+        cost_estimate=cost,
     )
 
 
@@ -451,13 +453,14 @@
 
 def stage_unpack(which, *args):
     out = jax.ShapeDtypeStruct((4, BLOCK, D), BF16)
-    return call(functools.partial(unpack_body, which), out, [SMEM, VMEM, HBM][: len(args)])(*args)
+    return call(functools.partial(unpack_body, which), out, [SMEM, VMEM, HBM][: len(args)], mib=(40, UNPACK_MIB)[which])(*args)
 
 
 def stage_cost_own(*args):
     outs = (f32(NJ, NI // 2), f32(1, NJ, 128), f32(1, NJ, 128), f32(NJ, 128))
     outs += (f32(16, 128), f32(8, 128), f32(24, 128))
-    return call(cost_own_body, outs, [SMEM] * 3 + [VMEM] * 2)(*args)
+    cost = pl.CostEstimate(flops=10**10, bytes_accessed=1, transcendentals=0)
+    return call(cost_own_body, outs, [SMEM] * 3 + [VMEM] * 2, cost=cost)(*args)
 
 
 def stage_cost_other(*args):
@@ -510,7 +513,7 @@
     ).astype(jnp.int32)
     one = spread(stage_unpack(0, info, raw), "y")
     two = spread(stage_unpack(1, info, raw, one), "x")
-    a_own, b_all = lax.optimization_barrier((one.reshape(NJ, D), two.reshape(NJ, D)))
+    a_own, b_all = one.reshape(NJ, D), two.reshape(NJ, D)
     a_other = lax.ppermute(a_own, "c", [(0, 1), (1, 0)])
     k1a, high, mass, b_norms, lift_i, lift_j, weights = stage_cost_own(
         info, gen_count, ref_count, a_own, b_all

time: 152 us -> 153 us (level)
  blocking collectives: 117 us -> 111 us
  Pallas kernels: 19.9 us -> 23 us
  starting transfers between devices: 12.5 us -> 15.5 us
    all_to_all x8 -> x7, blocking collectives: 83.1 us -> 76.9 us  [spread(): return lax.all_to_all(operand, axes, 0, 0, tiled=True)]
    all_to_all x0 -> x1, starting transfers between devices: none -> 4.16 us  [spread(): return lax.all_to_all(operand, axes, 0, 0, tiled=True)]
    pallas_call x2, Pallas kernels: 2.03 us -> 3.81 us  [stage_unpack(): call(functools.partial(unpack_body, which), out, [SMEM, VMEM, HBM][:len(a...]
  transfers between devices with their start and end apart: 1 -> 2, of which waited for: 1 -> 1; matrix products, arithmetic and copies ran while one was open for 0% -> 0% of each run, Pallas kernels for 2% -> 2%
where the time goes in v13:
time: 153 us; the launch traced here: 152 us
  blocking collectives  111 us (73%)
  Pallas kernels  23 us (15%)
  starting transfers between devices  15.5 us (10%)
    all_to_all x7, blocking collectives, spread(): return lax.all_to_all(operand, axes, 0, 0, tiled=True)  76.9 us
    all_gather x1, blocking collectives, local(): raw = lax.all_gather(packed, ('zh', 'zl'))  34.2 us
    ppermute x1, starting transfers between devices, local(): a_other = lax.ppermute(a_own, 'c', [(0, 1), (1, 0)])  11.3 us
    pallas_call x1, Pallas kernels, stage_cost_other(): call(cost_other_body, outs, [VMEM] * 6, scratch, (VMEM, HBM, VMEM))(*args)  4.56 us
    all_to_all x1, starting transfers between devices, spread(): return lax.all_to_all(operand, axes, 0, 0, tiled=True)  4.16 us
    pallas_call x2, Pallas kernels, stage_unpack(): call(functools.partial(unpack_body, which), out, [SMEM, VMEM, HBM][:len(a...  3.81 us
  transfers between devices with their start and end apart: 2, of which 1 were waited for; matrix products, arithmetic and copies ran while one was open for 0% of the time, Pallas kernels for 2%

profile of v13, /device:TPU:1, one launch (start us, length us, event | category | flops | bytes accessed | tf_op | source)
XLA Modules:
  0.0 152.3 jit_solution(14798966956692943845)
XLA Ops:
  0.6 1.5 shard_map.83
  2.2 34.2 %all-gather = bf16[3072,128]{1,0:T(8,128)(2,1)S(1)} all-gather(bf16[192,128]{1,0:T(8,128)(2,1)} %shard_map.83), channel_id=2, replica_groups=mesh['y'=4,'x'=4,'c'=2,'zh'=4,'zl'=4] {'zh','zl'}, dimensions={0}, use_global_device_ids=true | all-gather | bytes 835584 | tf_op jit(solution)/shard_map/all_gather | solution.py:503
  36.3 0.0 copy-start
  36.3 0.1 stack.31.info
  36.4 0.0 copy-start.2
  36.4 1.0 shard_map.84
  37.5 16.7 %all_to_all.40.refs_0_ = bf16[4,192,1024]{2,1,0:T(8,128)(2,1)} all-to-all(bf16[4,192,1024]{2,1,0:T(8,128)(2,1)S(1)} %shard_map.84), channel_id=1, replica_groups=mesh['y'=4,'x'=4,'c'=2,'zh'=4,'zl'=4] {'y'}, dimensions={0} | all-to-all | bytes 3145728 | tf_op jit(solution)/shard_map/all_to_all | solution.py:495
  54.1 0.0 copy-done
  54.1 0.0 copy-done.2
  54.1 2.8 %shard_map.85 = bf16[4,192,1024]{2,1,0:T(8,128)(2,1)} custom-call(s32[5]{0:T(128)} %copy-done.2, bf16[16,192,128]{2,1,0:T(8,128)(2,1)} %bitcast.15, bf16[4,192,1024]{2,1,0:T(8,128)(2,1)} %all_to_all.40.refs_0_), custom_call_target="tpu_custom_call" | custom-call | tf_op jit(solution)/shard_map/pallas_call | solution.py:456
  56.9 4.2 %all-to-all-start.1 = ((bf16[4,192,1024]{2,1,0:T(8,128)(2,1)}), bf16[4,192,1024]{2,1,0:T(8,128)(2,1)S(1)}, u32[]{:S(2)}, u32[]{:S(2)}) async-start(bf16[4,192,1024]{2,1,0:T(8,128)(2,1)} %shard_map.85), calls=%async_computation.1 | async-start | bytes 3145728 | tf_op jit(solution)/shard_map/all_to_all | solution.py:495
  61.1 0.0 copy-done.1
  61.1 11.3 %collective-permute-start = (bf16[768,1024]{1,0:T(8,128)(2,1)S(1)}, bf16[768,1024]{1,0:T(8,128)(2,1)}, u32[]{:S(2)}, u32[]{:S(2)}) collective-permute-start(bf16[768,1024]{1,0:T(8,128)(2,1)S(1)} %bitcast.18), channel_id=1, source_target_pairs={{0,16},{16,0},{1,17},{17,1},{2,18},{18,2},{3,19},{19,3},{4,20},{20... | collective-permute-start | bytes 4718600 | tf_op jit(solution)/shard_map/ppermute | solution.py:517
  72.4 1.2 all-to-all-done.1
  73.6 0.0 copy-done.3
  73.6 0.0 copy-done.4
  73.6 0.0 copy-done.5
  73.7 2.8 %shard_map.86 = (f32[768,768]{1,0:T(8,128)S(1)}, f32[1,768,128]{2,1,0:T(8,128)S(1)}, f32[1,768,128]{2,1,0:T(8,128)S(1)}, f32[768,128]{1,0:T(8,128)S(1)}, f32[16,...) custom-call(s32[5]{0:T(128)S(1)} %copy-done.3, s32[32]{0:T(128)S(1)} %copy-done.4, s32[32]{0:T(128)S(1)} %copy-done.5, ...), custom_call_target="tpu_custom_call" | custom-call | flops 10000000000 | bytes 1 | tf_op jit(solution)/shard_map/pallas_call | solution.py:463
  76.4 0.0 collective-permute-done.a_ref
  76.5 4.6 %shard_map.87 = (f32[768,256]{1,0:T(8,128)S(1)}, f32[13824,512]{1,0:T(8,128)}, f32[4,8,128]{2,1,0:T(8,128)S(1)}) custom-call(bf16[768,1024]{1,0:T(8,128)(2,1)} %collective-permute-done.a_ref, bf16[768,1024]{1,0:T(8,128)(2,1)S(1)} %bitcast.17, f32[16,128]{1,0:T(8,128)S(1)} %get-tuple-element.27.lift_i, f32[1,768,128]{2,1,0:T(8,128)S(1)} %get-tuple-element.28.high_in, ...), custom_call_target="tpu_custom_call" | custom-call | tf_op jit(solution)/shard_map/pallas_call | solution.py:469
  81.0 7.6 %all_to_all.41.got = f32[4,8,128]{2,1,0:T(8,128)S(1)} all-to-all(f32[4,8,128]{2,1,0:T(8,128)S(1)} %get-tuple-element.33), channel_id=1, replica_groups=mesh['y'=4,'x'=4,'c'=2,'zh'=4,'zl'=4] {'x'}, dimensions={0} | all-to-all | bytes 32768 | tf_op jit(solution)/shard_map/all_to_all | solution.py:495
  88.7 2.8 %shard_map.88 = (f32[8,24,128]{2,1,0:T(8,128)S(1)}, f32[6,128]{1,0:T(8,128)S(1)}) custom-call(f32[768,768]{1,0:T(8,128)S(1)} %get-tuple-element.26.k1a_ref, f32[768,256]{1,0:T(8,128)S(1)} %get-tuple-element.31.k1b_ref, f32[13824,512]{1,0:T(8,128)} %get-tuple-element.32.k2_hbm, f32[4,8,128]{2,1,0:T(8,128)S(1)} %all_to_all.41.got, ...), custom_call_target="tpu_custom_call" | custom-call | tf_op jit(solution)/shard_map/pallas_call | solution.py:477
  91.5 18.0 %all_to_all.42.got = f32[8,24,128]{2,1,0:T(8,128)S(1)} all-to-all(f32[8,24,128]{2,1,0:T(8,128)S(1)} %get-tuple-element.35), channel_id=1, replica_groups=mesh['y'=4,'x'=4,'c'=2,'zh'=4,'zl'=4] {'y','c'}, dimensions={0} | all-to-all | bytes 196608 | tf_op jit(solution)/shard_map/all_to_all | solution.py:495
  109.5 2.3 %shard_map.89 = (f32[4,16,128]{2,1,0:T(8,128)S(1)}, f32[12,128]{1,0:T(8,128)S(1)}) custom-call(f32[768,768]{1,0:T(8,128)S(1)} %get-tuple-element.26.k1a_ref, f32[768,256]{1,0:T(8,128)S(1)} %get-tuple-element.31.k1b_ref, f32[13824,512]{1,0:T(8,128)} %get-tuple-element.32.k2_hbm, f32[8,24,128]{2,1,0:T(8,128)S(1)} %all_to_all.42.got, ...), custom_call_target="tpu_custom_call" | custom-call | tf_op jit(solution)/shard_map/pallas_call | solution.py:482
  111.8 6.7 %all_to_all.43.got = f32[4,16,128]{2,1,0:T(8,128)S(1)} all-to-all(f32[4,16,128]{2,1,0:T(8,128)S(1)} %get-tuple-element.36), channel_id=1, replica_groups=mesh['y'=4,'x'=4,'c'=2,'zh'=4,'zl'=4] {'x'}, dimensions={0} | all-to-all | bytes 65536 | tf_op jit(solution)/shard_map/all_to_all | solution.py:495
  118.5 2.8 %shard_map.90 = (f32[8,24,128]{2,1,0:T(8,128)S(1)}, f32[6,128]{1,0:T(8,128)S(1)}) custom-call(f32[768,768]{1,0:T(8,128)S(1)} %get-tuple-element.26.k1a_ref, f32[768,256]{1,0:T(8,128)S(1)} %get-tuple-element.31.k1b_ref, f32[13824,512]{1,0:T(8,128)} %get-tuple-element.32.k2_hbm, f32[4,16,128]{2,1,0:T(8,128)S(1)} %all_to_all.43.got, ...), custom_call_target="tpu_custom_call" | custom-call | tf_op jit(solution)/shard_map/pallas_call | solution.py:487
  121.3 9.3 %all_to_all.44.got = f32[8,24,128]{2,1,0:T(8,128)S(1)} all-to-all(f32[8,24,128]{2,1,0:T(8,128)S(1)} %get-tuple-element.38), channel_id=1, replica_groups=mesh['y'=4,'x'=4,'c'=2,'zh'=4,'zl'=4] {'y','c'}, dimensions={0} | all-to-all | bytes 196608 | tf_op jit(solution)/shard_map/all_to_all | solution.py:495
  130.6 1.8 %shard_map.91 = f32[16,8,128]{2,1,0:T(8,128)S(1)} custom-call(f32[768,768]{1,0:T(8,128)S(1)} %get-tuple-element.26.k1a_ref, f32[768,256]{1,0:T(8,128)S(1)} %get-tuple-element.31.k1b_ref, f32[13824,512]{1,0:T(8,128)} %get-tuple-element.32.k2_hbm, f32[8,24,128]{2,1,0:T(8,128)S(1)} %all_to_all.44.got, f32[16,128]{1,0:T(8,128)S(1)} %get-tuple-element.27.lift_i, ...), custom_call_target="tpu_custom_call" | custom-call | tf_op jit(solution)/shard_map/pallas_call | solution.py:491
  132.4 9.5 %all_to_all.45.got = f32[16,8,128]{2,1,0:T(8,128)S(1)} all-to-all(f32[16,8,128]{2,1,0:T(8,128)S(1)} %shard_map.91), channel_id=1, replica_groups=mesh['y'=4,'x'=4,'c'=2,'zh'=4,'zl'=4] {'x','zl'}, dimensions={0} | all-to-all | bytes 131072 | tf_op jit(solution)/shard_map/all_to_all | solution.py:495
  141.9 0.7 shard_map.92
  142.6 9.0 %all_to_all.46 = f32[8,8,128]{2,1,0:T(8,128)S(1)} all-to-all(f32[8,8,128]{2,1,0:T(8,128)S(1)} %get-tuple-element.46), channel_id=1, replica_groups=mesh['y'=4,'x'=4,'c'=2,'zh'=4,'zl'=4] {'y','c'}, dimensions={0} | all-to-all | bytes 65536 | tf_op jit(solution)/shard_map/all_to_all | solution.py:495
  151.6 0.6 slice_reduce_fusion
  (4 shorter events, 0.0 us)
Async XLA Ops:
  36.3 17.8 %copy-start = (bf16[3072,128]{1,0:T(8,128)(2,1)}, bf16[3072,128]{1,0:T(8,128)(2,1)S(1)}, u32[]{:S(2)}) copy-start(bf16[3072,128]{1,0:T(8,128)(2,1)S(1)} %all-gather) | copy-start | bytes 2359300
  36.4 17.7 %copy-start.2 = (s32[5]{0:T(128)}, s32[5]{0:T(128)S(1)}, u32[]{:S(2)}) copy-start(s32[5]{0:T(128)S(1)} %stack.31.info) | copy-start | bytes 64
  56.9 4.2 %copy-start.1 = (bf16[4,192,1024]{2,1,0:T(8,128)(2,1)S(1)}, bf16[4,192,1024]{2,1,0:T(8,128)(2,1)}, u32[]{:S(2)}) copy-start(bf16[4,192,1024]{2,1,0:T(8,128)(2,1)} %all_to_all.40.refs_0_) | copy-start | bytes 4718596
  56.9 16.7 %copy-start.3 = (s32[5]{0:T(128)S(1)}, s32[5]{0:T(128)}, u32[]{:S(2)}) copy-start(s32[5]{0:T(128)} %copy-done.2) | copy-start | bytes 64
  56.9 16.7 %copy-start.4 = (s32[32]{0:T(128)S(1)}, s32[32]{0:T(128)}, u32[]{:S(2)}) copy-start(s32[32]{0:T(128)} %gen_count.1) | copy-start | bytes 388
  56.9 16.7 %copy-start.5 = (s32[32]{0:T(128)S(1)}, s32[32]{0:T(128)}, u32[]{:S(2)}) copy-start(s32[32]{0:T(128)} %ref_count.1) | copy-start | bytes 388
  56.9 16.7 %all-to-all-start.1 = ((bf16[4,192,1024]{2,1,0:T(8,128)(2,1)}), bf16[4,192,1024]{2,1,0:T(8,128)(2,1)S(1)}, u32[]{:S(2)}, u32[]{:S(2)}) async-start(bf16[4,192,1024]{2,1,0:T(8,128)(2,1)} %shard_map.85), calls=%async_computation.1 | async-start | bytes 3145728 | tf_op jit(solution)/shard_map/all_to_all | solution.py:495
  61.1 15.4 %collective-permute-start = (bf16[768,1024]{1,0:T(8,128)(2,1)S(1)}, bf16[768,1024]{1,0:T(8,128)(2,1)}, u32[]{:S(2)}, u32[]{:S(2)}) collective-permute-start(bf16[768,1024]{1,0:T(8,128)(2,1)S(1)} %bitcast.18), channel_id=1, source_target_pairs={{0,16},{16,0},{1,17},{17,1},{2,18},{18,2},{3,19},{19,3},{4,20},{20... | collective-permute-start | bytes 4718600 | tf_op jit(solution)/shard_map/ppermute | solution.py:517

commit v14 on v12

--- a/solution.py
+++ b/solution.py
@@ -71,20 +71,20 @@
         fetch(k2_hbm, k2_ref, sems, b).start()
 
 
-def lanes_block(tiles_of, count, heads, high_ref, mass_ref, base, joined=False):
+def lanes_block(tiles_of, count, heads, high_ref, mass_ref, base, before=None):
     for group in range(16):
         rows = pl.ds(base + group * 8, 8)
         tiles = tiles_of(rows)
         for v in range(count):
             xs = [heads[v][r : r + 1, :] - tile for r, tile in tiles]
             high = tree(jnp.maximum, xs)
-            if joined:
-                before = high_ref[v, rows, :]
-                high = jnp.maximum(high, before)
-                xs.append(before)
+            if before:
+                above = before[0][v, rows, :]
+                high = jnp.maximum(high, above)
+                xs.append(above)
             masses = [jnp.exp2(x - high) for x in xs]
-            if joined:
-                masses[-1] = masses[-1] * mass_ref[v, rows, :]
+            if before:
+                masses[-1] = masses[-1] * before[1][v, rows, :]
             high_ref[v, rows, :] = high
             mass_ref[v, rows, :] = tree(jnp.add, masses)
 
@@ -132,7 +132,8 @@
 
     def far(b, carry):
         fetch(k2_hbm, k2_ref, sems, b).wait()
-        lanes_block(far_tiles(k2_ref), count, heads, high_ref, mass_ref, pl.multiple_of(b * 128, 128), True)
+        start = pl.multiple_of(b * 128, 128)
+        lanes_block(far_tiles(k2_ref), count, heads, high_ref, mass_ref, start, (high_ref, mass_ref))
         return carry
 
     lax.fori_loop(0, RJ, near, 0)
@@ -140,10 +141,12 @@
     return lanes_result(count, high_ref, mass_ref)
 
 
-def reduce_rows(k1a_ref, k1b_ref, k2_hbm, k2_ref, sems, heads, head_ref, wide_ref, high_ref, mass_ref):
+def reduce_rows(k1a_ref, k1b_ref, k2_hbm, k2_ref, sems, heads, wide_ref, high_ref, mass_ref):
     count = len(heads)
     for v in range(count):
-        head_ref[v, 0:RJ, :] = heads[v]
+        for b in range(RJ):
+            row = jnp.broadcast_to(heads[v][b : b + 1, :], (128, 128))
+            wide_ref[v, b * 128 : (b + 1) * 128, :] = jnp.transpose(row)
 
     def block(b, wides, tile, r):
         spot = pl.ds(pl.multiple_of(b * 8, 8), 8)
@@ -156,10 +159,7 @@
             mass_ref[v, spot, cols] = tree(jnp.add, [jnp.exp2(x - high) for x in xs])
 
     def near(b, carry):
-        wides = []
-        for v in range(count):
-            wides.append(jnp.transpose(jnp.broadcast_to(head_ref[v, pl.ds(b, 1), :], (128, 128))))
-            wide_ref[v, pl.ds(pl.multiple_of(b * 128, 128), 128), :] = wides[v]
+        wides = [wide_ref[v, pl.ds(pl.multiple_of(b * 128, 128), 128), :] for v in range(count)]
         for r in range(NEAR):
             block(b, wides, lambda rows: near_tile(k1a_ref, k1b_ref, rows, r), r)
         return carry
@@ -196,16 +196,22 @@
     out[...] = jnp.transpose(wide).astype(jnp.bfloat16)
 
 
-def unpack_body(which, info, raw, *refs):
-    out = refs[-1]
+def unpack_body(info, raw, a_out, b_out):
     for k in range(D // 128):
         cols = slice(k * 128, (k + 1) * 128)
         even, odd = raw[2 * k], raw[2 * k + 1]
         gen = jnp.concatenate([even[:, :64], odd[:, :64]], axis=1)
         ref = jnp.concatenate([even[:, 64:], odd[:, 64:]], axis=1)
-        part = jnp.where(info[which] == 1, gen, ref)
+        a = jnp.where(info[0] == 1, gen, ref)
+        b_out[:, cols] = jnp.where(info[1] == 1, gen, ref)
         for n in range(4):
-            out[n, :, cols] = part
+            a_out[n, :, cols] = a
+
+
+def widen_body(own, a_half, out):
+    del a_half
+    for n in range(4):
+        out[n] = own[...]
 
 
 def norm_parts(values):
@@ -276,11 +282,11 @@
     return [(sq_ref[...] + norms[2 * n + s]) - scale * inner[:, s * 128 : (s + 1) * 128] for s in range(2)]
 
 
-def reduce_pair(head, source, at, high_ref, mass_ref, base, joined):
+def reduce_pair(head, source, at, high_ref, mass_ref, base, before):
     heads = [head[base : base + 2, :]]
     pair = lambda rows: [(s, source[rows, at + s * 128 : at + (s + 1) * 128]) for s in range(2)]
     for b in range(RJ):
-        lanes_block(pair, 1, heads, high_ref, mass_ref, b * 128, joined)
+        lanes_block(pair, 1, heads, high_ref, mass_ref, b * 128, before)
 
 
 def cost_own_body(
@@ -298,7 +304,8 @@
             for s, tile in enumerate(cost_tiles(a_ref, b_ref, sq_ref, norms, n)):
                 k1a_ref[:, (2 * n + s) * 128 : (2 * n + s + 1) * 128] = tile
         if n > 0:
-            reduce_pair(head, k1a_ref, (n - 1) * 256, high_ref, mass_ref, 2 * n - 2, n > 1)
+            before = (high_ref, mass_ref) if n > 1 else None
+            reduce_pair(head, k1a_ref, (n - 1) * 256, high_ref, mass_ref, 2 * n - 2, before)
 
 
 def cost_other_body(
@@ -306,8 +313,6 @@
 ):
     head = lift_i[...]
     norms = a_norms(a_ref)
-    high_ref[...] = high_in[...]
-    mass_ref[...] = mass_in[...]
     stores = [fetch(k2_ref, k2_hbm, out_sems, b) for b in range(RJ)]
     order = [1, 2, 0]
     for step in range(4):
@@ -319,7 +324,8 @@
         if step > 0:
             n = order[step - 1]
             source, at = (k1b_ref, 0) if n == 0 else (k2_ref, (n - 1) * 256)
-            reduce_pair(head, source, at, high_ref, mass_ref, RH + 2 * n, True)
+            before = (high_ref, mass_ref) if step > 1 else (high_in, mass_in)
+            reduce_pair(head, source, at, high_ref, mass_ref, RH + 2 * n, before)
         if step == 1:
             for store in stores:
                 store.start()
@@ -331,14 +337,14 @@
         store.wait()
 
 
-def second_body(k1a_ref, k1b_ref, k2_hbm, got, lift_j, out, g1_out, k2_ref, sems, head_ref, wide_ref, high_ref, mass_ref):
+def second_body(k1a_ref, k1b_ref, k2_hbm, got, lift_j, out, g1_out, k2_ref, sems, wide_ref, high_ref, mass_ref):
     core = lift_j[6:7, :]
     start_fetch(k2_hbm, k2_ref, sems)
     g1 = -merge(got, 4)[0:RJ, :]
     g1_out[...] = g1
     lift = lift_j[0:RJ, :]
     heads = [lift, lifted(g1, lift)]
-    results = reduce_rows(k1a_ref, k1b_ref, k2_hbm, k2_ref, sems, heads, head_ref, wide_ref, high_ref, mass_ref)
+    results = reduce_rows(k1a_ref, k1b_ref, k2_hbm, k2_ref, sems, heads, wide_ref, high_ref, mass_ref)
     sent = [turned(core, value) for value in results]
     for n in range(8):
         for v in range(2):
@@ -361,7 +367,7 @@
             out[n, v * 8 + RJ : v * 8 + 8, :] = jnp.zeros((8 - RJ, 128), jnp.float32)
 
 
-def fourth_body(k1a_ref, k1b_ref, k2_hbm, got, lift_j, g1, out, g3_out, k2_ref, sems, head_ref, wide_ref, high_ref, mass_ref):
+def fourth_body(k1a_ref, k1b_ref, k2_hbm, got, lift_j, g1, out, g3_out, k2_ref, sems, wide_ref, high_ref, mass_ref):
     core = lift_j[6:7, :]
     start_fetch(k2_hbm, k2_ref, sems)
     merged = -merge(got, 4)
@@ -370,7 +376,7 @@
     g3_out[...] = g3
     lift = lift_j[0:RJ, :]
     heads = [lifted(g2, lift), lifted(g3, lift)]
-    results = reduce_rows(k1a_ref, k1b_ref, k2_hbm, k2_ref, sems, heads, head_ref, wide_ref, high_ref, mass_ref)
+    results = reduce_rows(k1a_ref, k1b_ref, k2_hbm, k2_ref, sems, heads, wide_ref, high_ref, mass_ref)
     sent = [turned(core, value) for value in results]
     for n in range(8):
         for v in range(2):
@@ -440,7 +446,7 @@
 
 
 def row_scratch(count):
-    return [pltpu.VMEM((count, 8, 128), F32), pltpu.VMEM((count, NJ, 128), F32)] + [pltpu.VMEM((count, 8 * RJ, NI), F32)] * 2
+    return [pltpu.VMEM((count, NJ, 128), F32)] + [pltpu.VMEM((count, 8 * RJ, NI), F32)] * 2
 
 
 def stage_pack(*args):
@@ -449,9 +455,16 @@
     return call(pack_body, out, [HBM, HBM], scratch, mib=60)(*args)
 
 
-def stage_unpack(which, *args):
-    out = jax.ShapeDtypeStruct((4, BLOCK, D), BF16)
-    return call(functools.partial(unpack_body, which), out, [SMEM, VMEM, HBM][: len(args)])(*args)
+def bf16(*shape):
+    return jax.ShapeDtypeStruct(shape, BF16)
+
+
+def stage_unpack(*args):
+    return call(unpack_body, (bf16(4, BLOCK, D), bf16(BLOCK, D)), [SMEM, VMEM])(*args)
+
+
+def stage_widen(*args):
+    return call(widen_body, bf16(4, BLOCK, D), [VMEM, HBM])(*args)
 
 
 def stage_cost_own(*args):
@@ -508,8 +521,9 @@
             y,
         ]
     ).astype(jnp.int32)
-    one = spread(stage_unpack(0, info, raw), "y")
-    two = spread(stage_unpack(1, info, raw, one), "x")
+    a_wide, b_own = stage_unpack(info, raw)
+    one = spread(a_wide, "y")
+    two = spread(stage_widen(b_own, one), "x")
     a_own, b_all = lax.optimization_barrier((one.reshape(NJ, D), two.reshape(NJ, D)))
     a_other = lax.ppermute(a_own, "c", [(0, 1), (1, 0)])
     k1a, high, mass, b_norms, lift_i, lift_j, weights = stage_cost_own(

time: 152 us -> 150 us (0.987)
  no operation moved by 1% of the time
where the time goes in v14:
time: 150 us
  blocking collectives  117 us (78%)
  Pallas kernels  18.4 us (12%)
  starting transfers between devices  12.5 us (8%)
    all_to_all x8, blocking collectives, spread(): return lax.all_to_all(operand, axes, 0, 0, tiled=True)  82.9 us
    all_gather x1, blocking collectives, local(): raw = lax.all_gather(packed, ('zh', 'zl'))  34.2 us
    ppermute x1, starting transfers between devices, local(): a_other = lax.ppermute(a_own, 'c', [(0, 1), (1, 0)])  12.5 us
    pallas_call x1, Pallas kernels, stage_cost_other(): call(cost_other_body, outs, [VMEM] * 6, scratch, (VMEM, HBM, VMEM))(*args)  3.11 us
  transfers between devices with their start and end apart: 1, of which 1 were waited for; matrix products, arithmetic and copies ran while one was open for 0% of the time, Pallas kernels for 2%

profile of v14, /device:TPU:1, one launch (start us, length us, event | category | flops | bytes accessed | tf_op | source)
XLA Modules:
  0.0 149.6 jit_solution(4640572966653610007)
XLA Ops:
  0.6 1.5 %shard_map.83 = bf16[192,128]{1,0:T(8,128)(2,1)} custom-call(bf16[64,192]{1,0:T(8,128)(2,1)} %bitcast.19, bf16[64,192]{1,0:T(8,128)(2,1)} %bitcast.20), custom_call_target="tpu_custom_call" | custom-call | tf_op jit(solution)/shard_map/pallas_call | solution.py:455
  2.2 34.2 %all-gather = bf16[3072,128]{1,0:T(8,128)(2,1)S(1)} all-gather(bf16[192,128]{1,0:T(8,128)(2,1)} %shard_map.83), channel_id=2, replica_groups=mesh['y'=4,'x'=4,'c'=2,'zh'=4,'zl'=4] {'zh','zl'}, dimensions={0}, use_global_device_ids=true | all-gather | bytes 835584 | tf_op jit(solution)/shard_map/all_gather | solution.py:513
  36.3 0.1 stack.31.info
  36.4 1.1 shard_map.84
  37.5 16.6 %all_to_all.40.a_half = bf16[4,192,1024]{2,1,0:T(8,128)(2,1)S(1)} all-to-all(bf16[4,192,1024]{2,1,0:T(8,128)(2,1)S(1)} %get-tuple-element.30), channel_id=1, replica_groups=mesh['y'=4,'x'=4,'c'=2,'zh'=4,'zl'=4] {'y'}, dimensions={0} | all-to-all | bytes 3145728 | tf_op jit(solution)/shard_map/all_to_all | solution.py:505
  54.1 0.1 shard_map.85
  54.2 0.0 copy-start
  54.2 0.0 copy-start.1
  54.2 16.4 %all_to_all.41 = bf16[4,192,1024]{2,1,0:T(8,128)(2,1)S(1)} all-to-all(bf16[4,192,1024]{2,1,0:T(8,128)(2,1)S(1)} %shard_map.85), channel_id=1, replica_groups=mesh['y'=4,'x'=4,'c'=2,'zh'=4,'zl'=4] {'x'}, dimensions={0} | all-to-all | bytes 3145728 | tf_op jit(solution)/shard_map/all_to_all | solution.py:505
  70.6 12.5 %collective-permute-start = (bf16[768,1024]{1,0:T(8,128)(2,1)S(1)}, bf16[768,1024]{1,0:T(8,128)(2,1)S(1)}, u32[]{:S(2)}, u32[]{:S(2)}) collective-permute-start(bf16[768,1024]{1,0:T(8,128)(2,1)S(1)} %bitcast.14), channel_id=1, source_target_pairs={{0,16},{16,0},{1,17},{17,1},{2,18},{18,2},{3,19},{19,3},{4,20},{20... | collective-permute-start | bytes 4718600 | tf_op jit(solution)/shard_map/ppermute | solution.py:528
  83.1 0.0 copy-done
  83.1 0.0 copy-done.1
  83.1 2.8 %shard_map.86 = (f32[768,768]{1,0:T(8,128)S(1)}, f32[1,768,128]{2,1,0:T(8,128)S(1)}, f32[1,768,128]{2,1,0:T(8,128)S(1)}, f32[768,128]{1,0:T(8,128)S(1)}, f32[16,...) custom-call(s32[5]{0:T(128)S(1)} %stack.31.info, s32[32]{0:T(128)S(1)} %copy-done, s32[32]{0:T(128)S(1)} %copy-done.1, ...), custom_call_target="tpu_custom_call" | custom-call | tf_op jit(solution)/shard_map/pallas_call | solution.py:473
  85.9 0.2 collective-permute-done.a_ref
  86.1 3.1 %shard_map.87 = (f32[768,256]{1,0:T(8,128)S(1)}, f32[13824,512]{1,0:T(8,128)}, f32[4,8,128]{2,1,0:T(8,128)S(1)}) custom-call(bf16[768,1024]{1,0:T(8,128)(2,1)S(1)} %collective-permute-done.a_ref, bf16[768,1024]{1,0:T(8,128)(2,1)S(1)} %bitcast.17, f32[16,128]{1,0:T(8,128)S(1)} %get-tuple-element.35.lift_i, f32[1,768,128]{2,1,0:T(8,128)S(1)} %get-tuple-element.36.high_in, ...), custom_call_target="tpu_custom_call" | custom-call | tf_op jit(solution)/shard_map/pallas_call | solution.py:479
  89.2 6.6 %all_to_all.42.got = f32[4,8,128]{2,1,0:T(8,128)S(1)} all-to-all(f32[4,8,128]{2,1,0:T(8,128)S(1)} %get-tuple-element.41), channel_id=1, replica_groups=mesh['y'=4,'x'=4,'c'=2,'zh'=4,'zl'=4] {'x'}, dimensions={0} | all-to-all | bytes 32768 | tf_op jit(solution)/shard_map/all_to_all | solution.py:505
  95.8 2.5 %shard_map.88 = (f32[8,24,128]{2,1,0:T(8,128)S(1)}, f32[6,128]{1,0:T(8,128)S(1)}) custom-call(f32[768,768]{1,0:T(8,128)S(1)} %get-tuple-element.34.k1a_ref, f32[768,256]{1,0:T(8,128)S(1)} %get-tuple-element.39.k1b_ref, f32[13824,512]{1,0:T(8,128)} %get-tuple-element.40.k2_hbm, f32[4,8,128]{2,1,0:T(8,128)S(1)} %all_to_all.42.got, ...), custom_call_target="tpu_custom_call" | custom-call | tf_op jit(solution)/shard_map/pallas_call | solution.py:487
  98.2 8.9 %all_to_all.43.got = f32[8,24,128]{2,1,0:T(8,128)S(1)} all-to-all(f32[8,24,128]{2,1,0:T(8,128)S(1)} %get-tuple-element.43), channel_id=1, replica_groups=mesh['y'=4,'x'=4,'c'=2,'zh'=4,'zl'=4] {'y','c'}, dimensions={0} | all-to-all | bytes 196608 | tf_op jit(solution)/shard_map/all_to_all | solution.py:505
  107.1 2.3 %shard_map.89 = (f32[4,16,128]{2,1,0:T(8,128)S(1)}, f32[12,128]{1,0:T(8,128)S(1)}) custom-call(f32[768,768]{1,0:T(8,128)S(1)} %get-tuple-element.34.k1a_ref, f32[768,256]{1,0:T(8,128)S(1)} %get-tuple-element.39.k1b_ref, f32[13824,512]{1,0:T(8,128)} %get-tuple-element.40.k2_hbm, f32[8,24,128]{2,1,0:T(8,128)S(1)} %all_to_all.43.got, ...), custom_call_target="tpu_custom_call" | custom-call | tf_op jit(solution)/shard_map/pallas_call | solution.py:492
  109.5 6.7 %all_to_all.44.got = f32[4,16,128]{2,1,0:T(8,128)S(1)} all-to-all(f32[4,16,128]{2,1,0:T(8,128)S(1)} %get-tuple-element.44), channel_id=1, replica_groups=mesh['y'=4,'x'=4,'c'=2,'zh'=4,'zl'=4] {'x'}, dimensions={0} | all-to-all | bytes 65536 | tf_op jit(solution)/shard_map/all_to_all | solution.py:505
  116.1 2.5 %shard_map.90 = (f32[8,24,128]{2,1,0:T(8,128)S(1)}, f32[6,128]{1,0:T(8,128)S(1)}) custom-call(f32[768,768]{1,0:T(8,128)S(1)} %get-tuple-element.34.k1a_ref, f32[768,256]{1,0:T(8,128)S(1)} %get-tuple-element.39.k1b_ref, f32[13824,512]{1,0:T(8,128)} %get-tuple-element.40.k2_hbm, f32[4,16,128]{2,1,0:T(8,128)S(1)} %all_to_all.44.got, ...), custom_call_target="tpu_custom_call" | custom-call | tf_op jit(solution)/shard_map/pallas_call | solution.py:497
  118.6 9.3 %all_to_all.45.got = f32[8,24,128]{2,1,0:T(8,128)S(1)} all-to-all(f32[8,24,128]{2,1,0:T(8,128)S(1)} %get-tuple-element.46), channel_id=1, replica_groups=mesh['y'=4,'x'=4,'c'=2,'zh'=4,'zl'=4] {'y','c'}, dimensions={0} | all-to-all | bytes 196608 | tf_op jit(solution)/shard_map/all_to_all | solution.py:505
  128.0 1.8 %shard_map.91 = f32[16,8,128]{2,1,0:T(8,128)S(1)} custom-call(f32[768,768]{1,0:T(8,128)S(1)} %get-tuple-element.34.k1a_ref, f32[768,256]{1,0:T(8,128)S(1)} %get-tuple-element.39.k1b_ref, f32[13824,512]{1,0:T(8,128)} %get-tuple-element.40.k2_hbm, f32[8,24,128]{2,1,0:T(8,128)S(1)} %all_to_all.45.got, f32[16,128]{1,0:T(8,128)S(1)} %get-tuple-element.35.lift_i, ...), custom_call_target="tpu_custom_call" | custom-call | tf_op jit(solution)/shard_map/pallas_call | solution.py:501
  129.7 9.5 %all_to_all.46.got = f32[16,8,128]{2,1,0:T(8,128)S(1)} all-to-all(f32[16,8,128]{2,1,0:T(8,128)S(1)} %shard_map.91), channel_id=1, replica_groups=mesh['y'=4,'x'=4,'c'=2,'zh'=4,'zl'=4] {'x','zl'}, dimensions={0} | all-to-all | bytes 131072 | tf_op jit(solution)/shard_map/all_to_all | solution.py:505
  139.3 0.7 shard_map.92
  140.0 9.0 %all_to_all.47 = f32[8,8,128]{2,1,0:T(8,128)S(1)} all-to-all(f32[8,8,128]{2,1,0:T(8,128)S(1)} %get-tuple-element.54), channel_id=1, replica_groups=mesh['y'=4,'x'=4,'c'=2,'zh'=4,'zl'=4] {'y','c'}, dimensions={0} | all-to-all | bytes 65536 | tf_op jit(solution)/shard_map/all_to_all | solution.py:505
  149.0 0.6 slice_reduce_fusion
Async XLA Ops:
  54.2 28.9 %copy-start = (s32[32]{0:T(128)S(1)}, s32[32]{0:T(128)}, u32[]{:S(2)}) copy-start(s32[32]{0:T(128)} %gen_count.1) | copy-start | bytes 388
  54.2 28.9 %copy-start.1 = (s32[32]{0:T(128)S(1)}, s32[32]{0:T(128)}, u32[]{:S(2)}) copy-start(s32[32]{0:T(128)} %ref_count.1) | copy-start | bytes 388
  70.6 15.5 %collective-permute-start = (bf16[768,1024]{1,0:T(8,128)(2,1)S(1)}, bf16[768,1024]{1,0:T(8,128)(2,1)S(1)}, u32[]{:S(2)}, u32[]{:S(2)}) collective-permute-start(bf16[768,1024]{1,0:T(8,128)(2,1)S(1)} %bitcast.14), channel_id=1, source_target_pairs={{0,16},{16,0},{1,17},{17,1},{2,18},{18,2},{3,19},{19,3},{4,20},{20... | collective-permute-start | bytes 4718600 | tf_op jit(solution)/shard_map/ppermute | solution.py:528

commit v15 on v14

--- a/solution.py
+++ b/solution.py
@@ -136,8 +136,8 @@
         lanes_block(far_tiles(k2_ref), count, heads, high_ref, mass_ref, start, (high_ref, mass_ref))
         return carry
 
-    lax.fori_loop(0, RJ, near, 0)
-    lax.fori_loop(0, RJ, far, 0)
+    lax.fori_loop(0, RJ, near, 0, unroll=2)
+    lax.fori_loop(0, RJ, far, 0, unroll=2)
     return lanes_result(count, high_ref, mass_ref)
 
 
@@ -171,8 +171,8 @@
             block(b, wides, lambda rows: k2_ref[rows, (r - NEAR) * 128 : (r - NEAR + 1) * 128], r)
         return carry
 
-    lax.fori_loop(0, RJ, near, 0)
-    lax.fori_loop(0, RJ, far, 0)
+    lax.fori_loop(0, RJ, near, 0, unroll=2)
+    lax.fori_loop(0, RJ, far, 0, unroll=2)
     results = []
     for v in range(count):
         tops, totals = [], []

time: 150 us -> 150 us (level)
  no operation moved by 1% of the time
where the time goes in v15:
time: 150 us; the launch traced here: 149 us
  blocking collectives  117 us (78%)
  Pallas kernels  18 us (12%)
  starting transfers between devices  12.5 us (8%)
    all_to_all x8, blocking collectives, spread(): return lax.all_to_all(operand, axes, 0, 0, tiled=True)  82.9 us
    all_gather x1, blocking collectives, local(): raw = lax.all_gather(packed, ('zh', 'zl'))  34.2 us
    ppermute x1, starting transfers between devices, local(): a_other = lax.ppermute(a_own, 'c', [(0, 1), (1, 0)])  12.5 us
    pallas_call x1, Pallas kernels, stage_cost_other(): call(cost_other_body, outs, [VMEM] * 6, scratch, (VMEM, HBM, VMEM))(*args)  3.11 us
  transfers between devices with their start and end apart: 1, of which 1 were waited for; matrix products, arithmetic and copies ran while one was open for 0% of the time, Pallas kernels for 2%

profile of v15, /device:TPU:1, one launch (start us, length us, event | category | flops | bytes accessed | tf_op | source)
XLA Modules:
  0.0 149.2 jit_solution(15737103604149611191)
XLA Ops:
  0.6 1.5 %shard_map.83 = bf16[192,128]{1,0:T(8,128)(2,1)} custom-call(bf16[64,192]{1,0:T(8,128)(2,1)} %bitcast.19, bf16[64,192]{1,0:T(8,128)(2,1)} %bitcast.20), custom_call_target="tpu_custom_call" | custom-call | tf_op jit(solution)/shard_map/pallas_call | solution.py:455
  2.2 34.2 %all-gather = bf16[3072,128]{1,0:T(8,128)(2,1)S(1)} all-gather(bf16[192,128]{1,0:T(8,128)(2,1)} %shard_map.83), channel_id=2, replica_groups=mesh['y'=4,'x'=4,'c'=2,'zh'=4,'zl'=4] {'zh','zl'}, dimensions={0}, use_global_device_ids=true | all-gather | bytes 835584 | tf_op jit(solution)/shard_map/all_gather | solution.py:513
  36.3 0.1 stack.31.info
  36.4 1.1 shard_map.84
  37.5 16.6 %all_to_all.40.a_half = bf16[4,192,1024]{2,1,0:T(8,128)(2,1)S(1)} all-to-all(bf16[4,192,1024]{2,1,0:T(8,128)(2,1)S(1)} %get-tuple-element.30), channel_id=1, replica_groups=mesh['y'=4,'x'=4,'c'=2,'zh'=4,'zl'=4] {'y'}, dimensions={0} | all-to-all | bytes 3145728 | tf_op jit(solution)/shard_map/all_to_all | solution.py:505
  54.1 0.1 shard_map.85
  54.2 0.0 copy-start
  54.2 0.0 copy-start.1
  54.2 16.4 %all_to_all.41 = bf16[4,192,1024]{2,1,0:T(8,128)(2,1)S(1)} all-to-all(bf16[4,192,1024]{2,1,0:T(8,128)(2,1)S(1)} %shard_map.85), channel_id=1, replica_groups=mesh['y'=4,'x'=4,'c'=2,'zh'=4,'zl'=4] {'x'}, dimensions={0} | all-to-all | bytes 3145728 | tf_op jit(solution)/shard_map/all_to_all | solution.py:505
  70.6 12.5 %collective-permute-start = (bf16[768,1024]{1,0:T(8,128)(2,1)S(1)}, bf16[768,1024]{1,0:T(8,128)(2,1)S(1)}, u32[]{:S(2)}, u32[]{:S(2)}) collective-permute-start(bf16[768,1024]{1,0:T(8,128)(2,1)S(1)} %bitcast.14), channel_id=1, source_target_pairs={{0,16},{16,0},{1,17},{17,1},{2,18},{18,2},{3,19},{19,3},{4,20},{20... | collective-permute-start | bytes 4718600 | tf_op jit(solution)/shard_map/ppermute | solution.py:528
  83.1 0.0 copy-done
  83.1 0.0 copy-done.1
  83.1 2.8 %shard_map.86 = (f32[768,768]{1,0:T(8,128)S(1)}, f32[1,768,128]{2,1,0:T(8,128)S(1)}, f32[1,768,128]{2,1,0:T(8,128)S(1)}, f32[768,128]{1,0:T(8,128)S(1)}, f32[16,...) custom-call(s32[5]{0:T(128)S(1)} %stack.31.info, s32[32]{0:T(128)S(1)} %copy-done, s32[32]{0:T(128)S(1)} %copy-done.1, ...), custom_call_target="tpu_custom_call" | custom-call | tf_op jit(solution)/shard_map/pallas_call | solution.py:473
  85.9 0.2 collective-permute-done.a_ref
  86.1 3.1 %shard_map.87 = (f32[768,256]{1,0:T(8,128)S(1)}, f32[13824,512]{1,0:T(8,128)}, f32[4,8,128]{2,1,0:T(8,128)S(1)}) custom-call(bf16[768,1024]{1,0:T(8,128)(2,1)S(1)} %collective-permute-done.a_ref, bf16[768,1024]{1,0:T(8,128)(2,1)S(1)} %bitcast.17, f32[16,128]{1,0:T(8,128)S(1)} %get-tuple-element.35.lift_i, f32[1,768,128]{2,1,0:T(8,128)S(1)} %get-tuple-element.36.high_in, ...), custom_call_target="tpu_custom_call" | custom-call | tf_op jit(solution)/shard_map/pallas_call | solution.py:479
  89.2 6.6 %all_to_all.42.got = f32[4,8,128]{2,1,0:T(8,128)S(1)} all-to-all(f32[4,8,128]{2,1,0:T(8,128)S(1)} %get-tuple-element.41), channel_id=1, replica_groups=mesh['y'=4,'x'=4,'c'=2,'zh'=4,'zl'=4] {'x'}, dimensions={0} | all-to-all | bytes 32768 | tf_op jit(solution)/shard_map/all_to_all | solution.py:505
  95.8 2.3 %shard_map.88 = (f32[8,24,128]{2,1,0:T(8,128)S(1)}, f32[6,128]{1,0:T(8,128)S(1)}) custom-call(f32[768,768]{1,0:T(8,128)S(1)} %get-tuple-element.34.k1a_ref, f32[768,256]{1,0:T(8,128)S(1)} %get-tuple-element.39.k1b_ref, f32[13824,512]{1,0:T(8,128)} %get-tuple-element.40.k2_hbm, f32[4,8,128]{2,1,0:T(8,128)S(1)} %all_to_all.42.got, ...), custom_call_target="tpu_custom_call" | custom-call | tf_op jit(solution)/shard_map/pallas_call | solution.py:487
  98.1 8.9 %all_to_all.43.got = f32[8,24,128]{2,1,0:T(8,128)S(1)} all-to-all(f32[8,24,128]{2,1,0:T(8,128)S(1)} %get-tuple-element.43), channel_id=1, replica_groups=mesh['y'=4,'x'=4,'c'=2,'zh'=4,'zl'=4] {'y','c'}, dimensions={0} | all-to-all | bytes 196608 | tf_op jit(solution)/shard_map/all_to_all | solution.py:505
  106.9 2.3 %shard_map.89 = (f32[4,16,128]{2,1,0:T(8,128)S(1)}, f32[12,128]{1,0:T(8,128)S(1)}) custom-call(f32[768,768]{1,0:T(8,128)S(1)} %get-tuple-element.34.k1a_ref, f32[768,256]{1,0:T(8,128)S(1)} %get-tuple-element.39.k1b_ref, f32[13824,512]{1,0:T(8,128)} %get-tuple-element.40.k2_hbm, f32[8,24,128]{2,1,0:T(8,128)S(1)} %all_to_all.43.got, ...), custom_call_target="tpu_custom_call" | custom-call | tf_op jit(solution)/shard_map/pallas_call | solution.py:492
  109.3 6.7 %all_to_all.44.got = f32[4,16,128]{2,1,0:T(8,128)S(1)} all-to-all(f32[4,16,128]{2,1,0:T(8,128)S(1)} %get-tuple-element.44), channel_id=1, replica_groups=mesh['y'=4,'x'=4,'c'=2,'zh'=4,'zl'=4] {'x'}, dimensions={0} | all-to-all | bytes 65536 | tf_op jit(solution)/shard_map/all_to_all | solution.py:505
  115.9 2.3 %shard_map.90 = (f32[8,24,128]{2,1,0:T(8,128)S(1)}, f32[6,128]{1,0:T(8,128)S(1)}) custom-call(f32[768,768]{1,0:T(8,128)S(1)} %get-tuple-element.34.k1a_ref, f32[768,256]{1,0:T(8,128)S(1)} %get-tuple-element.39.k1b_ref, f32[13824,512]{1,0:T(8,128)} %get-tuple-element.40.k2_hbm, f32[4,16,128]{2,1,0:T(8,128)S(1)} %all_to_all.44.got, ...), custom_call_target="tpu_custom_call" | custom-call | tf_op jit(solution)/shard_map/pallas_call | solution.py:497
  118.2 9.3 %all_to_all.45.got = f32[8,24,128]{2,1,0:T(8,128)S(1)} all-to-all(f32[8,24,128]{2,1,0:T(8,128)S(1)} %get-tuple-element.46), channel_id=1, replica_groups=mesh['y'=4,'x'=4,'c'=2,'zh'=4,'zl'=4] {'y','c'}, dimensions={0} | all-to-all | bytes 196608 | tf_op jit(solution)/shard_map/all_to_all | solution.py:505
  127.6 1.8 %shard_map.91 = f32[16,8,128]{2,1,0:T(8,128)S(1)} custom-call(f32[768,768]{1,0:T(8,128)S(1)} %get-tuple-element.34.k1a_ref, f32[768,256]{1,0:T(8,128)S(1)} %get-tuple-element.39.k1b_ref, f32[13824,512]{1,0:T(8,128)} %get-tuple-element.40.k2_hbm, f32[8,24,128]{2,1,0:T(8,128)S(1)} %all_to_all.45.got, f32[16,128]{1,0:T(8,128)S(1)} %get-tuple-element.35.lift_i, ...), custom_call_target="tpu_custom_call" | custom-call | tf_op jit(solution)/shard_map/pallas_call | solution.py:501
  129.3 9.5 %all_to_all.46.got = f32[16,8,128]{2,1,0:T(8,128)S(1)} all-to-all(f32[16,8,128]{2,1,0:T(8,128)S(1)} %shard_map.91), channel_id=1, replica_groups=mesh['y'=4,'x'=4,'c'=2,'zh'=4,'zl'=4] {'x','zl'}, dimensions={0} | all-to-all | bytes 131072 | tf_op jit(solution)/shard_map/all_to_all | solution.py:505
  138.9 0.7 shard_map.92
  139.6 9.0 %all_to_all.47 = f32[8,8,128]{2,1,0:T(8,128)S(1)} all-to-all(f32[8,8,128]{2,1,0:T(8,128)S(1)} %get-tuple-element.54), channel_id=1, replica_groups=mesh['y'=4,'x'=4,'c'=2,'zh'=4,'zl'=4] {'y','c'}, dimensions={0} | all-to-all | bytes 65536 | tf_op jit(solution)/shard_map/all_to_all | solution.py:505
  148.6 0.6 slice_reduce_fusion
Async XLA Ops:
  54.2 28.9 %copy-start = (s32[32]{0:T(128)S(1)}, s32[32]{0:T(128)}, u32[]{:S(2)}) copy-start(s32[32]{0:T(128)} %gen_count.1) | copy-start | bytes 388
  54.2 28.9 %copy-start.1 = (s32[32]{0:T(128)S(1)}, s32[32]{0:T(128)}, u32[]{:S(2)}) copy-start(s32[32]{0:T(128)} %ref_count.1) | copy-start | bytes 388
  70.6 15.5 %collective-permute-start = (bf16[768,1024]{1,0:T(8,128)(2,1)S(1)}, bf16[768,1024]{1,0:T(8,128)(2,1)S(1)}, u32[]{:S(2)}, u32[]{:S(2)}) collective-permute-start(bf16[768,1024]{1,0:T(8,128)(2,1)S(1)} %bitcast.14), channel_id=1, source_target_pairs={{0,16},{16,0},{1,17},{17,1},{2,18},{18,2},{3,19},{19,3},{4,20},{20... | collective-permute-start | bytes 4718600 | tf_op jit(solution)/shard_map/ppermute | solution.py:528

commit v16 on v15

--- a/solution.py
+++ b/solution.py
@@ -171,8 +171,8 @@
             block(b, wides, lambda rows: k2_ref[rows, (r - NEAR) * 128 : (r - NEAR + 1) * 128], r)
         return carry
 
-    lax.fori_loop(0, RJ, near, 0, unroll=2)
-    lax.fori_loop(0, RJ, far, 0, unroll=2)
+    lax.fori_loop(0, RJ, near, 0, unroll=3)
+    lax.fori_loop(0, RJ, far, 0, unroll=3)
     results = []
     for v in range(count):
         tops, totals = [], []

time: 150 us -> 150 us (level)
  no operation moved by 1% of the time
where the time goes in v16:
time: 150 us; the launch traced here: 149 us
  blocking collectives  117 us (78%)
  Pallas kernels  18.2 us (12%)
  starting transfers between devices  12.5 us (8%)
    all_to_all x8, blocking collectives, spread(): return lax.all_to_all(operand, axes, 0, 0, tiled=True)  82.9 us
    all_gather x1, blocking collectives, local(): raw = lax.all_gather(packed, ('zh', 'zl'))  34.2 us
    ppermute x1, starting transfers between devices, local(): a_other = lax.ppermute(a_own, 'c', [(0, 1), (1, 0)])  12.5 us
    pallas_call x1, Pallas kernels, stage_cost_other(): call(cost_other_body, outs, [VMEM] * 6, scratch, (VMEM, HBM, VMEM))(*args)  3.11 us
  transfers between devices with their start and end apart: 1, of which 1 were waited for; matrix products, arithmetic and copies ran while one was open for 0% of the time, Pallas kernels for 2%

profile of v16, /device:TPU:1, one launch (start us, length us, event | category | flops | bytes accessed | tf_op | source)
XLA Modules:
  0.0 149.4 jit_solution(39996615568974595)
XLA Ops:
  0.6 1.5 %shard_map.83 = bf16[192,128]{1,0:T(8,128)(2,1)} custom-call(bf16[64,192]{1,0:T(8,128)(2,1)} %bitcast.19, bf16[64,192]{1,0:T(8,128)(2,1)} %bitcast.20), custom_call_target="tpu_custom_call" | custom-call | tf_op jit(solution)/shard_map/pallas_call | solution.py:455
  2.2 34.2 %all-gather = bf16[3072,128]{1,0:T(8,128)(2,1)S(1)} all-gather(bf16[192,128]{1,0:T(8,128)(2,1)} %shard_map.83), channel_id=2, replica_groups=mesh['y'=4,'x'=4,'c'=2,'zh'=4,'zl'=4] {'zh','zl'}, dimensions={0}, use_global_device_ids=true | all-gather | bytes 835584 | tf_op jit(solution)/shard_map/all_gather | solution.py:513
  36.3 0.1 stack.31.info
  36.4 1.1 shard_map.84
  37.5 16.6 %all_to_all.40.a_half = bf16[4,192,1024]{2,1,0:T(8,128)(2,1)S(1)} all-to-all(bf16[4,192,1024]{2,1,0:T(8,128)(2,1)S(1)} %get-tuple-element.30), channel_id=1, replica_groups=mesh['y'=4,'x'=4,'c'=2,'zh'=4,'zl'=4] {'y'}, dimensions={0} | all-to-all | bytes 3145728 | tf_op jit(solution)/shard_map/all_to_all | solution.py:505
  54.1 0.1 shard_map.85
  54.2 0.0 copy-start
  54.2 0.0 copy-start.1
  54.2 16.4 %all_to_all.41 = bf16[4,192,1024]{2,1,0:T(8,128)(2,1)S(1)} all-to-all(bf16[4,192,1024]{2,1,0:T(8,128)(2,1)S(1)} %shard_map.85), channel_id=1, replica_groups=mesh['y'=4,'x'=4,'c'=2,'zh'=4,'zl'=4] {'x'}, dimensions={0} | all-to-all | bytes 3145728 | tf_op jit(solution)/shard_map/all_to_all | solution.py:505
  70.6 12.5 %collective-permute-start = (bf16[768,1024]{1,0:T(8,128)(2,1)S(1)}, bf16[768,1024]{1,0:T(8,128)(2,1)S(1)}, u32[]{:S(2)}, u32[]{:S(2)}) collective-permute-start(bf16[768,1024]{1,0:T(8,128)(2,1)S(1)} %bitcast.14), channel_id=1, source_target_pairs={{0,16},{16,0},{1,17},{17,1},{2,18},{18,2},{3,19},{19,3},{4,20},{20... | collective-permute-start | bytes 4718600 | tf_op jit(solution)/shard_map/ppermute | solution.py:528
  83.1 0.0 copy-done
  83.1 0.0 copy-done.1
  83.1 2.8 %shard_map.86 = (f32[768,768]{1,0:T(8,128)S(1)}, f32[1,768,128]{2,1,0:T(8,128)S(1)}, f32[1,768,128]{2,1,0:T(8,128)S(1)}, f32[768,128]{1,0:T(8,128)S(1)}, f32[16,...) custom-call(s32[5]{0:T(128)S(1)} %stack.31.info, s32[32]{0:T(128)S(1)} %copy-done, s32[32]{0:T(128)S(1)} %copy-done.1, ...), custom_call_target="tpu_custom_call" | custom-call | tf_op jit(solution)/shard_map/pallas_call | solution.py:473
  85.9 0.2 collective-permute-done.a_ref
  86.1 3.1 %shard_map.87 = (f32[768,256]{1,0:T(8,128)S(1)}, f32[13824,512]{1,0:T(8,128)}, f32[4,8,128]{2,1,0:T(8,128)S(1)}) custom-call(bf16[768,1024]{1,0:T(8,128)(2,1)S(1)} %collective-permute-done.a_ref, bf16[768,1024]{1,0:T(8,128)(2,1)S(1)} %bitcast.17, f32[16,128]{1,0:T(8,128)S(1)} %get-tuple-element.35.lift_i, f32[1,768,128]{2,1,0:T(8,128)S(1)} %get-tuple-element.36.high_in, ...), custom_call_target="tpu_custom_call" | custom-call | tf_op jit(solution)/shard_map/pallas_call | solution.py:479
  89.2 6.6 %all_to_all.42.got = f32[4,8,128]{2,1,0:T(8,128)S(1)} all-to-all(f32[4,8,128]{2,1,0:T(8,128)S(1)} %get-tuple-element.41), channel_id=1, replica_groups=mesh['y'=4,'x'=4,'c'=2,'zh'=4,'zl'=4] {'x'}, dimensions={0} | all-to-all | bytes 32768 | tf_op jit(solution)/shard_map/all_to_all | solution.py:505
  95.8 2.4 %shard_map.88 = (f32[8,24,128]{2,1,0:T(8,128)S(1)}, f32[6,128]{1,0:T(8,128)S(1)}) custom-call(f32[768,768]{1,0:T(8,128)S(1)} %get-tuple-element.34.k1a_ref, f32[768,256]{1,0:T(8,128)S(1)} %get-tuple-element.39.k1b_ref, f32[13824,512]{1,0:T(8,128)} %get-tuple-element.40.k2_hbm, f32[4,8,128]{2,1,0:T(8,128)S(1)} %all_to_all.42.got, ...), custom_call_target="tpu_custom_call" | custom-call | tf_op jit(solution)/shard_map/pallas_call | solution.py:487
  98.2 8.9 %all_to_all.43.got = f32[8,24,128]{2,1,0:T(8,128)S(1)} all-to-all(f32[8,24,128]{2,1,0:T(8,128)S(1)} %get-tuple-element.43), channel_id=1, replica_groups=mesh['y'=4,'x'=4,'c'=2,'zh'=4,'zl'=4] {'y','c'}, dimensions={0} | all-to-all | bytes 196608 | tf_op jit(solution)/shard_map/all_to_all | solution.py:505
  107.0 2.3 %shard_map.89 = (f32[4,16,128]{2,1,0:T(8,128)S(1)}, f32[12,128]{1,0:T(8,128)S(1)}) custom-call(f32[768,768]{1,0:T(8,128)S(1)} %get-tuple-element.34.k1a_ref, f32[768,256]{1,0:T(8,128)S(1)} %get-tuple-element.39.k1b_ref, f32[13824,512]{1,0:T(8,128)} %get-tuple-element.40.k2_hbm, f32[8,24,128]{2,1,0:T(8,128)S(1)} %all_to_all.43.got, ...), custom_call_target="tpu_custom_call" | custom-call | tf_op jit(solution)/shard_map/pallas_call | solution.py:492
  109.3 6.7 %all_to_all.44.got = f32[4,16,128]{2,1,0:T(8,128)S(1)} all-to-all(f32[4,16,128]{2,1,0:T(8,128)S(1)} %get-tuple-element.44), channel_id=1, replica_groups=mesh['y'=4,'x'=4,'c'=2,'zh'=4,'zl'=4] {'x'}, dimensions={0} | all-to-all | bytes 65536 | tf_op jit(solution)/shard_map/all_to_all | solution.py:505
  116.0 2.4 %shard_map.90 = (f32[8,24,128]{2,1,0:T(8,128)S(1)}, f32[6,128]{1,0:T(8,128)S(1)}) custom-call(f32[768,768]{1,0:T(8,128)S(1)} %get-tuple-element.34.k1a_ref, f32[768,256]{1,0:T(8,128)S(1)} %get-tuple-element.39.k1b_ref, f32[13824,512]{1,0:T(8,128)} %get-tuple-element.40.k2_hbm, f32[4,16,128]{2,1,0:T(8,128)S(1)} %all_to_all.44.got, ...), custom_call_target="tpu_custom_call" | custom-call | tf_op jit(solution)/shard_map/pallas_call | solution.py:497
  118.4 9.3 %all_to_all.45.got = f32[8,24,128]{2,1,0:T(8,128)S(1)} all-to-all(f32[8,24,128]{2,1,0:T(8,128)S(1)} %get-tuple-element.46), channel_id=1, replica_groups=mesh['y'=4,'x'=4,'c'=2,'zh'=4,'zl'=4] {'y','c'}, dimensions={0} | all-to-all | bytes 196608 | tf_op jit(solution)/shard_map/all_to_all | solution.py:505
  127.7 1.8 %shard_map.91 = f32[16,8,128]{2,1,0:T(8,128)S(1)} custom-call(f32[768,768]{1,0:T(8,128)S(1)} %get-tuple-element.34.k1a_ref, f32[768,256]{1,0:T(8,128)S(1)} %get-tuple-element.39.k1b_ref, f32[13824,512]{1,0:T(8,128)} %get-tuple-element.40.k2_hbm, f32[8,24,128]{2,1,0:T(8,128)S(1)} %all_to_all.45.got, f32[16,128]{1,0:T(8,128)S(1)} %get-tuple-element.35.lift_i, ...), custom_call_target="tpu_custom_call" | custom-call | tf_op jit(solution)/shard_map/pallas_call | solution.py:501
  129.5 9.5 %all_to_all.46.got = f32[16,8,128]{2,1,0:T(8,128)S(1)} all-to-all(f32[16,8,128]{2,1,0:T(8,128)S(1)} %shard_map.91), channel_id=1, replica_groups=mesh['y'=4,'x'=4,'c'=2,'zh'=4,'zl'=4] {'x','zl'}, dimensions={0} | all-to-all | bytes 131072 | tf_op jit(solution)/shard_map/all_to_all | solution.py:505
  139.0 0.7 shard_map.92
  139.7 9.0 %all_to_all.47 = f32[8,8,128]{2,1,0:T(8,128)S(1)} all-to-all(f32[8,8,128]{2,1,0:T(8,128)S(1)} %get-tuple-element.54), channel_id=1, replica_groups=mesh['y'=4,'x'=4,'c'=2,'zh'=4,'zl'=4] {'y','c'}, dimensions={0} | all-to-all | bytes 65536 | tf_op jit(solution)/shard_map/all_to_all | solution.py:505
  148.8 0.6 slice_reduce_fusion
Async XLA Ops:
  54.2 28.9 %copy-start = (s32[32]{0:T(128)S(1)}, s32[32]{0:T(128)}, u32[]{:S(2)}) copy-start(s32[32]{0:T(128)} %gen_count.1) | copy-start | bytes 388
  54.2 28.9 %copy-start.1 = (s32[32]{0:T(128)S(1)}, s32[32]{0:T(128)}, u32[]{:S(2)}) copy-start(s32[32]{0:T(128)} %ref_count.1) | copy-start | bytes 388
  70.6 15.5 %collective-permute-start = (bf16[768,1024]{1,0:T(8,128)(2,1)S(1)}, bf16[768,1024]{1,0:T(8,128)(2,1)S(1)}, u32[]{:S(2)}, u32[]{:S(2)}) collective-permute-start(bf16[768,1024]{1,0:T(8,128)(2,1)S(1)} %bitcast.14), channel_id=1, source_target_pairs={{0,16},{16,0},{1,17},{17,1},{2,18},{18,2},{3,19},{19,3},{4,20},{20... | collective-permute-start | bytes 4718600 | tf_op jit(solution)/shard_map/ppermute | solution.py:528

commit v17 on v15

--- a/solution.py
+++ b/solution.py
@@ -412,7 +412,7 @@
         weight = weights[8 + 2 * n : 8 + 2 * n + 2, :]
         total -= jnp.sum(jnp.where(weight > 0.0, own[2][n] * weight, 0.0))
     for n in range(8):
-        share[n, :, :] = jnp.full((8, 128), total, jnp.float32)
+        share[n, :, :] = jnp.full((1, 128), total, jnp.float32)
 
     along_x, odd_y = weights[22:23, :], weights[23:24, :]
     low = lax.broadcasted_iota(jnp.int32, (1, 128), 1) < 64
@@ -536,7 +536,7 @@
     part, g3 = stage_fourth(*k, spread(part, "x"), lift_j, g1)
     part = stage_fifth(*k, spread(part, ("y", "c")), lift_i, f2, g3)
     got = spread(part, ("x", "zl"))
-    outs = (f32(1, BLOCK),) * 4 + (f32(8, 8, 128),)
+    outs = (f32(1, BLOCK),) * 4 + (f32(8, 1, 128),)
     *pots, share = call(last_body, outs, [VMEM, VMEM])(got, weights)
     divergence = jnp.sum(spread(share, ("y", "c"))[:, 0, 0])
     return *(pot.reshape(BLOCK) for pot in pots), divergence

time: 150 us -> 150 us (level)
  no operation moved by 1% of the time
where the time goes in v17:
time: 150 us; the launch traced here: 149 us
  blocking collectives  117 us (78%)
  Pallas kernels  18 us (12%)
  starting transfers between devices  12.5 us (8%)
    all_to_all x8, blocking collectives, spread(): return lax.all_to_all(operand, axes, 0, 0, tiled=True)  82.8 us
    all_gather x1, blocking collectives, local(): raw = lax.all_gather(packed, ('zh', 'zl'))  34.2 us
    ppermute x1, starting transfers between devices, local(): a_other = lax.ppermute(a_own, 'c', [(0, 1), (1, 0)])  12.5 us
    pallas_call x1, Pallas kernels, stage_cost_other(): call(cost_other_body, outs, [VMEM] * 6, scratch, (VMEM, HBM, VMEM))(*args)  3.11 us
  transfers between devices with their start and end apart: 1, of which 1 were waited for; matrix products, arithmetic and copies ran while one was open for 0% of the time, Pallas kernels for 2%

profile of v17, /device:TPU:1, one launch (start us, length us, event | category | flops | bytes accessed | tf_op | source)
XLA Modules:
  0.0 149.1 jit_solution(7690321316833841571)
XLA Ops:
  0.6 1.5 %shard_map.83 = bf16[192,128]{1,0:T(8,128)(2,1)} custom-call(bf16[64,192]{1,0:T(8,128)(2,1)} %bitcast.19, bf16[64,192]{1,0:T(8,128)(2,1)} %bitcast.20), custom_call_target="tpu_custom_call" | custom-call | tf_op jit(solution)/shard_map/pallas_call | solution.py:455
  2.2 34.2 %all-gather = bf16[3072,128]{1,0:T(8,128)(2,1)S(1)} all-gather(bf16[192,128]{1,0:T(8,128)(2,1)} %shard_map.83), channel_id=2, replica_groups=mesh['y'=4,'x'=4,'c'=2,'zh'=4,'zl'=4] {'zh','zl'}, dimensions={0}, use_global_device_ids=true | all-gather | bytes 835584 | tf_op jit(solution)/shard_map/all_gather | solution.py:513
  36.3 0.1 stack.31.info
  36.4 1.1 shard_map.84
  37.5 16.6 %all_to_all.40.a_half = bf16[4,192,1024]{2,1,0:T(8,128)(2,1)S(1)} all-to-all(bf16[4,192,1024]{2,1,0:T(8,128)(2,1)S(1)} %get-tuple-element.30), channel_id=1, replica_groups=mesh['y'=4,'x'=4,'c'=2,'zh'=4,'zl'=4] {'y'}, dimensions={0} | all-to-all | bytes 3145728 | tf_op jit(solution)/shard_map/all_to_all | solution.py:505
  54.1 0.1 shard_map.85
  54.2 0.0 copy-start
  54.2 0.0 copy-start.1
  54.2 16.4 %all_to_all.41 = bf16[4,192,1024]{2,1,0:T(8,128)(2,1)S(1)} all-to-all(bf16[4,192,1024]{2,1,0:T(8,128)(2,1)S(1)} %shard_map.85), channel_id=1, replica_groups=mesh['y'=4,'x'=4,'c'=2,'zh'=4,'zl'=4] {'x'}, dimensions={0} | all-to-all | bytes 3145728 | tf_op jit(solution)/shard_map/all_to_all | solution.py:505
  70.6 12.5 %collective-permute-start = (bf16[768,1024]{1,0:T(8,128)(2,1)S(1)}, bf16[768,1024]{1,0:T(8,128)(2,1)S(1)}, u32[]{:S(2)}, u32[]{:S(2)}) collective-permute-start(bf16[768,1024]{1,0:T(8,128)(2,1)S(1)} %bitcast.14), channel_id=1, source_target_pairs={{0,16},{16,0},{1,17},{17,1},{2,18},{18,2},{3,19},{19,3},{4,20},{20... | collective-permute-start | bytes 4718600 | tf_op jit(solution)/shard_map/ppermute | solution.py:528
  83.1 0.0 copy-done
  83.1 0.0 copy-done.1
  83.1 2.8 %shard_map.86 = (f32[768,768]{1,0:T(8,128)S(1)}, f32[1,768,128]{2,1,0:T(8,128)S(1)}, f32[1,768,128]{2,1,0:T(8,128)S(1)}, f32[768,128]{1,0:T(8,128)S(1)}, f32[16,...) custom-call(s32[5]{0:T(128)S(1)} %stack.31.info, s32[32]{0:T(128)S(1)} %copy-done, s32[32]{0:T(128)S(1)} %copy-done.1, ...), custom_call_target="tpu_custom_call" | custom-call | tf_op jit(solution)/shard_map/pallas_call | solution.py:473
  85.9 0.2 collective-permute-done.a_ref
  86.1 3.1 %shard_map.87 = (f32[768,256]{1,0:T(8,128)S(1)}, f32[13824,512]{1,0:T(8,128)}, f32[4,8,128]{2,1,0:T(8,128)S(1)}) custom-call(bf16[768,1024]{1,0:T(8,128)(2,1)S(1)} %collective-permute-done.a_ref, bf16[768,1024]{1,0:T(8,128)(2,1)S(1)} %bitcast.17, f32[16,128]{1,0:T(8,128)S(1)} %get-tuple-element.35.lift_i, f32[1,768,128]{2,1,0:T(8,128)S(1)} %get-tuple-element.36.high_in, ...), custom_call_target="tpu_custom_call" | custom-call | tf_op jit(solution)/shard_map/pallas_call | solution.py:479
  89.2 6.6 %all_to_all.42.got = f32[4,8,128]{2,1,0:T(8,128)S(1)} all-to-all(f32[4,8,128]{2,1,0:T(8,128)S(1)} %get-tuple-element.41), channel_id=1, replica_groups=mesh['y'=4,'x'=4,'c'=2,'zh'=4,'zl'=4] {'x'}, dimensions={0} | all-to-all | bytes 32768 | tf_op jit(solution)/shard_map/all_to_all | solution.py:505
  95.8 2.3 %shard_map.88 = (f32[8,24,128]{2,1,0:T(8,128)S(1)}, f32[6,128]{1,0:T(8,128)S(1)}) custom-call(f32[768,768]{1,0:T(8,128)S(1)} %get-tuple-element.34.k1a_ref, f32[768,256]{1,0:T(8,128)S(1)} %get-tuple-element.39.k1b_ref, f32[13824,512]{1,0:T(8,128)} %get-tuple-element.40.k2_hbm, f32[4,8,128]{2,1,0:T(8,128)S(1)} %all_to_all.42.got, ...), custom_call_target="tpu_custom_call" | custom-call | tf_op jit(solution)/shard_map/pallas_call | solution.py:487
  98.1 8.9 %all_to_all.43.got = f32[8,24,128]{2,1,0:T(8,128)S(1)} all-to-all(f32[8,24,128]{2,1,0:T(8,128)S(1)} %get-tuple-element.43), channel_id=1, replica_groups=mesh['y'=4,'x'=4,'c'=2,'zh'=4,'zl'=4] {'y','c'}, dimensions={0} | all-to-all | bytes 196608 | tf_op jit(solution)/shard_map/all_to_all | solution.py:505
  106.9 2.3 %shard_map.89 = (f32[4,16,128]{2,1,0:T(8,128)S(1)}, f32[12,128]{1,0:T(8,128)S(1)}) custom-call(f32[768,768]{1,0:T(8,128)S(1)} %get-tuple-element.34.k1a_ref, f32[768,256]{1,0:T(8,128)S(1)} %get-tuple-element.39.k1b_ref, f32[13824,512]{1,0:T(8,128)} %get-tuple-element.40.k2_hbm, f32[8,24,128]{2,1,0:T(8,128)S(1)} %all_to_all.43.got, ...), custom_call_target="tpu_custom_call" | custom-call | tf_op jit(solution)/shard_map/pallas_call | solution.py:492
  109.3 6.7 %all_to_all.44.got = f32[4,16,128]{2,1,0:T(8,128)S(1)} all-to-all(f32[4,16,128]{2,1,0:T(8,128)S(1)} %get-tuple-element.44), channel_id=1, replica_groups=mesh['y'=4,'x'=4,'c'=2,'zh'=4,'zl'=4] {'x'}, dimensions={0} | all-to-all | bytes 65536 | tf_op jit(solution)/shard_map/all_to_all | solution.py:505
  115.9 2.3 %shard_map.90 = (f32[8,24,128]{2,1,0:T(8,128)S(1)}, f32[6,128]{1,0:T(8,128)S(1)}) custom-call(f32[768,768]{1,0:T(8,128)S(1)} %get-tuple-element.34.k1a_ref, f32[768,256]{1,0:T(8,128)S(1)} %get-tuple-element.39.k1b_ref, f32[13824,512]{1,0:T(8,128)} %get-tuple-element.40.k2_hbm, f32[4,16,128]{2,1,0:T(8,128)S(1)} %all_to_all.44.got, ...), custom_call_target="tpu_custom_call" | custom-call | tf_op jit(solution)/shard_map/pallas_call | solution.py:497
  118.2 9.3 %all_to_all.45.got = f32[8,24,128]{2,1,0:T(8,128)S(1)} all-to-all(f32[8,24,128]{2,1,0:T(8,128)S(1)} %get-tuple-element.46), channel_id=1, replica_groups=mesh['y'=4,'x'=4,'c'=2,'zh'=4,'zl'=4] {'y','c'}, dimensions={0} | all-to-all | bytes 196608 | tf_op jit(solution)/shard_map/all_to_all | solution.py:505
  127.6 1.8 %shard_map.91 = f32[16,8,128]{2,1,0:T(8,128)S(1)} custom-call(f32[768,768]{1,0:T(8,128)S(1)} %get-tuple-element.34.k1a_ref, f32[768,256]{1,0:T(8,128)S(1)} %get-tuple-element.39.k1b_ref, f32[13824,512]{1,0:T(8,128)} %get-tuple-element.40.k2_hbm, f32[8,24,128]{2,1,0:T(8,128)S(1)} %all_to_all.45.got, f32[16,128]{1,0:T(8,128)S(1)} %get-tuple-element.35.lift_i, ...), custom_call_target="tpu_custom_call" | custom-call | tf_op jit(solution)/shard_map/pallas_call | solution.py:501
  129.3 9.5 %all_to_all.46.got = f32[16,8,128]{2,1,0:T(8,128)S(1)} all-to-all(f32[16,8,128]{2,1,0:T(8,128)S(1)} %shard_map.91), channel_id=1, replica_groups=mesh['y'=4,'x'=4,'c'=2,'zh'=4,'zl'=4] {'x','zl'}, dimensions={0} | all-to-all | bytes 131072 | tf_op jit(solution)/shard_map/all_to_all | solution.py:505
  138.9 0.7 shard_map.92
  139.6 8.9 %all_to_all.47 = f32[8,1,128]{2,1,0:T(1,128)S(1)} all-to-all(f32[8,1,128]{2,1,0:T(1,128)S(1)} %get-tuple-element.54), channel_id=1, replica_groups=mesh['y'=4,'x'=4,'c'=2,'zh'=4,'zl'=4] {'y','c'}, dimensions={0} | all-to-all | bytes 8192 | tf_op jit(solution)/shard_map/all_to_all | solution.py:505
  148.5 0.6 slice_reduce_fusion
Async XLA Ops:
  54.2 28.9 %copy-start = (s32[32]{0:T(128)S(1)}, s32[32]{0:T(128)}, u32[]{:S(2)}) copy-start(s32[32]{0:T(128)} %gen_count.1) | copy-start | bytes 388
  54.2 28.9 %copy-start.1 = (s32[32]{0:T(128)S(1)}, s32[32]{0:T(128)}, u32[]{:S(2)}) copy-start(s32[32]{0:T(128)} %ref_count.1) | copy-start | bytes 388
  70.6 15.5 %collective-permute-start = (bf16[768,1024]{1,0:T(8,128)(2,1)S(1)}, bf16[768,1024]{1,0:T(8,128)(2,1)S(1)}, u32[]{:S(2)}, u32[]{:S(2)}) collective-permute-start(bf16[768,1024]{1,0:T(8,128)(2,1)S(1)} %bitcast.14), channel_id=1, source_target_pairs={{0,16},{16,0},{1,17},{17,1},{2,18},{18,2},{3,19},{19,3},{4,20},{20... | collective-permute-start | bytes 4718600 | tf_op jit(solution)/shard_map/ppermute | solution.py:528
